TPU v7x, 128 devices: a whole 4x4x4 slice. The times are simulated.
128 devices in a mesh: vb: 8 (over z, core), ob: 16 (over x, y).
Axes of the slice: x: 4, y: 4, z: 4, core: 2. Of those that a mesh axis runs over, the one named last changes fastest.
Arguments:
- amplitudes: float32 [768, 8, 6144], P(('vb', 'ob')), may hold values from -6 to 6
- ovov: float32 [8, 6144, 6144], P(None, 'ob', 'vb'), may hold values from -0.109375 to 0.109375
- row_sizes: int32 [8], replicated, may hold values from 192 to 768, as said below
- pair_sizes: int32 [8], replicated, may hold values from 1536 to 6144, as said below
Outputs:
- residual: float32 [768, 8, 6144], P('ob', None, 'vb')
Inputs may be any that keep to these rules, and one draw needn't show every extreme that they name: `row_sizes`: one irrep fills all 768 row slots. `pair_sizes`: multiples of 64; one irrep fills all 6144 slots.
All inputs are finite; a program needn't handle non-finite values.
Results may differ from a plain program's by a relative error of at most 0.0003.
Values sent between devices are 32-bit elements; how exact they have to be, the bound alone decides.
No kernel may reach another device: no remote copies, remote signals or barrier semaphores. Data moves between devices by JAX's collectives and lax.ppermute only.
A program may use at most 192 MiB of HBM per device.

v0:
```python
import jax
import jax.numpy as jnp
from jax import lax
from jax.sharding import PartitionSpec as P


def local(amplitudes, ovov, row_sizes, pair_sizes):
    ob_count = lax.axis_size("ob")
    vb_count = lax.axis_size("vb")
    ob_index = lax.axis_index("ob")
    vb_index = lax.axis_index("vb")
    local_rows = amplitudes.shape[0]
    irrep_count = amplitudes.shape[1]
    stacked = lax.all_gather(amplitudes, "vb", axis=0, tiled=True)
    exchanged = lax.all_to_all(stacked, "ob", split_axis=2, concat_axis=0, tiled=True)
    pair_width = exchanged.shape[2]
    exchanged = exchanged.reshape(ob_count, vb_count, local_rows, irrep_count, pair_width)
    gathered = jnp.transpose(exchanged, (1, 0, 2, 3, 4)).reshape(
        vb_count * ob_count * local_rows, irrep_count, pair_width
    )
    all_rows = gathered.shape[0]
    pair_slice = gathered.shape[2]
    col_slice = ovov.shape[2]
    row_ids = lax.broadcasted_iota(jnp.int32, (all_rows, irrep_count), 0)
    row_live = row_ids < row_sizes[None, :]
    live_amp = jnp.where(row_live[:, :, None], gathered, jnp.zeros_like(gathered))
    pair_ids = ob_index * pair_slice + lax.broadcasted_iota(jnp.int32, (pair_slice,), 0)
    col_ids = vb_index * col_slice + lax.broadcasted_iota(jnp.int32, (col_slice,), 0)
    pair_live = pair_ids[None, :] < pair_sizes[:, None]
    col_live = col_ids[None, :] < pair_sizes[:, None]
    live_ovov = jnp.where(pair_live[:, :, None] & col_live[:, None, :], ovov, jnp.zeros_like(ovov))
    return lax.psum_scatter(
        jnp.einsum(
            "mgp,gpq->mgq",
            live_amp,
            live_ovov,
            precision=lax.Precision.HIGHEST,
            preferred_element_type=jnp.float32,
        ),
        "ob",
        scatter_dimension=0,
        tiled=True,
    )


def solution(mesh):
    placed = (P(("vb", "ob"), None, None), P(None, "ob", "vb"), P(), P())
    return jax.shard_map(
        local, mesh=mesh, in_specs=placed, out_specs=P("ob", None, "vb"), check_vma=False
    )
```

profile of v0, /device:TPU:0, one launch (start us, length us, event | category | flops | bytes accessed | tf_op | source)
XLA Modules:
  0.0 565.8 jit_solution(8897484492636498)
XLA Ops:
  6.5 0.0 all-gather.2.cloned.1.call-start
  6.5 0.7 all-gather.2.cloned.1.call-update
  7.3 58.6 %all-gather.2.cloned.1.call-done = f32[48,8,6144]{2,1,0:T(8,128)} async-done(((f32[6,8,6144]{2,1,0:T(8,128)}), f32[48,8,6144]{2,1,0:T(8,128)}) %all-gather.2.cloned.1.call-update) | async-done | bytes 9437200 | tf_op jit(solution)/shard_map/all_gather | solution.py:14
  65.9 17.4 %copy.27 = f32[48,8,6144]{0,1,2:T(8,128)} copy(f32[48,8,6144]{2,1,0:T(8,128)} %all-gather.2.cloned.1.call-done) | data formatting | bytes 18874368 | tf_op jit(solution)/shard_map/all_gather | solution.py:14
  83.3 26.8 %reshape.81 = f32[16,1,147456]{2,1,0:T(1,128)} reshape(f32[6144,8,48]{2,1,0:T(8,128)} %bitcast.13) | data formatting | bytes 18874368
  110.1 0.0 copy-start
  110.1 0.0 copy-start.1
  110.1 7.0 %all-to-all-start = ((f32[16,1,147456]{2,1,0:T(1,128)}), f32[16,1,147456]{2,1,0:T(1,128)}, u32[]{:S(2)}, u32[]{:S(2)}) async-start(f32[16,1,147456]{2,1,0:T(1,128)} %reshape.81), calls=%async_computation | async-start | bytes 18874368 | tf_op jit(solution)/shard_map/all_to_all | solution.py:15
  117.1 0.0 reduce-scatter.2.cloned.1.call-start
  117.2 0.0 copy-done
  117.2 0.1 broadcast_compare_fusion.1
  117.3 0.1 broadcast_compare_fusion
  117.4 0.0 copy-done.1
  117.4 0.1 iota_compare_fusion
  117.4 162.8 %all-to-all-done = f32[16,1,147456]{2,1,0:T(1,128)} async-done(((f32[16,1,147456]{2,1,0:T(1,128)}), f32[16,1,147456]{2,1,0:T(1,128)}, u32[]{:S(2)}, u32[]{:S(2)}) %all-to-all-start) | async-done | bytes 9437216 | tf_op jit(solution)/shard_map/all_to_all | solution.py:15
  280.2 0.5 broadcast.49
  280.7 28.0 %reduce = f32[16,147456]{1,0:T(8,128)} reduce(f32[16,1,147456]{2,1,0:T(1,128)} %all-to-all-done, f32[]{:T(128)} %broadcast.49), dimensions={1}, to_apply=%all_to_all.11.reduce_sub_computation | reduce | bytes 18874372 | tf_op jit(solution)/shard_map/all_to_all | solution.py:15
  308.7 23.7 %reshape.82 = f32[6144,8,48]{2,1,0:T(8,128)} reshape(f32[16,147456]{1,0:T(8,128)} %reduce) | data formatting | bytes 18874368
  332.5 17.7 %copy.29 = f32[16,48,8,384]{3,2,1,0:T(8,128)} copy(f32[16,48,8,384]{1,2,3,0:T(8,128)} %bitcast.14) | data formatting | bytes 18874368 | tf_op jit(solution)/shard_map/all_to_all | solution.py:15
  350.1 8.2 %copy.30 = f32[8,16,6,8,384]{4,3,2,1,0:T(8,128)} copy(f32[8,16,6,8,384]{4,3,2,0,1:T(8,128)} %bitcast.15) | data formatting | bytes 18874368 | tf_op jit(solution)/shard_map/transpose | solution.py:18
  358.3 4.8 bitcast_select_fusion
  363.1 50.3 %fusion.4 = f32[768,8,768]{0,2,1:T(8,128)} fusion(f32[768,8,384]{2,1,0:T(8,128)S(1)} %bitcast_select_fusion, f32[8,384,768]{2,1,0:T(8,128)} %param.5, pred[8,768]{1,0:T(8,128)(4,1)S(1)} %broadcast_compare_fusion, pred[8,384]{1,0:T(8,128)(4,1)S(1)} %broadcast_compare_fusion.1), kind=kOutput, calls=%fused_computation.5 | convolution fusion | flops 21747990528 | bytes 37757952 | tf_op jit(solution)/shard_map/mgp,gpq->mgq/dot_general | solution.py:33
  413.4 19.4 %copy.33 = f32[768,8,768]{2,1,0:T(8,128)} copy(f32[768,8,768]{0,2,1:T(8,128)} %fusion.4) | data formatting | bytes 37748736 | tf_op jit(solution)/shard_map/mgp,gpq->mgq/transpose | solution.py:33
  432.8 0.0 reduce-scatter.2.cloned.1.call-update
  432.8 126.2 %reduce-scatter.2.cloned.1.call-done = f32[48,8,768]{2,1,0:T(8,128)} async-done(((f32[768,8,768]{2,1,0:T(8,128)}), f32[48,8,768]{2,1,0:T(8,128)}) %reduce-scatter.2.cloned.1.call-update) | async-done | bytes 1179664 | tf_op jit(solution)/shard_map/reduce_scatter | solution.py:32
  (2 shorter events, 0.0 us)
Async XLA Ops:
  6.5 59.3 %all-gather.2.cloned.1.call-start = ((), (), s32[]{:S(2)}) async-start(), calls=%async_computation.2 | async-start | bytes 10616832 | tf_op jit(solution)/shard_map/all_gather | solution.py:14
  110.1 7.1 %copy-start = (s32[8]{0:T(128)S(1)}, s32[8]{0:T(128)}, u32[]{:S(2)}) copy-start(s32[8]{0:T(128)} %param.7) | copy-start | bytes 100
  110.1 7.2 %copy-start.1 = (s32[8]{0:T(128)S(1)}, s32[8]{0:T(128)}, u32[]{:S(2)}) copy-start(s32[8]{0:T(128)} %param.6) | copy-start | bytes 100
  110.1 170.1 %all-to-all-start = ((f32[16,1,147456]{2,1,0:T(1,128)}), f32[16,1,147456]{2,1,0:T(1,128)}, u32[]{:S(2)}, u32[]{:S(2)}) async-start(f32[16,1,147456]{2,1,0:T(1,128)} %reshape.81), calls=%async_computation | async-start | bytes 18874368 | tf_op jit(solution)/shard_map/all_to_all | solution.py:15
  117.1 441.8 %reduce-scatter.2.cloned.1.call-start = ((), (), s32[]{:S(2)}) async-start(), calls=%async_computation.3 | async-start | bytes 20054016 | tf_op jit(solution)/shard_map/reduce_scatter | solution.py:32
Sparse Core Ops, SparseCore 0:
  9.0 56.7 all-gather.1
  432.9 126.0 reduce-scatter.1
where the time goes:
time: 568 us; the launch traced here: 566 us
  waiting for transfers between devices  348 us (61%)
  local copies, waits for them, and re-layouts  114 us (20%)
  matrix products  50.3 us (9%)
  other arithmetic  33 us (6%)
  between operations  13.5 us (2%)
  starting transfers between devices  7.03 us (1%)
    all_to_all x1, waiting for transfers between devices, local(): lax.all_to_all(stacked, 'ob', split_axis=2, concat_axis=0, tiled=True)  163 us
    reduce_scatter x1, waiting for transfers between devices, local(): lax.psum_scatter(jnp.einsum('mgp,gpq->mgq', live_amp, live_ovov, precisio...  126 us
    all_gather x1, waiting for transfers between devices, local(): stacked = lax.all_gather(amplitudes, 'vb', axis=0, tiled=True)  58.6 us
    unnamed x6, local copies, waits for them, and re-layouts  50.5 us
    dot_general x1, matrix products, local(): jnp.einsum('mgp,gpq->mgq', live_amp, live_ovov, precision=lax.Precision.H...  50.3 us
    all_to_all x1, other arithmetic, local(): lax.all_to_all(stacked, 'ob', split_axis=2, concat_axis=0, tiled=True)  28 us
    transpose x1, local copies, waits for them, and re-layouts, local(): jnp.einsum('mgp,gpq->mgq', live_amp, live_ovov, precision=lax.Precision.H...  19.4 us
    all_to_all x2, local copies, waits for them, and re-layouts, local(): lax.all_to_all(stacked, 'ob', split_axis=2, concat_axis=0, tiled=True)  18.2 us
  transfers between devices with their start and end apart: 3, of which 3 were waited for; matrix products, arithmetic and copies ran while one was open for 0% of the time, Pallas kernels for 0%

commit v1 on v0

v1 whole, which is shorter than its diff:
```python
import functools

import jax
import jax.numpy as jnp
from jax import lax
from jax.experimental import pallas as pl
from jax.experimental.pallas import tpu as pltpu
from jax.sharding import PartitionSpec as P

SIDE = 4
VMEM = 48 * 1024 * 1024


def hops(stride, delta):
    pairs = []
    for i in range(SIDE * SIDE):
        d = (i // stride) % SIDE
        pairs.append((i, i + ((d + delta) % SIDE - d) * stride))
    return pairs


def split_kernel(sizes, origin, v_ref, hi_ref, lo_ref):
    g = pl.program_id(0)
    size = sizes[g]
    shape = v_ref.shape[1:]
    p = origin[0] + lax.broadcasted_iota(jnp.int32, shape, 0)
    q = origin[1] + lax.broadcasted_iota(jnp.int32, shape, 1)
    v = jnp.where((p < size) & (q < size), v_ref[0], 0.0)
    hi = v.astype(jnp.bfloat16)
    hi_ref[0] = hi
    lo_ref[0] = (v - hi.astype(jnp.float32)).astype(jnp.bfloat16)


def split_ovov(ovov, pair_sizes, origin):
    g, p, q = ovov.shape
    spec = pl.BlockSpec((1, p, q), lambda i, *_: (i, 0, 0))
    return pl.pallas_call(
        split_kernel,
        grid_spec=pltpu.PrefetchScalarGridSpec(
            num_scalar_prefetch=2, grid=(g,), in_specs=[spec], out_specs=[spec, spec]
        ),
        out_shape=[jax.ShapeDtypeStruct(ovov.shape, jnp.bfloat16)] * 2,
        compiler_params=pltpu.CompilerParams(vmem_limit_bytes=VMEM),
        cost_estimate=pl.CostEstimate(flops=0, bytes_accessed=2 * ovov.size * 4, transcendentals=0),
        name="split_ovov",
    )(pair_sizes, origin, ovov)


def product(a_refs, hi_ref, lo_ref):
    a = jnp.concatenate([r[0, 0, 0] for r in a_refs], axis=0)
    a_hi = a.astype(jnp.bfloat16)
    a_lo = (a - a_hi.astype(jnp.float32)).astype(jnp.bfloat16)
    dot = functools.partial(jnp.dot, preferred_element_type=jnp.float32)
    return dot(a_hi, hi_ref[0]) + (dot(a_lo, hi_ref[0]) + dot(a_hi, lo_ref[0]))


def first_kernel(blocks, a0, a1, a2, a3, hi, lo, out_a, out_b):
    rows = a0.shape[3]
    acc = product((a0, a1, a2, a3), hi, lo)
    for k in range(2):
        out_a[k, 0] = acc[k * rows : (k + 1) * rows]
        out_b[k, 0] = acc[(k + 2) * rows : (k + 3) * rows]


def second_kernel(half, blocks, a0, a1, a2, a3, hi, lo, recv, out):
    rows = a0.shape[3]
    acc = product((a0, a1, a2, a3), hi, lo)
    for k in range(SIDE):
        part = acc[k * rows : (k + 1) * rows]
        if k // 2 == half:
            part = part + recv[k % 2, 0]
        out[k, 0] = part


def third_kernel(blocks, a0, a1, a2, a3, hi, lo, recv_p, recv_m, o0, o1, o2, o3):
    rows = a0.shape[3]
    acc = product((a0, a1, a2, a3), hi, lo)
    for k, out in enumerate((o0, o1, o2, o3)):
        j = blocks[SIDE + k]
        out[0] = acc[k * rows : (k + 1) * rows] + recv_p[j, 0] + recv_m[j, 0]


def chunk_call(kernel, amp, a_first, split, v_first, count, blocks, recvs, outs, name):
    rows, depth = amp.shape[3:]
    hi, lo = split
    cols = hi.shape[2]

    def a_spec(k):
        return pl.BlockSpec(
            (1, 1, 1, rows, depth), lambda g, b: (b[k] // 2, a_first + g, b[k] % 2, 0, 0)
        )

    v_spec = pl.BlockSpec((1, depth, cols), lambda g, b: (v_first + g, 0, 0))

    def io_spec(lead):
        if lead == 0:
            return pl.BlockSpec((1, rows, cols), lambda g, b: (g, 0, 0))
        return pl.BlockSpec((lead, 1, rows, cols), lambda g, b: (0, g, 0, 0))

    def io_shape(lead):
        shape = (count, rows, cols) if lead == 0 else (lead, count, rows, cols)
        return jax.ShapeDtypeStruct(shape, jnp.float32)

    recv_bytes = sum(r.size * 4 for r in recvs)
    return pl.pallas_call(
        kernel,
        grid_spec=pltpu.PrefetchScalarGridSpec(
            num_scalar_prefetch=1,
            grid=(count,),
            in_specs=[a_spec(k) for k in range(SIDE)]
            + [v_spec, v_spec]
            + [io_spec(r.shape[0]) for r in recvs],
            out_specs=[io_spec(lead) for lead in outs],
        ),
        out_shape=[io_shape(lead) for lead in outs],
        compiler_params=pltpu.CompilerParams(vmem_limit_bytes=VMEM),
        cost_estimate=pl.CostEstimate(
            flops=3 * 2 * SIDE * rows * depth * cols * count,
            bytes_accessed=count * (depth * cols * 4 + SIDE * rows * (depth + cols) * 4) + recv_bytes,
            transcendentals=0,
        ),
        name=name,
    )(blocks, amp, amp, amp, amp, hi, lo, *recvs)


def finish_kernel(counts, sizes, origin, *refs):
    out = refs[-1]
    rows, _, cols = out.shape
    row = origin[0] + lax.broadcasted_iota(jnp.int32, (rows, cols), 0)
    at = 0
    for first, count in counts:
        parts = refs[at : at + 4]
        at += 4
        for g in range(count):
            total = (parts[0][g] + parts[1][g]) + (parts[2][g] + parts[3][g])
            out[:, first + g, :] = jnp.where(row < sizes[first + g], total, 0.0)


def finish(groups, row_sizes, origin, shape):
    counts = [(first, parts[0].shape[0]) for first, parts in groups]
    flat = [p for _, parts in groups for p in parts]
    vmem = pl.BlockSpec(memory_space=pltpu.VMEM)
    smem = pl.BlockSpec(memory_space=pltpu.SMEM)
    return pl.pallas_call(
        functools.partial(finish_kernel, counts),
        in_specs=[smem, smem] + [vmem] * len(flat),
        out_specs=vmem,
        out_shape=jax.ShapeDtypeStruct(shape, jnp.float32),
        compiler_params=pltpu.CompilerParams(vmem_limit_bytes=VMEM),
        name="finish",
    )(row_sizes, origin, *flat)


X_HOPS = {d: hops(SIDE, d) for d in (1, 2, -1)}
Y_HOPS = {d: hops(1, d) for d in (1, 2, -1)}


def local(amplitudes, ovov, row_sizes, pair_sizes):
    ob = lax.axis_index("ob")
    vb = lax.axis_index("vb")
    x, y = ob // SIDE, ob % SIDE
    local_rows, irreps, pairs = amplitudes.shape
    obs = lax.axis_size("ob")
    depth, cols = ovov.shape[1:]
    out_rows = local_rows * lax.axis_size("vb")

    origin = jnp.stack([ob * depth, vb * cols]).astype(jnp.int32)
    split = split_ovov(ovov, pair_sizes, origin)

    mine = jnp.transpose(amplitudes.reshape(local_rows, irreps, obs, depth), (2, 0, 1, 3))
    mine = lax.all_to_all(
        mine.reshape(obs, local_rows * irreps, depth), "ob", split_axis=0, concat_axis=0, tiled=True
    )
    mine = jnp.transpose(mine.reshape(obs * local_rows, irreps, depth), (1, 0, 2))

    def dest(axis, delta):
        k = jnp.arange(SIDE, dtype=jnp.int32)
        if axis == "x":
            return ((x + delta) % SIDE) * SIDE + k
        return k * SIDE + (y + delta) % SIDE

    def own(axis):
        other = y if axis == "x" else x
        k = (other + jnp.arange(SIDE, dtype=jnp.int32)) % SIDE
        b = x * SIDE + k if axis == "x" else k * SIDE + y
        return jnp.concatenate([b, k]).astype(jnp.int32)

    chains = []
    for first, size in ((0, 4), (4, 4)):
        gathered = lax.all_gather(mine[first : first + size], "vb", axis=0)
        gathered = gathered.reshape(-1, size, 2, out_rows, depth)
        half = size // 2
        for axis, at in (("x", 0), ("y", half)):
            chains.append((axis, gathered, at, first + at, half))

    groups = []
    for axis, amp, a_first, v_first, count in chains:
        here = X_HOPS if axis == "x" else Y_HOPS
        there = Y_HOPS if axis == "x" else X_HOPS
        call = functools.partial(
            lambda kernel, blocks, recvs, outs, name, a=amp, f=a_first, v=v_first, c=count: chunk_call(
                kernel, a, f, split, v, c, blocks, recvs, outs, name
            )
        )
        far_a, far_b = call(first_kernel, dest(axis, 2), [], [2, 2], f"{axis}_far")
        from_left = lax.ppermute(far_a, "ob", here[1])
        from_right = lax.ppermute(far_b, "ob", here[-1])
        (up,) = call(functools.partial(second_kernel, 0), dest(axis, 1), [from_left], [4], f"{axis}_up")
        (down,) = call(functools.partial(second_kernel, 1), dest(axis, -1), [from_right], [4], f"{axis}_down")
        from_left = lax.ppermute(up, "ob", here[1])
        from_right = lax.ppermute(down, "ob", here[-1])
        parts = call(third_kernel, own(axis), [from_left, from_right], [0, 0, 0, 0], f"{axis}_own")
        groups.append(
            (
                v_first,
                [
                    parts[0],
                    lax.ppermute(parts[1], "ob", there[1]),
                    lax.ppermute(parts[2], "ob", there[2]),
                    lax.ppermute(parts[3], "ob", there[-1]),
                ],
            )
        )
    origin = jnp.stack([ob * out_rows, vb * cols]).astype(jnp.int32)
    return finish(groups, row_sizes, origin, (out_rows, irreps, cols))


def solution(mesh):
    placed = (P(("vb", "ob"), None, None), P(None, "ob", "vb"), P(), P())
    return jax.shard_map(
        local, mesh=mesh, in_specs=placed, out_specs=P("ob", None, "vb"), check_vma=False
    )
```

time: 568 us -> 285 us (0.50)
  waiting for transfers between devices: 348 us -> 103 us
  local copies, waits for them, and re-layouts: 114 us -> 18.6 us
  Pallas kernels: 0 us -> 76 us
  matrix products: 50.3 us -> 0 us
  starting transfers between devices: 7.03 us -> 43.9 us
  other arithmetic: 33 us -> 0.35 us
  blocking collectives: 0 us -> 25.4 us
    all_to_all x1 -> x0, waiting for transfers between devices: 163 us -> none  [local(): lax.all_to_all(stacked, 'ob', split_axis=2, concat_axis=0, tiled=True)]
    reduce_scatter x1 -> x0, waiting for transfers between devices: 126 us -> none  [local(): lax.psum_scatter(jnp.einsum('mgp,gpq->mgq', live_amp, live_ovov, precisio...]
    pallas_call x0 -> x18, Pallas kernels: none -> 76 us  [the longest x16 63.8 us: chunk_call(): pl.pallas_call(kernel, grid_spec=pltpu.PrefetchScalarGridSpec(num_scalar_...]
    ppermute x0 -> x28, waiting for transfers between devices: none -> 65.6 us  [the longest x4 28.9 us: local(): from_left = lax.ppermute(far_a, 'ob', here[1])]
    dot_general x1 -> x0, matrix products: 50.3 us -> none  [local(): jnp.einsum('mgp,gpq->mgq', live_amp, live_ovov, precision=lax.Precision.H...]
    ppermute x0 -> x28, starting transfers between devices: none -> 43.8 us  [the longest x4 10.6 us: local(): from_right = lax.ppermute(down, 'ob', here[-1])]
    unnamed x6 -> x39, local copies, waits for them, and re-layouts: 50.5 us -> 16.3 us
    all_to_all x1 -> x0, other arithmetic: 28 us -> none  [local(): lax.all_to_all(stacked, 'ob', split_axis=2, concat_axis=0, tiled=True)]
  transfers between devices with their start and end apart: 3 -> 30, of which waited for: 3 -> 11; matrix products, arithmetic and copies ran while one was open for 0% -> 0% of each run, Pallas kernels for 0% -> 26%
where the time goes in v1:
time: 285 us; the launch traced here: 281 us
  waiting for transfers between devices  103 us (36%)
  Pallas kernels  76 us (27%)
  starting transfers between devices  43.9 us (15%)
  blocking collectives  25.4 us (9%)
  local copies, waits for them, and re-layouts  18.6 us (7%)
  between operations  13.6 us (5%)
    pallas_call x16, Pallas kernels, chunk_call(): pl.pallas_call(kernel, grid_spec=pltpu.PrefetchScalarGridSpec(num_scalar_...  63.8 us
    all_gather x2, waiting for transfers between devices, local(): gathered = lax.all_gather(mine[first:first + size], 'vb', axis=0)  37.8 us
    ppermute x4, waiting for transfers between devices, local(): from_left = lax.ppermute(far_a, 'ob', here[1])  28.9 us
    ppermute x4, waiting for transfers between devices, local(): from_right = lax.ppermute(down, 'ob', here[-1])  27.8 us
    all_to_all x1, blocking collectives, local(): lax.all_to_all(mine.reshape(obs, local_rows * irreps, depth), 'ob', split...  25.4 us
    unnamed x39, local copies, waits for them, and re-layouts  16.3 us
    ppermute x4, starting transfers between devices, local(): from_right = lax.ppermute(down, 'ob', here[-1])  10.6 us
    ppermute x4, starting transfers between devices, local(): lax.ppermute(parts[2], 'ob', there[2])  10.1 us
  transfers between devices with their start and end apart: 30, of which 11 were waited for; matrix products, arithmetic and copies ran while one was open for 0% of the time, Pallas kernels for 26%

profile of v1, /device:TPU:0, one launch (start us, length us, event | category | flops | bytes accessed | tf_op | source)
XLA Modules:
  0.0 281.3 jit_solution(6871890323194827158)
XLA Ops:
  8.4 25.4 %all_to_all.5 = f32[16,48,384]{2,1,0:T(8,128)S(1)} all-to-all(f32[16,48,384]{2,1,0:T(8,128)S(1)} %bitcast.87), channel_id=1, replica_groups=mesh['vb'=8,'ob'=16] {'ob'}, dimensions={0} | all-to-all | bytes 2359296 | tf_op jit(solution)/shard_map/all_to_all | solution.py:171
  35.9 9.4 %split_ovov.1 = (bf16[8,384,768]{2,1,0:T(8,128)(2,1)S(1)}, bf16[8,384,768]{2,1,0:T(8,128)(2,1)}) custom-call(s32[8]{0:T(128)S(1)} %copy-done.14, s32[2]{0:T(128)S(1)} %pad_add_fusion.2.origin, f32[8,384,768]{2,1,0:T(8,128)} %v_ref.1), custom_call_target="tpu_custom_call" | custom-call | bytes 18874368 | tf_op jit(solution)/shard_map/split_ovov/pallas_call | solution.py:37
  45.2 2.1 copy-done.3
  47.4 21.2 %all-gather.5.cloned.1.call-done = f32[32,96,384]{2,1,0:T(8,128)} async-done(((f32[4,96,384]{2,1,0:T(8,128)}), f32[32,96,384]{2,1,0:T(8,128)}) %all-gather.5.cloned.1.call-update) | async-done | bytes 4718608 | tf_op jit(solution)/shard_map/all_gather | solution.py:190
  68.5 2.3 copy-done.1
  70.9 3.8 %x_far.2 = (f32[2,2,48,768]{3,2,1,0:T(8,128)}, f32[2,2,48,768]{3,2,1,0:T(8,128)S(1)}) custom-call(s32[4]{0:T(128)S(1)} %iota_add_fusion.1.blocks, f32[8,4,2,48,384]{4,3,2,1,0:T(8,128)S(1)} %bitcast.78, f32[8,4,2,48,384]{4,3,2,1,0:T(8,128)S(1)} %bitcast.79, f32[8,4,2,48,384]{4,3,2,1,0:T(8,128)S(1)} %bitcast.80, f32[8,4,2,48,384]{4,3,2,1,0:T(8,128)S(1)} %bitcast.81, ...), custom_call_target="tpu_custom_call" | custom-call | flops 679477248 | bytes 4128768 | tf_op jit(solution)/shard_map/x_far/pallas_call | solution.py:105
  76.1 1.8 collective-permute-start.2
  77.9 2.7 copy-done.2
  80.5 3.8 %y_far.2 = (f32[2,2,48,768]{3,2,1,0:T(8,128)}, f32[2,2,48,768]{3,2,1,0:T(8,128)S(1)}) custom-call(s32[4]{0:T(128)S(1)} %fusion.3.blocks, f32[8,4,2,48,384]{4,3,2,1,0:T(8,128)S(1)} %bitcast.82, f32[8,4,2,48,384]{4,3,2,1,0:T(8,128)S(1)} %bitcast.83, f32[8,4,2,48,384]{4,3,2,1,0:T(8,128)S(1)} %bitcast.84, f32[8,4,2,48,384]{4,3,2,1,0:T(8,128)S(1)} %bitcast.85, ...), custom_call_target="tpu_custom_call" | custom-call | flops 679477248 | bytes 4128768 | tf_op jit(solution)/shard_map/y_far/pallas_call | solution.py:105
  84.3 1.5 collective-permute-start.7
  85.8 2.1 collective-permute-start.9
  87.9 16.7 %all-gather.7.cloned.1.call-done = f32[32,96,384]{2,1,0:T(8,128)} async-done(((f32[4,96,384]{2,1,0:T(8,128)}), f32[32,96,384]{2,1,0:T(8,128)}) %all-gather.7.cloned.1.call-update) | async-done | bytes 4718608 | tf_op jit(solution)/shard_map/all_gather | solution.py:190
  104.6 2.3 copy-done
  106.9 3.9 %x_far.3 = (f32[2,2,48,768]{3,2,1,0:T(8,128)}, f32[2,2,48,768]{3,2,1,0:T(8,128)}) custom-call(s32[4]{0:T(128)S(1)} %iota_add_fusion.1.blocks, f32[8,4,2,48,384]{4,3,2,1,0:T(8,128)S(1)} %bitcast.44, f32[8,4,2,48,384]{4,3,2,1,0:T(8,128)S(1)} %bitcast.45, f32[8,4,2,48,384]{4,3,2,1,0:T(8,128)S(1)} %bitcast.46, f32[8,4,2,48,384]{4,3,2,1,0:T(8,128)S(1)} %bitcast.47, ...), custom_call_target="tpu_custom_call" | custom-call | flops 679477248 | bytes 4128768 | tf_op jit(solution)/shard_map/x_far/pallas_call | solution.py:105
  112.3 1.8 collective-permute-start.16
  114.0 4.1 %x_up.2 = f32[4,2,48,768]{3,2,1,0:T(8,128)} custom-call(s32[4]{0:T(128)S(1)} %iota_add_fusion.2.blocks, f32[8,4,2,48,384]{4,3,2,1,0:T(8,128)} %bitcast.54, f32[8,4,2,48,384]{4,3,2,1,0:T(8,128)} %bitcast.55, f32[8,4,2,48,384]{4,3,2,1,0:T(8,128)} %bitcast.56, f32[8,4,2,48,384]{4,3,2,1,0:T(8,128)} %bitcast.57, bf16[8,384,768]{2,1,0:T(8,128)(2,1)} %copy-done.3, ...), custom_call_target="tpu_custom_call" | custom-call | flops 679477248 | bytes 4718592 | tf_op jit(solution)/shard_map/x_up/pallas_call | solution.py:105
  118.5 4.4 %x_down.2 = f32[4,2,48,768]{3,2,1,0:T(8,128)} custom-call(s32[4]{0:T(128)S(1)} %iota_add_fusion.blocks, f32[8,4,2,48,384]{4,3,2,1,0:T(8,128)} %bitcast.61, f32[8,4,2,48,384]{4,3,2,1,0:T(8,128)} %bitcast.59, f32[8,4,2,48,384]{4,3,2,1,0:T(8,128)} %bitcast.60, f32[8,4,2,48,384]{4,3,2,1,0:T(8,128)} %bitcast.58, bf16[8,384,768]{2,1,0:T(8,128)(2,1)} %copy-done.3, ...), custom_call_target="tpu_custom_call" | custom-call | flops 679477248 | bytes 4718592 | tf_op jit(solution)/shard_map/x_down/pallas_call | solution.py:105
  123.7 3.0 %collective-permute-start.3 = (f32[4,2,48,768]{3,2,1,0:T(8,128)}, f32[4,2,48,768]{3,2,1,0:T(8,128)S(1)}, u32[]{:S(2)}, u32[]{:S(2)}) collective-permute-start(f32[4,2,48,768]{3,2,1,0:T(8,128)} %x_down.2), channel_id=1, source_target_pairs={{0,12},{1,13},{2,14},{3,15},{4,0},{5,1},{6,2},{7,3},{8,4},{9,5},{1... | collective-permute-start | bytes 3538952 | tf_op jit(solution)/shard_map/ppermute | solution.py:211
  127.7 4.1 %y_up.2 = f32[4,2,48,768]{3,2,1,0:T(8,128)} custom-call(s32[4]{0:T(128)S(1)} %fusion.4.blocks, f32[8,4,2,48,384]{4,3,2,1,0:T(8,128)} %bitcast.62, f32[8,4,2,48,384]{4,3,2,1,0:T(8,128)} %bitcast.63, f32[8,4,2,48,384]{4,3,2,1,0:T(8,128)} %bitcast.64, f32[8,4,2,48,384]{4,3,2,1,0:T(8,128)} %bitcast.65, bf16[8,384,768]{2,1,0:T(8,128)(2,1)} %copy-done.3, ...), custom_call_target="tpu_custom_call" | custom-call | flops 679477248 | bytes 4718592 | tf_op jit(solution)/shard_map/y_up/pallas_call | solution.py:105
  132.7 1.5 collective-permute-start.8
  134.2 3.1 %y_far.3 = (f32[2,2,48,768]{3,2,1,0:T(8,128)S(1)}, f32[2,2,48,768]{3,2,1,0:T(8,128)S(1)}) custom-call(s32[4]{0:T(128)S(1)} %fusion.3.blocks, f32[8,4,2,48,384]{4,3,2,1,0:T(8,128)S(1)} %bitcast.50, f32[8,4,2,48,384]{4,3,2,1,0:T(8,128)S(1)} %bitcast.51, f32[8,4,2,48,384]{4,3,2,1,0:T(8,128)S(1)} %bitcast.52, f32[8,4,2,48,384]{4,3,2,1,0:T(8,128)S(1)} %bitcast.53, ...), custom_call_target="tpu_custom_call" | custom-call | flops 679477248 | bytes 4128768 | tf_op jit(solution)/shard_map/y_far/pallas_call | solution.py:105
  137.4 1.6 collective-permute-start.21
  139.0 1.7 collective-permute-start.23
  140.7 4.2 %x_up.3 = f32[4,2,48,768]{3,2,1,0:T(8,128)} custom-call(s32[4]{0:T(128)S(1)} %iota_add_fusion.2.blocks, f32[8,4,2,48,384]{4,3,2,1,0:T(8,128)} %bitcast.20, f32[8,4,2,48,384]{4,3,2,1,0:T(8,128)} %bitcast.21, f32[8,4,2,48,384]{4,3,2,1,0:T(8,128)} %bitcast.22, f32[8,4,2,48,384]{4,3,2,1,0:T(8,128)} %bitcast.23, bf16[8,384,768]{2,1,0:T(8,128)(2,1)} %copy-done.3, ...), custom_call_target="tpu_custom_call" | custom-call | flops 679477248 | bytes 4718592 | tf_op jit(solution)/shard_map/x_up/pallas_call | solution.py:105
  144.9 28.9 %collective-permute-done.21.recv = f32[2,2,48,768]{3,2,1,0:T(8,128)S(1)} collective-permute-done((f32[2,2,48,768]{3,2,1,0:T(8,128)S(1)}, f32[2,2,48,768]{3,2,1,0:T(8,128)S(1)}, u32[]{:S(2)}, u32[]{:S(2)}) %collective-permute-start.21) | collective-permute-done | bytes 589856 | tf_op jit(solution)/shard_map/ppermute | solution.py:206
  173.8 4.2 %x_down.3 = f32[4,2,48,768]{3,2,1,0:T(8,128)} custom-call(s32[4]{0:T(128)S(1)} %iota_add_fusion.blocks, f32[8,4,2,48,384]{4,3,2,1,0:T(8,128)} %bitcast.27, f32[8,4,2,48,384]{4,3,2,1,0:T(8,128)} %bitcast.25, f32[8,4,2,48,384]{4,3,2,1,0:T(8,128)} %bitcast.26, f32[8,4,2,48,384]{4,3,2,1,0:T(8,128)} %bitcast.24, bf16[8,384,768]{2,1,0:T(8,128)(2,1)} %copy-done.3, ...), custom_call_target="tpu_custom_call" | custom-call | flops 679477248 | bytes 4718592 | tf_op jit(solution)/shard_map/x_down/pallas_call | solution.py:105
  178.9 3.2 %collective-permute-start.17 = (f32[4,2,48,768]{3,2,1,0:T(8,128)}, f32[4,2,48,768]{3,2,1,0:T(8,128)}, u32[]{:S(2)}, u32[]{:S(2)}) collective-permute-start(f32[4,2,48,768]{3,2,1,0:T(8,128)} %x_down.3), channel_id=1, source_target_pairs={{0,12},{1,13},{2,14},{3,15},{4,0},{5,1},{6,2},{7,3},{8,4},{9,5},{1... | collective-permute-start | bytes 3538952 | tf_op jit(solution)/shard_map/ppermute | solution.py:211
  183.2 4.1 %y_down.2 = f32[4,2,48,768]{3,2,1,0:T(8,128)} custom-call(s32[4]{0:T(128)S(1)} %fusion.2.blocks, f32[8,4,2,48,384]{4,3,2,1,0:T(8,128)} %bitcast.66, f32[8,4,2,48,384]{4,3,2,1,0:T(8,128)} %bitcast.67, f32[8,4,2,48,384]{4,3,2,1,0:T(8,128)} %bitcast.68, f32[8,4,2,48,384]{4,3,2,1,0:T(8,128)} %bitcast.69, bf16[8,384,768]{2,1,0:T(8,128)(2,1)} %copy-done.3, ...), custom_call_target="tpu_custom_call" | custom-call | flops 679477248 | bytes 4718592 | tf_op jit(solution)/shard_map/y_down/pallas_call | solution.py:105
  187.3 1.6 collective-permute-start.10
  188.9 4.1 %y_up.3 = f32[4,2,48,768]{3,2,1,0:T(8,128)} custom-call(s32[4]{0:T(128)S(1)} %fusion.4.blocks, f32[8,4,2,48,384]{4,3,2,1,0:T(8,128)} %bitcast.28, f32[8,4,2,48,384]{4,3,2,1,0:T(8,128)} %bitcast.29, f32[8,4,2,48,384]{4,3,2,1,0:T(8,128)} %bitcast.30, f32[8,4,2,48,384]{4,3,2,1,0:T(8,128)} %bitcast.31, bf16[8,384,768]{2,1,0:T(8,128)(2,1)} %copy-done.3, ...), custom_call_target="tpu_custom_call" | custom-call | flops 679477248 | bytes 4718592 | tf_op jit(solution)/shard_map/y_up/pallas_call | solution.py:105
  193.6 4.2 %y_down.3 = f32[4,2,48,768]{3,2,1,0:T(8,128)} custom-call(s32[4]{0:T(128)S(1)} %fusion.2.blocks, f32[8,4,2,48,384]{4,3,2,1,0:T(8,128)} %bitcast.32, f32[8,4,2,48,384]{4,3,2,1,0:T(8,128)} %bitcast.33, f32[8,4,2,48,384]{4,3,2,1,0:T(8,128)} %bitcast.34, f32[8,4,2,48,384]{4,3,2,1,0:T(8,128)} %bitcast.35, bf16[8,384,768]{2,1,0:T(8,128)(2,1)} %copy-done.3, ...), custom_call_target="tpu_custom_call" | custom-call | flops 679477248 | bytes 4718592 | tf_op jit(solution)/shard_map/y_down/pallas_call | solution.py:105
  197.8 2.8 collective-permute-start.24
  200.7 3.3 %x_own.2 = (f32[2,48,768]{2,1,0:T(8,128)S(1)}, f32[2,48,768]{2,1,0:T(8,128)S(1)}, f32[2,48,768]{2,1,0:T(8,128)S(1)}, f32[2,48,768]{2,1,0:T(8,128)S(1)}) custom-call(s32[8]{0:T(128)S(1)} %pad_add_fusion.1.blocks, f32[8,4,2,48,384]{4,3,2,1,0:T(8,128)} %bitcast.70, f32[8,4,2,48,384]{4,3,2,1,0:T(8,128)} %bitcast.71, f32[8,4,2,48,384]{4,3,2,1,0:T(8,128)} %bitcast.72, ...), custom_call_target="tpu_custom_call" | custom-call | flops 679477248 | bytes 6488064 | tf_op jit(solution)/shard_map/x_own/pallas_call | solution.py:105
  205.7 1.8 collective-permute-start.5
  207.6 4.5 %x_own.3 = (f32[2,48,768]{2,1,0:T(8,128)S(1)}, f32[2,48,768]{2,1,0:T(8,128)S(1)}, f32[2,48,768]{2,1,0:T(8,128)}, f32[2,48,768]{2,1,0:T(8,128)}) custom-call(s32[8]{0:T(128)S(1)} %pad_add_fusion.1.blocks, f32[8,4,2,48,384]{4,3,2,1,0:T(8,128)} %bitcast.36, f32[8,4,2,48,384]{4,3,2,1,0:T(8,128)} %bitcast.37, f32[8,4,2,48,384]{4,3,2,1,0:T(8,128)} %bitcast.38, ...), custom_call_target="tpu_custom_call" | custom-call | flops 679477248 | bytes 6488064 | tf_op jit(solution)/shard_map/x_own/pallas_call | solution.py:105
  212.1 4.5 %collective-permute-done.10.recv_m = f32[4,2,48,768]{3,2,1,0:T(8,128)} collective-permute-done((f32[4,2,48,768]{3,2,1,0:T(8,128)}, f32[4,2,48,768]{3,2,1,0:T(8,128)}, u32[]{:S(2)}, u32[]{:S(2)}) %collective-permute-start.10) | collective-permute-done | bytes 1179680 | tf_op jit(solution)/shard_map/ppermute | solution.py:211
  216.6 2.7 collective-permute-start.6
  219.3 3.5 %y_own.2 = (f32[2,48,768]{2,1,0:T(8,128)S(1)}, f32[2,48,768]{2,1,0:T(8,128)S(1)}, f32[2,48,768]{2,1,0:T(8,128)S(1)}, f32[2,48,768]{2,1,0:T(8,128)S(1)}) custom-call(s32[8]{0:T(128)S(1)} %pad_add_fusion.3.blocks, f32[8,4,2,48,384]{4,3,2,1,0:T(8,128)} %bitcast.74, f32[8,4,2,48,384]{4,3,2,1,0:T(8,128)} %bitcast.75, f32[8,4,2,48,384]{4,3,2,1,0:T(8,128)} %bitcast.76, ...), custom_call_target="tpu_custom_call" | custom-call | flops 679477248 | bytes 6488064 | tf_op jit(solution)/shard_map/y_own/pallas_call | solution.py:105
  222.9 1.6 collective-permute-done.22.recv_p
  224.5 22.2 %collective-permute-done.24.recv_m = f32[4,2,48,768]{3,2,1,0:T(8,128)} collective-permute-done((f32[4,2,48,768]{3,2,1,0:T(8,128)}, f32[4,2,48,768]{3,2,1,0:T(8,128)}, u32[]{:S(2)}, u32[]{:S(2)}) %collective-permute-start.24) | collective-permute-done | bytes 1179680 | tf_op jit(solution)/shard_map/ppermute | solution.py:211
  246.7 1.6 collective-permute-start.13
  249.2 4.5 %y_own.3 = (f32[2,48,768]{2,1,0:T(8,128)S(1)}, f32[2,48,768]{2,1,0:T(8,128)}, f32[2,48,768]{2,1,0:T(8,128)}, f32[2,48,768]{2,1,0:T(8,128)}) custom-call(s32[8]{0:T(128)S(1)} %pad_add_fusion.3.blocks, f32[8,4,2,48,384]{4,3,2,1,0:T(8,128)} %bitcast.40, f32[8,4,2,48,384]{4,3,2,1,0:T(8,128)} %bitcast.41, f32[8,4,2,48,384]{4,3,2,1,0:T(8,128)} %bitcast.42, ...), custom_call_target="tpu_custom_call" | custom-call | flops 679477248 | bytes 6488064 | tf_op jit(solution)/shard_map/y_own/pallas_call | solution.py:105
  253.7 4.8 %collective-permute-start.19 = (f32[2,48,768]{2,1,0:T(8,128)}, f32[2,48,768]{2,1,0:T(8,128)S(1)}, u32[]{:S(2)}, u32[]{:S(2)}) collective-permute-start(f32[2,48,768]{2,1,0:T(8,128)} %get-tuple-element.49), channel_id=1, source_target_pairs={{0,2},{1,3},{2,0},{3,1},{4,6},{5,7},{6,4},{7,5},{8,10},{9,11},{10,... | collective-permute-start | bytes 884744 | tf_op jit(solution)/shard_map/ppermute | solution.py:219
  258.7 3.5 %collective-permute-start.26 = (f32[2,48,768]{2,1,0:T(8,128)}, f32[2,48,768]{2,1,0:T(8,128)}, u32[]{:S(2)}, u32[]{:S(2)}) collective-permute-start(f32[2,48,768]{2,1,0:T(8,128)} %get-tuple-element.55), channel_id=1, source_target_pairs={{0,8},{1,9},{2,10},{3,11},{4,12},{5,13},{6,14},{7,15},{8,0},{9,1},... | collective-permute-start | bytes 884744 | tf_op jit(solution)/shard_map/ppermute | solution.py:219
  262.2 2.0 collective-permute-start.27
  264.3 1.8 collective-permute-done.20.refs_11_
  266.8 3.6 %collective-permute-done.26.refs_14_ = f32[2,48,768]{2,1,0:T(8,128)} collective-permute-done((f32[2,48,768]{2,1,0:T(8,128)}, f32[2,48,768]{2,1,0:T(8,128)}, u32[]{:S(2)}, u32[]{:S(2)}) %collective-permute-start.26) | collective-permute-done | bytes 294944 | tf_op jit(solution)/shard_map/ppermute | solution.py:219
  271.6 2.8 %finish.1 = f32[48,8,768]{2,1,0:T(8,128)} custom-call(s32[8]{0:T(128)S(1)} %copy-done.15, s32[2]{0:T(128)S(1)} %pad_add_fusion.origin, f32[2,48,768]{2,1,0:T(8,128)S(1)} %copy-done.13, f32[2,48,768]{2,1,0:T(8,128)S(1)} %collective-permute-done.4.refs_1_, f32[2,48,768]{2,1,0:T(8,128)S(1)} %collective-permute-done.5.refs_2_, ...), custom_call_target="tpu_custom_call" | custom-call | tf_op jit(solution)/shard_map/finish/pallas_call | solution.py:144
  (89 shorter events, 17.5 us)
Async XLA Ops:
  6.5 62.0 %all-gather.5.cloned.1.call-start = ((), (), s32[]{:S(2)}) async-start(), calls=%async_computation.1 | async-start | bytes 5308416 | tf_op jit(solution)/shard_map/all_gather | solution.py:190
  34.8 1.1 copy-start.14
  34.8 69.8 %all-gather.7.cloned.1.call-start = ((), (), s32[]{:S(2)}) async-start(), calls=%async_computation.2 | async-start | bytes 5308416 | tf_op jit(solution)/shard_map/all_gather | solution.py:190
  45.2 2.1 copy-start.3
  68.5 2.3 copy-start.1
  74.6 37.6 %collective-permute-start = (f32[2,2,48,768]{3,2,1,0:T(8,128)}, f32[2,2,48,768]{3,2,1,0:T(8,128)S(1)}, u32[]{:S(2)}, u32[]{:S(2)}) collective-permute-start(f32[2,2,48,768]{3,2,1,0:T(8,128)} %get-tuple-element.33), channel_id=1, source_target_pairs={{0,4},{1,5},{2,6},{3,7},{4,8},{5,9},{6,10},{7,11},{8,12},{9,13},{1... | collective-permute-start | bytes 1769480 | tf_op jit(solution)/shard_map/ppermute | solution.py:206
  76.1 42.1 %collective-permute-start.2 = (f32[2,2,48,768]{3,2,1,0:T(8,128)S(1)}, f32[2,2,48,768]{3,2,1,0:T(8,128)S(1)}, u32[]{:S(2)}, u32[]{:S(2)}) collective-permute-start(f32[2,2,48,768]{3,2,1,0:T(8,128)S(1)} %get-tuple-element.34), channel_id=1, source_target_pairs={{0,12},{1,13},{2,14},{3,15},{4,0},{5,1},{6,2},{7,3},{8,4},{9,5},{1... | collective-permute-start | bytes 1769480 | tf_op jit(solution)/shard_map/ppermute | solution.py:207
  77.9 2.7 copy-start.2
  84.3 1.5 copy-start.16
  84.3 38.5 %collective-permute-start.7 = (f32[2,2,48,768]{3,2,1,0:T(8,128)}, f32[2,2,48,768]{3,2,1,0:T(8,128)S(1)}, u32[]{:S(2)}, u32[]{:S(2)}) collective-permute-start(f32[2,2,48,768]{3,2,1,0:T(8,128)} %get-tuple-element.39), channel_id=1, source_target_pairs={{0,1},{1,2},{2,3},{3,0},{4,5},{5,6},{6,7},{7,4},{8,9},{9,10},{10,1... | collective-permute-start | bytes 1769480 | tf_op jit(solution)/shard_map/ppermute | solution.py:206
  85.8 46.0 %collective-permute-start.9 = (f32[2,2,48,768]{3,2,1,0:T(8,128)}, f32[2,2,48,768]{3,2,1,0:T(8,128)S(1)}, u32[]{:S(2)}, u32[]{:S(2)}) collective-permute-start(f32[2,2,48,768]{3,2,1,0:T(8,128)} %copy-done.16), channel_id=1, source_target_pairs={{0,3},{1,0},{2,1},{3,2},{4,7},{5,4},{6,5},{7,6},{8,11},{9,8},{10,9... | collective-permute-start | bytes 1769480 | tf_op jit(solution)/shard_map/ppermute | solution.py:207
  104.6 2.3 copy-start
  110.8 26.6 %collective-permute-start.14 = (f32[2,2,48,768]{3,2,1,0:T(8,128)}, f32[2,2,48,768]{3,2,1,0:T(8,128)}, u32[]{:S(2)}, u32[]{:S(2)}) collective-permute-start(f32[2,2,48,768]{3,2,1,0:T(8,128)} %get-tuple-element.45), channel_id=1, source_target_pairs={{0,4},{1,5},{2,6},{3,7},{4,8},{5,9},{6,10},{7,11},{8,12},{9,13},{1... | collective-permute-start | bytes 1769480 | tf_op jit(solution)/shard_map/ppermute | solution.py:206
  112.3 26.7 %collective-permute-start.16 = (f32[2,2,48,768]{3,2,1,0:T(8,128)}, f32[2,2,48,768]{3,2,1,0:T(8,128)}, u32[]{:S(2)}, u32[]{:S(2)}) collective-permute-start(f32[2,2,48,768]{3,2,1,0:T(8,128)} %get-tuple-element.46), channel_id=1, source_target_pairs={{0,12},{1,13},{2,14},{3,15},{4,0},{5,1},{6,2},{7,3},{8,4},{9,5},{1... | collective-permute-start | bytes 1769480 | tf_op jit(solution)/shard_map/ppermute | solution.py:207
  118.2 69.2 %collective-permute-start.1 = (f32[4,2,48,768]{3,2,1,0:T(8,128)}, f32[4,2,48,768]{3,2,1,0:T(8,128)S(1)}, u32[]{:S(2)}, u32[]{:S(2)}) collective-permute-start(f32[4,2,48,768]{3,2,1,0:T(8,128)} %x_up.2), channel_id=1, source_target_pairs={{0,4},{1,5},{2,6},{3,7},{4,8},{5,9},{6,10},{7,11},{8,12},{9,13},{1... | collective-permute-start | bytes 3538952 | tf_op jit(solution)/shard_map/ppermute | solution.py:210
  118.5 15.7 %slice-start = ((s8[4718592]{0:T(1024)(128)(4,1)}), s8[4194304]{0:T(1024)(128)(4,1)S(1)}, s32[]{:S(2)}) async-start(s8[4718592]{0:T(1024)(128)(4,1)} %bitcast.48), calls=%async_computation.3 | async-start | bytes 8388608
  122.9 11.4 %slice-start.1 = ((s8[4718592]{0:T(1024)(128)(4,1)}), s8[524288]{0:T(1024)(128)(4,1)S(1)}, s32[]{:S(2)}) async-start(s8[4718592]{0:T(1024)(128)(4,1)} %bitcast.48), calls=%async_computation.4 | async-start | bytes 1048576
  122.9 0.8 copy-start.6
  123.7 69.3 %collective-permute-start.3 = (f32[4,2,48,768]{3,2,1,0:T(8,128)}, f32[4,2,48,768]{3,2,1,0:T(8,128)S(1)}, u32[]{:S(2)}, u32[]{:S(2)}) collective-permute-start(f32[4,2,48,768]{3,2,1,0:T(8,128)} %x_down.2), channel_id=1, source_target_pairs={{0,12},{1,13},{2,14},{3,15},{4,0},{5,1},{6,2},{7,3},{8,4},{9,5},{1... | collective-permute-start | bytes 3538952 | tf_op jit(solution)/shard_map/ppermute | solution.py:211
  126.7 1.1 copy-start.7
  131.9 0.9 copy-start.4
  132.7 65.0 %collective-permute-start.8 = (f32[4,2,48,768]{3,2,1,0:T(8,128)}, f32[4,2,48,768]{3,2,1,0:T(8,128)S(1)}, u32[]{:S(2)}, u32[]{:S(2)}) collective-permute-start(f32[4,2,48,768]{3,2,1,0:T(8,128)} %y_up.2), channel_id=1, source_target_pairs={{0,1},{1,2},{2,3},{3,0},{4,5},{5,6},{6,7},{7,4},{8,9},{9,10},{10,1... | collective-permute-start | bytes 3538952 | tf_op jit(solution)/shard_map/ppermute | solution.py:210
  137.4 36.4 %collective-permute-start.21 = (f32[2,2,48,768]{3,2,1,0:T(8,128)S(1)}, f32[2,2,48,768]{3,2,1,0:T(8,128)S(1)}, u32[]{:S(2)}, u32[]{:S(2)}) collective-permute-start(f32[2,2,48,768]{3,2,1,0:T(8,128)S(1)} %get-tuple-element.51), channel_id=1, source_target_pairs={{0,1},{1,2},{2,3},{3,0},{4,5},{5,6},{6,7},{7,4},{8,9},{9,10},{10,1... | collective-permute-start | bytes 1769480 | tf_op jit(solution)/shard_map/ppermute | solution.py:206
  139.0 39.1 %collective-permute-start.23 = (f32[2,2,48,768]{3,2,1,0:T(8,128)S(1)}, f32[2,2,48,768]{3,2,1,0:T(8,128)S(1)}, u32[]{:S(2)}, u32[]{:S(2)}) collective-permute-start(f32[2,2,48,768]{3,2,1,0:T(8,128)S(1)} %get-tuple-element.52), channel_id=1, source_target_pairs={{0,3},{1,0},{2,1},{3,2},{4,7},{5,4},{6,5},{7,6},{8,11},{9,8},{10,9... | collective-permute-start | bytes 1769480 | tf_op jit(solution)/shard_map/ppermute | solution.py:207
  173.8 4.2 %copy-start.10 = (f32[2,2,48,768]{3,2,1,0:T(8,128)}, f32[2,2,48,768]{3,2,1,0:T(8,128)S(1)}, u32[]{:S(2)}) copy-start(f32[2,2,48,768]{3,2,1,0:T(8,128)S(1)} %collective-permute-done.21.recv) | copy-start | bytes 1769476
  173.8 30.9 %collective-permute-start.15 = (f32[4,2,48,768]{3,2,1,0:T(8,128)}, f32[4,2,48,768]{3,2,1,0:T(8,128)}, u32[]{:S(2)}, u32[]{:S(2)}) collective-permute-start(f32[4,2,48,768]{3,2,1,0:T(8,128)} %x_up.3), channel_id=1, source_target_pairs={{0,4},{1,5},{2,6},{3,7},{4,8},{5,9},{6,10},{7,11},{8,12},{9,13},{1... | collective-permute-start | bytes 3538952 | tf_op jit(solution)/shard_map/ppermute | solution.py:210
  178.0 0.8 copy-start.8
  178.9 26.9 %collective-permute-start.17 = (f32[4,2,48,768]{3,2,1,0:T(8,128)}, f32[4,2,48,768]{3,2,1,0:T(8,128)}, u32[]{:S(2)}, u32[]{:S(2)}) collective-permute-start(f32[4,2,48,768]{3,2,1,0:T(8,128)} %x_down.3), channel_id=1, source_target_pairs={{0,12},{1,13},{2,14},{3,15},{4,0},{5,1},{6,2},{7,3},{8,4},{9,5},{1... | collective-permute-start | bytes 3538952 | tf_op jit(solution)/shard_map/ppermute | solution.py:211
  182.1 1.1 copy-start.5
  183.2 5.8 %copy-start.11 = (f32[2,2,48,768]{3,2,1,0:T(8,128)S(1)}, f32[2,2,48,768]{3,2,1,0:T(8,128)}, u32[]{:S(2)}) copy-start(f32[2,2,48,768]{3,2,1,0:T(8,128)} %copy-done.10) | copy-start | bytes 1769476
  187.3 6.3 %copy-start.9 = (f32[2,2,48,768]{3,2,1,0:T(8,128)S(1)}, f32[2,2,48,768]{3,2,1,0:T(8,128)}, u32[]{:S(2)}) copy-start(f32[2,2,48,768]{3,2,1,0:T(8,128)} %copy-done.8) | copy-start | bytes 1769476
  187.3 29.3 %collective-permute-start.10 = (f32[4,2,48,768]{3,2,1,0:T(8,128)}, f32[4,2,48,768]{3,2,1,0:T(8,128)}, u32[]{:S(2)}, u32[]{:S(2)}) collective-permute-start(f32[4,2,48,768]{3,2,1,0:T(8,128)} %y_down.2), channel_id=1, source_target_pairs={{0,3},{1,0},{2,1},{3,2},{4,7},{5,4},{6,5},{7,6},{8,11},{9,8},{10,9... | collective-permute-start | bytes 3538952 | tf_op jit(solution)/shard_map/ppermute | solution.py:211
  193.0 31.4 %collective-permute-start.22 = (f32[4,2,48,768]{3,2,1,0:T(8,128)}, f32[4,2,48,768]{3,2,1,0:T(8,128)}, u32[]{:S(2)}, u32[]{:S(2)}) collective-permute-start(f32[4,2,48,768]{3,2,1,0:T(8,128)} %y_up.3), channel_id=1, source_target_pairs={{0,1},{1,2},{2,3},{3,0},{4,5},{5,6},{6,7},{7,4},{8,9},{9,10},{10,1... | collective-permute-start | bytes 3538952 | tf_op jit(solution)/shard_map/ppermute | solution.py:210
  197.8 48.9 %collective-permute-start.24 = (f32[4,2,48,768]{3,2,1,0:T(8,128)}, f32[4,2,48,768]{3,2,1,0:T(8,128)}, u32[]{:S(2)}, u32[]{:S(2)}) collective-permute-start(f32[4,2,48,768]{3,2,1,0:T(8,128)} %y_down.3), channel_id=1, source_target_pairs={{0,3},{1,0},{2,1},{3,2},{4,7},{5,4},{6,5},{7,6},{8,11},{9,8},{10,9... | collective-permute-start | bytes 3538952 | tf_op jit(solution)/shard_map/ppermute | solution.py:211
  204.7 42.0 %collective-permute-start.4 = (f32[2,48,768]{2,1,0:T(8,128)S(1)}, f32[2,48,768]{2,1,0:T(8,128)S(1)}, u32[]{:S(2)}, u32[]{:S(2)}) collective-permute-start(f32[2,48,768]{2,1,0:T(8,128)S(1)} %get-tuple-element.36), channel_id=1, source_target_pairs={{0,1},{1,2},{2,3},{3,0},{4,5},{5,6},{6,7},{7,4},{8,9},{9,10},{10,1... | collective-permute-start | bytes 884744 | tf_op jit(solution)/shard_map/ppermute | solution.py:218
  205.7 42.6 %collective-permute-start.5 = (f32[2,48,768]{2,1,0:T(8,128)S(1)}, f32[2,48,768]{2,1,0:T(8,128)S(1)}, u32[]{:S(2)}, u32[]{:S(2)}) collective-permute-start(f32[2,48,768]{2,1,0:T(8,128)S(1)} %get-tuple-element.37), channel_id=1, source_target_pairs={{0,2},{1,3},{2,0},{3,1},{4,6},{5,7},{6,4},{7,5},{8,10},{9,11},{10,... | collective-permute-start | bytes 884744 | tf_op jit(solution)/shard_map/ppermute | solution.py:219
  216.6 37.1 %collective-permute-start.6 = (f32[2,48,768]{2,1,0:T(8,128)S(1)}, f32[2,48,768]{2,1,0:T(8,128)S(1)}, u32[]{:S(2)}, u32[]{:S(2)}) collective-permute-start(f32[2,48,768]{2,1,0:T(8,128)S(1)} %get-tuple-element.38), channel_id=1, source_target_pairs={{0,3},{1,0},{2,1},{3,2},{4,7},{5,4},{6,5},{7,6},{8,11},{9,8},{10,9... | collective-permute-start | bytes 884744 | tf_op jit(solution)/shard_map/ppermute | solution.py:220
  224.5 34.0 %collective-permute-start.11 = (f32[2,48,768]{2,1,0:T(8,128)S(1)}, f32[2,48,768]{2,1,0:T(8,128)S(1)}, u32[]{:S(2)}, u32[]{:S(2)}) collective-permute-start(f32[2,48,768]{2,1,0:T(8,128)S(1)} %get-tuple-element.42), channel_id=1, source_target_pairs={{0,4},{1,5},{2,6},{3,7},{4,8},{5,9},{6,10},{7,11},{8,12},{9,13},{1... | collective-permute-start | bytes 884744 | tf_op jit(solution)/shard_map/ppermute | solution.py:218
  246.7 11.8 %collective-permute-start.12 = (f32[2,48,768]{2,1,0:T(8,128)S(1)}, f32[2,48,768]{2,1,0:T(8,128)S(1)}, u32[]{:S(2)}, u32[]{:S(2)}) collective-permute-start(f32[2,48,768]{2,1,0:T(8,128)S(1)} %get-tuple-element.43), channel_id=1, source_target_pairs={{0,8},{1,9},{2,10},{3,11},{4,12},{5,13},{6,14},{7,15},{8,0},{9,1},... | collective-permute-start | bytes 884744 | tf_op jit(solution)/shard_map/ppermute | solution.py:219
  246.7 12.0 %collective-permute-start.13 = (f32[2,48,768]{2,1,0:T(8,128)S(1)}, f32[2,48,768]{2,1,0:T(8,128)S(1)}, u32[]{:S(2)}, u32[]{:S(2)}) collective-permute-start(f32[2,48,768]{2,1,0:T(8,128)S(1)} %get-tuple-element.44), channel_id=1, source_target_pairs={{0,12},{1,13},{2,14},{3,15},{4,0},{5,1},{6,2},{7,3},{8,4},{9,5},{1... | collective-permute-start | bytes 884744 | tf_op jit(solution)/shard_map/ppermute | solution.py:220
  248.3 23.3 %copy-start.13 = (f32[2,48,768]{2,1,0:T(8,128)S(1)}, f32[2,48,768]{2,1,0:T(8,128)}, u32[]{:S(2)}) copy-start(f32[2,48,768]{2,1,0:T(8,128)} %copy-done.12) | copy-start | bytes 884740
  248.3 23.3 %copy-start.15 = (s32[8]{0:T(128)S(1)}, s32[8]{0:T(128)}, u32[]{:S(2)}) copy-start(s32[8]{0:T(128)} %sizes.3) | copy-start | bytes 100
  248.3 13.9 %collective-permute-start.18 = (f32[2,48,768]{2,1,0:T(8,128)S(1)}, f32[2,48,768]{2,1,0:T(8,128)S(1)}, u32[]{:S(2)}, u32[]{:S(2)}) collective-permute-start(f32[2,48,768]{2,1,0:T(8,128)S(1)} %get-tuple-element.48), channel_id=1, source_target_pairs={{0,1},{1,2},{2,3},{3,0},{4,5},{5,6},{6,7},{7,4},{8,9},{9,10},{10,1... | collective-permute-start | bytes 884744 | tf_op jit(solution)/shard_map/ppermute | solution.py:218
  253.7 10.6 %collective-permute-start.19 = (f32[2,48,768]{2,1,0:T(8,128)}, f32[2,48,768]{2,1,0:T(8,128)S(1)}, u32[]{:S(2)}, u32[]{:S(2)}) collective-permute-start(f32[2,48,768]{2,1,0:T(8,128)} %get-tuple-element.49), channel_id=1, source_target_pairs={{0,2},{1,3},{2,0},{3,1},{4,6},{5,7},{6,4},{7,5},{8,10},{9,11},{10,... | collective-permute-start | bytes 884744 | tf_op jit(solution)/shard_map/ppermute | solution.py:219
  258.5 7.6 %collective-permute-start.20 = (f32[2,48,768]{2,1,0:T(8,128)}, f32[2,48,768]{2,1,0:T(8,128)}, u32[]{:S(2)}, u32[]{:S(2)}) collective-permute-start(f32[2,48,768]{2,1,0:T(8,128)} %get-tuple-element.50), channel_id=1, source_target_pairs={{0,3},{1,0},{2,1},{3,2},{4,7},{5,4},{6,5},{7,6},{8,11},{9,8},{10,9... | collective-permute-start | bytes 884744 | tf_op jit(solution)/shard_map/ppermute | solution.py:220
  258.5 8.3 %collective-permute-start.25 = (f32[2,48,768]{2,1,0:T(8,128)}, f32[2,48,768]{2,1,0:T(8,128)}, u32[]{:S(2)}, u32[]{:S(2)}) collective-permute-start(f32[2,48,768]{2,1,0:T(8,128)} %get-tuple-element.54), channel_id=1, source_target_pairs={{0,4},{1,5},{2,6},{3,7},{4,8},{5,9},{6,10},{7,11},{8,12},{9,13},{1... | collective-permute-start | bytes 884744 | tf_op jit(solution)/shard_map/ppermute | solution.py:218
  258.7 11.7 %collective-permute-start.26 = (f32[2,48,768]{2,1,0:T(8,128)}, f32[2,48,768]{2,1,0:T(8,128)}, u32[]{:S(2)}, u32[]{:S(2)}) collective-permute-start(f32[2,48,768]{2,1,0:T(8,128)} %get-tuple-element.55), channel_id=1, source_target_pairs={{0,8},{1,9},{2,10},{3,11},{4,12},{5,13},{6,14},{7,15},{8,0},{9,1},... | collective-permute-start | bytes 884744 | tf_op jit(solution)/shard_map/ppermute | solution.py:219
  262.2 9.4 %collective-permute-start.27 = (f32[2,48,768]{2,1,0:T(8,128)}, f32[2,48,768]{2,1,0:T(8,128)}, u32[]{:S(2)}, u32[]{:S(2)}) collective-permute-start(f32[2,48,768]{2,1,0:T(8,128)} %get-tuple-element.56), channel_id=1, source_target_pairs={{0,12},{1,13},{2,14},{3,15},{4,0},{5,1},{6,2},{7,3},{8,4},{9,5},{1... | collective-permute-start | bytes 884744 | tf_op jit(solution)/shard_map/ppermute | solution.py:220
  (1 other events, 0.7 us)
Sparse Core Ops, SparseCore 0:
  35.0 33.5 all-gather.4
  70.2 34.3 all-gather.6

commit v2 on v0

v2 whole, which is shorter than its diff:
```python
import functools

import jax
import jax.numpy as jnp
import numpy as np
from jax import lax
from jax.experimental import pallas as pl
from jax.experimental.pallas import tpu as pltpu
from jax.sharding import PartitionSpec as P

SIDE = 4
VMEM = 48 * 1024 * 1024
SOURCES = [(dz, dc) for dz in (0, -1, 1, 2) for dc in (0, 1)]


def hops(count, stride, delta):
    pairs = []
    for i in range(count):
        d = (i // stride) % SIDE
        pairs.append((i, i + ((d + delta) % SIDE - d) * stride))
    return pairs


X_HOPS = {d: hops(16, SIDE, d) for d in (1, 2, -1)}
Y_HOPS = {d: hops(16, 1, d) for d in (1, 2, -1)}
Z_HOPS = {d: hops(8, 2, d) for d in (1, 2, -1)}
SWAP = [(i, i ^ 1) for i in range(8)]


def places(axis):
    table = np.zeros((8, 16, 16), np.int32)
    for vb in range(8):
        for ob in range(16):
            x, y = divmod(ob, SIDE)
            for a, (dz, dc) in enumerate(SOURCES):
                source = 2 * ((vb // 2 + dz) % SIDE) + ((vb % 2) ^ dc)
                for h in range(2):
                    to_x, to_y = divmod(2 * source + h, SIDE)
                    rel_x, rel_y = (to_x - x) % SIDE, (to_y - y) % SIDE
                    first, second = (rel_x, rel_y) if axis == "x" else (rel_y, rel_x)
                    table[vb, ob, 2 * a + h] = SIDE * first + second
    return table


PLACES = np.concatenate([places("x"), places("y")], axis=2)


def product_kernel(v_first, place_at, place, sizes, origin, *refs):
    pieces, (v_ref, send_p, send_m, up, down, own, a_all, v_all) = refs[:8], refs[8:]
    rows = send_p.shape[2]
    depth = v_ref.shape[1]
    for a, piece in enumerate(pieces):
        for h in range(2):
            block = piece[0, h * rows : (h + 1) * rows]
            hi = block.astype(jnp.bfloat16)
            lo = (block - hi.astype(jnp.float32)).astype(jnp.bfloat16)
            at = pl.ds(pl.multiple_of(place[place_at + 2 * a + h] * rows, rows), rows)
            a_all[at, 0:depth] = hi
            a_all[at, depth : 2 * depth] = lo
            a_all[at, 2 * depth : 3 * depth] = hi
    size = sizes[v_first + pl.program_id(0)]
    shape = v_ref.shape[1:]
    p = origin[0] + lax.broadcasted_iota(jnp.int32, shape, 0)
    q = origin[1] + lax.broadcasted_iota(jnp.int32, shape, 1)
    v = jnp.where((p < size) & (q < size), v_ref[0], 0.0)
    hi = v.astype(jnp.bfloat16)
    v_all[0:depth] = hi
    v_all[depth : 2 * depth] = hi
    v_all[2 * depth : 3 * depth] = (v - hi.astype(jnp.float32)).astype(jnp.bfloat16)

    def chunk(k):
        acc = jnp.dot(
            a_all[SIDE * rows * k : SIDE * rows * (k + 1)], v_all[...], preferred_element_type=jnp.float32
        )
        return [acc[rows * s : rows * (s + 1)] for s in range(SIDE)]

    far = chunk(2)
    send_p[0, 0], send_p[1, 0], send_m[0, 0], send_m[1, 0] = far
    up[0, 0], up[1, 0], send_p[2, 0], send_p[3, 0] = chunk(1)
    send_m[2, 0], send_m[3, 0], down[0, 0], down[1, 0] = chunk(3)
    own[0, 0], own[1, 0], own[2, 0], own[3, 0] = chunk(0)


def product(pieces, a_first, ovov, v_first, count, place, place_at, sizes, origin, name):
    rows2, depth = pieces[0].shape[1:]
    rows = rows2 // 2
    cols = ovov.shape[2]
    leads = (4, 4, 2, 2, 4)
    total = 16 * rows
    return pl.pallas_call(
        functools.partial(product_kernel, v_first, place_at),
        grid_spec=pltpu.PrefetchScalarGridSpec(
            num_scalar_prefetch=3,
            grid=(count,),
            in_specs=[pl.BlockSpec((1, rows2, depth), lambda g, *_: (a_first + g, 0, 0))] * 8
            + [pl.BlockSpec((1, depth, cols), lambda g, *_: (v_first + g, 0, 0))],
            out_specs=[pl.BlockSpec((n, 1, rows, cols), lambda g, *_: (0, g, 0, 0)) for n in leads],
            scratch_shapes=[
                pltpu.VMEM((total, 3 * depth), jnp.bfloat16),
                pltpu.VMEM((3 * depth, cols), jnp.bfloat16),
            ],
        ),
        out_shape=[jax.ShapeDtypeStruct((n, count, rows, cols), jnp.float32) for n in leads],
        compiler_params=pltpu.CompilerParams(vmem_limit_bytes=VMEM),
        cost_estimate=pl.CostEstimate(
            flops=6 * total * depth * cols * count,
            bytes_accessed=4 * count * (depth * cols + total * (depth + cols)),
            transcendentals=0,
        ),
        name=name,
    )(place, sizes, origin, *pieces, ovov)


def add_kernel(up, down, recv_p, recv_m, out_p, out_m):
    out_p[...] = up[...] + recv_p[...]
    out_m[...] = down[...] + recv_m[...]


def add_far(up, down, recv_p, recv_m, name):
    lead, count, rows, cols = up.shape
    spec = pl.BlockSpec((lead, 1, rows, cols), lambda g: (0, g, 0, 0))
    return pl.pallas_call(
        add_kernel,
        grid=(count,),
        in_specs=[spec] * 4,
        out_specs=[spec] * 2,
        out_shape=[jax.ShapeDtypeStruct(up.shape, jnp.float32)] * 2,
        compiler_params=pltpu.CompilerParams(vmem_limit_bytes=VMEM),
        cost_estimate=pl.CostEstimate(flops=2 * up.size, bytes_accessed=24 * up.size, transcendentals=0),
        name=name,
    )(up, down, recv_p, recv_m)


def own_kernel(counts, *refs):
    ins, outs = refs[:-4], refs[-4:]
    at = 0
    for i, count in enumerate(counts):
        own, p1, m1, p2, m2 = ins[5 * i : 5 * i + 5]
        for g in range(count):
            outs[0][at + g] = own[0, g] + (p2[0, g] + m1[2, g])
            outs[1][at + g] = own[1, g] + (p2[1, g] + m1[3, g])
            outs[2][at + g] = own[2, g] + (m2[0, g] + p1[2, g])
            outs[3][at + g] = own[3, g] + (m2[1, g] + p1[3, g])
        at += count


def add_own(groups, name):
    counts = [group[0].shape[1] for group in groups]
    rows, cols = groups[0][0].shape[2:]
    flat = [r for group in groups for r in group]
    vmem = pl.BlockSpec(memory_space=pltpu.VMEM)
    shape = jax.ShapeDtypeStruct((sum(counts), rows, cols), jnp.float32)
    return pl.pallas_call(
        functools.partial(own_kernel, counts),
        in_specs=[vmem] * len(flat),
        out_specs=[vmem] * 4,
        out_shape=[shape] * 4,
        compiler_params=pltpu.CompilerParams(vmem_limit_bytes=VMEM),
        cost_estimate=pl.CostEstimate(
            flops=2 * 4 * shape.size, bytes_accessed=4 * (4 * shape.size + sum(r.size for r in flat)), transcendentals=0
        ),
        name=name,
    )(*flat)


def finish_kernel(order, sizes, origin, *refs):
    out = refs[-1]
    rows, _, cols = out.shape
    row = origin[0] + lax.broadcasted_iota(jnp.int32, (rows, cols), 0)
    for i, irreps in enumerate(order):
        parts = refs[4 * i : 4 * i + 4]
        for at, g in enumerate(irreps):
            total = (parts[0][at] + parts[1][at]) + (parts[2][at] + parts[3][at])
            out[:, g, :] = jnp.where(row < sizes[g], total, 0.0)


def finish(order, parts, row_sizes, origin, shape):
    flat = [p for four in parts for p in four]
    vmem = pl.BlockSpec(memory_space=pltpu.VMEM)
    smem = pl.BlockSpec(memory_space=pltpu.SMEM)
    return pl.pallas_call(
        functools.partial(finish_kernel, order),
        in_specs=[smem, smem] + [vmem] * len(flat),
        out_specs=vmem,
        out_shape=jax.ShapeDtypeStruct(shape, jnp.float32),
        compiler_params=pltpu.CompilerParams(vmem_limit_bytes=VMEM),
        name="finish",
    )(row_sizes, origin, *flat)


GROUPS = ((0, 2, 2), (4, 2, 2))


def local(amplitudes, ovov, row_sizes, pair_sizes):
    ob = lax.axis_index("ob")
    vb = lax.axis_index("vb")
    local_rows, irreps, pairs = amplitudes.shape
    obs = lax.axis_size("ob")
    depth, cols = ovov.shape[1:]
    out_rows = local_rows * lax.axis_size("vb")
    place = lax.dynamic_slice(jnp.asarray(PLACES), (vb, ob, 0), (1, 1, 32)).reshape(32)

    origin = jnp.stack([ob * depth, vb * cols]).astype(jnp.int32)

    mine = jnp.transpose(amplitudes.reshape(local_rows, irreps, obs, depth), (2, 0, 1, 3))
    mine = lax.all_to_all(
        mine.reshape(obs, local_rows * irreps, depth), "ob", split_axis=0, concat_axis=0, tiled=True
    )
    mine = jnp.transpose(mine.reshape(obs * local_rows, irreps, depth), (1, 0, 2))

    own = {"x": [], "y": []}
    order = {"x": [], "y": []}
    for i, (first, nx, ny) in enumerate(GROUPS):
        held = mine[first : first + nx + ny]
        pieces = []
        for dz in (0, -1, 1, 2):
            moved = lax.ppermute(held, "vb", Z_HOPS[-dz if dz != 2 else 2]) if dz else held
            pieces += [moved, lax.ppermute(moved, "vb", SWAP)]
        for axis, at, count in (("x", 0, nx), ("y", nx, ny)):
            here = X_HOPS if axis == "x" else Y_HOPS
            send_p, send_m, up, down, mid = product(
                pieces, at, ovov, first + at, count, place, 16 * (axis == "y"), pair_sizes, origin, f"{axis}_product"
            )
            p1 = lax.ppermute(send_p, "ob", here[1])
            m1 = lax.ppermute(send_m, "ob", here[-1])
            send_p, send_m = add_far(up, down, p1, m1, f"{axis}_add")
            p2 = lax.ppermute(send_p, "ob", here[1])
            m2 = lax.ppermute(send_m, "ob", here[-1])
            own[axis].append((mid, p1, m1, p2, m2))
            order[axis] += range(first + at, first + at + count)

    parts = []
    for axis in ("x", "y"):
        there = Y_HOPS if axis == "x" else X_HOPS
        four = add_own(own[axis], f"{axis}_own")
        parts.append([four[0]] + [lax.ppermute(four[k], "ob", there[d]) for k, d in ((1, 1), (2, 2), (3, -1))])
    origin = jnp.stack([ob * out_rows, vb * cols]).astype(jnp.int32)
    return finish([order["x"], order["y"]], parts, row_sizes, origin, (out_rows, irreps, cols))


def solution(mesh):
    placed = (P(("vb", "ob"), None, None), P(None, "ob", "vb"), P(), P())
    return jax.shard_map(
        local, mesh=mesh, in_specs=placed, out_specs=P("ob", None, "vb"), check_vma=False
    )
```

time: 568 us -> 247 us (0.43)
  waiting for transfers between devices: 348 us -> 117 us
  local copies, waits for them, and re-layouts: 114 us -> 8.91 us
  matrix products: 50.3 us -> 0 us
  starting transfers between devices: 7.03 us -> 51.6 us
  Pallas kernels: 0 us -> 42.1 us
  other arithmetic: 33 us -> 0.15 us
  blocking collectives: 0 us -> 25.4 us
  between operations: 13.5 us -> 0.26 us
    all_to_all x1 -> x0, waiting for transfers between devices: 163 us -> none  [local(): lax.all_to_all(stacked, 'ob', split_axis=2, concat_axis=0, tiled=True)]
    reduce_scatter x1 -> x0, waiting for transfers between devices: 126 us -> none  [local(): lax.psum_scatter(jnp.einsum('mgp,gpq->mgq', live_amp, live_ovov, precisio...]
    ppermute x0 -> x36, waiting for transfers between devices: none -> 117 us  [the longest x4 37.3 us: local(): p1 = lax.ppermute(send_p, 'ob', here[1])]
    all_gather x1 -> x0, waiting for transfers between devices: 58.6 us -> none  [local(): stacked = lax.all_gather(amplitudes, 'vb', axis=0, tiled=True)]
    ppermute x0 -> x36, starting transfers between devices: none -> 51.6 us  [the longest x6 23.6 us: local(): lax.ppermute(held, 'vb', Z_HOPS[-dz if dz != 2 else 2])]
    dot_general x1 -> x0, matrix products: 50.3 us -> none  [local(): jnp.einsum('mgp,gpq->mgq', live_amp, live_ovov, precision=lax.Precision.H...]
    unnamed x6 -> x53, local copies, waits for them, and re-layouts: 50.5 us -> 7.53 us
    pallas_call x0 -> x11, Pallas kernels: none -> 42.1 us  [the longest x4 29.3 us: product(): pl.pallas_call(functools.partial(product_kernel, v_first, place_at), grid...]
  transfers between devices with their start and end apart: 3 -> 36, of which waited for: 3 -> 15; matrix products, arithmetic and copies ran while one was open for 0% -> 0% of each run, Pallas kernels for 0% -> 16%
where the time goes in v2:
time: 247 us; the launch traced here: 246 us
  waiting for transfers between devices  117 us (47%)
  starting transfers between devices  51.6 us (21%)
  Pallas kernels  42.1 us (17%)
  blocking collectives  25.4 us (10%)
  local copies, waits for them, and re-layouts  8.91 us (4%)
    ppermute x4, waiting for transfers between devices, local(): p1 = lax.ppermute(send_p, 'ob', here[1])  37.3 us
    ppermute x6, waiting for transfers between devices, local(): lax.ppermute(held, 'vb', Z_HOPS[-dz if dz != 2 else 2])  32.4 us
    pallas_call x4, Pallas kernels, product(): pl.pallas_call(functools.partial(product_kernel, v_first, place_at), grid...  29.3 us
    all_to_all x1, blocking collectives, local(): lax.all_to_all(mine.reshape(obs, local_rows * irreps, depth), 'ob', split...  25.4 us
    ppermute x6, starting transfers between devices, local(): lax.ppermute(held, 'vb', Z_HOPS[-dz if dz != 2 else 2])  23.6 us
    ppermute x6, waiting for transfers between devices, local(): lax.ppermute(four[k], 'ob', there[d])  15.3 us
    ppermute x4, waiting for transfers between devices, local(): m2 = lax.ppermute(send_m, 'ob', here[-1])  14 us
    ppermute x4, waiting for transfers between devices, local(): p2 = lax.ppermute(send_p, 'ob', here[1])  13.8 us
  transfers between devices with their start and end apart: 36, of which 15 were waited for; matrix products, arithmetic and copies ran while one was open for 0% of the time, Pallas kernels for 16%

profile of v2, /device:TPU:0, one launch (start us, length us, event | category | flops | bytes accessed | tf_op | source)
XLA Modules:
  0.0 245.7 jit_solution(2795140105527988185)
XLA Ops:
  0.0 1.5 copy.13
  1.9 25.4 %all_to_all.5 = f32[16,48,384]{2,1,0:T(8,128)S(1)} all-to-all(f32[16,48,384]{2,1,0:T(8,128)S(1)} %bitcast.22), channel_id=1, replica_groups=mesh['vb'=8,'ob'=16] {'ob'}, dimensions={0} | all-to-all | bytes 2359296 | tf_op jit(solution)/shard_map/all_to_all | solution.py:206
  27.7 2.0 collective-permute-start.1
  29.7 2.2 collective-permute-start.3
  31.9 1.8 collective-permute-start.5
  33.6 1.0 collective-permute-start.12
  34.7 2.2 collective-permute-start.14
  36.9 9.1 %collective-permute-done.1.refs_2_ = f32[4,96,384]{2,1,0:T(8,128)S(1)} collective-permute-done((f32[4,96,384]{2,1,0:T(8,128)S(1)}, f32[4,96,384]{2,1,0:T(8,128)S(1)}, u32[]{:S(2)}, u32[]{:S(2)}) %collective-permute-start.1) | collective-permute-done | bytes 589856 | tf_op jit(solution)/shard_map/ppermute | solution.py:217
  46.0 14.4 %collective-permute-start.16 = (f32[4,96,384]{2,1,0:T(8,128)S(1)}, f32[4,96,384]{2,1,0:T(8,128)}, u32[]{:S(2)}, u32[]{:S(2)}) collective-permute-start(f32[4,96,384]{2,1,0:T(8,128)S(1)} %get-tuple-element.77.refs_0_), channel_id=1, source_target_pairs={{0,64},{16,80},{32,96},{48,112},{64,0},{80,16},{96,32},{112,48},{1... | collective-permute-start | bytes 1769480 | tf_op jit(solution)/shard_map/ppermute | solution.py:217
  60.9 10.1 %collective-permute-done.12.refs_2_ = f32[4,96,384]{2,1,0:T(8,128)S(1)} collective-permute-done((f32[4,96,384]{2,1,0:T(8,128)S(1)}, f32[4,96,384]{2,1,0:T(8,128)S(1)}, u32[]{:S(2)}, u32[]{:S(2)}) %collective-permute-start.12) | collective-permute-done | bytes 589856 | tf_op jit(solution)/shard_map/ppermute | solution.py:217
  71.0 11.9 %collective-permute-done.14.refs_4_ = f32[4,96,384]{2,1,0:T(8,128)S(1)} collective-permute-done((f32[4,96,384]{2,1,0:T(8,128)S(1)}, f32[4,96,384]{2,1,0:T(8,128)S(1)}, u32[]{:S(2)}, u32[]{:S(2)}) %collective-permute-start.14) | collective-permute-done | bytes 589856 | tf_op jit(solution)/shard_map/ppermute | solution.py:217
  82.9 0.7 dynamic-slice_bitcast_fusion.place
  83.6 1.4 collective-permute-done.16.refs_6_
  85.6 7.5 %x_product.2 = (f32[4,2,48,768]{3,2,1,0:T(8,128)}, f32[4,2,48,768]{3,2,1,0:T(8,128)}, f32[2,2,48,768]{3,2,1,0:T(8,128)S(1)}, f32[2,2,48,768]{3,2,1,0:T(8,128)S(1)}, f32[4,2,48,768]{3,2,1,0:T(8,128)}) custom-call(s32[32]{0:T(128)S(1)} %dynamic-slice_bitcast_fusion.place, s32[8]{0:T(128)S(1)} %copy-done.24, s32[2]{0:T(128)S(1)} %pad_add_fusion.1.origin, ...), custom_call_target="tpu_custom_call" | custom-call | flops 2717908992 | bytes 9437184 | tf_op jit(solution)/shard_map/x_product/pallas_call | solution.py:90
  93.0 0.8 copy-done.16
  93.8 0.8 copy-done.18
  95.2 2.7 %collective-permute-start.8 = (f32[4,2,48,768]{3,2,1,0:T(8,128)}, f32[4,2,48,768]{3,2,1,0:T(8,128)S(1)}, u32[]{:S(2)}, u32[]{:S(2)}) collective-permute-start(f32[4,2,48,768]{3,2,1,0:T(8,128)} %get-tuple-element.43), channel_id=1, source_target_pairs={{0,12},{1,13},{2,14},{3,15},{4,0},{5,1},{6,2},{7,3},{8,4},{9,5},{1... | collective-permute-start | bytes 3538952 | tf_op jit(solution)/shard_map/ppermute | solution.py:225
  97.9 7.2 %x_product.3 = (f32[4,2,48,768]{3,2,1,0:T(8,128)}, f32[4,2,48,768]{3,2,1,0:T(8,128)}, f32[2,2,48,768]{3,2,1,0:T(8,128)S(1)}, f32[2,2,48,768]{3,2,1,0:T(8,128)S(1)}, f32[4,2,48,768]{3,2,1,0:T(8,128)}) custom-call(s32[32]{0:T(128)S(1)} %dynamic-slice_bitcast_fusion.place, s32[8]{0:T(128)S(1)} %copy-done.24, s32[2]{0:T(128)S(1)} %pad_add_fusion.1.origin, ...), custom_call_target="tpu_custom_call" | custom-call | flops 2717908992 | bytes 9437184 | tf_op jit(solution)/shard_map/x_product/pallas_call | solution.py:90
  105.1 0.8 copy-done.22
  106.0 3.2 %collective-permute-start.19 = (f32[4,2,48,768]{3,2,1,0:T(8,128)}, f32[4,2,48,768]{3,2,1,0:T(8,128)S(1)}, u32[]{:S(2)}, u32[]{:S(2)}) collective-permute-start(f32[4,2,48,768]{3,2,1,0:T(8,128)} %get-tuple-element.50), channel_id=1, source_target_pairs={{0,12},{1,13},{2,14},{3,15},{4,0},{5,1},{6,2},{7,3},{8,4},{9,5},{1... | collective-permute-start | bytes 3538952 | tf_op jit(solution)/shard_map/ppermute | solution.py:225
  109.2 7.5 %y_product.2 = (f32[4,2,48,768]{3,2,1,0:T(8,128)}, f32[4,2,48,768]{3,2,1,0:T(8,128)}, f32[2,2,48,768]{3,2,1,0:T(8,128)S(1)}, f32[2,2,48,768]{3,2,1,0:T(8,128)S(1)}, f32[4,2,48,768]{3,2,1,0:T(8,128)}) custom-call(s32[32]{0:T(128)S(1)} %dynamic-slice_bitcast_fusion.place, s32[8]{0:T(128)S(1)} %copy-done.24, s32[2]{0:T(128)S(1)} %pad_add_fusion.1.origin, ...), custom_call_target="tpu_custom_call" | custom-call | flops 2717908992 | bytes 9437184 | tf_op jit(solution)/shard_map/y_product/pallas_call | solution.py:90
  116.7 0.8 copy-done.12
  117.5 0.8 copy-done.14
  118.8 6.0 %collective-permute-done.7.recv_p.refs_1_ = f32[4,2,48,768]{3,2,1,0:T(8,128)S(1)} collective-permute-done((f32[4,2,48,768]{3,2,1,0:T(8,128)}, f32[4,2,48,768]{3,2,1,0:T(8,128)S(1)}, u32[]{:S(2)}, u32[]{:S(2)}) %collective-permute-start.7) | collective-permute-done | bytes 1179680 | tf_op jit(solution)/shard_map/ppermute | solution.py:224
  124.9 1.3 collective-permute-start.26
  126.2 1.1 copy-done.9
  127.2 7.2 %y_product.3 = (f32[4,2,48,768]{3,2,1,0:T(8,128)}, f32[4,2,48,768]{3,2,1,0:T(8,128)}, f32[2,2,48,768]{3,2,1,0:T(8,128)S(1)}, f32[2,2,48,768]{3,2,1,0:T(8,128)S(1)}, f32[4,2,48,768]{3,2,1,0:T(8,128)}) custom-call(s32[32]{0:T(128)S(1)} %dynamic-slice_bitcast_fusion.place, s32[8]{0:T(128)S(1)} %copy-done.24, s32[2]{0:T(128)S(1)} %pad_add_fusion.1.origin, ...), custom_call_target="tpu_custom_call" | custom-call | flops 2717908992 | bytes 9437184 | tf_op jit(solution)/shard_map/y_product/pallas_call | solution.py:90
  134.5 0.8 collective-permute-start.29
  135.2 14.4 %collective-permute-done.18.recv_p.refs_6_ = f32[4,2,48,768]{3,2,1,0:T(8,128)S(1)} collective-permute-done((f32[4,2,48,768]{3,2,1,0:T(8,128)}, f32[4,2,48,768]{3,2,1,0:T(8,128)S(1)}, u32[]{:S(2)}, u32[]{:S(2)}) %collective-permute-start.18) | collective-permute-done | bytes 1179680 | tf_op jit(solution)/shard_map/ppermute | solution.py:224
  149.7 1.3 collective-permute-start.30
  152.7 2.7 %collective-permute-start.10 = (f32[2,2,48,768]{3,2,1,0:T(8,128)S(1)}, f32[2,2,48,768]{3,2,1,0:T(8,128)S(1)}, u32[]{:S(2)}, u32[]{:S(2)}) collective-permute-start(f32[2,2,48,768]{3,2,1,0:T(8,128)S(1)} %get-tuple-element.47), channel_id=1, source_target_pairs={{0,12},{1,13},{2,14},{3,15},{4,0},{5,1},{6,2},{7,3},{8,4},{9,5},{1... | collective-permute-start | bytes 1769480 | tf_op jit(solution)/shard_map/ppermute | solution.py:228
  155.4 16.9 %collective-permute-done.29.recv_p.refs_6_ = f32[4,2,48,768]{3,2,1,0:T(8,128)S(1)} collective-permute-done((f32[4,2,48,768]{3,2,1,0:T(8,128)}, f32[4,2,48,768]{3,2,1,0:T(8,128)S(1)}, u32[]{:S(2)}, u32[]{:S(2)}) %collective-permute-start.29) | collective-permute-done | bytes 1179680 | tf_op jit(solution)/shard_map/ppermute | solution.py:224
  173.0 4.4 %collective-permute-done.30.recv_m.refs_7_ = f32[4,2,48,768]{3,2,1,0:T(8,128)S(1)} collective-permute-done((f32[4,2,48,768]{3,2,1,0:T(8,128)}, f32[4,2,48,768]{3,2,1,0:T(8,128)S(1)}, u32[]{:S(2)}, u32[]{:S(2)}) %collective-permute-start.30) | collective-permute-done | bytes 1179680 | tf_op jit(solution)/shard_map/ppermute | solution.py:225
  178.5 2.7 %collective-permute-start.28 = (f32[2,2,48,768]{3,2,1,0:T(8,128)S(1)}, f32[2,2,48,768]{3,2,1,0:T(8,128)S(1)}, u32[]{:S(2)}, u32[]{:S(2)}) collective-permute-start(f32[2,2,48,768]{3,2,1,0:T(8,128)S(1)} %get-tuple-element.65), channel_id=1, source_target_pairs={{0,3},{1,0},{2,1},{3,2},{4,7},{5,4},{6,5},{7,6},{8,11},{9,8},{10,9... | collective-permute-start | bytes 1769480 | tf_op jit(solution)/shard_map/ppermute | solution.py:228
  181.2 3.2 %collective-permute-start.32 = (f32[2,2,48,768]{3,2,1,0:T(8,128)S(1)}, f32[2,2,48,768]{3,2,1,0:T(8,128)S(1)}, u32[]{:S(2)}, u32[]{:S(2)}) collective-permute-start(f32[2,2,48,768]{3,2,1,0:T(8,128)S(1)} %get-tuple-element.72), channel_id=1, source_target_pairs={{0,3},{1,0},{2,1},{3,2},{4,7},{5,4},{6,5},{7,6},{8,11},{9,8},{10,9... | collective-permute-start | bytes 1769480 | tf_op jit(solution)/shard_map/ppermute | solution.py:228
  184.4 1.4 collective-permute-done.21.refs_9_
  185.9 4.1 %x_own.1 = (f32[4,48,768]{2,1,0:T(8,128)S(1)}, f32[4,48,768]{2,1,0:T(8,128)S(1)}, f32[4,48,768]{2,1,0:T(8,128)}, f32[4,48,768]{2,1,0:T(8,128)}) custom-call(f32[4,2,48,768]{3,2,1,0:T(8,128)S(1)} %copy-done.11, f32[4,2,48,768]{3,2,1,0:T(8,128)} %copy-done, f32[4,2,48,768]{3,2,1,0:T(8,128)} %copy-done.2, f32[2,2,48,768]{3,2,1,0:T(8,128)S(1)} %collective-permute-done.9.refs_3_, ...), custom_call_target="tpu_custom_call" | custom-call | flops 1179648 | bytes 11796480 | tf_op jit(solution)/shard_map/x_own/pallas_call | solution.py:153
  190.0 4.9 %collective-permute-done.27.refs_3_ = f32[2,2,48,768]{3,2,1,0:T(8,128)S(1)} collective-permute-done((f32[2,2,48,768]{3,2,1,0:T(8,128)S(1)}, f32[2,2,48,768]{3,2,1,0:T(8,128)S(1)}, u32[]{:S(2)}, u32[]{:S(2)}) %collective-permute-start.27) | collective-permute-done | bytes 589856 | tf_op jit(solution)/shard_map/ppermute | solution.py:227
  195.2 3.5 %collective-permute-start.24 = (f32[4,48,768]{2,1,0:T(8,128)}, f32[4,48,768]{2,1,0:T(8,128)S(1)}, u32[]{:S(2)}, u32[]{:S(2)}) collective-permute-start(f32[4,48,768]{2,1,0:T(8,128)} %get-tuple-element.58), channel_id=1, source_target_pairs={{0,3},{1,0},{2,1},{3,2},{4,7},{5,4},{6,5},{7,6},{8,11},{9,8},{10,9... | collective-permute-start | bytes 1769480 | tf_op jit(solution)/shard_map/ppermute | solution.py:236
  198.7 8.9 %collective-permute-done.31.refs_8_ = f32[2,2,48,768]{3,2,1,0:T(8,128)S(1)} collective-permute-done((f32[2,2,48,768]{3,2,1,0:T(8,128)S(1)}, f32[2,2,48,768]{3,2,1,0:T(8,128)S(1)}, u32[]{:S(2)}, u32[]{:S(2)}) %collective-permute-start.31) | collective-permute-done | bytes 589856 | tf_op jit(solution)/shard_map/ppermute | solution.py:227
  207.5 12.6 %collective-permute-done.32.refs_9_ = f32[2,2,48,768]{3,2,1,0:T(8,128)S(1)} collective-permute-done((f32[2,2,48,768]{3,2,1,0:T(8,128)S(1)}, f32[2,2,48,768]{3,2,1,0:T(8,128)S(1)}, u32[]{:S(2)}, u32[]{:S(2)}) %collective-permute-start.32) | collective-permute-done | bytes 589856 | tf_op jit(solution)/shard_map/ppermute | solution.py:228
  220.1 4.1 %y_own.1 = (f32[4,48,768]{2,1,0:T(8,128)S(1)}, f32[4,48,768]{2,1,0:T(8,128)}, f32[4,48,768]{2,1,0:T(8,128)}, f32[4,48,768]{2,1,0:T(8,128)}) custom-call(f32[4,2,48,768]{3,2,1,0:T(8,128)S(1)} %copy-done.10, f32[4,2,48,768]{3,2,1,0:T(8,128)} %copy-done.1, f32[4,2,48,768]{3,2,1,0:T(8,128)} %copy-done.3, f32[2,2,48,768]{3,2,1,0:T(8,128)S(1)} %collective-permute-done.27.refs_3_, ...), custom_call_target="tpu_custom_call" | custom-call | flops 1179648 | bytes 11796480 | tf_op jit(solution)/shard_map/y_own/pallas_call | solution.py:153
  224.2 1.4 collective-permute-start.34
  225.6 1.8 collective-permute-start.35
  227.5 3.8 %collective-permute-done.23.refs_2_ = f32[4,48,768]{2,1,0:T(8,128)S(1)} collective-permute-done((f32[4,48,768]{2,1,0:T(8,128)}, f32[4,48,768]{2,1,0:T(8,128)S(1)}, u32[]{:S(2)}, u32[]{:S(2)}) %collective-permute-start.23) | collective-permute-done | bytes 589856 | tf_op jit(solution)/shard_map/ppermute | solution.py:236
  231.3 10.5 %collective-permute-done.33.refs_5_ = f32[4,48,768]{2,1,0:T(8,128)S(1)} collective-permute-done((f32[4,48,768]{2,1,0:T(8,128)}, f32[4,48,768]{2,1,0:T(8,128)S(1)}, u32[]{:S(2)}, u32[]{:S(2)}) %collective-permute-start.33) | collective-permute-done | bytes 589856 | tf_op jit(solution)/shard_map/ppermute | solution.py:236
  241.8 1.0 collective-permute-done.35.refs_7_
  242.8 2.9 %finish.1 = f32[48,8,768]{2,1,0:T(8,128)} custom-call(s32[8]{0:T(128)S(1)} %copy-done.25, s32[2]{0:T(128)S(1)} %pad_add_fusion.origin, f32[4,48,768]{2,1,0:T(8,128)S(1)} %get-tuple-element.55.refs_0_, f32[4,48,768]{2,1,0:T(8,128)S(1)} %collective-permute-done.22.refs_1_, f32[4,48,768]{2,1,0:T(8,128)S(1)} %collective-permute-done.23.refs_2_, ...), custom_call_target="tpu_custom_call" | custom-call | tf_op jit(solution)/shard_map/finish/pallas_call | solution.py:181
  (95 shorter events, 6.8 us)
Async XLA Ops:
  27.5 58.1 %copy-start.24 = (s32[8]{0:T(128)S(1)}, s32[8]{0:T(128)}, u32[]{:S(2)}) copy-start(s32[8]{0:T(128)} %sizes.8) | copy-start | bytes 100
  27.6 7.1 %collective-permute-start = (f32[4,96,384]{2,1,0:T(8,128)S(1)}, f32[4,96,384]{2,1,0:T(8,128)S(1)}, u32[]{:S(2)}, u32[]{:S(2)}) collective-permute-start(f32[4,96,384]{2,1,0:T(8,128)S(1)} %get-tuple-element.78.refs_0_), channel_id=1, source_target_pairs={{0,16},{16,0},{32,48},{48,32},{64,80},{80,64},{96,112},{112,96},{1... | collective-permute-start | bytes 1769480 | tf_op jit(solution)/shard_map/ppermute | solution.py:218
  27.7 18.3 %collective-permute-start.1 = (f32[4,96,384]{2,1,0:T(8,128)S(1)}, f32[4,96,384]{2,1,0:T(8,128)S(1)}, u32[]{:S(2)}, u32[]{:S(2)}) collective-permute-start(f32[4,96,384]{2,1,0:T(8,128)S(1)} %get-tuple-element.78.refs_0_), channel_id=1, source_target_pairs={{0,32},{16,48},{32,64},{48,80},{64,96},{80,112},{96,0},{112,16},{1... | collective-permute-start | bytes 1769480 | tf_op jit(solution)/shard_map/ppermute | solution.py:217
  29.7 30.7 %collective-permute-start.3 = (f32[4,96,384]{2,1,0:T(8,128)S(1)}, f32[4,96,384]{2,1,0:T(8,128)}, u32[]{:S(2)}, u32[]{:S(2)}) collective-permute-start(f32[4,96,384]{2,1,0:T(8,128)S(1)} %get-tuple-element.78.refs_0_), channel_id=1, source_target_pairs={{0,96},{16,112},{32,0},{48,16},{64,32},{80,48},{96,64},{112,80},{1... | collective-permute-start | bytes 1769480 | tf_op jit(solution)/shard_map/ppermute | solution.py:217
  31.9 28.5 %collective-permute-start.5 = (f32[4,96,384]{2,1,0:T(8,128)S(1)}, f32[4,96,384]{2,1,0:T(8,128)}, u32[]{:S(2)}, u32[]{:S(2)}) collective-permute-start(f32[4,96,384]{2,1,0:T(8,128)S(1)} %get-tuple-element.78.refs_0_), channel_id=1, source_target_pairs={{0,64},{16,80},{32,96},{48,112},{64,0},{80,16},{96,32},{112,48},{1... | collective-permute-start | bytes 1769480 | tf_op jit(solution)/shard_map/ppermute | solution.py:217
  33.6 37.3 %collective-permute-start.12 = (f32[4,96,384]{2,1,0:T(8,128)S(1)}, f32[4,96,384]{2,1,0:T(8,128)S(1)}, u32[]{:S(2)}, u32[]{:S(2)}) collective-permute-start(f32[4,96,384]{2,1,0:T(8,128)S(1)} %get-tuple-element.77.refs_0_), channel_id=1, source_target_pairs={{0,32},{16,48},{32,64},{48,80},{64,96},{80,112},{96,0},{112,16},{1... | collective-permute-start | bytes 1769480 | tf_op jit(solution)/shard_map/ppermute | solution.py:217
  34.7 48.2 %collective-permute-start.14 = (f32[4,96,384]{2,1,0:T(8,128)S(1)}, f32[4,96,384]{2,1,0:T(8,128)S(1)}, u32[]{:S(2)}, u32[]{:S(2)}) collective-permute-start(f32[4,96,384]{2,1,0:T(8,128)S(1)} %get-tuple-element.77.refs_0_), channel_id=1, source_target_pairs={{0,96},{16,112},{32,0},{48,16},{64,32},{80,48},{96,64},{112,80},{1... | collective-permute-start | bytes 1769480 | tf_op jit(solution)/shard_map/ppermute | solution.py:217
  46.0 39.0 %collective-permute-start.16 = (f32[4,96,384]{2,1,0:T(8,128)S(1)}, f32[4,96,384]{2,1,0:T(8,128)}, u32[]{:S(2)}, u32[]{:S(2)}) collective-permute-start(f32[4,96,384]{2,1,0:T(8,128)S(1)} %get-tuple-element.77.refs_0_), channel_id=1, source_target_pairs={{0,64},{16,80},{32,96},{48,112},{64,0},{80,16},{96,32},{112,48},{1... | collective-permute-start | bytes 1769480 | tf_op jit(solution)/shard_map/ppermute | solution.py:217
  60.4 24.6 %collective-permute-start.2 = (f32[4,96,384]{2,1,0:T(8,128)S(1)}, f32[4,96,384]{2,1,0:T(8,128)}, u32[]{:S(2)}, u32[]{:S(2)}) collective-permute-start(f32[4,96,384]{2,1,0:T(8,128)S(1)} %collective-permute-done.1.refs_2_), channel_id=1, source_target_pairs={{0,16},{16,0},{32,48},{48,32},{64,80},{80,64},{96,112},{112,96},{1... | collective-permute-start | bytes 1769480 | tf_op jit(solution)/shard_map/ppermute | solution.py:218
  60.4 25.1 %collective-permute-start.4 = (f32[4,96,384]{2,1,0:T(8,128)}, f32[4,96,384]{2,1,0:T(8,128)}, u32[]{:S(2)}, u32[]{:S(2)}) collective-permute-start(f32[4,96,384]{2,1,0:T(8,128)} %collective-permute-done.3.refs_4_), channel_id=1, source_target_pairs={{0,16},{16,0},{32,48},{48,32},{64,80},{80,64},{96,112},{112,96},{1... | collective-permute-start | bytes 1769480 | tf_op jit(solution)/shard_map/ppermute | solution.py:218
  71.0 14.6 %collective-permute-start.6 = (f32[4,96,384]{2,1,0:T(8,128)}, f32[4,96,384]{2,1,0:T(8,128)}, u32[]{:S(2)}, u32[]{:S(2)}) collective-permute-start(f32[4,96,384]{2,1,0:T(8,128)} %collective-permute-done.5.refs_6_), channel_id=1, source_target_pairs={{0,16},{16,0},{32,48},{48,32},{64,80},{80,64},{96,112},{112,96},{1... | collective-permute-start | bytes 1769480 | tf_op jit(solution)/shard_map/ppermute | solution.py:218
  82.9 12.3 %collective-permute-start.11 = (f32[4,96,384]{2,1,0:T(8,128)S(1)}, f32[4,96,384]{2,1,0:T(8,128)S(1)}, u32[]{:S(2)}, u32[]{:S(2)}) collective-permute-start(f32[4,96,384]{2,1,0:T(8,128)S(1)} %get-tuple-element.77.refs_0_), channel_id=1, source_target_pairs={{0,16},{16,0},{32,48},{48,32},{64,80},{80,64},{96,112},{112,96},{1... | collective-permute-start | bytes 1769480 | tf_op jit(solution)/shard_map/ppermute | solution.py:218
  85.0 13.0 %collective-permute-start.13 = (f32[4,96,384]{2,1,0:T(8,128)S(1)}, f32[4,96,384]{2,1,0:T(8,128)S(1)}, u32[]{:S(2)}, u32[]{:S(2)}) collective-permute-start(f32[4,96,384]{2,1,0:T(8,128)S(1)} %collective-permute-done.12.refs_2_), channel_id=1, source_target_pairs={{0,16},{16,0},{32,48},{48,32},{64,80},{80,64},{96,112},{112,96},{1... | collective-permute-start | bytes 1769480 | tf_op jit(solution)/shard_map/ppermute | solution.py:218
  85.0 12.9 %collective-permute-start.15 = (f32[4,96,384]{2,1,0:T(8,128)S(1)}, f32[4,96,384]{2,1,0:T(8,128)S(1)}, u32[]{:S(2)}, u32[]{:S(2)}) collective-permute-start(f32[4,96,384]{2,1,0:T(8,128)S(1)} %collective-permute-done.14.refs_4_), channel_id=1, source_target_pairs={{0,16},{16,0},{32,48},{48,32},{64,80},{80,64},{96,112},{112,96},{1... | collective-permute-start | bytes 1769480 | tf_op jit(solution)/shard_map/ppermute | solution.py:218
  85.5 12.4 %collective-permute-start.17 = (f32[4,96,384]{2,1,0:T(8,128)}, f32[4,96,384]{2,1,0:T(8,128)S(1)}, u32[]{:S(2)}, u32[]{:S(2)}) collective-permute-start(f32[4,96,384]{2,1,0:T(8,128)} %collective-permute-done.16.refs_6_), channel_id=1, source_target_pairs={{0,16},{16,0},{32,48},{48,32},{64,80},{80,64},{96,112},{112,96},{1... | collective-permute-start | bytes 1769480 | tf_op jit(solution)/shard_map/ppermute | solution.py:218
  94.7 30.2 %collective-permute-start.7 = (f32[4,2,48,768]{3,2,1,0:T(8,128)}, f32[4,2,48,768]{3,2,1,0:T(8,128)S(1)}, u32[]{:S(2)}, u32[]{:S(2)}) collective-permute-start(f32[4,2,48,768]{3,2,1,0:T(8,128)} %get-tuple-element.42), channel_id=1, source_target_pairs={{0,4},{1,5},{2,6},{3,7},{4,8},{5,9},{6,10},{7,11},{8,12},{9,13},{1... | collective-permute-start | bytes 3538952 | tf_op jit(solution)/shard_map/ppermute | solution.py:224
  95.2 39.3 %collective-permute-start.8 = (f32[4,2,48,768]{3,2,1,0:T(8,128)}, f32[4,2,48,768]{3,2,1,0:T(8,128)S(1)}, u32[]{:S(2)}, u32[]{:S(2)}) collective-permute-start(f32[4,2,48,768]{3,2,1,0:T(8,128)} %get-tuple-element.43), channel_id=1, source_target_pairs={{0,12},{1,13},{2,14},{3,15},{4,0},{5,1},{6,2},{7,3},{8,4},{9,5},{1... | collective-permute-start | bytes 3538952 | tf_op jit(solution)/shard_map/ppermute | solution.py:225
  106.0 10.7 %copy-start.20 = (f32[2,2,48,768]{3,2,1,0:T(8,128)}, f32[2,2,48,768]{3,2,1,0:T(8,128)S(1)}, u32[]{:S(2)}) copy-start(f32[2,2,48,768]{3,2,1,0:T(8,128)S(1)} %get-tuple-element.51.up) | copy-start | bytes 1769476
  106.0 43.7 %collective-permute-start.18 = (f32[4,2,48,768]{3,2,1,0:T(8,128)}, f32[4,2,48,768]{3,2,1,0:T(8,128)S(1)}, u32[]{:S(2)}, u32[]{:S(2)}) collective-permute-start(f32[4,2,48,768]{3,2,1,0:T(8,128)} %get-tuple-element.49), channel_id=1, source_target_pairs={{0,4},{1,5},{2,6},{3,7},{4,8},{5,9},{6,10},{7,11},{8,12},{9,13},{1... | collective-permute-start | bytes 3538952 | tf_op jit(solution)/shard_map/ppermute | solution.py:224
  106.0 45.5 %collective-permute-start.19 = (f32[4,2,48,768]{3,2,1,0:T(8,128)}, f32[4,2,48,768]{3,2,1,0:T(8,128)S(1)}, u32[]{:S(2)}, u32[]{:S(2)}) collective-permute-start(f32[4,2,48,768]{3,2,1,0:T(8,128)} %get-tuple-element.50), channel_id=1, source_target_pairs={{0,12},{1,13},{2,14},{3,15},{4,0},{5,1},{6,2},{7,3},{8,4},{9,5},{1... | collective-permute-start | bytes 3538952 | tf_op jit(solution)/shard_map/ppermute | solution.py:225
  118.4 34.3 %collective-permute-start.25 = (f32[4,2,48,768]{3,2,1,0:T(8,128)}, f32[4,2,48,768]{3,2,1,0:T(8,128)S(1)}, u32[]{:S(2)}, u32[]{:S(2)}) collective-permute-start(f32[4,2,48,768]{3,2,1,0:T(8,128)} %get-tuple-element.60), channel_id=1, source_target_pairs={{0,1},{1,2},{2,3},{3,0},{4,5},{5,6},{6,7},{7,4},{8,9},{9,10},{10,1... | collective-permute-start | bytes 3538952 | tf_op jit(solution)/shard_map/ppermute | solution.py:224
  124.9 26.1 %copy-start = (f32[4,2,48,768]{3,2,1,0:T(8,128)}, f32[4,2,48,768]{3,2,1,0:T(8,128)S(1)}, u32[]{:S(2)}) copy-start(f32[4,2,48,768]{3,2,1,0:T(8,128)S(1)} %collective-permute-done.7.recv_p.refs_1_) | copy-start | bytes 3538948
  124.9 30.5 %collective-permute-start.26 = (f32[4,2,48,768]{3,2,1,0:T(8,128)}, f32[4,2,48,768]{3,2,1,0:T(8,128)S(1)}, u32[]{:S(2)}, u32[]{:S(2)}) collective-permute-start(f32[4,2,48,768]{3,2,1,0:T(8,128)} %get-tuple-element.61), channel_id=1, source_target_pairs={{0,3},{1,0},{2,1},{3,2},{4,7},{5,4},{6,5},{7,6},{8,11},{9,8},{10,9... | collective-permute-start | bytes 3538952 | tf_op jit(solution)/shard_map/ppermute | solution.py:225
  127.2 23.8 %copy-start.17 = (f32[2,2,48,768]{3,2,1,0:T(8,128)S(1)}, f32[2,2,48,768]{3,2,1,0:T(8,128)}, u32[]{:S(2)}) copy-start(f32[2,2,48,768]{3,2,1,0:T(8,128)} %copy-done.16) | copy-start | bytes 1769476
  127.2 23.8 %copy-start.19 = (f32[2,2,48,768]{3,2,1,0:T(8,128)S(1)}, f32[2,2,48,768]{3,2,1,0:T(8,128)}, u32[]{:S(2)}) copy-start(f32[2,2,48,768]{3,2,1,0:T(8,128)} %copy-done.18) | copy-start | bytes 1769476
  134.4 17.0 %copy-start.2 = (f32[4,2,48,768]{3,2,1,0:T(8,128)}, f32[4,2,48,768]{3,2,1,0:T(8,128)S(1)}, u32[]{:S(2)}) copy-start(f32[4,2,48,768]{3,2,1,0:T(8,128)S(1)} %collective-permute-done.8.recv_m.refs_2_) | copy-start | bytes 3538948
  134.5 37.8 %collective-permute-start.29 = (f32[4,2,48,768]{3,2,1,0:T(8,128)}, f32[4,2,48,768]{3,2,1,0:T(8,128)S(1)}, u32[]{:S(2)}, u32[]{:S(2)}) collective-permute-start(f32[4,2,48,768]{3,2,1,0:T(8,128)} %get-tuple-element.67), channel_id=1, source_target_pairs={{0,1},{1,2},{2,3},{3,0},{4,5},{5,6},{6,7},{7,4},{8,9},{9,10},{10,1... | collective-permute-start | bytes 3538952 | tf_op jit(solution)/shard_map/ppermute | solution.py:224
  149.7 27.7 %collective-permute-start.30 = (f32[4,2,48,768]{3,2,1,0:T(8,128)}, f32[4,2,48,768]{3,2,1,0:T(8,128)S(1)}, u32[]{:S(2)}, u32[]{:S(2)}) collective-permute-start(f32[4,2,48,768]{3,2,1,0:T(8,128)} %get-tuple-element.68), channel_id=1, source_target_pairs={{0,3},{1,0},{2,1},{3,2},{4,7},{5,4},{6,5},{7,6},{8,11},{9,8},{10,9... | collective-permute-start | bytes 3538952 | tf_op jit(solution)/shard_map/ppermute | solution.py:225
  151.5 27.0 %collective-permute-start.9 = (f32[2,2,48,768]{3,2,1,0:T(8,128)S(1)}, f32[2,2,48,768]{3,2,1,0:T(8,128)S(1)}, u32[]{:S(2)}, u32[]{:S(2)}) collective-permute-start(f32[2,2,48,768]{3,2,1,0:T(8,128)S(1)} %get-tuple-element.46), channel_id=1, source_target_pairs={{0,4},{1,5},{2,6},{3,7},{4,8},{5,9},{6,10},{7,11},{8,12},{9,13},{1... | collective-permute-start | bytes 1769480 | tf_op jit(solution)/shard_map/ppermute | solution.py:227
  152.2 20.3 %copy-start.13 = (f32[2,2,48,768]{3,2,1,0:T(8,128)S(1)}, f32[2,2,48,768]{3,2,1,0:T(8,128)}, u32[]{:S(2)}) copy-start(f32[2,2,48,768]{3,2,1,0:T(8,128)} %copy-done.12) | copy-start | bytes 1769476
  152.2 20.3 %copy-start.15 = (f32[2,2,48,768]{3,2,1,0:T(8,128)S(1)}, f32[2,2,48,768]{3,2,1,0:T(8,128)}, u32[]{:S(2)}) copy-start(f32[2,2,48,768]{3,2,1,0:T(8,128)} %copy-done.14) | copy-start | bytes 1769476
  152.7 20.3 %copy-start.1 = (f32[4,2,48,768]{3,2,1,0:T(8,128)}, f32[4,2,48,768]{3,2,1,0:T(8,128)S(1)}, u32[]{:S(2)}) copy-start(f32[4,2,48,768]{3,2,1,0:T(8,128)S(1)} %collective-permute-done.25.recv_p.refs_1_) | copy-start | bytes 3538948
  152.7 28.5 %collective-permute-start.10 = (f32[2,2,48,768]{3,2,1,0:T(8,128)S(1)}, f32[2,2,48,768]{3,2,1,0:T(8,128)S(1)}, u32[]{:S(2)}, u32[]{:S(2)}) collective-permute-start(f32[2,2,48,768]{3,2,1,0:T(8,128)S(1)} %get-tuple-element.47), channel_id=1, source_target_pairs={{0,12},{1,13},{2,14},{3,15},{4,0},{5,1},{6,2},{7,3},{8,4},{9,5},{1... | collective-permute-start | bytes 1769480 | tf_op jit(solution)/shard_map/ppermute | solution.py:228
  155.4 17.6 %copy-start.3 = (f32[4,2,48,768]{3,2,1,0:T(8,128)}, f32[4,2,48,768]{3,2,1,0:T(8,128)S(1)}, u32[]{:S(2)}) copy-start(f32[4,2,48,768]{3,2,1,0:T(8,128)S(1)} %collective-permute-done.26.recv_m.refs_2_) | copy-start | bytes 3538948
  155.4 25.8 %collective-permute-start.20 = (f32[2,2,48,768]{3,2,1,0:T(8,128)S(1)}, f32[2,2,48,768]{3,2,1,0:T(8,128)S(1)}, u32[]{:S(2)}, u32[]{:S(2)}) collective-permute-start(f32[2,2,48,768]{3,2,1,0:T(8,128)S(1)} %get-tuple-element.53), channel_id=1, source_target_pairs={{0,4},{1,5},{2,6},{3,7},{4,8},{5,9},{6,10},{7,11},{8,12},{9,13},{1... | collective-permute-start | bytes 1769480 | tf_op jit(solution)/shard_map/ppermute | solution.py:227
  172.2 13.6 %collective-permute-start.21 = (f32[2,2,48,768]{3,2,1,0:T(8,128)S(1)}, f32[2,2,48,768]{3,2,1,0:T(8,128)S(1)}, u32[]{:S(2)}, u32[]{:S(2)}) collective-permute-start(f32[2,2,48,768]{3,2,1,0:T(8,128)S(1)} %get-tuple-element.54), channel_id=1, source_target_pairs={{0,12},{1,13},{2,14},{3,15},{4,0},{5,1},{6,2},{7,3},{8,4},{9,5},{1... | collective-permute-start | bytes 1769480 | tf_op jit(solution)/shard_map/ppermute | solution.py:228
  177.4 17.5 %collective-permute-start.27 = (f32[2,2,48,768]{3,2,1,0:T(8,128)S(1)}, f32[2,2,48,768]{3,2,1,0:T(8,128)S(1)}, u32[]{:S(2)}, u32[]{:S(2)}) collective-permute-start(f32[2,2,48,768]{3,2,1,0:T(8,128)S(1)} %get-tuple-element.64), channel_id=1, source_target_pairs={{0,1},{1,2},{2,3},{3,0},{4,5},{5,6},{6,7},{7,4},{8,9},{9,10},{10,1... | collective-permute-start | bytes 1769480 | tf_op jit(solution)/shard_map/ppermute | solution.py:227
  178.5 16.7 %collective-permute-start.28 = (f32[2,2,48,768]{3,2,1,0:T(8,128)S(1)}, f32[2,2,48,768]{3,2,1,0:T(8,128)S(1)}, u32[]{:S(2)}, u32[]{:S(2)}) collective-permute-start(f32[2,2,48,768]{3,2,1,0:T(8,128)S(1)} %get-tuple-element.65), channel_id=1, source_target_pairs={{0,3},{1,0},{2,1},{3,2},{4,7},{5,4},{6,5},{7,6},{8,11},{9,8},{10,9... | collective-permute-start | bytes 1769480 | tf_op jit(solution)/shard_map/ppermute | solution.py:228
  181.2 26.3 %collective-permute-start.31 = (f32[2,2,48,768]{3,2,1,0:T(8,128)S(1)}, f32[2,2,48,768]{3,2,1,0:T(8,128)S(1)}, u32[]{:S(2)}, u32[]{:S(2)}) collective-permute-start(f32[2,2,48,768]{3,2,1,0:T(8,128)S(1)} %get-tuple-element.71), channel_id=1, source_target_pairs={{0,1},{1,2},{2,3},{3,0},{4,5},{5,6},{6,7},{7,4},{8,9},{9,10},{10,1... | collective-permute-start | bytes 1769480 | tf_op jit(solution)/shard_map/ppermute | solution.py:227
  181.2 38.9 %collective-permute-start.32 = (f32[2,2,48,768]{3,2,1,0:T(8,128)S(1)}, f32[2,2,48,768]{3,2,1,0:T(8,128)S(1)}, u32[]{:S(2)}, u32[]{:S(2)}) collective-permute-start(f32[2,2,48,768]{3,2,1,0:T(8,128)S(1)} %get-tuple-element.72), channel_id=1, source_target_pairs={{0,3},{1,0},{2,1},{3,2},{4,7},{5,4},{6,5},{7,6},{8,11},{9,8},{10,9... | collective-permute-start | bytes 1769480 | tf_op jit(solution)/shard_map/ppermute | solution.py:228
  185.9 34.2 %copy-start.10 = (f32[4,2,48,768]{3,2,1,0:T(8,128)S(1)}, f32[4,2,48,768]{3,2,1,0:T(8,128)}, u32[]{:S(2)}) copy-start(f32[4,2,48,768]{3,2,1,0:T(8,128)} %get-tuple-element.59.refs_0_) | copy-start | bytes 3538948
  190.0 35.7 %collective-permute-start.22 = (f32[4,48,768]{2,1,0:T(8,128)S(1)}, f32[4,48,768]{2,1,0:T(8,128)S(1)}, u32[]{:S(2)}, u32[]{:S(2)}) collective-permute-start(f32[4,48,768]{2,1,0:T(8,128)S(1)} %get-tuple-element.56), channel_id=1, source_target_pairs={{0,1},{1,2},{2,3},{3,0},{4,5},{5,6},{6,7},{7,4},{8,9},{9,10},{10,1... | collective-permute-start | bytes 1769480 | tf_op jit(solution)/shard_map/ppermute | solution.py:236
  194.9 36.4 %collective-permute-start.23 = (f32[4,48,768]{2,1,0:T(8,128)}, f32[4,48,768]{2,1,0:T(8,128)S(1)}, u32[]{:S(2)}, u32[]{:S(2)}) collective-permute-start(f32[4,48,768]{2,1,0:T(8,128)} %get-tuple-element.57), channel_id=1, source_target_pairs={{0,2},{1,3},{2,0},{3,1},{4,6},{5,7},{6,4},{7,5},{8,10},{9,11},{10,... | collective-permute-start | bytes 1769480 | tf_op jit(solution)/shard_map/ppermute | solution.py:236
  195.2 36.1 %collective-permute-start.24 = (f32[4,48,768]{2,1,0:T(8,128)}, f32[4,48,768]{2,1,0:T(8,128)S(1)}, u32[]{:S(2)}, u32[]{:S(2)}) collective-permute-start(f32[4,48,768]{2,1,0:T(8,128)} %get-tuple-element.58), channel_id=1, source_target_pairs={{0,3},{1,0},{2,1},{3,2},{4,7},{5,4},{6,5},{7,6},{8,11},{9,8},{10,9... | collective-permute-start | bytes 1769480 | tf_op jit(solution)/shard_map/ppermute | solution.py:236
  220.1 22.7 %copy-start.25 = (s32[8]{0:T(128)S(1)}, s32[8]{0:T(128)}, u32[]{:S(2)}) copy-start(s32[8]{0:T(128)} %sizes.9) | copy-start | bytes 100
  224.2 17.6 %collective-permute-start.33 = (f32[4,48,768]{2,1,0:T(8,128)}, f32[4,48,768]{2,1,0:T(8,128)S(1)}, u32[]{:S(2)}, u32[]{:S(2)}) collective-permute-start(f32[4,48,768]{2,1,0:T(8,128)} %get-tuple-element.74), channel_id=1, source_target_pairs={{0,4},{1,5},{2,6},{3,7},{4,8},{5,9},{6,10},{7,11},{8,12},{9,13},{1... | collective-permute-start | bytes 1769480 | tf_op jit(solution)/shard_map/ppermute | solution.py:236
  224.2 17.6 %collective-permute-start.34 = (f32[4,48,768]{2,1,0:T(8,128)}, f32[4,48,768]{2,1,0:T(8,128)}, u32[]{:S(2)}, u32[]{:S(2)}) collective-permute-start(f32[4,48,768]{2,1,0:T(8,128)} %get-tuple-element.75), channel_id=1, source_target_pairs={{0,8},{1,9},{2,10},{3,11},{4,12},{5,13},{6,14},{7,15},{8,0},{9,1},... | collective-permute-start | bytes 1769480 | tf_op jit(solution)/shard_map/ppermute | solution.py:236
  225.6 17.2 %collective-permute-start.35 = (f32[4,48,768]{2,1,0:T(8,128)}, f32[4,48,768]{2,1,0:T(8,128)}, u32[]{:S(2)}, u32[]{:S(2)}) collective-permute-start(f32[4,48,768]{2,1,0:T(8,128)} %get-tuple-element.76), channel_id=1, source_target_pairs={{0,12},{1,13},{2,14},{3,15},{4,0},{5,1},{6,2},{7,3},{8,4},{9,5},{1... | collective-permute-start | bytes 1769480 | tf_op jit(solution)/shard_map/ppermute | solution.py:236
  (14 other events, 32.5 us)

commit v3 on v2

v3 whole, which is shorter than its diff:
```python
import functools

import jax
import jax.numpy as jnp
import numpy as np
from jax import lax
from jax.experimental import pallas as pl
from jax.experimental.pallas import tpu as pltpu
from jax.sharding import PartitionSpec as P

SIDE = 4
VMEM = 20 * 1024 * 1024
LIGHT = pl.CostEstimate(flops=0, bytes_accessed=0, transcendentals=0)
SOURCES = [(dz, dc) for dz in (0, -1, 1, 2) for dc in (0, 1)]


def hops(count, stride, delta):
    pairs = []
    for i in range(count):
        d = (i // stride) % SIDE
        pairs.append((i, i + ((d + delta) % SIDE - d) * stride))
    return pairs


Z_HOPS = {d: hops(8, 2, d) for d in (1, 2, -1)}
SWAP = [(i, i ^ 1) for i in range(8)]


def apart(count, stride, delta, cores):
    up, down = hops(count, stride, delta), hops(count, stride, -delta)
    return [(down if cores(i) else up)[i] for i in range(count)]


Z_APART = [apart(8, 2, d, lambda i: i % 2) for d in (1, -1)]
X_HOPS = {d: apart(128, SIDE, d, lambda i: i // 16 % 2) for d in (1, 2, -1)}
Y_HOPS = {d: apart(128, 1, d, lambda i: i // 16 % 2) for d in (1, 2, -1)}
BOTH = ("vb", "ob")


def places(axis):
    table = np.zeros((8, 16, 16), np.int32)
    for vb in range(8):
        for ob in range(16):
            x, y = divmod(ob, SIDE)
            for a, (dz, dc) in enumerate(SOURCES):
                core = (vb % 2) ^ dc
                source = 2 * ((vb // 2 + (-dz if core else dz)) % SIDE) + core
                for h in range(2):
                    to_x, to_y = divmod(2 * source + h, SIDE)
                    sign = -1 if vb % 2 else 1
                    rel_x, rel_y = sign * (to_x - x) % SIDE, sign * (to_y - y) % SIDE
                    first, second = (rel_x, rel_y) if axis == "x" else (rel_y, rel_x)
                    table[vb, ob, 2 * a + h] = SIDE * first + second
    return table


PLACES = np.concatenate([places("x"), places("y")], axis=2)


def product_kernel(v_first, place_at, place, sizes, origin, *refs):
    pieces, (v_ref, send_p, send_m, up, down, own, a_all, v_all) = refs[:8], refs[8:]
    rows = send_p.shape[1]
    depth = v_ref.shape[1]
    for a, piece in enumerate(pieces):
        for h in range(2):
            block = piece[0, h * rows : (h + 1) * rows]
            hi = block.astype(jnp.bfloat16)
            lo = (block - hi.astype(jnp.float32)).astype(jnp.bfloat16)
            at = pl.ds(pl.multiple_of(place[place_at + 2 * a + h] * rows, rows), rows)
            a_all[at, 0:depth] = hi
            a_all[at, depth : 2 * depth] = lo
            a_all[at, 2 * depth : 3 * depth] = hi
    size = sizes[v_first + pl.program_id(0)]
    shape = v_ref.shape[1:]
    p = origin[0] + lax.broadcasted_iota(jnp.int32, shape, 0)
    q = origin[1] + lax.broadcasted_iota(jnp.int32, shape, 1)
    v = jnp.where((p < size) & (q < size), v_ref[0], 0.0)
    hi = v.astype(jnp.bfloat16)
    v_all[0:depth] = hi
    v_all[depth : 2 * depth] = hi
    v_all[2 * depth : 3 * depth] = (v - hi.astype(jnp.float32)).astype(jnp.bfloat16)

    def chunk(k):
        acc = jnp.dot(
            a_all[SIDE * rows * k : SIDE * rows * (k + 1)], v_all[...], preferred_element_type=jnp.float32
        )
        return [acc[rows * s : rows * (s + 1)] for s in range(SIDE)]

    far = chunk(2)
    send_p[0], send_p[1], send_m[0], send_m[1] = far
    up[0], up[1], send_p[2], send_p[3] = chunk(1)
    send_m[2], send_m[3], down[0], down[1] = chunk(3)
    own[0], own[1], own[2], own[3] = chunk(0)


def product(pieces, skip, ovov, v_first, count, place, place_at, sizes, origin, name):
    rows2, depth = pieces[0][0].shape[1:]
    rows = rows2 // 2
    cols = ovov.shape[2]
    leads = (4, 4, 2, 2, 4)
    total = 16 * rows
    return pl.pallas_call(
        functools.partial(product_kernel, v_first, place_at),
        grid_spec=pltpu.PrefetchScalarGridSpec(
            num_scalar_prefetch=3,
            grid=(count,),
            in_specs=[
                pl.BlockSpec((1, rows2, depth), lambda g, *_, at=at: (at + skip + g, 0, 0)) for _, at in pieces
            ]
            + [pl.BlockSpec((1, depth, cols), lambda g, *_: (v_first + g, 0, 0))],
            out_specs=[pl.BlockSpec((n, rows, cols), lambda g, *_: (g, 0, 0)) for n in leads],
            scratch_shapes=[
                pltpu.VMEM((total, 3 * depth), jnp.bfloat16),
                pltpu.VMEM((3 * depth, cols), jnp.bfloat16),
            ],
        ),
        out_shape=[
            jax.ShapeDtypeStruct((n * count, rows, cols), jnp.float32) for n in leads
        ],
        compiler_params=pltpu.CompilerParams(vmem_limit_bytes=VMEM),
        cost_estimate=LIGHT,
        name=name,
    )(place, sizes, origin, *[piece for piece, _ in pieces], ovov)


def add_kernel(mid, recv, out):
    out[...] = mid[...] + recv[...]


def add_far(mid, recv, name):
    lead, rows, cols = mid.shape
    spec = pl.BlockSpec((2, rows, cols), lambda g: (g, 0, 0))
    return pl.pallas_call(
        add_kernel,
        grid=(lead // 2,),
        in_specs=[spec, pl.BlockSpec((2, rows, cols), lambda g: (2 * g, 0, 0))],
        out_specs=spec,
        out_shape=jax.ShapeDtypeStruct(mid.shape, jnp.float32),
        compiler_params=pltpu.CompilerParams(vmem_limit_bytes=VMEM),
        cost_estimate=LIGHT,
        name=name,
    )(mid, recv)


def own_kernel(counts, *refs):
    ins, outs = refs[:-4], refs[-4:]
    at = 0
    for i, count in enumerate(counts):
        own, p1, m1, p2, m2 = ins[5 * i : 5 * i + 5]
        for g in range(count):
            a, b = 4 * g, 2 * g
            outs[0][at + g] = own[a] + (p2[b] + m1[a + 2])
            outs[1][at + g] = own[a + 1] + (p2[b + 1] + m1[a + 3])
            outs[2][at + g] = own[a + 2] + (m2[b] + p1[a + 2])
            outs[3][at + g] = own[a + 3] + (m2[b + 1] + p1[a + 3])
        at += count


def add_own(groups, name):
    counts = [group[0].shape[0] // 4 for group in groups]
    rows, cols = groups[0][0].shape[1:]
    flat = [r for group in groups for r in group]
    vmem = pl.BlockSpec(memory_space=pltpu.VMEM)
    return pl.pallas_call(
        functools.partial(own_kernel, counts),
        in_specs=[vmem] * len(flat),
        out_specs=[vmem] * 4,
        out_shape=[jax.ShapeDtypeStruct((sum(counts), rows, cols), jnp.float32)] * 4,
        compiler_params=pltpu.CompilerParams(vmem_limit_bytes=VMEM),
        cost_estimate=LIGHT,
        name=name,
    )(*flat)


def finish_kernel(order, sizes, origin, *refs):
    out = refs[-1]
    rows, _, cols = out.shape
    row = origin[0] + lax.broadcasted_iota(jnp.int32, (rows, cols), 0)
    for i, irreps in enumerate(order):
        parts = refs[4 * i : 4 * i + 4]
        for at, g in enumerate(irreps):
            total = (parts[0][at] + parts[1][at]) + (parts[2][at] + parts[3][at])
            out[:, g, :] = jnp.where(row < sizes[g], total, 0.0)


def finish(order, parts, row_sizes, origin, shape):
    flat = [p for four in parts for p in four]
    vmem = pl.BlockSpec(memory_space=pltpu.VMEM)
    smem = pl.BlockSpec(memory_space=pltpu.SMEM)
    return pl.pallas_call(
        functools.partial(finish_kernel, order),
        in_specs=[smem, smem] + [vmem] * len(flat),
        out_specs=vmem,
        out_shape=jax.ShapeDtypeStruct(shape, jnp.float32),
        compiler_params=pltpu.CompilerParams(vmem_limit_bytes=VMEM),
        cost_estimate=LIGHT,
        name="finish",
    )(row_sizes, origin, *flat)


GROUPS = ((0, 1, 1), (2, 1, 1), (4, 2, 2))


def tie_kernel(*refs):
    pass


def tie(values, after):
    if not after:
        return list(values)
    anywhere = pl.BlockSpec(memory_space=pl.ANY)
    return pl.pallas_call(
        tie_kernel,
        in_specs=[anywhere] * (len(values) + len(after)),
        out_specs=[anywhere] * len(values),
        out_shape=[jax.ShapeDtypeStruct(v.shape, v.dtype) for v in values],
        input_output_aliases={i: i for i in range(len(values))},
        cost_estimate=LIGHT,
        name="tie",
    )(*values, *after)


def local(amplitudes, ovov, row_sizes, pair_sizes):
    ob = lax.axis_index("ob")
    vb = lax.axis_index("vb")
    local_rows, irreps, pairs = amplitudes.shape
    obs = lax.axis_size("ob")
    depth, cols = ovov.shape[1:]
    out_rows = local_rows * lax.axis_size("vb")
    place = lax.dynamic_slice(jnp.asarray(PLACES), (vb, ob, 0), (1, 1, 32)).reshape(32)

    origin = jnp.stack([ob * depth, vb * cols]).astype(jnp.int32)

    mine = jnp.transpose(amplitudes.reshape(local_rows, irreps, obs, depth), (2, 0, 1, 3))
    mine = lax.all_to_all(
        mine.reshape(obs, local_rows * irreps, depth), "ob", split_axis=0, concat_axis=0, tiled=True
    )
    mine = jnp.transpose(mine.reshape(obs * local_rows, irreps, depth), (1, 0, 2))

    mine_swapped = lax.ppermute(mine, "vb", SWAP)
    axes = (("x", X_HOPS, Y_HOPS, 0), ("y", Y_HOPS, X_HOPS, 16))
    order = {axis: [] for axis, *_ in axes}
    sums = {axis: [] for axis, *_ in axes}
    parts_of = [mine[first : first + nx + ny] for first, nx, ny in GROUPS]
    landed, sent, got, newer, older = [], [], [], [], []

    def gather(held):
        return [lax.ppermute(held, "vb", pairs) for pairs in (*Z_APART, Z_HOPS[2])]

    landed = gather(parts_of[0])
    for t, (first, nx, ny) in enumerate(GROUPS):
        if t + 1 < len(GROUPS):
            following, *landed = tie([parts_of[t + 1], *landed], sent) if sent else (parts_of[t + 1], *landed)
            (following,) = tie([following], landed)
        else:
            landed = tie(landed, sent + got)
        pieces = [(mine, first), (mine_swapped, first)]
        (swapped,) = tie([lax.ppermute(jnp.concatenate(landed), "vb", SWAP)], older if t > 1 else got)
        for i, moved in enumerate(landed):
            pieces += [(moved, 0), (swapped, i * (nx + ny))]
        if t + 1 < len(GROUPS):
            landed = gather(following)
        sent, got, older = [], [], newer
        newer = []
        for axis, here, there, place_at in axes:
            skip, count = (0, nx) if axis == "x" else (nx, ny)
            order[axis] += range(first + skip, first + skip + count)
            send_p, send_m, up, down, mid = product(
                pieces, skip, ovov, first + skip, count, place, place_at, pair_sizes, origin, f"{axis}_product"
            )
            sent.append(send_p)
            p1 = lax.ppermute(send_p, BOTH, here[1])
            m1 = lax.ppermute(send_m, BOTH, here[-1])
            got += [p1, m1]
            p2 = lax.ppermute(add_far(up, p1, f"{axis}_add"), BOTH, here[1])
            m2 = lax.ppermute(add_far(down, m1, f"{axis}_add"), BOTH, here[-1])
            newer += [p2, m2]
            sums[axis].append((mid, p1, m1, p2, m2))

    parts = []
    for axis, here, there, _ in axes:
        four = add_own(sums[axis], f"{axis}_own")
        parts.append([four[0]] + [lax.ppermute(four[k], BOTH, there[d]) for k, d in ((1, 1), (2, 2), (3, -1))])
    origin = jnp.stack([ob * out_rows, vb * cols]).astype(jnp.int32)
    return finish([order[axis] for axis, *_ in axes], parts, row_sizes, origin, (out_rows, irreps, cols))


def solution(mesh):
    placed = (P(("vb", "ob"), None, None), P(None, "ob", "vb"), P(), P())
    return jax.shard_map(
        local, mesh=mesh, in_specs=placed, out_specs=P("ob", None, "vb"), check_vma=False
    )
```

time: 247 us -> 282 us (1.14)
  local copies, waits for them, and re-layouts: 8.91 us -> 40.9 us
  waiting for transfers between devices: 117 us -> 108 us
  starting transfers between devices: 51.6 us -> 60.3 us
  other arithmetic: 0.15 us -> 4.89 us
  Pallas kernels: 42.1 us -> 38.8 us
    unnamed x53 -> x137, local copies, waits for them, and re-layouts: 7.53 us -> 38 us
    ppermute x36 -> x43, waiting for transfers between devices: 117 us -> 108 us  [the longest x6 39.6 us: local(): p1 = lax.ppermute(send_p, BOTH, here[1])]
    ppermute x36 -> x43, starting transfers between devices: 51.6 us -> 60.3 us  [the longest x6 18.6 us: local(): m1 = lax.ppermute(send_m, BOTH, here[-1])]
    pallas_call x4 -> x6, Pallas kernels: 29.3 us -> 24.6 us  [product(): pl.pallas_call(functools.partial(product_kernel, v_first, place_at), grid...]
    concatenate x0 -> x3, other arithmetic: none -> 4.74 us  [local(): jnp.concatenate(landed)]
    pallas_call x4 -> x18, Pallas kernels: 1.73 us -> 5.67 us  [the longest x12 5.67 us: add_far(): pl.pallas_call(add_kernel, grid=(lead // 2,), in_specs=[spec, pl.BlockSpe...]
  transfers between devices with their start and end apart: 36 -> 43, of which waited for: 15 -> 14; matrix products, arithmetic and copies ran while one was open for 0% -> 2% of each run, Pallas kernels for 16% -> 11%
where the time goes in v3:
time: 282 us; the launch traced here: 279 us
  waiting for transfers between devices  108 us (38%)
  starting transfers between devices  60.3 us (21%)
  local copies, waits for them, and re-layouts  40.9 us (15%)
  Pallas kernels  38.8 us (14%)
  blocking collectives  25.4 us (9%)
  other arithmetic  4.89 us (2%)
    ppermute x6, waiting for transfers between devices, local(): p1 = lax.ppermute(send_p, BOTH, here[1])  39.6 us
    unnamed x137, local copies, waits for them, and re-layouts  38 us
    ppermute x6, waiting for transfers between devices, local(): p2 = lax.ppermute(add_far(up, p1, f'{axis}_add'), BOTH, here[1])  28.4 us
    ppermute x6, waiting for transfers between devices, local(): lax.ppermute(four[k], BOTH, there[d])  26.3 us
    all_to_all x1, blocking collectives, local(): lax.all_to_all(mine.reshape(obs, local_rows * irreps, depth), 'ob', split...  25.4 us
    pallas_call x6, Pallas kernels, product(): pl.pallas_call(functools.partial(product_kernel, v_first, place_at), grid...  24.6 us
    ppermute x6, starting transfers between devices, local(): m1 = lax.ppermute(send_m, BOTH, here[-1])  18.6 us
    ppermute x9, starting transfers between devices, gather(): return [lax.ppermute(held, 'vb', pairs) for pairs in (*Z_APART, Z_HOPS[2])]  16.5 us
  transfers between devices with their start and end apart: 43, of which 14 were waited for; matrix products, arithmetic and copies ran while one was open for 2% of the time, Pallas kernels for 11%

profile of v3, /device:TPU:0, one launch (start us, length us, event | category | flops | bytes accessed | tf_op | source)
XLA Modules:
  0.0 279.3 jit_solution(13294987536597819219)
XLA Ops:
  1.9 25.4 %all_to_all.5 = f32[16,48,384]{2,1,0:T(8,128)S(1)} all-to-all(f32[16,48,384]{2,1,0:T(8,128)S(1)} %bitcast.30), channel_id=1, replica_groups=mesh['vb'=8,'ob'=16] {'ob'}, dimensions={0} | all-to-all | bytes 2359296 | tf_op jit(solution)/shard_map/all_to_all | solution.py:235
  28.2 1.9 collective-permute-start.1
  30.2 3.6 %collective-permute-start.3 = (f32[2,96,384]{2,1,0:T(8,128)S(1)}, f32[2,96,384]{2,1,0:T(8,128)S(1)}, u32[]{:S(2)}, u32[]{:S(2)}) collective-permute-start(f32[2,96,384]{2,1,0:T(8,128)S(1)} %get-tuple-element.96), channel_id=1, source_target_pairs={{0,64},{16,80},{32,96},{48,112},{64,0},{80,16},{96,32},{112,48},{1... | collective-permute-start | bytes 884744 | tf_op jit(solution)/shard_map/ppermute | solution.py:248
  34.8 9.6 %collective-permute-done.1.refs_2_.refs_1_ = f32[2,96,384]{2,1,0:T(8,128)S(1)} collective-permute-done((f32[2,96,384]{2,1,0:T(8,128)S(1)}, f32[2,96,384]{2,1,0:T(8,128)S(1)}, u32[]{:S(2)}, u32[]{:S(2)}) %collective-permute-start.1) | collective-permute-done | bytes 294944 | tf_op jit(solution)/shard_map/ppermute | solution.py:248
  44.3 2.8 %collective-permute-done.3.refs_6_.refs_3_ = f32[2,96,384]{2,1,0:T(8,128)S(1)} collective-permute-done((f32[2,96,384]{2,1,0:T(8,128)S(1)}, f32[2,96,384]{2,1,0:T(8,128)S(1)}, u32[]{:S(2)}, u32[]{:S(2)}) %collective-permute-start.3) | collective-permute-done | bytes 294944 | tf_op jit(solution)/shard_map/ppermute | solution.py:248
  48.3 3.2 %collective-permute-start.10 = (f32[2,96,384]{2,1,0:T(8,128)}, f32[2,96,384]{2,1,0:T(8,128)S(1)}, u32[]{:S(2)}, u32[]{:S(2)}) collective-permute-start(f32[2,96,384]{2,1,0:T(8,128)} %tie.6), channel_id=1, source_target_pairs={{0,96},{16,48},{32,0},{48,80},{64,32},{80,112},{96,64},{112,16},{1... | collective-permute-start | bytes 884744 | tf_op jit(solution)/shard_map/ppermute | solution.py:248
  52.3 4.1 %copy-done = f32[8,384,768]{2,1,0:T(8,128)S(1)} copy-done((f32[8,384,768]{2,1,0:T(8,128)S(1)}, f32[8,384,768]{2,1,0:T(8,128)}, u32[]{:S(2)}) %copy-start) | copy-done | bytes 9437208
  59.3 4.3 %x_product.3 = (f32[4,48,768]{2,1,0:T(8,128)}, f32[4,48,768]{2,1,0:T(8,128)}, f32[2,48,768]{2,1,0:T(8,128)S(1)}, f32[2,48,768]{2,1,0:T(8,128)S(1)}, f32[4,48,768]{2,1,0:T(8,128)S(1)}) custom-call(s32[32]{0:T(128)S(1)} %dynamic-slice_bitcast_fusion.place, s32[8]{0:T(128)S(1)} %copy-done.66, s32[2]{0:T(128)S(1)} %pad_add_fusion.1.origin, ...), custom_call_target="tpu_custom_call" | custom-call | tf_op jit(solution)/shard_map/x_product/pallas_call | solution.py:102
  65.6 2.8 %collective-permute-start.6 = (f32[4,48,768]{2,1,0:T(8,128)}, f32[4,48,768]{2,1,0:T(8,128)}, u32[]{:S(2)}, u32[]{:S(2)}) collective-permute-start(f32[4,48,768]{2,1,0:T(8,128)} %get-tuple-element.52), channel_id=1, source_target_pairs={{0,12},{1,13},{2,14},{3,15},{4,0},{5,1},{6,2},{7,3},{8,4},{9,5},{1... | collective-permute-start | bytes 1769480 | tf_op jit(solution)/shard_map/ppermute | solution.py:273
  69.3 4.4 %y_product.3 = (f32[4,48,768]{2,1,0:T(8,128)}, f32[4,48,768]{2,1,0:T(8,128)}, f32[2,48,768]{2,1,0:T(8,128)S(1)}, f32[2,48,768]{2,1,0:T(8,128)S(1)}, f32[4,48,768]{2,1,0:T(8,128)S(1)}) custom-call(s32[32]{0:T(128)S(1)} %dynamic-slice_bitcast_fusion.place, s32[8]{0:T(128)S(1)} %copy-done.66, s32[2]{0:T(128)S(1)} %pad_add_fusion.1.origin, ...), custom_call_target="tpu_custom_call" | custom-call | tf_op jit(solution)/shard_map/y_product/pallas_call | solution.py:102
  77.0 2.1 pad_maximum_fusion.2
  79.4 2.9 %collective-permute-start.14 = (f32[4,48,768]{2,1,0:T(8,128)}, f32[4,48,768]{2,1,0:T(8,128)}, u32[]{:S(2)}, u32[]{:S(2)}) collective-permute-start(f32[4,48,768]{2,1,0:T(8,128)} %get-tuple-element.59), channel_id=1, source_target_pairs={{0,3},{1,0},{2,1},{3,2},{4,7},{5,4},{6,5},{7,6},{8,11},{9,8},{10,9... | collective-permute-start | bytes 1769480 | tf_op jit(solution)/shard_map/ppermute | solution.py:273
  83.6 2.1 collective-permute-start.20
  85.6 10.9 %collective-permute-done.13.refs_3_.recv.refs_1_ = f32[4,48,768]{2,1,0:T(8,128)} collective-permute-done((f32[4,48,768]{2,1,0:T(8,128)}, f32[4,48,768]{2,1,0:T(8,128)}, u32[]{:S(2)}, u32[]{:S(2)}) %collective-permute-start.13) | collective-permute-done | bytes 589856 | tf_op jit(solution)/shard_map/ppermute | solution.py:272
  96.5 3.5 %collective-permute-start.21 = (f32[4,96,384]{2,1,0:T(8,128)}, f32[4,96,384]{2,1,0:T(8,128)}, u32[]{:S(2)}, u32[]{:S(2)}) collective-permute-start(f32[4,96,384]{2,1,0:T(8,128)} %tie.9), channel_id=1, source_target_pairs={{0,64},{16,80},{32,96},{48,112},{64,0},{80,16},{96,32},{112,48},{1... | collective-permute-start | bytes 1769480 | tf_op jit(solution)/shard_map/ppermute | solution.py:248
  101.0 3.7 %copy-done.1 = f32[8,384,768]{2,1,0:T(8,128)S(1)} copy-done((f32[8,384,768]{2,1,0:T(8,128)S(1)}, f32[8,384,768]{2,1,0:T(8,128)}, u32[]{:S(2)}) %copy-start.1) | copy-done | bytes 9437208
  109.0 2.5 x_product.4
  113.9 3.2 %collective-permute-start.16 = (f32[4,48,768]{2,1,0:T(8,128)S(1)}, f32[4,48,768]{2,1,0:T(8,128)S(1)}, u32[]{:S(2)}, u32[]{:S(2)}) collective-permute-start(f32[4,48,768]{2,1,0:T(8,128)S(1)} %get-tuple-element.62), channel_id=1, source_target_pairs={{0,12},{1,13},{2,14},{3,15},{4,0},{5,1},{6,2},{7,3},{8,4},{9,5},{1... | collective-permute-start | bytes 1769480 | tf_op jit(solution)/shard_map/ppermute | solution.py:273
  117.1 2.5 y_product.4
  121.9 3.2 %collective-permute-start.23 = (f32[4,48,768]{2,1,0:T(8,128)S(1)}, f32[4,48,768]{2,1,0:T(8,128)}, u32[]{:S(2)}, u32[]{:S(2)}) collective-permute-start(f32[4,48,768]{2,1,0:T(8,128)S(1)} %get-tuple-element.67), channel_id=1, source_target_pairs={{0,3},{1,0},{2,1},{3,2},{4,7},{5,4},{6,5},{7,6},{8,11},{9,8},{10,9... | collective-permute-start | bytes 1769480 | tf_op jit(solution)/shard_map/ppermute | solution.py:273
  125.1 2.9 %collective-permute-done.15.recv.refs_5_.refs_6_ = f32[4,48,768]{2,1,0:T(8,128)S(1)} collective-permute-done((f32[4,48,768]{2,1,0:T(8,128)S(1)}, f32[4,48,768]{2,1,0:T(8,128)S(1)}, u32[]{:S(2)}, u32[]{:S(2)}) %collective-permute-start.15) | collective-permute-done | bytes 589856 | tf_op jit(solution)/shard_map/ppermute | solution.py:272
  128.1 6.4 %collective-permute-done.22.refs_7_.recv.refs_6_ = f32[4,48,768]{2,1,0:T(8,128)S(1)} collective-permute-done((f32[4,48,768]{2,1,0:T(8,128)S(1)}, f32[4,48,768]{2,1,0:T(8,128)S(1)}, u32[]{:S(2)}, u32[]{:S(2)}) %collective-permute-start.22) | collective-permute-done | bytes 589856 | tf_op jit(solution)/shard_map/ppermute | solution.py:272
  135.3 1.6 pad_maximum_fusion
  139.5 3.0 %collective-permute-start.8 = (f32[2,48,768]{2,1,0:T(8,128)S(1)}, f32[2,48,768]{2,1,0:T(8,128)S(1)}, u32[]{:S(2)}, u32[]{:S(2)}) collective-permute-start(f32[2,48,768]{2,1,0:T(8,128)S(1)} %x_add.7), channel_id=1, source_target_pairs={{0,12},{1,13},{2,14},{3,15},{4,0},{5,1},{6,2},{7,3},{8,4},{9,5},{1... | collective-permute-start | bytes 884744 | tf_op jit(solution)/shard_map/ppermute | solution.py:276
  145.0 2.9 %collective-permute-start.26 = (f32[2,48,768]{2,1,0:T(8,128)S(1)}, f32[2,48,768]{2,1,0:T(8,128)S(1)}, u32[]{:S(2)}, u32[]{:S(2)}) collective-permute-start(f32[2,48,768]{2,1,0:T(8,128)S(1)} %y_add.7), channel_id=1, source_target_pairs={{0,3},{1,0},{2,1},{3,2},{4,7},{5,4},{6,5},{7,6},{8,11},{9,8},{10,9... | collective-permute-start | bytes 884744 | tf_op jit(solution)/shard_map/ppermute | solution.py:276
  147.9 6.3 %collective-permute-done.25.refs_3_ = f32[2,48,768]{2,1,0:T(8,128)S(1)} collective-permute-done((f32[2,48,768]{2,1,0:T(8,128)S(1)}, f32[2,48,768]{2,1,0:T(8,128)S(1)}, u32[]{:S(2)}, u32[]{:S(2)}) %collective-permute-start.25) | collective-permute-done | bytes 294944 | tf_op jit(solution)/shard_map/ppermute | solution.py:275
  156.9 3.7 %copy-done.2 = f32[8,384,768]{2,1,0:T(8,128)S(1)} copy-done((f32[8,384,768]{2,1,0:T(8,128)S(1)}, f32[8,384,768]{2,1,0:T(8,128)}, u32[]{:S(2)}) %copy-start.2) | copy-done | bytes 9437208
  164.4 5.4 %x_product.5 = (f32[8,48,768]{2,1,0:T(8,128)S(1)}, f32[8,48,768]{2,1,0:T(8,128)S(1)}, f32[4,48,768]{2,1,0:T(8,128)S(1)}, f32[4,48,768]{2,1,0:T(8,128)S(1)}, f32[8,48,768]{2,1,0:T(8,128)S(1)}) custom-call(s32[32]{0:T(128)S(1)} %dynamic-slice_bitcast_fusion.place, s32[8]{0:T(128)S(1)} %copy-done.66, s32[2]{0:T(128)S(1)} %pad_add_fusion.1.origin, ...), custom_call_target="tpu_custom_call" | custom-call | tf_op jit(solution)/shard_map/x_product/pallas_call | solution.py:102
  170.0 3.2 %collective-permute-start.28 = (f32[8,48,768]{2,1,0:T(8,128)S(1)}, f32[8,48,768]{2,1,0:T(8,128)S(1)}, u32[]{:S(2)}, u32[]{:S(2)}) collective-permute-start(f32[8,48,768]{2,1,0:T(8,128)S(1)} %get-tuple-element.75), channel_id=1, source_target_pairs={{0,12},{1,13},{2,14},{3,15},{4,0},{5,1},{6,2},{7,3},{8,4},{9,5},{1... | collective-permute-start | bytes 3538952 | tf_op jit(solution)/shard_map/ppermute | solution.py:273
  173.2 5.4 %y_product.5 = (f32[8,48,768]{2,1,0:T(8,128)S(1)}, f32[8,48,768]{2,1,0:T(8,128)S(1)}, f32[4,48,768]{2,1,0:T(8,128)S(1)}, f32[4,48,768]{2,1,0:T(8,128)S(1)}, f32[8,48,768]{2,1,0:T(8,128)S(1)}) custom-call(s32[32]{0:T(128)S(1)} %dynamic-slice_bitcast_fusion.place, s32[8]{0:T(128)S(1)} %copy-done.66, s32[2]{0:T(128)S(1)} %pad_add_fusion.1.origin, ...), custom_call_target="tpu_custom_call" | custom-call | tf_op jit(solution)/shard_map/y_product/pallas_call | solution.py:102
  178.7 3.2 %collective-permute-start.37 = (f32[8,48,768]{2,1,0:T(8,128)S(1)}, f32[8,48,768]{2,1,0:T(8,128)S(1)}, u32[]{:S(2)}, u32[]{:S(2)}) collective-permute-start(f32[8,48,768]{2,1,0:T(8,128)S(1)} %get-tuple-element.88), channel_id=1, source_target_pairs={{0,3},{1,0},{2,1},{3,2},{4,7},{5,4},{6,5},{7,6},{8,11},{9,8},{10,9... | collective-permute-start | bytes 3538952 | tf_op jit(solution)/shard_map/ppermute | solution.py:273
  181.9 16.7 %collective-permute-done.27.recv.refs_11_ = f32[8,48,768]{2,1,0:T(8,128)S(1)} collective-permute-done((f32[8,48,768]{2,1,0:T(8,128)S(1)}, f32[8,48,768]{2,1,0:T(8,128)S(1)}, u32[]{:S(2)}, u32[]{:S(2)}) %collective-permute-start.27) | collective-permute-done | bytes 1179680 | tf_op jit(solution)/shard_map/ppermute | solution.py:272
  198.9 3.2 %collective-permute-start.30 = (f32[4,48,768]{2,1,0:T(8,128)S(1)}, f32[4,48,768]{2,1,0:T(8,128)S(1)}, u32[]{:S(2)}, u32[]{:S(2)}) collective-permute-start(f32[4,48,768]{2,1,0:T(8,128)S(1)} %x_add.11), channel_id=1, source_target_pairs={{0,12},{1,13},{2,14},{3,15},{4,0},{5,1},{6,2},{7,3},{8,4},{9,5},{1... | collective-permute-start | bytes 1769480 | tf_op jit(solution)/shard_map/ppermute | solution.py:276
  202.4 2.7 collective-permute-done.36.recv.refs_11_
  205.1 2.0 collective-permute-start.18
  207.8 12.4 %collective-permute-done.17.refs_8_ = f32[2,48,768]{2,1,0:T(8,128)S(1)} collective-permute-done((f32[2,48,768]{2,1,0:T(8,128)S(1)}, f32[2,48,768]{2,1,0:T(8,128)S(1)}, u32[]{:S(2)}, u32[]{:S(2)}) %collective-permute-start.17) | collective-permute-done | bytes 294944 | tf_op jit(solution)/shard_map/ppermute | solution.py:275
  220.3 2.7 x_own.1
  223.0 2.0 collective-permute-start.31
  226.3 3.2 %collective-permute-start.35 = (f32[2,48,768]{2,1,0:T(8,128)S(1)}, f32[2,48,768]{2,1,0:T(8,128)S(1)}, u32[]{:S(2)}, u32[]{:S(2)}) collective-permute-start(f32[2,48,768]{2,1,0:T(8,128)S(1)} %y_add.9), channel_id=1, source_target_pairs={{0,3},{1,0},{2,1},{3,2},{4,7},{5,4},{6,5},{7,6},{8,11},{9,8},{10,9... | collective-permute-start | bytes 884744 | tf_op jit(solution)/shard_map/ppermute | solution.py:276
  229.5 9.7 %collective-permute-done.34.refs_8_ = f32[2,48,768]{2,1,0:T(8,128)S(1)} collective-permute-done((f32[2,48,768]{2,1,0:T(8,128)S(1)}, f32[2,48,768]{2,1,0:T(8,128)S(1)}, u32[]{:S(2)}, u32[]{:S(2)}) %collective-permute-start.34) | collective-permute-done | bytes 294944 | tf_op jit(solution)/shard_map/ppermute | solution.py:275
  239.2 1.5 collective-permute-start.32
  240.7 1.6 collective-permute-done.35.refs_9_
  243.8 3.0 %y_own.1 = (f32[4,48,768]{2,1,0:T(8,128)S(1)}, f32[4,48,768]{2,1,0:T(8,128)}, f32[4,48,768]{2,1,0:T(8,128)}, f32[4,48,768]{2,1,0:T(8,128)}) custom-call(f32[4,48,768]{2,1,0:T(8,128)S(1)} %copy-done.41, f32[4,48,768]{2,1,0:T(8,128)} %collective-permute-done.13.refs_3_.recv.refs_1_, f32[4,48,768]{2,1,0:T(8,128)} %collective-permute-done.14.refs_4_.recv.refs_2_, ...), custom_call_target="tpu_custom_call" | custom-call | tf_op jit(solution)/shard_map/y_own/pallas_call | solution.py:164
  247.7 2.3 collective-permute-start.42
  250.1 5.1 %collective-permute-done.32.refs_2_ = f32[4,48,768]{2,1,0:T(8,128)S(1)} collective-permute-done((f32[4,48,768]{2,1,0:T(8,128)}, f32[4,48,768]{2,1,0:T(8,128)S(1)}, u32[]{:S(2)}, u32[]{:S(2)}) %collective-permute-start.32) | collective-permute-done | bytes 589856 | tf_op jit(solution)/shard_map/ppermute | solution.py:283
  255.3 6.0 %collective-permute-done.33.refs_3_ = f32[4,48,768]{2,1,0:T(8,128)S(1)} collective-permute-done((f32[4,48,768]{2,1,0:T(8,128)}, f32[4,48,768]{2,1,0:T(8,128)S(1)}, u32[]{:S(2)}, u32[]{:S(2)}) %collective-permute-start.33) | collective-permute-done | bytes 589856 | tf_op jit(solution)/shard_map/ppermute | solution.py:283
  261.3 15.2 %collective-permute-done.40.refs_5_ = f32[4,48,768]{2,1,0:T(8,128)S(1)} collective-permute-done((f32[4,48,768]{2,1,0:T(8,128)}, f32[4,48,768]{2,1,0:T(8,128)S(1)}, u32[]{:S(2)}, u32[]{:S(2)}) %collective-permute-start.40) | collective-permute-done | bytes 589856 | tf_op jit(solution)/shard_map/ppermute | solution.py:283
  276.5 2.8 %finish.1 = f32[48,8,768]{2,1,0:T(8,128)} custom-call(s32[8]{0:T(128)S(1)} %copy-done.67, s32[2]{0:T(128)S(1)} %pad_add_fusion.origin, f32[4,48,768]{2,1,0:T(8,128)S(1)} %get-tuple-element.78.refs_0_, f32[4,48,768]{2,1,0:T(8,128)S(1)} %collective-permute-done.31.refs_1_, f32[4,48,768]{2,1,0:T(8,128)S(1)} %collective-permute-done.32.refs_2_, ...), custom_call_target="tpu_custom_call" | custom-call | tf_op jit(solution)/shard_map/finish/pallas_call | solution.py:190
  (213 shorter events, 43.5 us)
Async XLA Ops:
  28.2 16.1 %collective-permute-start.1 = (f32[2,96,384]{2,1,0:T(8,128)S(1)}, f32[2,96,384]{2,1,0:T(8,128)S(1)}, u32[]{:S(2)}, u32[]{:S(2)}) collective-permute-start(f32[2,96,384]{2,1,0:T(8,128)S(1)} %get-tuple-element.96), channel_id=1, source_target_pairs={{0,32},{16,112},{32,64},{48,16},{64,96},{80,48},{96,0},{112,80},{1... | collective-permute-start | bytes 884744 | tf_op jit(solution)/shard_map/ppermute | solution.py:248
  30.2 17.0 %collective-permute-start.3 = (f32[2,96,384]{2,1,0:T(8,128)S(1)}, f32[2,96,384]{2,1,0:T(8,128)S(1)}, u32[]{:S(2)}, u32[]{:S(2)}) collective-permute-start(f32[2,96,384]{2,1,0:T(8,128)S(1)} %get-tuple-element.96), channel_id=1, source_target_pairs={{0,64},{16,80},{32,96},{48,112},{64,0},{80,16},{96,32},{112,48},{1... | collective-permute-start | bytes 884744 | tf_op jit(solution)/shard_map/ppermute | solution.py:248
  33.7 13.4 %collective-permute-start.2 = (f32[2,96,384]{2,1,0:T(8,128)S(1)}, f32[2,96,384]{2,1,0:T(8,128)S(1)}, u32[]{:S(2)}, u32[]{:S(2)}) collective-permute-start(f32[2,96,384]{2,1,0:T(8,128)S(1)} %get-tuple-element.96), channel_id=1, source_target_pairs={{0,96},{16,48},{32,0},{48,80},{64,32},{80,112},{96,64},{112,16},{1... | collective-permute-start | bytes 884744 | tf_op jit(solution)/shard_map/ppermute | solution.py:248
  34.7 17.6 %collective-permute-start = (f32[8,96,384]{2,1,0:T(8,128)S(1)}, f32[8,96,384]{2,1,0:T(8,128)S(1)}, u32[]{:S(2)}, u32[]{:S(2)}) collective-permute-start(f32[8,96,384]{2,1,0:T(8,128)S(1)} %bitcast.22), channel_id=1, source_target_pairs={{0,16},{16,0},{32,48},{48,32},{64,80},{80,64},{96,112},{112,96},{1... | collective-permute-start | bytes 3538952 | tf_op jit(solution)/shard_map/ppermute | solution.py:240
  48.2 4.1 %collective-permute-start.4 = (f32[6,96,384]{2,1,0:T(8,128)}, f32[6,96,384]{2,1,0:T(8,128)}, u32[]{:S(2)}, u32[]{:S(2)}) collective-permute-start(f32[6,96,384]{2,1,0:T(8,128)} %pad_maximum_fusion.1), channel_id=1, source_target_pairs={{0,16},{16,0},{32,48},{48,32},{64,80},{80,64},{96,112},{112,96},{1... | collective-permute-start | bytes 2654216 | tf_op jit(solution)/shard_map/ppermute | solution.py:258
  48.3 27.8 %collective-permute-start.9 = (f32[2,96,384]{2,1,0:T(8,128)}, f32[2,96,384]{2,1,0:T(8,128)S(1)}, u32[]{:S(2)}, u32[]{:S(2)}) collective-permute-start(f32[2,96,384]{2,1,0:T(8,128)} %tie.6), channel_id=1, source_target_pairs={{0,32},{16,112},{32,64},{48,16},{64,96},{80,48},{96,0},{112,80},{1... | collective-permute-start | bytes 884744 | tf_op jit(solution)/shard_map/ppermute | solution.py:248
  48.3 27.7 %collective-permute-start.10 = (f32[2,96,384]{2,1,0:T(8,128)}, f32[2,96,384]{2,1,0:T(8,128)S(1)}, u32[]{:S(2)}, u32[]{:S(2)}) collective-permute-start(f32[2,96,384]{2,1,0:T(8,128)} %tie.6), channel_id=1, source_target_pairs={{0,96},{16,48},{32,0},{48,80},{64,32},{80,112},{96,64},{112,16},{1... | collective-permute-start | bytes 884744 | tf_op jit(solution)/shard_map/ppermute | solution.py:248
  51.5 24.5 %collective-permute-start.11 = (f32[2,96,384]{2,1,0:T(8,128)}, f32[2,96,384]{2,1,0:T(8,128)S(1)}, u32[]{:S(2)}, u32[]{:S(2)}) collective-permute-start(f32[2,96,384]{2,1,0:T(8,128)} %tie.6), channel_id=1, source_target_pairs={{0,64},{16,80},{32,96},{48,112},{64,0},{80,16},{96,32},{112,48},{1... | collective-permute-start | bytes 884744 | tf_op jit(solution)/shard_map/ppermute | solution.py:248
  65.1 17.2 %collective-permute-start.5 = (f32[4,48,768]{2,1,0:T(8,128)}, f32[4,48,768]{2,1,0:T(8,128)}, u32[]{:S(2)}, u32[]{:S(2)}) collective-permute-start(f32[4,48,768]{2,1,0:T(8,128)} %get-tuple-element.51.refs_4_), channel_id=1, source_target_pairs={{0,4},{1,5},{2,6},{3,7},{4,8},{5,9},{6,10},{7,11},{8,12},{9,13},{1... | collective-permute-start | bytes 1769480 | tf_op jit(solution)/shard_map/ppermute | solution.py:272
  65.6 18.0 %collective-permute-start.6 = (f32[4,48,768]{2,1,0:T(8,128)}, f32[4,48,768]{2,1,0:T(8,128)}, u32[]{:S(2)}, u32[]{:S(2)}) collective-permute-start(f32[4,48,768]{2,1,0:T(8,128)} %get-tuple-element.52), channel_id=1, source_target_pairs={{0,12},{1,13},{2,14},{3,15},{4,0},{5,1},{6,2},{7,3},{8,4},{9,5},{1... | collective-permute-start | bytes 1769480 | tf_op jit(solution)/shard_map/ppermute | solution.py:273
  79.1 20.9 %collective-permute-start.12 = (f32[6,96,384]{2,1,0:T(8,128)}, f32[6,96,384]{2,1,0:T(8,128)S(1)}, u32[]{:S(2)}, u32[]{:S(2)}) collective-permute-start(f32[6,96,384]{2,1,0:T(8,128)} %pad_maximum_fusion.2), channel_id=1, source_target_pairs={{0,16},{16,0},{32,48},{48,32},{64,80},{80,64},{96,112},{112,96},{1... | collective-permute-start | bytes 2654216 | tf_op jit(solution)/shard_map/ppermute | solution.py:258
  79.1 17.4 %collective-permute-start.13 = (f32[4,48,768]{2,1,0:T(8,128)}, f32[4,48,768]{2,1,0:T(8,128)}, u32[]{:S(2)}, u32[]{:S(2)}) collective-permute-start(f32[4,48,768]{2,1,0:T(8,128)} %get-tuple-element.55.refs_5_), channel_id=1, source_target_pairs={{0,1},{1,2},{2,3},{3,0},{4,5},{5,6},{6,7},{7,4},{8,9},{9,10},{10,1... | collective-permute-start | bytes 1769480 | tf_op jit(solution)/shard_map/ppermute | solution.py:272
  79.4 20.6 %collective-permute-start.14 = (f32[4,48,768]{2,1,0:T(8,128)}, f32[4,48,768]{2,1,0:T(8,128)}, u32[]{:S(2)}, u32[]{:S(2)}) collective-permute-start(f32[4,48,768]{2,1,0:T(8,128)} %get-tuple-element.59), channel_id=1, source_target_pairs={{0,3},{1,0},{2,1},{3,2},{4,7},{5,4},{6,5},{7,6},{8,11},{9,8},{10,9... | collective-permute-start | bytes 1769480 | tf_op jit(solution)/shard_map/ppermute | solution.py:273
  82.4 39.5 %collective-permute-start.19 = (f32[4,96,384]{2,1,0:T(8,128)}, f32[4,96,384]{2,1,0:T(8,128)S(1)}, u32[]{:S(2)}, u32[]{:S(2)}) collective-permute-start(f32[4,96,384]{2,1,0:T(8,128)} %tie.9), channel_id=1, source_target_pairs={{0,32},{16,112},{32,64},{48,16},{64,96},{80,48},{96,0},{112,80},{1... | collective-permute-start | bytes 1769480 | tf_op jit(solution)/shard_map/ppermute | solution.py:248
  83.6 38.4 %collective-permute-start.20 = (f32[4,96,384]{2,1,0:T(8,128)}, f32[4,96,384]{2,1,0:T(8,128)S(1)}, u32[]{:S(2)}, u32[]{:S(2)}) collective-permute-start(f32[4,96,384]{2,1,0:T(8,128)} %tie.9), channel_id=1, source_target_pairs={{0,96},{16,48},{32,0},{48,80},{64,32},{80,112},{96,64},{112,16},{1... | collective-permute-start | bytes 1769480 | tf_op jit(solution)/shard_map/ppermute | solution.py:248
  96.5 28.6 %collective-permute-start.21 = (f32[4,96,384]{2,1,0:T(8,128)}, f32[4,96,384]{2,1,0:T(8,128)}, u32[]{:S(2)}, u32[]{:S(2)}) collective-permute-start(f32[4,96,384]{2,1,0:T(8,128)} %tie.9), channel_id=1, source_target_pairs={{0,64},{16,80},{32,96},{48,112},{64,0},{80,16},{96,32},{112,48},{1... | collective-permute-start | bytes 1769480 | tf_op jit(solution)/shard_map/ppermute | solution.py:248
  113.9 14.2 %collective-permute-start.15 = (f32[4,48,768]{2,1,0:T(8,128)S(1)}, f32[4,48,768]{2,1,0:T(8,128)S(1)}, u32[]{:S(2)}, u32[]{:S(2)}) collective-permute-start(f32[4,48,768]{2,1,0:T(8,128)S(1)} %get-tuple-element.61.refs_3_), channel_id=1, source_target_pairs={{0,4},{1,5},{2,6},{3,7},{4,8},{5,9},{6,10},{7,11},{8,12},{9,13},{1... | collective-permute-start | bytes 1769480 | tf_op jit(solution)/shard_map/ppermute | solution.py:272
  113.9 14.2 %collective-permute-start.16 = (f32[4,48,768]{2,1,0:T(8,128)S(1)}, f32[4,48,768]{2,1,0:T(8,128)S(1)}, u32[]{:S(2)}, u32[]{:S(2)}) collective-permute-start(f32[4,48,768]{2,1,0:T(8,128)S(1)} %get-tuple-element.62), channel_id=1, source_target_pairs={{0,12},{1,13},{2,14},{3,15},{4,0},{5,1},{6,2},{7,3},{8,4},{9,5},{1... | collective-permute-start | bytes 1769480 | tf_op jit(solution)/shard_map/ppermute | solution.py:273
  121.9 12.6 %collective-permute-start.22 = (f32[4,48,768]{2,1,0:T(8,128)S(1)}, f32[4,48,768]{2,1,0:T(8,128)S(1)}, u32[]{:S(2)}, u32[]{:S(2)}) collective-permute-start(f32[4,48,768]{2,1,0:T(8,128)S(1)} %get-tuple-element.66.refs_4_), channel_id=1, source_target_pairs={{0,1},{1,2},{2,3},{3,0},{4,5},{5,6},{6,7},{7,4},{8,9},{9,10},{10,1... | collective-permute-start | bytes 1769480 | tf_op jit(solution)/shard_map/ppermute | solution.py:272
  121.9 12.6 %collective-permute-start.23 = (f32[4,48,768]{2,1,0:T(8,128)S(1)}, f32[4,48,768]{2,1,0:T(8,128)}, u32[]{:S(2)}, u32[]{:S(2)}) collective-permute-start(f32[4,48,768]{2,1,0:T(8,128)S(1)} %get-tuple-element.67), channel_id=1, source_target_pairs={{0,3},{1,0},{2,1},{3,2},{4,7},{5,4},{6,5},{7,6},{8,11},{9,8},{10,9... | collective-permute-start | bytes 1769480 | tf_op jit(solution)/shard_map/ppermute | solution.py:273
  136.9 18.8 %collective-permute-start.24 = (f32[12,96,384]{2,1,0:T(8,128)S(1)}, f32[12,96,384]{2,1,0:T(8,128)S(1)}, u32[]{:S(2)}, u32[]{:S(2)}) collective-permute-start(f32[12,96,384]{2,1,0:T(8,128)S(1)} %pad_maximum_fusion), channel_id=1, source_target_pairs={{0,16},{16,0},{32,48},{48,32},{64,80},{80,64},{96,112},{112,96},{1... | collective-permute-start | bytes 5308424 | tf_op jit(solution)/shard_map/ppermute | solution.py:258
  138.1 9.8 %collective-permute-start.7 = (f32[2,48,768]{2,1,0:T(8,128)S(1)}, f32[2,48,768]{2,1,0:T(8,128)S(1)}, u32[]{:S(2)}, u32[]{:S(2)}) collective-permute-start(f32[2,48,768]{2,1,0:T(8,128)S(1)} %x_add.6), channel_id=1, source_target_pairs={{0,4},{1,5},{2,6},{3,7},{4,8},{5,9},{6,10},{7,11},{8,12},{9,13},{1... | collective-permute-start | bytes 884744 | tf_op jit(solution)/shard_map/ppermute | solution.py:275
  139.5 8.4 %collective-permute-start.8 = (f32[2,48,768]{2,1,0:T(8,128)S(1)}, f32[2,48,768]{2,1,0:T(8,128)S(1)}, u32[]{:S(2)}, u32[]{:S(2)}) collective-permute-start(f32[2,48,768]{2,1,0:T(8,128)S(1)} %x_add.7), channel_id=1, source_target_pairs={{0,12},{1,13},{2,14},{3,15},{4,0},{5,1},{6,2},{7,3},{8,4},{9,5},{1... | collective-permute-start | bytes 884744 | tf_op jit(solution)/shard_map/ppermute | solution.py:276
  143.5 10.7 %collective-permute-start.25 = (f32[2,48,768]{2,1,0:T(8,128)S(1)}, f32[2,48,768]{2,1,0:T(8,128)S(1)}, u32[]{:S(2)}, u32[]{:S(2)}) collective-permute-start(f32[2,48,768]{2,1,0:T(8,128)S(1)} %y_add.6), channel_id=1, source_target_pairs={{0,1},{1,2},{2,3},{3,0},{4,5},{5,6},{6,7},{7,4},{8,9},{9,10},{10,1... | collective-permute-start | bytes 884744 | tf_op jit(solution)/shard_map/ppermute | solution.py:275
  145.0 9.9 %collective-permute-start.26 = (f32[2,48,768]{2,1,0:T(8,128)S(1)}, f32[2,48,768]{2,1,0:T(8,128)S(1)}, u32[]{:S(2)}, u32[]{:S(2)}) collective-permute-start(f32[2,48,768]{2,1,0:T(8,128)S(1)} %y_add.7), channel_id=1, source_target_pairs={{0,3},{1,0},{2,1},{3,2},{4,7},{5,4},{6,5},{7,6},{8,11},{9,8},{10,9... | collective-permute-start | bytes 884744 | tf_op jit(solution)/shard_map/ppermute | solution.py:276
  169.9 28.7 %collective-permute-start.27 = (f32[8,48,768]{2,1,0:T(8,128)S(1)}, f32[8,48,768]{2,1,0:T(8,128)S(1)}, u32[]{:S(2)}, u32[]{:S(2)}) collective-permute-start(f32[8,48,768]{2,1,0:T(8,128)S(1)} %get-tuple-element.74), channel_id=1, source_target_pairs={{0,4},{1,5},{2,6},{3,7},{4,8},{5,9},{6,10},{7,11},{8,12},{9,13},{1... | collective-permute-start | bytes 3538952 | tf_op jit(solution)/shard_map/ppermute | solution.py:272
  170.0 28.8 %collective-permute-start.28 = (f32[8,48,768]{2,1,0:T(8,128)S(1)}, f32[8,48,768]{2,1,0:T(8,128)S(1)}, u32[]{:S(2)}, u32[]{:S(2)}) collective-permute-start(f32[8,48,768]{2,1,0:T(8,128)S(1)} %get-tuple-element.75), channel_id=1, source_target_pairs={{0,12},{1,13},{2,14},{3,15},{4,0},{5,1},{6,2},{7,3},{8,4},{9,5},{1... | collective-permute-start | bytes 3538952 | tf_op jit(solution)/shard_map/ppermute | solution.py:273
  178.6 26.5 %collective-permute-start.36 = (f32[8,48,768]{2,1,0:T(8,128)S(1)}, f32[8,48,768]{2,1,0:T(8,128)S(1)}, u32[]{:S(2)}, u32[]{:S(2)}) collective-permute-start(f32[8,48,768]{2,1,0:T(8,128)S(1)} %get-tuple-element.87), channel_id=1, source_target_pairs={{0,1},{1,2},{2,3},{3,0},{4,5},{5,6},{6,7},{7,4},{8,9},{9,10},{10,1... | collective-permute-start | bytes 3538952 | tf_op jit(solution)/shard_map/ppermute | solution.py:272
  178.7 28.5 %collective-permute-start.37 = (f32[8,48,768]{2,1,0:T(8,128)S(1)}, f32[8,48,768]{2,1,0:T(8,128)S(1)}, u32[]{:S(2)}, u32[]{:S(2)}) collective-permute-start(f32[8,48,768]{2,1,0:T(8,128)S(1)} %get-tuple-element.88), channel_id=1, source_target_pairs={{0,3},{1,0},{2,1},{3,2},{4,7},{5,4},{6,5},{7,6},{8,11},{9,8},{10,9... | collective-permute-start | bytes 3538952 | tf_op jit(solution)/shard_map/ppermute | solution.py:273
  198.7 21.5 %collective-permute-start.29 = (f32[4,48,768]{2,1,0:T(8,128)S(1)}, f32[4,48,768]{2,1,0:T(8,128)S(1)}, u32[]{:S(2)}, u32[]{:S(2)}) collective-permute-start(f32[4,48,768]{2,1,0:T(8,128)S(1)} %x_add.10), channel_id=1, source_target_pairs={{0,4},{1,5},{2,6},{3,7},{4,8},{5,9},{6,10},{7,11},{8,12},{9,13},{1... | collective-permute-start | bytes 1769480 | tf_op jit(solution)/shard_map/ppermute | solution.py:275
  198.9 21.3 %collective-permute-start.30 = (f32[4,48,768]{2,1,0:T(8,128)S(1)}, f32[4,48,768]{2,1,0:T(8,128)S(1)}, u32[]{:S(2)}, u32[]{:S(2)}) collective-permute-start(f32[4,48,768]{2,1,0:T(8,128)S(1)} %x_add.11), channel_id=1, source_target_pairs={{0,12},{1,13},{2,14},{3,15},{4,0},{5,1},{6,2},{7,3},{8,4},{9,5},{1... | collective-permute-start | bytes 1769480 | tf_op jit(solution)/shard_map/ppermute | solution.py:276
  202.2 18.0 %collective-permute-start.17 = (f32[2,48,768]{2,1,0:T(8,128)S(1)}, f32[2,48,768]{2,1,0:T(8,128)S(1)}, u32[]{:S(2)}, u32[]{:S(2)}) collective-permute-start(f32[2,48,768]{2,1,0:T(8,128)S(1)} %x_add.8), channel_id=1, source_target_pairs={{0,4},{1,5},{2,6},{3,7},{4,8},{5,9},{6,10},{7,11},{8,12},{9,13},{1... | collective-permute-start | bytes 884744 | tf_op jit(solution)/shard_map/ppermute | solution.py:275
  205.1 15.1 %collective-permute-start.18 = (f32[2,48,768]{2,1,0:T(8,128)S(1)}, f32[2,48,768]{2,1,0:T(8,128)S(1)}, u32[]{:S(2)}, u32[]{:S(2)}) collective-permute-start(f32[2,48,768]{2,1,0:T(8,128)S(1)} %x_add.9), channel_id=1, source_target_pairs={{0,12},{1,13},{2,14},{3,15},{4,0},{5,1},{6,2},{7,3},{8,4},{9,5},{1... | collective-permute-start | bytes 884744 | tf_op jit(solution)/shard_map/ppermute | solution.py:276
  207.3 36.5 %collective-permute-start.38 = (f32[4,48,768]{2,1,0:T(8,128)S(1)}, f32[4,48,768]{2,1,0:T(8,128)S(1)}, u32[]{:S(2)}, u32[]{:S(2)}) collective-permute-start(f32[4,48,768]{2,1,0:T(8,128)S(1)} %y_add.10), channel_id=1, source_target_pairs={{0,1},{1,2},{2,3},{3,0},{4,5},{5,6},{6,7},{7,4},{8,9},{9,10},{10,1... | collective-permute-start | bytes 1769480 | tf_op jit(solution)/shard_map/ppermute | solution.py:275
  220.2 23.6 %collective-permute-start.39 = (f32[4,48,768]{2,1,0:T(8,128)S(1)}, f32[4,48,768]{2,1,0:T(8,128)S(1)}, u32[]{:S(2)}, u32[]{:S(2)}) collective-permute-start(f32[4,48,768]{2,1,0:T(8,128)S(1)} %y_add.11), channel_id=1, source_target_pairs={{0,3},{1,0},{2,1},{3,2},{4,7},{5,4},{6,5},{7,6},{8,11},{9,8},{10,9... | collective-permute-start | bytes 1769480 | tf_op jit(solution)/shard_map/ppermute | solution.py:276
  223.0 24.7 %collective-permute-start.31 = (f32[4,48,768]{2,1,0:T(8,128)S(1)}, f32[4,48,768]{2,1,0:T(8,128)S(1)}, u32[]{:S(2)}, u32[]{:S(2)}) collective-permute-start(f32[4,48,768]{2,1,0:T(8,128)S(1)} %get-tuple-element.79), channel_id=1, source_target_pairs={{0,1},{1,2},{2,3},{3,0},{4,5},{5,6},{6,7},{7,4},{8,9},{9,10},{10,1... | collective-permute-start | bytes 1769480 | tf_op jit(solution)/shard_map/ppermute | solution.py:283
  225.0 18.8 %copy-start.33 = (f32[2,48,768]{2,1,0:T(8,128)S(1)}, f32[2,48,768]{2,1,0:T(8,128)}, u32[]{:S(2)}) copy-start(f32[2,48,768]{2,1,0:T(8,128)} %copy-done.32) | copy-start | bytes 884740
  225.0 18.8 %copy-start.35 = (f32[2,48,768]{2,1,0:T(8,128)S(1)}, f32[2,48,768]{2,1,0:T(8,128)}, u32[]{:S(2)}) copy-start(f32[2,48,768]{2,1,0:T(8,128)} %copy-done.34) | copy-start | bytes 884740
  225.0 18.8 %copy-start.41 = (f32[4,48,768]{2,1,0:T(8,128)S(1)}, f32[4,48,768]{2,1,0:T(8,128)}, u32[]{:S(2)}) copy-start(f32[4,48,768]{2,1,0:T(8,128)} %copy-done.40) | copy-start | bytes 1769476
  225.0 18.8 %copy-start.45 = (f32[4,48,768]{2,1,0:T(8,128)S(1)}, f32[4,48,768]{2,1,0:T(8,128)}, u32[]{:S(2)}) copy-start(f32[4,48,768]{2,1,0:T(8,128)} %copy-done.44) | copy-start | bytes 1769476
  225.1 14.1 %collective-permute-start.34 = (f32[2,48,768]{2,1,0:T(8,128)S(1)}, f32[2,48,768]{2,1,0:T(8,128)S(1)}, u32[]{:S(2)}, u32[]{:S(2)}) collective-permute-start(f32[2,48,768]{2,1,0:T(8,128)S(1)} %y_add.8), channel_id=1, source_target_pairs={{0,1},{1,2},{2,3},{3,0},{4,5},{5,6},{6,7},{7,4},{8,9},{9,10},{10,1... | collective-permute-start | bytes 884744 | tf_op jit(solution)/shard_map/ppermute | solution.py:275
  226.3 16.0 %collective-permute-start.35 = (f32[2,48,768]{2,1,0:T(8,128)S(1)}, f32[2,48,768]{2,1,0:T(8,128)S(1)}, u32[]{:S(2)}, u32[]{:S(2)}) collective-permute-start(f32[2,48,768]{2,1,0:T(8,128)S(1)} %y_add.9), channel_id=1, source_target_pairs={{0,3},{1,0},{2,1},{3,2},{4,7},{5,4},{6,5},{7,6},{8,11},{9,8},{10,9... | collective-permute-start | bytes 884744 | tf_op jit(solution)/shard_map/ppermute | solution.py:276
  239.2 16.1 %collective-permute-start.32 = (f32[4,48,768]{2,1,0:T(8,128)}, f32[4,48,768]{2,1,0:T(8,128)S(1)}, u32[]{:S(2)}, u32[]{:S(2)}) collective-permute-start(f32[4,48,768]{2,1,0:T(8,128)} %get-tuple-element.80), channel_id=1, source_target_pairs={{0,2},{1,3},{2,0},{3,1},{4,6},{5,7},{6,4},{7,5},{8,10},{9,11},{10,... | collective-permute-start | bytes 1769480 | tf_op jit(solution)/shard_map/ppermute | solution.py:283
  242.3 19.0 %collective-permute-start.33 = (f32[4,48,768]{2,1,0:T(8,128)}, f32[4,48,768]{2,1,0:T(8,128)S(1)}, u32[]{:S(2)}, u32[]{:S(2)}) collective-permute-start(f32[4,48,768]{2,1,0:T(8,128)} %get-tuple-element.81), channel_id=1, source_target_pairs={{0,3},{1,0},{2,1},{3,2},{4,7},{5,4},{6,5},{7,6},{8,11},{9,8},{10,9... | collective-permute-start | bytes 1769480 | tf_op jit(solution)/shard_map/ppermute | solution.py:283
  243.8 32.7 %copy-start.67 = (s32[8]{0:T(128)S(1)}, s32[8]{0:T(128)}, u32[]{:S(2)}) copy-start(s32[8]{0:T(128)} %sizes.13) | copy-start | bytes 100
  246.8 29.7 %collective-permute-start.40 = (f32[4,48,768]{2,1,0:T(8,128)}, f32[4,48,768]{2,1,0:T(8,128)S(1)}, u32[]{:S(2)}, u32[]{:S(2)}) collective-permute-start(f32[4,48,768]{2,1,0:T(8,128)} %get-tuple-element.92), channel_id=1, source_target_pairs={{0,4},{1,5},{2,6},{3,7},{4,8},{5,9},{6,10},{7,11},{8,12},{9,13},{1... | collective-permute-start | bytes 1769480 | tf_op jit(solution)/shard_map/ppermute | solution.py:283
  246.8 29.7 %collective-permute-start.41 = (f32[4,48,768]{2,1,0:T(8,128)}, f32[4,48,768]{2,1,0:T(8,128)}, u32[]{:S(2)}, u32[]{:S(2)}) collective-permute-start(f32[4,48,768]{2,1,0:T(8,128)} %get-tuple-element.93), channel_id=1, source_target_pairs={{0,8},{1,9},{2,10},{3,11},{4,12},{5,13},{6,14},{7,15},{8,0},{9,1},... | collective-permute-start | bytes 1769480 | tf_op jit(solution)/shard_map/ppermute | solution.py:283
  247.7 28.7 %collective-permute-start.42 = (f32[4,48,768]{2,1,0:T(8,128)}, f32[4,48,768]{2,1,0:T(8,128)}, u32[]{:S(2)}, u32[]{:S(2)}) collective-permute-start(f32[4,48,768]{2,1,0:T(8,128)} %get-tuple-element.94), channel_id=1, source_target_pairs={{0,12},{1,13},{2,14},{3,15},{4,0},{5,1},{6,2},{7,3},{8,4},{9,5},{1... | collective-permute-start | bytes 1769480 | tf_op jit(solution)/shard_map/ppermute | solution.py:283
  (63 other events, 264.3 us)

commit v4 on v3

v4 whole, which is shorter than its diff:
```python
import functools

import jax
import jax.numpy as jnp
import numpy as np
from jax import lax
from jax.experimental import pallas as pl
from jax.experimental.pallas import tpu as pltpu
from jax.sharding import PartitionSpec as P

SIDE = 4
VMEM = 63 * 1024 * 1024
LIGHT = pl.CostEstimate(flops=0, bytes_accessed=0, transcendentals=0)
def hops(count, stride, delta):
    pairs = []
    for i in range(count):
        d = (i // stride) % SIDE
        pairs.append((i, i + ((d + delta) % SIDE - d) * stride))
    return pairs


def apart(count, stride, delta, cores):
    up, down = hops(count, stride, delta), hops(count, stride, -delta)
    return [(down if cores(i) else up)[i] for i in range(count)]


X_HOPS = {d: apart(128, SIDE, d, lambda i: i // 16 % 2) for d in (1, 2, -1)}
Y_HOPS = {d: apart(128, 1, d, lambda i: i // 16 % 2) for d in (1, 2, -1)}
BOTH = ("vb", "ob")


def places(axis):
    table = np.zeros((8, 16, 16), np.int32)
    for vb in range(8):
        for ob in range(16):
            x, y = divmod(ob, SIDE)
            sign = -1 if vb % 2 else 1
            for block in range(16):
                to_x, to_y = divmod(block, SIDE)
                rel_x, rel_y = sign * (to_x - x) % SIDE, sign * (to_y - y) % SIDE
                first, second = (rel_x, rel_y) if axis == "x" else (rel_y, rel_x)
                table[vb, ob, block] = SIDE * first + second
    return table


PLACES = np.concatenate([places("x"), places("y")], axis=2)


def product_kernel(v_first, place_at, place, sizes, origin, *refs):
    pieces, v_ref, (send_p, send_m, up, down, own, a_all, v_all) = refs[:8], refs[8], refs[-7:]
    rows = send_p.shape[1]
    depth = v_ref.shape[1]
    for a, piece in enumerate(pieces):
        for h in range(2):
            block = piece[0, 0, h * rows : (h + 1) * rows]
            hi = block.astype(jnp.bfloat16)
            lo = (block - hi.astype(jnp.float32)).astype(jnp.bfloat16)
            at = pl.ds(pl.multiple_of(place[place_at + 2 * a + h] * rows, rows), rows)
            a_all[at, 0:depth] = hi
            a_all[at, depth : 2 * depth] = lo
            a_all[at, 2 * depth : 3 * depth] = hi
    size = sizes[v_first + pl.program_id(0)]
    shape = v_ref.shape[1:]
    p = origin[0] + lax.broadcasted_iota(jnp.int32, shape, 0)
    q = origin[1] + lax.broadcasted_iota(jnp.int32, shape, 1)
    v = jnp.where((p < size) & (q < size), v_ref[0], 0.0)
    hi = v.astype(jnp.bfloat16)
    v_all[0:depth] = hi
    v_all[depth : 2 * depth] = hi
    v_all[2 * depth : 3 * depth] = (v - hi.astype(jnp.float32)).astype(jnp.bfloat16)

    def chunk(k):
        acc = jnp.dot(
            a_all[SIDE * rows * k : SIDE * rows * (k + 1)], v_all[...], preferred_element_type=jnp.float32
        )
        return [acc[rows * s : rows * (s + 1)] for s in range(SIDE)]

    far = chunk(2)
    send_p[0], send_p[1], send_m[0], send_m[1] = far
    up[0], up[1], send_p[2], send_p[3] = chunk(1)
    send_m[2], send_m[3], down[0], down[1] = chunk(3)
    own[0], own[1], own[2], own[3] = chunk(0)


def product(amp, skip, ovov, v_first, count, place, place_at, sizes, origin, after, name):
    sources, _, rows2, depth = amp.shape
    rows = rows2 // 2
    cols = ovov.shape[2]
    leads = (4, 4, 2, 2, 4)
    total = 16 * rows
    return pl.pallas_call(
        functools.partial(product_kernel, v_first, place_at),
        grid_spec=pltpu.PrefetchScalarGridSpec(
            num_scalar_prefetch=3,
            grid=(count,),
            in_specs=[
                pl.BlockSpec((1, 1, rows2, depth), lambda g, *_, s=s: (s, skip + g, 0, 0)) for s in range(sources)
            ]
            + [pl.BlockSpec((1, depth, cols), lambda g, *_: (v_first + g, 0, 0))]
            + [pl.BlockSpec(memory_space=pl.ANY)] * len(after),
            out_specs=[pl.BlockSpec((n, rows, cols), lambda g, *_: (g, 0, 0)) for n in leads],
            scratch_shapes=[
                pltpu.VMEM((total, 3 * depth), jnp.bfloat16),
                pltpu.VMEM((3 * depth, cols), jnp.bfloat16),
            ],
        ),
        out_shape=[
            jax.ShapeDtypeStruct((n * count, rows, cols), jnp.float32) for n in leads
        ],
        compiler_params=pltpu.CompilerParams(vmem_limit_bytes=VMEM),
        cost_estimate=LIGHT,
        name=name,
    )(place, sizes, origin, *[amp] * sources, ovov, *after)


def add_kernel(mid, recv, out):
    out[...] = mid[...] + recv[...]


def add_far(mid, recv, name):
    lead, rows, cols = mid.shape
    spec = pl.BlockSpec((2, rows, cols), lambda g: (g, 0, 0))
    return pl.pallas_call(
        add_kernel,
        grid=(lead // 2,),
        in_specs=[spec, pl.BlockSpec((2, rows, cols), lambda g: (2 * g, 0, 0))],
        out_specs=spec,
        out_shape=jax.ShapeDtypeStruct(mid.shape, jnp.float32),
        compiler_params=pltpu.CompilerParams(vmem_limit_bytes=VMEM),
        cost_estimate=LIGHT,
        name=name,
    )(mid, recv)


def own_kernel(own, p1, m1, p2, m2, *refs):
    outs = refs[-4:]
    outs[0][0] = own[0] + (p2[0] + m1[0])
    outs[1][0] = own[1] + (p2[1] + m1[1])
    outs[2][0] = own[2] + (m2[0] + p1[0])
    outs[3][0] = own[3] + (m2[1] + p1[1])


def add_own(own, p1, m1, p2, m2, at, total, into, name):
    rows, cols = own.shape[1:]
    half = pl.BlockSpec((2, rows, cols), lambda g: (2 * g + 1, 0, 0))
    last = pl.BlockSpec((2, rows, cols), lambda g: (g, 0, 0))
    return pl.pallas_call(
        own_kernel,
        grid=(own.shape[0] // 4,),
        in_specs=[pl.BlockSpec((4, rows, cols), lambda g: (g, 0, 0)), half, half, last, last]
        + [pl.BlockSpec(memory_space=pl.ANY)] * len(into),
        out_specs=[pl.BlockSpec((1, rows, cols), lambda g: (at + g, 0, 0))] * 4,
        out_shape=[jax.ShapeDtypeStruct((total, rows, cols), jnp.float32)] * 4,
        input_output_aliases={5 + i: i for i in range(len(into))},
        compiler_params=pltpu.CompilerParams(vmem_limit_bytes=VMEM),
        cost_estimate=LIGHT,
        name=name,
    )(own, p1, m1, p2, m2, *into)


def finish_kernel(order, sizes, origin, *refs):
    out = refs[-1]
    rows, _, cols = out.shape
    row = origin[0] + lax.broadcasted_iota(jnp.int32, (rows, cols), 0)
    for i, irreps in enumerate(order):
        parts = refs[4 * i : 4 * i + 4]
        for at, g in enumerate(irreps):
            total = (parts[0][at] + parts[1][at]) + (parts[2][at] + parts[3][at])
            out[:, g, :] = jnp.where(row < sizes[g], total, 0.0)


def finish(order, parts, row_sizes, origin, shape):
    rows, irreps, cols = shape
    width = 256
    flat = [p for four in parts for p in four]
    return pl.pallas_call(
        functools.partial(finish_kernel, order),
        grid_spec=pltpu.PrefetchScalarGridSpec(
            num_scalar_prefetch=2,
            grid=(cols // width,),
            in_specs=[pl.BlockSpec((p.shape[0], rows, width), lambda c, *_: (0, 0, c)) for p in flat],
            out_specs=pl.BlockSpec((rows, irreps, width), lambda c, *_: (0, 0, c)),
        ),
        out_shape=jax.ShapeDtypeStruct(shape, jnp.float32),
        compiler_params=pltpu.CompilerParams(vmem_limit_bytes=VMEM),
        cost_estimate=LIGHT,
        name="finish",
    )(row_sizes, origin, *flat)


GROUPS = ((0, 2, 2), (4, 2, 2))


def local(amplitudes, ovov, row_sizes, pair_sizes):
    ob = lax.axis_index("ob")
    vb = lax.axis_index("vb")
    local_rows, irreps, pairs = amplitudes.shape
    obs = lax.axis_size("ob")
    depth, cols = ovov.shape[1:]
    out_rows = local_rows * lax.axis_size("vb")
    place = lax.dynamic_slice(jnp.asarray(PLACES), (vb, ob, 0), (1, 1, 32)).reshape(32)

    origin = jnp.stack([ob * depth, vb * cols]).astype(jnp.int32)

    axes = (("x", X_HOPS, Y_HOPS, 0), ("y", Y_HOPS, X_HOPS, 16))
    order = {axis: [] for axis, *_ in axes}
    sums = {axis: [] for axis, *_ in axes}
    got = {}

    gathered = []
    for first, nx, ny in GROUPS:
        count = nx + ny
        mine = amplitudes[:, first : first + count].reshape(local_rows, count, obs, depth)
        mine = jnp.transpose(mine, (2, 0, 1, 3)).reshape(obs, local_rows * count, depth)
        mine = lax.all_to_all(mine, "ob", split_axis=0, concat_axis=0, tiled=True)
        mine = jnp.transpose(mine.reshape(obs * local_rows, count, depth), (1, 0, 2))
        gathered.append(lax.all_gather(mine, "vb", axis=0))

    for (first, nx, ny), amp in zip(GROUPS, gathered):
        for axis, here, there, place_at in axes:
            skip, count = (0, nx) if axis == "x" else (nx, ny)
            order[axis] += range(first + skip, first + skip + count)
            send_p, send_m, up, down, mid = product(
                amp, skip, ovov, first + skip, count, place, place_at, pair_sizes, origin, got.get(axis, []), f"{axis}_product"
            )
            p1 = lax.ppermute(send_p, BOTH, here[1])
            m1 = lax.ppermute(send_m, BOTH, here[-1])
            got[axis] = [p1, m1]
            p2 = lax.ppermute(add_far(up, p1, f"{axis}_add"), BOTH, here[1])
            m2 = lax.ppermute(add_far(down, m1, f"{axis}_add"), BOTH, here[-1])
            sums[axis].append((mid, p1, m1, p2, m2))

    parts = []
    for axis, here, there, _ in axes:
        four, at = [], 0
        for group in sums[axis]:
            four = add_own(*group, at, len(order[axis]), four, f"{axis}_own")
            at += group[0].shape[0] // 4
        parts.append([four[0]] + [lax.ppermute(four[k], BOTH, there[d]) for k, d in ((1, 1), (2, 2), (3, -1))])
    origin = jnp.stack([ob * out_rows, vb * cols]).astype(jnp.int32)
    return finish([order[axis] for axis, *_ in axes], parts, row_sizes, origin, (out_rows, irreps, cols))


def solution(mesh):
    placed = (P(("vb", "ob"), None, None), P(None, "ob", "vb"), P(), P())
    return jax.shard_map(
        local, mesh=mesh, in_specs=placed, out_specs=P("ob", None, "vb"), check_vma=False
    )
```

time: 282 us -> 234 us (0.83)
  local copies, waits for them, and re-layouts: 40.9 us -> 6.07 us
  waiting for transfers between devices: 108 us -> 79 us
  starting transfers between devices: 60.3 us -> 35.5 us
  Pallas kernels: 38.8 us -> 63.4 us
  between operations: 0.63 us -> 13.5 us
  blocking collectives: 25.4 us -> 33.4 us
  other arithmetic: 4.89 us -> 1.25 us
    ppermute x6 -> x4, waiting for transfers between devices: 39.6 us -> 0.97 us  [local(): p1 = lax.ppermute(send_p, BOTH, here[1])]
    unnamed x137 -> x4, local copies, waits for them, and re-layouts: 38 us -> 0.01 us
    all_gather x0 -> x2, waiting for transfers between devices: none -> 29.7 us  [local(): gathered.append(lax.all_gather(mine, 'vb', axis=0))]
    ppermute x6 -> x4, waiting for transfers between devices: 28.4 us -> 6.57 us  [local(): p2 = lax.ppermute(add_far(up, p1, f'{axis}_add'), BOTH, here[1])]
    ppermute x13 -> x0, starting transfers between devices: 16.6 us -> none  [the longest x9 16.5 us: gather(): return [lax.ppermute(held, 'vb', pairs) for pairs in (*Z_APART, Z_HOPS[2])]]
    ppermute x13 -> x0, waiting for transfers between devices: 12.4 us -> none  [the longest x9 12.4 us: gather(): return [lax.ppermute(held, 'vb', pairs) for pairs in (*Z_APART, Z_HOPS[2])]]
    ppermute x6 -> x4, waiting for transfers between devices: 0.02 us -> 12.1 us  [local(): m1 = lax.ppermute(send_m, BOTH, here[-1])]
    pallas_call x12 -> x8, Pallas kernels: 5.67 us -> 16.1 us  [add_far(): pl.pallas_call(add_kernel, grid=(lead // 2,), in_specs=[spec, pl.BlockSpe...]
  transfers between devices with their start and end apart: 43 -> 24, of which waited for: 14 -> 14; matrix products, arithmetic and copies ran while one was open for 2% -> 2% of each run, Pallas kernels for 11% -> 25%
where the time goes in v4:
time: 234 us; the launch traced here: 232 us
  waiting for transfers between devices  79 us (34%)
  Pallas kernels  63.4 us (27%)
  starting transfers between devices  35.5 us (15%)
  blocking collectives  33.4 us (14%)
  between operations  13.5 us (6%)
  local copies, waits for them, and re-layouts  6.07 us (3%)
    all_to_all x2, blocking collectives, local(): mine = lax.all_to_all(mine, 'ob', split_axis=0, concat_axis=0, tiled=True)  33.4 us
    pallas_call x4, Pallas kernels, product(): pl.pallas_call(functools.partial(product_kernel, v_first, place_at), grid...  30.8 us
    all_gather x2, waiting for transfers between devices, local(): gathered.append(lax.all_gather(mine, 'vb', axis=0))  29.7 us
    ppermute x6, waiting for transfers between devices, local(): lax.ppermute(four[k], BOTH, there[d])  23.1 us
    pallas_call x8, Pallas kernels, add_far(): pl.pallas_call(add_kernel, grid=(lead // 2,), in_specs=[spec, pl.BlockSpe...  16.1 us
    ppermute x6, starting transfers between devices, local(): lax.ppermute(four[k], BOTH, there[d])  13.1 us
    ppermute x4, waiting for transfers between devices, local(): m1 = lax.ppermute(send_m, BOTH, here[-1])  12.1 us
    pallas_call x4, Pallas kernels, add_own(): pl.pallas_call(own_kernel, grid=(own.shape[0] // 4,), in_specs=[pl.BlockS...  11.5 us
  transfers between devices with their start and end apart: 24, of which 14 were waited for; matrix products, arithmetic and copies ran while one was open for 2% of the time, Pallas kernels for 25%

profile of v4, /device:TPU:0, one launch (start us, length us, event | category | flops | bytes accessed | tf_op | source)
XLA Modules:
  0.0 232.1 jit_solution(14307402073474405755)
XLA Ops:
  6.5 1.8 fusion
  8.9 19.1 %all_to_all.10 = f32[16,24,384]{2,1,0:T(8,128)S(1)} all-to-all(f32[16,24,384]{2,1,0:T(8,128)S(1)} %copy.20), channel_id=1, replica_groups=mesh['vb'=8,'ob'=16] {'ob'}, dimensions={0} | all-to-all | bytes 1179648 | tf_op jit(solution)/shard_map/all_to_all | solution.py:215
  28.2 0.9 copy.21
  29.6 14.3 %all_to_all.11 = f32[16,24,384]{2,1,0:T(8,128)S(1)} all-to-all(f32[16,24,384]{2,1,0:T(8,128)S(1)} %copy.18), channel_id=1, replica_groups=mesh['vb'=8,'ob'=16] {'ob'}, dimensions={0} | all-to-all | bytes 1179648 | tf_op jit(solution)/shard_map/all_to_all | solution.py:215
  44.1 0.9 copy.19
  45.6 1.2 dynamic-slice_bitcast_fusion.place
  46.8 15.8 %all-gather.7.cloned.1.call-done = f32[32,96,384]{2,1,0:T(8,128)} async-done(((f32[4,96,384]{2,1,0:T(8,128)}), f32[32,96,384]{2,1,0:T(8,128)}) %all-gather.7.cloned.1.call-update) | async-done | bytes 4718608 | tf_op jit(solution)/shard_map/all_gather | solution.py:217
  62.6 7.6 %y_product.2 = (f32[8,48,768]{2,1,0:T(8,128)}, f32[8,48,768]{2,1,0:T(8,128)}, f32[4,48,768]{2,1,0:T(8,128)}, f32[4,48,768]{2,1,0:T(8,128)}, f32[8,48,768]{2,1,0:T(8,128)}) custom-call(s32[32]{0:T(128)} %dynamic-slice_bitcast_fusion.place, s32[8]{0:T(128)} %sizes.8, s32[2]{0:T(128)} %pad_add_fusion.1.origin, f32[8,4,96,384]{3,2,1,0:T(8,128)} %bitcast.31, ...), custom_call_target="tpu_custom_call" | custom-call | tf_op jit(solution)/shard_map/y_product/pallas_call | solution.py:91
  70.2 1.6 collective-permute-start.11
  71.7 1.8 collective-permute-start.12
  73.5 7.9 %x_product.2 = (f32[8,48,768]{2,1,0:T(8,128)}, f32[8,48,768]{2,1,0:T(8,128)}, f32[4,48,768]{2,1,0:T(8,128)}, f32[4,48,768]{2,1,0:T(8,128)}, f32[8,48,768]{2,1,0:T(8,128)}) custom-call(s32[32]{0:T(128)} %dynamic-slice_bitcast_fusion.place, s32[8]{0:T(128)} %sizes.8, s32[2]{0:T(128)} %pad_add_fusion.1.origin, f32[8,4,96,384]{3,2,1,0:T(8,128)} %bitcast.39, ...), custom_call_target="tpu_custom_call" | custom-call | tf_op jit(solution)/shard_map/x_product/pallas_call | solution.py:91
  81.4 1.5 collective-permute-start
  83.0 1.8 collective-permute-start.1
  84.7 13.9 %all-gather.5.cloned.1.call-done = f32[32,96,384]{2,1,0:T(8,128)} async-done(((f32[4,96,384]{2,1,0:T(8,128)}), f32[32,96,384]{2,1,0:T(8,128)}) %all-gather.5.cloned.1.call-update) | async-done | bytes 4718608 | tf_op jit(solution)/shard_map/all_gather | solution.py:217
  99.0 7.6 %y_product.3 = (f32[8,48,768]{2,1,0:T(8,128)}, f32[8,48,768]{2,1,0:T(8,128)}, f32[4,48,768]{2,1,0:T(8,128)}, f32[4,48,768]{2,1,0:T(8,128)}, f32[8,48,768]{2,1,0:T(8,128)}) custom-call(s32[32]{0:T(128)} %dynamic-slice_bitcast_fusion.place, s32[8]{0:T(128)} %sizes.8, s32[2]{0:T(128)} %pad_add_fusion.1.origin, f32[8,4,96,384]{3,2,1,0:T(8,128)} %bitcast.15, ...), custom_call_target="tpu_custom_call" | custom-call | tf_op jit(solution)/shard_map/y_product/pallas_call | solution.py:91
  106.6 3.8 %collective-permute-start.14 = (f32[8,48,768]{2,1,0:T(8,128)}, f32[8,48,768]{2,1,0:T(8,128)}, u32[]{:S(2)}, u32[]{:S(2)}) collective-permute-start(f32[8,48,768]{2,1,0:T(8,128)} %get-tuple-element.63), channel_id=1, source_target_pairs={{0,3},{1,0},{2,1},{3,2},{4,7},{5,4},{6,5},{7,6},{8,11},{9,8},{10,9... | collective-permute-start | bytes 3538952 | tf_op jit(solution)/shard_map/ppermute | solution.py:227
  110.4 0.8 collective-permute-done.refs_9_.recv.p1
  111.2 7.6 %x_product.3 = (f32[8,48,768]{2,1,0:T(8,128)}, f32[8,48,768]{2,1,0:T(8,128)}, f32[4,48,768]{2,1,0:T(8,128)}, f32[4,48,768]{2,1,0:T(8,128)}, f32[8,48,768]{2,1,0:T(8,128)}) custom-call(s32[32]{0:T(128)} %dynamic-slice_bitcast_fusion.place, s32[8]{0:T(128)} %sizes.8, s32[2]{0:T(128)} %pad_add_fusion.1.origin, f32[8,4,96,384]{3,2,1,0:T(8,128)} %bitcast.23, ...), custom_call_target="tpu_custom_call" | custom-call | tf_op jit(solution)/shard_map/x_product/pallas_call | solution.py:91
  118.8 2.0 collective-permute-start.3
  120.9 2.0 y_add.6
  123.0 2.0 y_add.7
  125.0 11.9 %collective-permute-done.14.recv.m1 = f32[8,48,768]{2,1,0:T(8,128)} collective-permute-done((f32[8,48,768]{2,1,0:T(8,128)}, f32[8,48,768]{2,1,0:T(8,128)}, u32[]{:S(2)}, u32[]{:S(2)}) %collective-permute-start.14) | collective-permute-done | bytes 1179680 | tf_op jit(solution)/shard_map/ppermute | solution.py:227
  137.0 3.7 %collective-permute-start.18 = (f32[4,48,768]{2,1,0:T(8,128)}, f32[4,48,768]{2,1,0:T(8,128)}, u32[]{:S(2)}, u32[]{:S(2)}) collective-permute-start(f32[4,48,768]{2,1,0:T(8,128)} %y_add.7), channel_id=1, source_target_pairs={{0,3},{1,0},{2,1},{3,2},{4,7},{5,4},{6,5},{7,6},{8,11},{9,8},{10,9... | collective-permute-start | bytes 1769480 | tf_op jit(solution)/shard_map/ppermute | solution.py:230
  140.7 2.0 y_add.5
  142.6 2.0 y_add.4
  144.6 4.4 %collective-permute-done.17.p2 = f32[4,48,768]{2,1,0:T(8,128)S(1)} collective-permute-done((f32[4,48,768]{2,1,0:T(8,128)}, f32[4,48,768]{2,1,0:T(8,128)S(1)}, u32[]{:S(2)}, u32[]{:S(2)}) %collective-permute-start.17) | collective-permute-done | bytes 589856 | tf_op jit(solution)/shard_map/ppermute | solution.py:229
  149.0 2.2 x_add.6
  151.2 2.0 x_add.7
  153.2 1.5 collective-permute-start.6
  154.7 1.8 collective-permute-start.7
  156.5 2.0 x_add.5
  158.5 2.0 x_add.4
  160.4 1.5 collective-permute-start.5
  162.3 1.3 collective-permute-start.4
  163.6 2.9 %y_own.2 = (f32[4,48,768]{2,1,0:T(8,128)}, f32[4,48,768]{2,1,0:T(8,128)}, f32[4,48,768]{2,1,0:T(8,128)}, f32[4,48,768]{2,1,0:T(8,128)}) custom-call(f32[8,48,768]{2,1,0:T(8,128)} %get-tuple-element.66.own, f32[8,48,768]{2,1,0:T(8,128)} %collective-permute-done.11.refs_9_.recv.p1, f32[8,48,768]{2,1,0:T(8,128)} %collective-permute-done.12.refs_10_.recv.m1, ...), custom_call_target="tpu_custom_call" | custom-call | tf_op jit(solution)/shard_map/y_own/pallas_call | solution.py:147
  166.5 2.9 %y_own.3 = (f32[4,48,768]{2,1,0:T(8,128)}, f32[4,48,768]{2,1,0:T(8,128)}, f32[4,48,768]{2,1,0:T(8,128)}, f32[4,48,768]{2,1,0:T(8,128)}) custom-call(f32[8,48,768]{2,1,0:T(8,128)} %get-tuple-element.61.own, f32[8,48,768]{2,1,0:T(8,128)} %collective-permute-done.13.recv.p1, ...), custom_call_target="tpu_custom_call", output_to_operand_aliasing={{0}: (5, {}), {1}: (6, {}), {2}: (7, {}), {3}: (8, {})} | custom-call | tf_op jit(solution)/shard_map/y_own/pallas_call | solution.py:147
  169.4 1.5 collective-permute-start.19
  171.3 2.9 %x_own.2 = (f32[4,48,768]{2,1,0:T(8,128)}, f32[4,48,768]{2,1,0:T(8,128)}, f32[4,48,768]{2,1,0:T(8,128)}, f32[4,48,768]{2,1,0:T(8,128)}) custom-call(f32[8,48,768]{2,1,0:T(8,128)} %get-tuple-element.48.own, f32[8,48,768]{2,1,0:T(8,128)} %collective-permute-done.refs_9_.recv.p1, f32[8,48,768]{2,1,0:T(8,128)} %collective-permute-done.1.refs_10_.recv.m1, ...), custom_call_target="tpu_custom_call" | custom-call | tf_op jit(solution)/shard_map/x_own/pallas_call | solution.py:147
  174.2 2.7 %collective-permute-start.20 = (f32[4,48,768]{2,1,0:T(8,128)}, f32[4,48,768]{2,1,0:T(8,128)}, u32[]{:S(2)}, u32[]{:S(2)}) collective-permute-start(f32[4,48,768]{2,1,0:T(8,128)} %get-tuple-element.75), channel_id=1, source_target_pairs={{0,8},{1,9},{2,10},{3,11},{4,12},{5,13},{6,14},{7,15},{8,0},{9,1},... | collective-permute-start | bytes 1769480 | tf_op jit(solution)/shard_map/ppermute | solution.py:239
  176.9 1.5 collective-permute-start.21
  178.3 5.6 %collective-permute-done.5.m2 = f32[4,48,768]{2,1,0:T(8,128)} collective-permute-done((f32[4,48,768]{2,1,0:T(8,128)}, f32[4,48,768]{2,1,0:T(8,128)}, u32[]{:S(2)}, u32[]{:S(2)}) %collective-permute-start.5) | collective-permute-done | bytes 589856 | tf_op jit(solution)/shard_map/ppermute | solution.py:230
  183.9 2.2 collective-permute-done.4.p2
  186.1 2.8 %x_own.3 = (f32[4,48,768]{2,1,0:T(8,128)}, f32[4,48,768]{2,1,0:T(8,128)}, f32[4,48,768]{2,1,0:T(8,128)}, f32[4,48,768]{2,1,0:T(8,128)}) custom-call(f32[8,48,768]{2,1,0:T(8,128)} %get-tuple-element.43.own, f32[8,48,768]{2,1,0:T(8,128)} %collective-permute-done.2.recv.p1, ...), custom_call_target="tpu_custom_call", output_to_operand_aliasing={{0}: (5, {}), {1}: (6, {}), {2}: (7, {}), {3}: (8, {})} | custom-call | tf_op jit(solution)/shard_map/x_own/pallas_call | solution.py:147
  189.0 6.9 %collective-permute-start.10 = (f32[4,48,768]{2,1,0:T(8,128)}, f32[4,48,768]{2,1,0:T(8,128)}, u32[]{:S(2)}, u32[]{:S(2)}) collective-permute-start(f32[4,48,768]{2,1,0:T(8,128)} %get-tuple-element.58), channel_id=1, source_target_pairs={{0,3},{1,0},{2,1},{3,2},{4,7},{5,4},{6,5},{7,6},{8,11},{9,8},{10,9... | collective-permute-start | bytes 1769480 | tf_op jit(solution)/shard_map/ppermute | solution.py:239
  195.9 12.6 %collective-permute-done.19.refs_5_ = f32[4,48,768]{2,1,0:T(8,128)S(1)} collective-permute-done((f32[4,48,768]{2,1,0:T(8,128)}, f32[4,48,768]{2,1,0:T(8,128)S(1)}, u32[]{:S(2)}, u32[]{:S(2)}) %collective-permute-start.19) | collective-permute-done | bytes 589856 | tf_op jit(solution)/shard_map/ppermute | solution.py:239
  209.7 9.2 %collective-permute-done.10.refs_3_ = f32[4,48,768]{2,1,0:T(8,128)} collective-permute-done((f32[4,48,768]{2,1,0:T(8,128)}, f32[4,48,768]{2,1,0:T(8,128)}, u32[]{:S(2)}, u32[]{:S(2)}) %collective-permute-start.10) | collective-permute-done | bytes 589856 | tf_op jit(solution)/shard_map/ppermute | solution.py:239
  219.0 1.3 collective-permute-done.9.refs_2_
  220.3 5.0 %finish.1 = f32[48,8,768]{2,1,0:T(8,128)} custom-call(s32[8]{0:T(128)} %sizes.9, s32[2]{0:T(128)} %pad_add_fusion.origin, f32[4,48,768]{2,1,0:T(8,128)} %get-tuple-element.55.refs_0_, f32[4,48,768]{2,1,0:T(8,128)} %collective-permute-done.8.refs_1_, f32[4,48,768]{2,1,0:T(8,128)} %collective-permute-done.9.refs_2_, ...), custom_call_target="tpu_custom_call" | custom-call | tf_op jit(solution)/shard_map/finish/pallas_call | solution.py:176
  (37 shorter events, 4.8 us)
Async XLA Ops:
  6.5 56.0 %all-gather.7.cloned.1.call-start = ((), (), s32[]{:S(2)}) async-start(), calls=%async_computation.3 | async-start | bytes 5308416 | tf_op jit(solution)/shard_map/all_gather | solution.py:217
  29.1 69.6 %all-gather.5.cloned.1.call-start = ((), (), s32[]{:S(2)}) async-start(), calls=%async_computation.2 | async-start | bytes 5308416 | tf_op jit(solution)/shard_map/all_gather | solution.py:217
  70.2 28.6 %collective-permute-start.11 = (f32[8,48,768]{2,1,0:T(8,128)}, f32[8,48,768]{2,1,0:T(8,128)}, u32[]{:S(2)}, u32[]{:S(2)}) collective-permute-start(f32[8,48,768]{2,1,0:T(8,128)} %get-tuple-element.59), channel_id=1, source_target_pairs={{0,1},{1,2},{2,3},{3,0},{4,5},{5,6},{6,7},{7,4},{8,9},{9,10},{10,1... | collective-permute-start | bytes 3538952 | tf_op jit(solution)/shard_map/ppermute | solution.py:226
  71.7 27.2 %collective-permute-start.12 = (f32[8,48,768]{2,1,0:T(8,128)}, f32[8,48,768]{2,1,0:T(8,128)}, u32[]{:S(2)}, u32[]{:S(2)}) collective-permute-start(f32[8,48,768]{2,1,0:T(8,128)} %get-tuple-element.60), channel_id=1, source_target_pairs={{0,3},{1,0},{2,1},{3,2},{4,7},{5,4},{6,5},{7,6},{8,11},{9,8},{10,9... | collective-permute-start | bytes 3538952 | tf_op jit(solution)/shard_map/ppermute | solution.py:227
  81.4 29.7 %collective-permute-start = (f32[8,48,768]{2,1,0:T(8,128)}, f32[8,48,768]{2,1,0:T(8,128)}, u32[]{:S(2)}, u32[]{:S(2)}) collective-permute-start(f32[8,48,768]{2,1,0:T(8,128)} %get-tuple-element.41), channel_id=1, source_target_pairs={{0,4},{1,5},{2,6},{3,7},{4,8},{5,9},{6,10},{7,11},{8,12},{9,13},{1... | collective-permute-start | bytes 3538952 | tf_op jit(solution)/shard_map/ppermute | solution.py:226
  83.0 28.2 %collective-permute-start.1 = (f32[8,48,768]{2,1,0:T(8,128)}, f32[8,48,768]{2,1,0:T(8,128)}, u32[]{:S(2)}, u32[]{:S(2)}) collective-permute-start(f32[8,48,768]{2,1,0:T(8,128)} %get-tuple-element.42), channel_id=1, source_target_pairs={{0,12},{1,13},{2,14},{3,15},{4,0},{5,1},{6,2},{7,3},{8,4},{9,5},{1... | collective-permute-start | bytes 3538952 | tf_op jit(solution)/shard_map/ppermute | solution.py:227
  106.6 30.4 %collective-permute-start.14 = (f32[8,48,768]{2,1,0:T(8,128)}, f32[8,48,768]{2,1,0:T(8,128)}, u32[]{:S(2)}, u32[]{:S(2)}) collective-permute-start(f32[8,48,768]{2,1,0:T(8,128)} %get-tuple-element.63), channel_id=1, source_target_pairs={{0,3},{1,0},{2,1},{3,2},{4,7},{5,4},{6,5},{7,6},{8,11},{9,8},{10,9... | collective-permute-start | bytes 3538952 | tf_op jit(solution)/shard_map/ppermute | solution.py:227
  110.4 32.3 %collective-permute-start.13 = (f32[8,48,768]{2,1,0:T(8,128)}, f32[8,48,768]{2,1,0:T(8,128)}, u32[]{:S(2)}, u32[]{:S(2)}) collective-permute-start(f32[8,48,768]{2,1,0:T(8,128)} %get-tuple-element.62), channel_id=1, source_target_pairs={{0,1},{1,2},{2,3},{3,0},{4,5},{5,6},{6,7},{7,4},{8,9},{9,10},{10,1... | collective-permute-start | bytes 3538952 | tf_op jit(solution)/shard_map/ppermute | solution.py:226
  118.8 34.4 %collective-permute-start.3 = (f32[8,48,768]{2,1,0:T(8,128)}, f32[8,48,768]{2,1,0:T(8,128)}, u32[]{:S(2)}, u32[]{:S(2)}) collective-permute-start(f32[8,48,768]{2,1,0:T(8,128)} %get-tuple-element.45), channel_id=1, source_target_pairs={{0,12},{1,13},{2,14},{3,15},{4,0},{5,1},{6,2},{7,3},{8,4},{9,5},{1... | collective-permute-start | bytes 3538952 | tf_op jit(solution)/shard_map/ppermute | solution.py:227
  120.8 33.9 %collective-permute-start.2 = (f32[8,48,768]{2,1,0:T(8,128)}, f32[8,48,768]{2,1,0:T(8,128)}, u32[]{:S(2)}, u32[]{:S(2)}) collective-permute-start(f32[8,48,768]{2,1,0:T(8,128)} %get-tuple-element.44), channel_id=1, source_target_pairs={{0,4},{1,5},{2,6},{3,7},{4,8},{5,9},{6,10},{7,11},{8,12},{9,13},{1... | collective-permute-start | bytes 3538952 | tf_op jit(solution)/shard_map/ppermute | solution.py:226
  122.9 26.2 %collective-permute-start.17 = (f32[4,48,768]{2,1,0:T(8,128)}, f32[4,48,768]{2,1,0:T(8,128)S(1)}, u32[]{:S(2)}, u32[]{:S(2)}) collective-permute-start(f32[4,48,768]{2,1,0:T(8,128)} %y_add.6), channel_id=1, source_target_pairs={{0,1},{1,2},{2,3},{3,0},{4,5},{5,6},{6,7},{7,4},{8,9},{9,10},{10,1... | collective-permute-start | bytes 1769480 | tf_op jit(solution)/shard_map/ppermute | solution.py:229
  137.0 23.5 %collective-permute-start.18 = (f32[4,48,768]{2,1,0:T(8,128)}, f32[4,48,768]{2,1,0:T(8,128)}, u32[]{:S(2)}, u32[]{:S(2)}) collective-permute-start(f32[4,48,768]{2,1,0:T(8,128)} %y_add.7), channel_id=1, source_target_pairs={{0,3},{1,0},{2,1},{3,2},{4,7},{5,4},{6,5},{7,6},{8,11},{9,8},{10,9... | collective-permute-start | bytes 1769480 | tf_op jit(solution)/shard_map/ppermute | solution.py:230
  142.6 19.7 %collective-permute-start.16 = (f32[4,48,768]{2,1,0:T(8,128)}, f32[4,48,768]{2,1,0:T(8,128)}, u32[]{:S(2)}, u32[]{:S(2)}) collective-permute-start(f32[4,48,768]{2,1,0:T(8,128)} %y_add.5), channel_id=1, source_target_pairs={{0,3},{1,0},{2,1},{3,2},{4,7},{5,4},{6,5},{7,6},{8,11},{9,8},{10,9... | collective-permute-start | bytes 1769480 | tf_op jit(solution)/shard_map/ppermute | solution.py:230
  149.0 2.2 copy-start.1
  149.0 17.4 %collective-permute-start.15 = (f32[4,48,768]{2,1,0:T(8,128)}, f32[4,48,768]{2,1,0:T(8,128)}, u32[]{:S(2)}, u32[]{:S(2)}) collective-permute-start(f32[4,48,768]{2,1,0:T(8,128)} %y_add.4), channel_id=1, source_target_pairs={{0,1},{1,2},{2,3},{3,0},{4,5},{5,6},{6,7},{7,4},{8,9},{9,10},{10,1... | collective-permute-start | bytes 1769480 | tf_op jit(solution)/shard_map/ppermute | solution.py:229
  153.2 17.6 %collective-permute-start.6 = (f32[4,48,768]{2,1,0:T(8,128)}, f32[4,48,768]{2,1,0:T(8,128)}, u32[]{:S(2)}, u32[]{:S(2)}) collective-permute-start(f32[4,48,768]{2,1,0:T(8,128)} %x_add.6), channel_id=1, source_target_pairs={{0,4},{1,5},{2,6},{3,7},{4,8},{5,9},{6,10},{7,11},{8,12},{9,13},{1... | collective-permute-start | bytes 1769480 | tf_op jit(solution)/shard_map/ppermute | solution.py:229
  154.7 16.6 %collective-permute-start.7 = (f32[4,48,768]{2,1,0:T(8,128)}, f32[4,48,768]{2,1,0:T(8,128)}, u32[]{:S(2)}, u32[]{:S(2)}) collective-permute-start(f32[4,48,768]{2,1,0:T(8,128)} %x_add.7), channel_id=1, source_target_pairs={{0,12},{1,13},{2,14},{3,15},{4,0},{5,1},{6,2},{7,3},{8,4},{9,5},{1... | collective-permute-start | bytes 1769480 | tf_op jit(solution)/shard_map/ppermute | solution.py:230
  160.4 23.5 %collective-permute-start.5 = (f32[4,48,768]{2,1,0:T(8,128)}, f32[4,48,768]{2,1,0:T(8,128)}, u32[]{:S(2)}, u32[]{:S(2)}) collective-permute-start(f32[4,48,768]{2,1,0:T(8,128)} %x_add.5), channel_id=1, source_target_pairs={{0,12},{1,13},{2,14},{3,15},{4,0},{5,1},{6,2},{7,3},{8,4},{9,5},{1... | collective-permute-start | bytes 1769480 | tf_op jit(solution)/shard_map/ppermute | solution.py:230
  162.3 23.8 %collective-permute-start.4 = (f32[4,48,768]{2,1,0:T(8,128)}, f32[4,48,768]{2,1,0:T(8,128)}, u32[]{:S(2)}, u32[]{:S(2)}) collective-permute-start(f32[4,48,768]{2,1,0:T(8,128)} %x_add.4), channel_id=1, source_target_pairs={{0,4},{1,5},{2,6},{3,7},{4,8},{5,9},{6,10},{7,11},{8,12},{9,13},{1... | collective-permute-start | bytes 1769480 | tf_op jit(solution)/shard_map/ppermute | solution.py:229
  169.4 39.1 %collective-permute-start.19 = (f32[4,48,768]{2,1,0:T(8,128)}, f32[4,48,768]{2,1,0:T(8,128)S(1)}, u32[]{:S(2)}, u32[]{:S(2)}) collective-permute-start(f32[4,48,768]{2,1,0:T(8,128)} %get-tuple-element.74), channel_id=1, source_target_pairs={{0,4},{1,5},{2,6},{3,7},{4,8},{5,9},{6,10},{7,11},{8,12},{9,13},{1... | collective-permute-start | bytes 1769480 | tf_op jit(solution)/shard_map/ppermute | solution.py:239
  174.2 35.5 %collective-permute-start.20 = (f32[4,48,768]{2,1,0:T(8,128)}, f32[4,48,768]{2,1,0:T(8,128)}, u32[]{:S(2)}, u32[]{:S(2)}) collective-permute-start(f32[4,48,768]{2,1,0:T(8,128)} %get-tuple-element.75), channel_id=1, source_target_pairs={{0,8},{1,9},{2,10},{3,11},{4,12},{5,13},{6,14},{7,15},{8,0},{9,1},... | collective-permute-start | bytes 1769480 | tf_op jit(solution)/shard_map/ppermute | solution.py:239
  176.9 32.9 %collective-permute-start.21 = (f32[4,48,768]{2,1,0:T(8,128)}, f32[4,48,768]{2,1,0:T(8,128)}, u32[]{:S(2)}, u32[]{:S(2)}) collective-permute-start(f32[4,48,768]{2,1,0:T(8,128)} %get-tuple-element.76), channel_id=1, source_target_pairs={{0,12},{1,13},{2,14},{3,15},{4,0},{5,1},{6,2},{7,3},{8,4},{9,5},{1... | collective-permute-start | bytes 1769480 | tf_op jit(solution)/shard_map/ppermute | solution.py:239
  189.0 30.0 %collective-permute-start.10 = (f32[4,48,768]{2,1,0:T(8,128)}, f32[4,48,768]{2,1,0:T(8,128)}, u32[]{:S(2)}, u32[]{:S(2)}) collective-permute-start(f32[4,48,768]{2,1,0:T(8,128)} %get-tuple-element.58), channel_id=1, source_target_pairs={{0,3},{1,0},{2,1},{3,2},{4,7},{5,4},{6,5},{7,6},{8,11},{9,8},{10,9... | collective-permute-start | bytes 1769480 | tf_op jit(solution)/shard_map/ppermute | solution.py:239
  195.9 23.1 %collective-permute-start.8 = (f32[4,48,768]{2,1,0:T(8,128)}, f32[4,48,768]{2,1,0:T(8,128)}, u32[]{:S(2)}, u32[]{:S(2)}) collective-permute-start(f32[4,48,768]{2,1,0:T(8,128)} %get-tuple-element.56), channel_id=1, source_target_pairs={{0,1},{1,2},{2,3},{3,0},{4,5},{5,6},{6,7},{7,4},{8,9},{9,10},{10,1... | collective-permute-start | bytes 1769480 | tf_op jit(solution)/shard_map/ppermute | solution.py:239
  208.5 11.8 %copy-start = (f32[4,48,768]{2,1,0:T(8,128)}, f32[4,48,768]{2,1,0:T(8,128)S(1)}, u32[]{:S(2)}) copy-start(f32[4,48,768]{2,1,0:T(8,128)S(1)} %collective-permute-done.19.refs_5_) | copy-start | bytes 1769476
  208.5 11.8 %collective-permute-start.9 = (f32[4,48,768]{2,1,0:T(8,128)}, f32[4,48,768]{2,1,0:T(8,128)}, u32[]{:S(2)}, u32[]{:S(2)}) collective-permute-start(f32[4,48,768]{2,1,0:T(8,128)} %get-tuple-element.57), channel_id=1, source_target_pairs={{0,2},{1,3},{2,0},{3,1},{4,6},{5,7},{6,4},{7,5},{8,10},{9,11},{10,... | collective-permute-start | bytes 1769480 | tf_op jit(solution)/shard_map/ppermute | solution.py:239
Sparse Core Ops, SparseCore 0:
  29.2 33.3 all-gather.6
  64.3 34.3 all-gather.4

commit v5 on v4

--- a/solution.py
+++ b/solution.py
@@ -10,6 +10,7 @@
 
 SIDE = 4
 VMEM = 63 * 1024 * 1024
+WIDTH = 256
 LIGHT = pl.CostEstimate(flops=0, bytes_accessed=0, transcendentals=0)
 def hops(count, stride, delta):
     pairs = []
@@ -49,20 +50,23 @@
 def product_kernel(v_first, place_at, place, sizes, origin, *refs):
     pieces, v_ref, (send_p, send_m, up, down, own, a_all, v_all) = refs[:8], refs[8], refs[-7:]
     rows = send_p.shape[1]
-    depth = v_ref.shape[1]
-    for a, piece in enumerate(pieces):
-        for h in range(2):
-            block = piece[0, 0, h * rows : (h + 1) * rows]
-            hi = block.astype(jnp.bfloat16)
-            lo = (block - hi.astype(jnp.float32)).astype(jnp.bfloat16)
-            at = pl.ds(pl.multiple_of(place[place_at + 2 * a + h] * rows, rows), rows)
-            a_all[at, 0:depth] = hi
-            a_all[at, depth : 2 * depth] = lo
-            a_all[at, 2 * depth : 3 * depth] = hi
+    depth, width = v_ref.shape[1:]
+
+    @pl.when(pl.program_id(1) == 0)
+    def _():
+        for a, piece in enumerate(pieces):
+            for h in range(2):
+                block = piece[0, 0, h * rows : (h + 1) * rows]
+                hi = block.astype(jnp.bfloat16)
+                lo = (block - hi.astype(jnp.float32)).astype(jnp.bfloat16)
+                at = pl.ds(pl.multiple_of(place[place_at + 2 * a + h] * rows, rows), rows)
+                a_all[at, 0:depth] = hi
+                a_all[at, depth : 2 * depth] = lo
+                a_all[at, 2 * depth : 3 * depth] = hi
+
     size = sizes[v_first + pl.program_id(0)]
-    shape = v_ref.shape[1:]
-    p = origin[0] + lax.broadcasted_iota(jnp.int32, shape, 0)
-    q = origin[1] + lax.broadcasted_iota(jnp.int32, shape, 1)
+    p = origin[0] + lax.broadcasted_iota(jnp.int32, (depth, width), 0)
+    q = origin[1] + pl.program_id(1) * width + lax.broadcasted_iota(jnp.int32, (depth, width), 1)
     v = jnp.where((p < size) & (q < size), v_ref[0], 0.0)
     hi = v.astype(jnp.bfloat16)
     v_all[0:depth] = hi
@@ -92,16 +96,16 @@
         functools.partial(product_kernel, v_first, place_at),
         grid_spec=pltpu.PrefetchScalarGridSpec(
             num_scalar_prefetch=3,
-            grid=(count,),
+            grid=(count, cols // WIDTH),
             in_specs=[
                 pl.BlockSpec((1, 1, rows2, depth), lambda g, *_, s=s: (s, skip + g, 0, 0)) for s in range(sources)
             ]
-            + [pl.BlockSpec((1, depth, cols), lambda g, *_: (v_first + g, 0, 0))]
+            + [pl.BlockSpec((1, depth, WIDTH), lambda g, c, *_: (v_first + g, 0, c))]
             + [pl.BlockSpec(memory_space=pl.ANY)] * len(after),
-            out_specs=[pl.BlockSpec((n, rows, cols), lambda g, *_: (g, 0, 0)) for n in leads],
+            out_specs=[pl.BlockSpec((n, rows, WIDTH), lambda g, c, *_: (g, 0, c)) for n in leads],
             scratch_shapes=[
                 pltpu.VMEM((total, 3 * depth), jnp.bfloat16),
-                pltpu.VMEM((3 * depth, cols), jnp.bfloat16),
+                pltpu.VMEM((3 * depth, WIDTH), jnp.bfloat16),
             ],
         ),
         out_shape=[
@@ -113,23 +117,24 @@
     )(place, sizes, origin, *[amp] * sources, ovov, *after)
 
 
-def add_kernel(mid, recv, out):
-    out[...] = mid[...] + recv[...]
-
-
-def add_far(mid, recv, name):
+def add_kernel(mid, recv, *refs):
+    refs[-1][...] = mid[...] + recv[...]
+
+
+def add_far(mid, recv, after, name):
     lead, rows, cols = mid.shape
     spec = pl.BlockSpec((2, rows, cols), lambda g: (g, 0, 0))
     return pl.pallas_call(
         add_kernel,
         grid=(lead // 2,),
-        in_specs=[spec, pl.BlockSpec((2, rows, cols), lambda g: (2 * g, 0, 0))],
+        in_specs=[spec, pl.BlockSpec((2, rows, cols), lambda g: (2 * g, 0, 0))]
+        + [pl.BlockSpec(memory_space=pl.ANY)] * len(after),
         out_specs=spec,
         out_shape=jax.ShapeDtypeStruct(mid.shape, jnp.float32),
         compiler_params=pltpu.CompilerParams(vmem_limit_bytes=VMEM),
         cost_estimate=LIGHT,
         name=name,
-    )(mid, recv)
+    )(mid, recv, *after)
 
 
 def own_kernel(own, p1, m1, p2, m2, *refs):
@@ -171,15 +176,14 @@
 
 def finish(order, parts, row_sizes, origin, shape):
     rows, irreps, cols = shape
-    width = 256
     flat = [p for four in parts for p in four]
     return pl.pallas_call(
         functools.partial(finish_kernel, order),
         grid_spec=pltpu.PrefetchScalarGridSpec(
             num_scalar_prefetch=2,
-            grid=(cols // width,),
-            in_specs=[pl.BlockSpec((p.shape[0], rows, width), lambda c, *_: (0, 0, c)) for p in flat],
-            out_specs=pl.BlockSpec((rows, irreps, width), lambda c, *_: (0, 0, c)),
+            grid=(cols // WIDTH,),
+            in_specs=[pl.BlockSpec((p.shape[0], rows, WIDTH), lambda c, *_: (0, 0, c)) for p in flat],
+            out_specs=pl.BlockSpec((rows, irreps, WIDTH), lambda c, *_: (0, 0, c)),
         ),
         out_shape=jax.ShapeDtypeStruct(shape, jnp.float32),
         compiler_params=pltpu.CompilerParams(vmem_limit_bytes=VMEM),
@@ -202,10 +206,9 @@
 
     origin = jnp.stack([ob * depth, vb * cols]).astype(jnp.int32)
 
-    axes = (("x", X_HOPS, Y_HOPS, 0), ("y", Y_HOPS, X_HOPS, 16))
-    order = {axis: [] for axis, *_ in axes}
-    sums = {axis: [] for axis, *_ in axes}
-    got = {}
+    axes = {"y": (Y_HOPS, X_HOPS, 16), "x": (X_HOPS, Y_HOPS, 0)}
+    order = {axis: [] for axis in axes}
+    sums = {axis: [] for axis in axes}
 
     gathered = []
     for first, nx, ny in GROUPS:
@@ -216,29 +219,44 @@
         mine = jnp.transpose(mine.reshape(obs * local_rows, count, depth), (1, 0, 2))
         gathered.append(lax.all_gather(mine, "vb", axis=0))
 
-    for (first, nx, ny), amp in zip(GROUPS, gathered):
-        for axis, here, there, place_at in axes:
-            skip, count = (0, nx) if axis == "x" else (nx, ny)
-            order[axis] += range(first + skip, first + skip + count)
-            send_p, send_m, up, down, mid = product(
-                amp, skip, ovov, first + skip, count, place, place_at, pair_sizes, origin, got.get(axis, []), f"{axis}_product"
-            )
-            p1 = lax.ppermute(send_p, BOTH, here[1])
-            m1 = lax.ppermute(send_m, BOTH, here[-1])
-            got[axis] = [p1, m1]
-            p2 = lax.ppermute(add_far(up, p1, f"{axis}_add"), BOTH, here[1])
-            m2 = lax.ppermute(add_far(down, m1, f"{axis}_add"), BOTH, here[-1])
-            sums[axis].append((mid, p1, m1, p2, m2))
+    def first_step(axis, t, waits):
+        first, nx, ny = GROUPS[t]
+        skip, count = (0, nx) if axis == "x" else (nx, ny)
+        order[axis] += range(first + skip, first + skip + count)
+        here, _, place_at = axes[axis]
+        send_p, send_m, up, down, mid = product(
+            gathered[t], skip, ovov, first + skip, count, place, place_at, pair_sizes, origin, waits, f"{axis}_product"
+        )
+        p1 = lax.ppermute(send_p, BOTH, here[1])
+        m1 = lax.ppermute(send_m, BOTH, here[-1])
+        return send_p, up, down, mid, p1, m1
+
+    def second_step(axis, now, waits):
+        here = axes[axis][0]
+        _, up, down, mid, p1, m1 = now
+        added = [add_far(up, p1, waits, f"{axis}_add"), add_far(down, m1, waits, f"{axis}_add")]
+        handed = [lax.ppermute(added[0], BOTH, here[1]), lax.ppermute(added[1], BOTH, here[-1])]
+        sums[axis].append((mid, p1, m1, *handed))
+        return added, handed
+
+    y1 = first_step("y", 0, [])
+    x1 = first_step("x", 0, [])
+    y1_added, y1_handed = second_step("y", y1, [])
+    y2 = first_step("y", 1, y1_added)
+    x1_added, x1_handed = second_step("x", x1, [y2[0]])
+    x2 = first_step("x", 1, x1_added + y1_handed)
+    second_step("y", y2, x1_handed)
+    second_step("x", x2, [])
 
     parts = []
-    for axis, here, there, _ in axes:
+    for axis, (_, there, _) in axes.items():
         four, at = [], 0
         for group in sums[axis]:
             four = add_own(*group, at, len(order[axis]), four, f"{axis}_own")
             at += group[0].shape[0] // 4
         parts.append([four[0]] + [lax.ppermute(four[k], BOTH, there[d]) for k, d in ((1, 1), (2, 2), (3, -1))])
     origin = jnp.stack([ob * out_rows, vb * cols]).astype(jnp.int32)
-    return finish([order[axis] for axis, *_ in axes], parts, row_sizes, origin, (out_rows, irreps, cols))
+    return finish([order[axis] for axis in axes], parts, row_sizes, origin, (out_rows, irreps, cols))
 
 
 def solution(mesh):

time: 234 us -> 236 us (level)
  Pallas kernels: 63.4 us -> 68.1 us
  waiting for transfers between devices: 79 us -> 76 us
    all_gather x2, waiting for transfers between devices: 29.7 us -> 15.7 us  [local(): gathered.append(lax.all_gather(mine, 'vb', axis=0))]
    ppermute x16, waiting for transfers between devices: 26.1 us -> 38 us  [the longest x4 18 us: first_step(): p1 = lax.ppermute(send_p, BOTH, here[1])]
    pallas_call x4, Pallas kernels: 30.8 us -> 35.8 us  [product(): pl.pallas_call(functools.partial(product_kernel, v_first, place_at), grid...]
  transfers between devices with their start and end apart: 24 -> 24, of which waited for: 14 -> 8; matrix products, arithmetic and copies ran while one was open for 2% -> 2% of each run, Pallas kernels for 25% -> 27%
where the time goes in v5:
time: 236 us; the launch traced here: 234 us
  waiting for transfers between devices  76 us (32%)
  Pallas kernels  68.1 us (29%)
  starting transfers between devices  35 us (15%)
  blocking collectives  33.4 us (14%)
  between operations  13.5 us (6%)
  local copies, waits for them, and re-layouts  6.97 us (3%)
    pallas_call x4, Pallas kernels, product(): pl.pallas_call(functools.partial(product_kernel, v_first, place_at), grid...  35.8 us
    all_to_all x2, blocking collectives, local(): mine = lax.all_to_all(mine, 'ob', split_axis=0, concat_axis=0, tiled=True)  33.4 us
    ppermute x6, waiting for transfers between devices, local(): lax.ppermute(four[k], BOTH, there[d])  22.2 us
    ppermute x4, waiting for transfers between devices, first_step(): p1 = lax.ppermute(send_p, BOTH, here[1])  18 us
    pallas_call x8, Pallas kernels, add_far(): pl.pallas_call(add_kernel, grid=(lead // 2,), in_specs=[spec, pl.BlockSpe...  15.9 us
    all_gather x2, waiting for transfers between devices, local(): gathered.append(lax.all_gather(mine, 'vb', axis=0))  15.7 us
    ppermute x4, waiting for transfers between devices, second_step(): lax.ppermute(added[1], BOTH, here[-1])  14.2 us
    ppermute x6, starting transfers between devices, local(): lax.ppermute(four[k], BOTH, there[d])  12.4 us
  transfers between devices with their start and end apart: 24, of which 8 were waited for; matrix products, arithmetic and copies ran while one was open for 2% of the time, Pallas kernels for 27%

profile of v5, /device:TPU:0, one launch (start us, length us, event | category | flops | bytes accessed | tf_op | source)
XLA Modules:
  0.0 234.2 jit_solution(17215758210652321349)
XLA Ops:
  6.5 1.8 fusion
  8.9 19.1 %all_to_all.10 = f32[16,24,384]{2,1,0:T(8,128)S(1)} all-to-all(f32[16,24,384]{2,1,0:T(8,128)S(1)} %copy.20), channel_id=1, replica_groups=mesh['vb'=8,'ob'=16] {'ob'}, dimensions={0} | all-to-all | bytes 1179648 | tf_op jit(solution)/shard_map/all_to_all | solution.py:218
  28.2 0.9 copy.21
  29.6 14.3 %all_to_all.11 = f32[16,24,384]{2,1,0:T(8,128)S(1)} all-to-all(f32[16,24,384]{2,1,0:T(8,128)S(1)} %copy.18), channel_id=1, replica_groups=mesh['vb'=8,'ob'=16] {'ob'}, dimensions={0} | all-to-all | bytes 1179648 | tf_op jit(solution)/shard_map/all_to_all | solution.py:218
  44.1 0.9 copy.19
  45.6 1.3 dynamic-slice_bitcast_fusion.place
  46.9 15.7 %all-gather.7.cloned.1.call-done = f32[32,96,384]{2,1,0:T(8,128)} async-done(((f32[4,96,384]{2,1,0:T(8,128)}), f32[32,96,384]{2,1,0:T(8,128)}) %all-gather.7.cloned.1.call-update) | async-done | bytes 4718608 | tf_op jit(solution)/shard_map/all_gather | solution.py:220
  62.6 8.9 %y_product.2 = (f32[8,48,768]{2,1,0:T(8,128)}, f32[8,48,768]{2,1,0:T(8,128)}, f32[4,48,768]{2,1,0:T(8,128)}, f32[4,48,768]{2,1,0:T(8,128)}, f32[8,48,768]{2,1,0:T(8,128)}) custom-call(s32[32]{0:T(128)} %dynamic-slice_bitcast_fusion.place, s32[8]{0:T(128)} %sizes.8, s32[2]{0:T(128)} %pad_add_fusion.1.origin, f32[8,4,96,384]{3,2,1,0:T(8,128)} %bitcast.31, ...), custom_call_target="tpu_custom_call" | custom-call | tf_op jit(solution)/shard_map/y_product/pallas_call | solution.py:95
  71.5 1.6 collective-permute-start
  73.1 1.8 collective-permute-start.1
  74.8 8.9 %x_product.2 = (f32[8,48,768]{2,1,0:T(8,128)}, f32[8,48,768]{2,1,0:T(8,128)}, f32[4,48,768]{2,1,0:T(8,128)}, f32[4,48,768]{2,1,0:T(8,128)}, f32[8,48,768]{2,1,0:T(8,128)}) custom-call(s32[32]{0:T(128)} %dynamic-slice_bitcast_fusion.place, s32[8]{0:T(128)} %sizes.8, s32[2]{0:T(128)} %pad_add_fusion.1.origin, f32[8,4,96,384]{3,2,1,0:T(8,128)} %bitcast.39, ...), custom_call_target="tpu_custom_call" | custom-call | tf_op jit(solution)/shard_map/x_product/pallas_call | solution.py:95
  83.7 1.5 collective-permute-start.4
  85.3 1.8 collective-permute-start.6
  87.0 13.1 %collective-permute-done.recv.p1 = f32[8,48,768]{2,1,0:T(8,128)} collective-permute-done((f32[8,48,768]{2,1,0:T(8,128)}, f32[8,48,768]{2,1,0:T(8,128)}, u32[]{:S(2)}, u32[]{:S(2)}) %collective-permute-start) | collective-permute-done | bytes 1179680 | tf_op jit(solution)/shard_map/ppermute | solution.py:230
  100.1 2.0 y_add.4.refs_9_
  102.1 1.6 collective-permute-start.10
  103.7 2.0 y_add.5.refs_10_
  105.7 1.6 collective-permute-start.11
  107.4 8.9 %y_product.3 = (f32[8,48,768]{2,1,0:T(8,128)}, f32[8,48,768]{2,1,0:T(8,128)}, f32[4,48,768]{2,1,0:T(8,128)}, f32[4,48,768]{2,1,0:T(8,128)}, f32[8,48,768]{2,1,0:T(8,128)}) custom-call(s32[32]{0:T(128)} %dynamic-slice_bitcast_fusion.place, s32[8]{0:T(128)} %sizes.8, s32[2]{0:T(128)} %pad_add_fusion.1.origin, f32[8,4,96,384]{3,2,1,0:T(8,128)} %bitcast.15, ...), custom_call_target="tpu_custom_call" | custom-call | tf_op jit(solution)/shard_map/y_product/pallas_call | solution.py:95
  116.3 2.0 x_add.4.refs_9_
  118.3 1.5 collective-permute-start.5
  119.8 2.0 collective-permute-start.3
  121.8 2.0 x_add.5.refs_10_
  123.8 9.0 %x_product.3 = (f32[8,48,768]{2,1,0:T(8,128)}, f32[8,48,768]{2,1,0:T(8,128)}, f32[4,48,768]{2,1,0:T(8,128)}, f32[4,48,768]{2,1,0:T(8,128)}, f32[8,48,768]{2,1,0:T(8,128)}) custom-call(s32[32]{0:T(128)} %dynamic-slice_bitcast_fusion.place, s32[8]{0:T(128)} %sizes.8, s32[2]{0:T(128)} %pad_add_fusion.1.origin, f32[8,4,96,384]{3,2,1,0:T(8,128)} %bitcast.23, ...), custom_call_target="tpu_custom_call" | custom-call | tf_op jit(solution)/shard_map/x_product/pallas_call | solution.py:95
  132.8 1.5 collective-permute-start.15
  134.3 1.8 collective-permute-start.7
  136.7 14.2 %collective-permute-done.7.refs_1_.m2 = f32[4,48,768]{2,1,0:T(8,128)} collective-permute-done((f32[4,48,768]{2,1,0:T(8,128)}, f32[4,48,768]{2,1,0:T(8,128)}, u32[]{:S(2)}, u32[]{:S(2)}) %collective-permute-start.7) | collective-permute-done | bytes 589856 | tf_op jit(solution)/shard_map/ppermute | solution.py:238
  150.9 2.0 y_add.7
  152.9 3.2 %collective-permute-start.9 = (f32[4,48,768]{2,1,0:T(8,128)}, f32[4,48,768]{2,1,0:T(8,128)S(1)}, u32[]{:S(2)}, u32[]{:S(2)}) collective-permute-start(f32[4,48,768]{2,1,0:T(8,128)} %y_add.7), channel_id=1, source_target_pairs={{0,3},{1,0},{2,1},{3,2},{4,7},{5,4},{6,5},{7,6},{8,11},{9,8},{10,9... | collective-permute-start | bytes 1769480 | tf_op jit(solution)/shard_map/ppermute | solution.py:238
  156.1 2.0 y_add.6
  158.1 4.9 %collective-permute-done.15.recv.p1 = f32[8,48,768]{2,1,0:T(8,128)} collective-permute-done((f32[8,48,768]{2,1,0:T(8,128)}, f32[8,48,768]{2,1,0:T(8,128)}, u32[]{:S(2)}, u32[]{:S(2)}) %collective-permute-start.15) | collective-permute-done | bytes 1179680 | tf_op jit(solution)/shard_map/ppermute | solution.py:230
  162.9 2.0 x_add.6
  165.4 5.8 %collective-permute-done.16.recv.m1 = f32[8,48,768]{2,1,0:T(8,128)} collective-permute-done((f32[8,48,768]{2,1,0:T(8,128)}, f32[8,48,768]{2,1,0:T(8,128)}, u32[]{:S(2)}, u32[]{:S(2)}) %collective-permute-start.16) | collective-permute-done | bytes 1179680 | tf_op jit(solution)/shard_map/ppermute | solution.py:231
  171.1 2.0 x_add.7
  173.1 1.8 collective-permute-start.18
  174.9 2.9 %y_own.2 = (f32[4,48,768]{2,1,0:T(8,128)}, f32[4,48,768]{2,1,0:T(8,128)}, f32[4,48,768]{2,1,0:T(8,128)}, f32[4,48,768]{2,1,0:T(8,128)}) custom-call(f32[8,48,768]{2,1,0:T(8,128)} %get-tuple-element.54.own, f32[8,48,768]{2,1,0:T(8,128)} %collective-permute-done.recv.p1, f32[8,48,768]{2,1,0:T(8,128)} %collective-permute-done.1.recv.m1, ...), custom_call_target="tpu_custom_call" | custom-call | tf_op jit(solution)/shard_map/y_own/pallas_call | solution.py:152
  177.8 0.8 copy-done.2
  178.6 2.9 %y_own.3 = (f32[4,48,768]{2,1,0:T(8,128)}, f32[4,48,768]{2,1,0:T(8,128)}, f32[4,48,768]{2,1,0:T(8,128)}, f32[4,48,768]{2,1,0:T(8,128)}) custom-call(f32[8,48,768]{2,1,0:T(8,128)} %get-tuple-element.45.own, f32[8,48,768]{2,1,0:T(8,128)} %collective-permute-done.2.recv.p1, ...), custom_call_target="tpu_custom_call", output_to_operand_aliasing={{0}: (5, {}), {1}: (6, {}), {2}: (7, {}), {3}: (8, {})} | custom-call | tf_op jit(solution)/shard_map/y_own/pallas_call | solution.py:152
  181.7 2.8 %x_own.2 = (f32[4,48,768]{2,1,0:T(8,128)}, f32[4,48,768]{2,1,0:T(8,128)}, f32[4,48,768]{2,1,0:T(8,128)}, f32[4,48,768]{2,1,0:T(8,128)}) custom-call(f32[8,48,768]{2,1,0:T(8,128)} %get-tuple-element.68.own, f32[8,48,768]{2,1,0:T(8,128)} %collective-permute-done.4.recv.p1, f32[8,48,768]{2,1,0:T(8,128)} %collective-permute-done.6.recv.m1, ...), custom_call_target="tpu_custom_call" | custom-call | tf_op jit(solution)/shard_map/x_own/pallas_call | solution.py:152
  184.5 1.2 collective-permute-start.13
  185.8 1.8 collective-permute-start.14
  187.6 2.8 %x_own.3 = (f32[4,48,768]{2,1,0:T(8,128)}, f32[4,48,768]{2,1,0:T(8,128)}, f32[4,48,768]{2,1,0:T(8,128)}, f32[4,48,768]{2,1,0:T(8,128)}) custom-call(f32[8,48,768]{2,1,0:T(8,128)} %get-tuple-element.63.own, f32[8,48,768]{2,1,0:T(8,128)} %collective-permute-done.15.recv.p1, ...), custom_call_target="tpu_custom_call", output_to_operand_aliasing={{0}: (5, {}), {1}: (6, {}), {2}: (7, {}), {3}: (8, {})} | custom-call | tf_op jit(solution)/shard_map/x_own/pallas_call | solution.py:152
  190.9 4.2 %collective-permute-start.20 = (f32[4,48,768]{2,1,0:T(8,128)}, f32[4,48,768]{2,1,0:T(8,128)}, u32[]{:S(2)}, u32[]{:S(2)}) collective-permute-start(f32[4,48,768]{2,1,0:T(8,128)} %get-tuple-element.75), channel_id=1, source_target_pairs={{0,2},{1,3},{2,0},{3,1},{4,6},{5,7},{6,4},{7,5},{8,10},{9,11},{10,... | collective-permute-start | bytes 1769480 | tf_op jit(solution)/shard_map/ppermute | solution.py:257
  195.1 15.1 %collective-permute-done.12.refs_1_ = f32[4,48,768]{2,1,0:T(8,128)S(1)} collective-permute-done((f32[4,48,768]{2,1,0:T(8,128)}, f32[4,48,768]{2,1,0:T(8,128)S(1)}, u32[]{:S(2)}, u32[]{:S(2)}) %collective-permute-start.12) | collective-permute-done | bytes 589856 | tf_op jit(solution)/shard_map/ppermute | solution.py:257
  210.3 4.4 %collective-permute-start.21 = (f32[4,48,768]{2,1,0:T(8,128)}, f32[4,48,768]{2,1,0:T(8,128)}, u32[]{:S(2)}, u32[]{:S(2)}) collective-permute-start(f32[4,48,768]{2,1,0:T(8,128)} %get-tuple-element.76), channel_id=1, source_target_pairs={{0,3},{1,0},{2,1},{3,2},{4,7},{5,4},{6,5},{7,6},{8,11},{9,8},{10,9... | collective-permute-start | bytes 1769480 | tf_op jit(solution)/shard_map/ppermute | solution.py:257
  215.2 2.1 collective-permute-done.20.refs_6_
  217.4 5.0 %collective-permute-done.21.refs_7_ = f32[4,48,768]{2,1,0:T(8,128)} collective-permute-done((f32[4,48,768]{2,1,0:T(8,128)}, f32[4,48,768]{2,1,0:T(8,128)}, u32[]{:S(2)}, u32[]{:S(2)}) %collective-permute-start.21) | collective-permute-done | bytes 589856 | tf_op jit(solution)/shard_map/ppermute | solution.py:257
  222.4 5.0 %finish.1 = f32[48,8,768]{2,1,0:T(8,128)} custom-call(s32[8]{0:T(128)} %sizes.9, s32[2]{0:T(128)} %pad_add_fusion.origin, f32[4,48,768]{2,1,0:T(8,128)} %get-tuple-element.59.refs_0_, f32[4,48,768]{2,1,0:T(8,128)} %copy-done.1, f32[4,48,768]{2,1,0:T(8,128)} %collective-permute-done.13.refs_2_, f32[4,48,768]{2,1,0:T(8,128)} %collective-permute-done.14.refs_3_, ...), custom_call_target="tpu_custom_call" | custom-call | tf_op jit(solution)/shard_map/finish/pallas_call | solution.py:180
  (39 shorter events, 4.4 us)
Async XLA Ops:
  6.5 56.0 %all-gather.7.cloned.1.call-start = ((), (), s32[]{:S(2)}) async-start(), calls=%async_computation.3 | async-start | bytes 5308416 | tf_op jit(solution)/shard_map/all_gather | solution.py:220
  29.1 78.3 %all-gather.5.cloned.1.call-start = ((), (), s32[]{:S(2)}) async-start(), calls=%async_computation.2 | async-start | bytes 5308416 | tf_op jit(solution)/shard_map/all_gather | solution.py:220
  71.5 28.6 %collective-permute-start = (f32[8,48,768]{2,1,0:T(8,128)}, f32[8,48,768]{2,1,0:T(8,128)}, u32[]{:S(2)}, u32[]{:S(2)}) collective-permute-start(f32[8,48,768]{2,1,0:T(8,128)} %get-tuple-element.42), channel_id=1, source_target_pairs={{0,1},{1,2},{2,3},{3,0},{4,5},{5,6},{6,7},{7,4},{8,9},{9,10},{10,1... | collective-permute-start | bytes 3538952 | tf_op jit(solution)/shard_map/ppermute | solution.py:230
  73.1 30.7 %collective-permute-start.1 = (f32[8,48,768]{2,1,0:T(8,128)}, f32[8,48,768]{2,1,0:T(8,128)}, u32[]{:S(2)}, u32[]{:S(2)}) collective-permute-start(f32[8,48,768]{2,1,0:T(8,128)} %get-tuple-element.44), channel_id=1, source_target_pairs={{0,3},{1,0},{2,1},{3,2},{4,7},{5,4},{6,5},{7,6},{8,11},{9,8},{10,9... | collective-permute-start | bytes 3538952 | tf_op jit(solution)/shard_map/ppermute | solution.py:231
  83.7 32.6 %collective-permute-start.4 = (f32[8,48,768]{2,1,0:T(8,128)}, f32[8,48,768]{2,1,0:T(8,128)}, u32[]{:S(2)}, u32[]{:S(2)}) collective-permute-start(f32[8,48,768]{2,1,0:T(8,128)} %get-tuple-element.50), channel_id=1, source_target_pairs={{0,4},{1,5},{2,6},{3,7},{4,8},{5,9},{6,10},{7,11},{8,12},{9,13},{1... | collective-permute-start | bytes 3538952 | tf_op jit(solution)/shard_map/ppermute | solution.py:230
  85.3 36.5 %collective-permute-start.6 = (f32[8,48,768]{2,1,0:T(8,128)}, f32[8,48,768]{2,1,0:T(8,128)}, u32[]{:S(2)}, u32[]{:S(2)}) collective-permute-start(f32[8,48,768]{2,1,0:T(8,128)} %get-tuple-element.52), channel_id=1, source_target_pairs={{0,12},{1,13},{2,14},{3,15},{4,0},{5,1},{6,2},{7,3},{8,4},{9,5},{1... | collective-permute-start | bytes 3538952 | tf_op jit(solution)/shard_map/ppermute | solution.py:231
  102.1 21.7 %collective-permute-start.10 = (f32[4,48,768]{2,1,0:T(8,128)}, f32[4,48,768]{2,1,0:T(8,128)}, u32[]{:S(2)}, u32[]{:S(2)}) collective-permute-start(f32[4,48,768]{2,1,0:T(8,128)} %y_add.4.refs_9_), channel_id=1, source_target_pairs={{0,1},{1,2},{2,3},{3,0},{4,5},{5,6},{6,7},{7,4},{8,9},{9,10},{10,1... | collective-permute-start | bytes 1769480 | tf_op jit(solution)/shard_map/ppermute | solution.py:238
  105.7 18.1 %collective-permute-start.11 = (f32[4,48,768]{2,1,0:T(8,128)}, f32[4,48,768]{2,1,0:T(8,128)}, u32[]{:S(2)}, u32[]{:S(2)}) collective-permute-start(f32[4,48,768]{2,1,0:T(8,128)} %y_add.5.refs_10_), channel_id=1, source_target_pairs={{0,3},{1,0},{2,1},{3,2},{4,7},{5,4},{6,5},{7,6},{8,11},{9,8},{10,9... | collective-permute-start | bytes 1769480 | tf_op jit(solution)/shard_map/ppermute | solution.py:238
  118.3 17.8 %collective-permute-start.5 = (f32[4,48,768]{2,1,0:T(8,128)}, f32[4,48,768]{2,1,0:T(8,128)S(1)}, u32[]{:S(2)}, u32[]{:S(2)}) collective-permute-start(f32[4,48,768]{2,1,0:T(8,128)} %x_add.4.refs_9_), channel_id=1, source_target_pairs={{0,4},{1,5},{2,6},{3,7},{4,8},{5,9},{6,10},{7,11},{8,12},{9,13},{1... | collective-permute-start | bytes 1769480 | tf_op jit(solution)/shard_map/ppermute | solution.py:238
  119.8 31.1 %collective-permute-start.3 = (f32[8,48,768]{2,1,0:T(8,128)}, f32[8,48,768]{2,1,0:T(8,128)}, u32[]{:S(2)}, u32[]{:S(2)}) collective-permute-start(f32[8,48,768]{2,1,0:T(8,128)} %get-tuple-element.47), channel_id=1, source_target_pairs={{0,3},{1,0},{2,1},{3,2},{4,7},{5,4},{6,5},{7,6},{8,11},{9,8},{10,9... | collective-permute-start | bytes 3538952 | tf_op jit(solution)/shard_map/ppermute | solution.py:231
  121.7 34.3 %collective-permute-start.2 = (f32[8,48,768]{2,1,0:T(8,128)}, f32[8,48,768]{2,1,0:T(8,128)}, u32[]{:S(2)}, u32[]{:S(2)}) collective-permute-start(f32[8,48,768]{2,1,0:T(8,128)} %get-tuple-element.46.refs_0_), channel_id=1, source_target_pairs={{0,1},{1,2},{2,3},{3,0},{4,5},{5,6},{6,7},{7,4},{8,9},{9,10},{10,1... | collective-permute-start | bytes 3538952 | tf_op jit(solution)/shard_map/ppermute | solution.py:230
  132.8 30.1 %collective-permute-start.15 = (f32[8,48,768]{2,1,0:T(8,128)}, f32[8,48,768]{2,1,0:T(8,128)}, u32[]{:S(2)}, u32[]{:S(2)}) collective-permute-start(f32[8,48,768]{2,1,0:T(8,128)} %get-tuple-element.64), channel_id=1, source_target_pairs={{0,4},{1,5},{2,6},{3,7},{4,8},{5,9},{6,10},{7,11},{8,12},{9,13},{1... | collective-permute-start | bytes 3538952 | tf_op jit(solution)/shard_map/ppermute | solution.py:230
  134.3 16.6 %collective-permute-start.7 = (f32[4,48,768]{2,1,0:T(8,128)}, f32[4,48,768]{2,1,0:T(8,128)}, u32[]{:S(2)}, u32[]{:S(2)}) collective-permute-start(f32[4,48,768]{2,1,0:T(8,128)} %x_add.5.refs_10_), channel_id=1, source_target_pairs={{0,12},{1,13},{2,14},{3,15},{4,0},{5,1},{6,2},{7,3},{8,4},{9,5},{1... | collective-permute-start | bytes 1769480 | tf_op jit(solution)/shard_map/ppermute | solution.py:238
  136.1 14.8 %copy-start = (f32[4,48,768]{2,1,0:T(8,128)}, f32[4,48,768]{2,1,0:T(8,128)S(1)}, u32[]{:S(2)}) copy-start(f32[4,48,768]{2,1,0:T(8,128)S(1)} %collective-permute-done.5.refs_0_.p2) | copy-start | bytes 1769476
  136.1 35.0 %collective-permute-start.16 = (f32[8,48,768]{2,1,0:T(8,128)}, f32[8,48,768]{2,1,0:T(8,128)}, u32[]{:S(2)}, u32[]{:S(2)}) collective-permute-start(f32[8,48,768]{2,1,0:T(8,128)} %get-tuple-element.65), channel_id=1, source_target_pairs={{0,12},{1,13},{2,14},{3,15},{4,0},{5,1},{6,2},{7,3},{8,4},{9,5},{1... | collective-permute-start | bytes 3538952 | tf_op jit(solution)/shard_map/ppermute | solution.py:231
  152.9 24.9 %collective-permute-start.9 = (f32[4,48,768]{2,1,0:T(8,128)}, f32[4,48,768]{2,1,0:T(8,128)S(1)}, u32[]{:S(2)}, u32[]{:S(2)}) collective-permute-start(f32[4,48,768]{2,1,0:T(8,128)} %y_add.7), channel_id=1, source_target_pairs={{0,3},{1,0},{2,1},{3,2},{4,7},{5,4},{6,5},{7,6},{8,11},{9,8},{10,9... | collective-permute-start | bytes 1769480 | tf_op jit(solution)/shard_map/ppermute | solution.py:238
  158.1 19.7 %collective-permute-start.8 = (f32[4,48,768]{2,1,0:T(8,128)}, f32[4,48,768]{2,1,0:T(8,128)}, u32[]{:S(2)}, u32[]{:S(2)}) collective-permute-start(f32[4,48,768]{2,1,0:T(8,128)} %y_add.6), channel_id=1, source_target_pairs={{0,1},{1,2},{2,3},{3,0},{4,5},{5,6},{6,7},{7,4},{8,9},{9,10},{10,1... | collective-permute-start | bytes 1769480 | tf_op jit(solution)/shard_map/ppermute | solution.py:238
  164.9 22.7 %collective-permute-start.17 = (f32[4,48,768]{2,1,0:T(8,128)}, f32[4,48,768]{2,1,0:T(8,128)}, u32[]{:S(2)}, u32[]{:S(2)}) collective-permute-start(f32[4,48,768]{2,1,0:T(8,128)} %x_add.6), channel_id=1, source_target_pairs={{0,4},{1,5},{2,6},{3,7},{4,8},{5,9},{6,10},{7,11},{8,12},{9,13},{1... | collective-permute-start | bytes 1769480 | tf_op jit(solution)/shard_map/ppermute | solution.py:238
  173.1 14.5 %collective-permute-start.18 = (f32[4,48,768]{2,1,0:T(8,128)}, f32[4,48,768]{2,1,0:T(8,128)}, u32[]{:S(2)}, u32[]{:S(2)}) collective-permute-start(f32[4,48,768]{2,1,0:T(8,128)} %x_add.7), channel_id=1, source_target_pairs={{0,12},{1,13},{2,14},{3,15},{4,0},{5,1},{6,2},{7,3},{8,4},{9,5},{1... | collective-permute-start | bytes 1769480 | tf_op jit(solution)/shard_map/ppermute | solution.py:238
  177.8 0.8 copy-start.2
  181.5 28.8 %collective-permute-start.12 = (f32[4,48,768]{2,1,0:T(8,128)}, f32[4,48,768]{2,1,0:T(8,128)S(1)}, u32[]{:S(2)}, u32[]{:S(2)}) collective-permute-start(f32[4,48,768]{2,1,0:T(8,128)} %get-tuple-element.60), channel_id=1, source_target_pairs={{0,4},{1,5},{2,6},{3,7},{4,8},{5,9},{6,10},{7,11},{8,12},{9,13},{1... | collective-permute-start | bytes 1769480 | tf_op jit(solution)/shard_map/ppermute | solution.py:257
  184.5 30.7 %collective-permute-start.13 = (f32[4,48,768]{2,1,0:T(8,128)}, f32[4,48,768]{2,1,0:T(8,128)}, u32[]{:S(2)}, u32[]{:S(2)}) collective-permute-start(f32[4,48,768]{2,1,0:T(8,128)} %get-tuple-element.61), channel_id=1, source_target_pairs={{0,8},{1,9},{2,10},{3,11},{4,12},{5,13},{6,14},{7,15},{8,0},{9,1},... | collective-permute-start | bytes 1769480 | tf_op jit(solution)/shard_map/ppermute | solution.py:257
  185.8 29.5 %collective-permute-start.14 = (f32[4,48,768]{2,1,0:T(8,128)}, f32[4,48,768]{2,1,0:T(8,128)}, u32[]{:S(2)}, u32[]{:S(2)}) collective-permute-start(f32[4,48,768]{2,1,0:T(8,128)} %get-tuple-element.62), channel_id=1, source_target_pairs={{0,12},{1,13},{2,14},{3,15},{4,0},{5,1},{6,2},{7,3},{8,4},{9,5},{1... | collective-permute-start | bytes 1769480 | tf_op jit(solution)/shard_map/ppermute | solution.py:257
  190.5 24.8 %collective-permute-start.19 = (f32[4,48,768]{2,1,0:T(8,128)}, f32[4,48,768]{2,1,0:T(8,128)}, u32[]{:S(2)}, u32[]{:S(2)}) collective-permute-start(f32[4,48,768]{2,1,0:T(8,128)} %get-tuple-element.74), channel_id=1, source_target_pairs={{0,1},{1,2},{2,3},{3,0},{4,5},{5,6},{6,7},{7,4},{8,9},{9,10},{10,1... | collective-permute-start | bytes 1769480 | tf_op jit(solution)/shard_map/ppermute | solution.py:257
  190.9 26.5 %collective-permute-start.20 = (f32[4,48,768]{2,1,0:T(8,128)}, f32[4,48,768]{2,1,0:T(8,128)}, u32[]{:S(2)}, u32[]{:S(2)}) collective-permute-start(f32[4,48,768]{2,1,0:T(8,128)} %get-tuple-element.75), channel_id=1, source_target_pairs={{0,2},{1,3},{2,0},{3,1},{4,6},{5,7},{6,4},{7,5},{8,10},{9,11},{10,... | collective-permute-start | bytes 1769480 | tf_op jit(solution)/shard_map/ppermute | solution.py:257
  210.3 12.1 %copy-start.1 = (f32[4,48,768]{2,1,0:T(8,128)}, f32[4,48,768]{2,1,0:T(8,128)S(1)}, u32[]{:S(2)}) copy-start(f32[4,48,768]{2,1,0:T(8,128)S(1)} %collective-permute-done.12.refs_1_) | copy-start | bytes 1769476
  210.3 12.1 %collective-permute-start.21 = (f32[4,48,768]{2,1,0:T(8,128)}, f32[4,48,768]{2,1,0:T(8,128)}, u32[]{:S(2)}, u32[]{:S(2)}) collective-permute-start(f32[4,48,768]{2,1,0:T(8,128)} %get-tuple-element.76), channel_id=1, source_target_pairs={{0,3},{1,0},{2,1},{3,2},{4,7},{5,4},{6,5},{7,6},{8,11},{9,8},{10,9... | collective-permute-start | bytes 1769480 | tf_op jit(solution)/shard_map/ppermute | solution.py:257
Sparse Core Ops, SparseCore 0:
  29.2 33.3 all-gather.6
  64.3 34.3 all-gather.4

commit v6 on v4

v6 whole, which is shorter than its diff:
```python
import functools

import jax
import jax.numpy as jnp
import numpy as np
from jax import lax
from jax.experimental import pallas as pl
from jax.experimental.pallas import tpu as pltpu
from jax.sharding import PartitionSpec as P

SIDE = 4
VMEM = 63 * 1024 * 1024
WIDTH = 256
LIGHT = pl.CostEstimate(flops=0, bytes_accessed=0, transcendentals=0)
def hops(count, stride, delta):
    pairs = []
    for i in range(count):
        d = (i // stride) % SIDE
        pairs.append((i, i + ((d + delta) % SIDE - d) * stride))
    return pairs


def apart(count, stride, delta, cores):
    up, down = hops(count, stride, delta), hops(count, stride, -delta)
    return [(down if cores(i) else up)[i] for i in range(count)]


X_HOPS = {d: apart(128, SIDE, d, lambda i: i // 16 % 2) for d in (1, 2, -1)}
Y_HOPS = {d: apart(128, 1, d, lambda i: i // 16 % 2) for d in (1, 2, -1)}
BOTH = ("vb", "ob")


ORDER = [(2, 0), (2, 1), (1, 2), (1, 3)] + [(2, 2), (2, 3), (3, 0), (3, 1)]
ORDER += [(1, 0), (1, 1)] + [(3, 2), (3, 3)] + [(0, k) for k in range(SIDE)]


def block_table():
    table = np.zeros((8, 16, 32), np.int32)
    for vb in range(8):
        for ob in range(16):
            x, y = divmod(ob, SIDE)
            sign = -1 if vb % 2 else 1
            for i, (near, far) in enumerate(ORDER):
                table[vb, ob, i] = (x + sign * near) % SIDE * SIDE + (y + sign * far) % SIDE
                table[vb, ob, 16 + i] = (x + sign * far) % SIDE * SIDE + (y + sign * near) % SIDE
    return table


BLOCKS = block_table()


def product_kernel(first, x_count, leads, blocks, sizes, origin, *refs):
    pieces, v_ref, outs, (a_all, v_all) = refs[:8], refs[8], refs[-2 - 2 * len(leads) : -2], refs[-2:]
    rows, depth = pieces[0].shape[3:]
    for i, piece in enumerate(pieces):
        block = piece[0, 0, 0]
        hi = block.astype(jnp.bfloat16)
        at = slice(rows * i, rows * (i + 1))
        a_all[at, 0:depth] = hi
        a_all[at, depth : 2 * depth] = (block - hi.astype(jnp.float32)).astype(jnp.bfloat16)
        a_all[at, 2 * depth : 3 * depth] = hi
    size = sizes[first + pl.program_id(0)]
    shape = v_ref.shape[1:]
    p = origin[0] + lax.broadcasted_iota(jnp.int32, shape, 0)
    q = origin[1] + lax.broadcasted_iota(jnp.int32, shape, 1)
    v = jnp.where((p < size) & (q < size), v_ref[0], 0.0)
    hi = v.astype(jnp.bfloat16)
    v_all[0:depth] = hi
    v_all[depth : 2 * depth] = hi
    v_all[2 * depth : 3 * depth] = (v - hi.astype(jnp.float32)).astype(jnp.bfloat16)

    def write(targets):
        at = 0
        for lead, out in zip(leads, targets):
            acc = jnp.dot(
                a_all[rows * at : rows * (at + lead)], v_all[...], preferred_element_type=jnp.float32
            )
            for k in range(lead):
                out[k, 0] = acc[rows * k : rows * (k + 1)]
            at += lead

    @pl.when(pl.program_id(0) < x_count)
    def _():
        write(outs[: len(leads)])

    @pl.when(pl.program_id(0) >= x_count)
    def _():
        write(outs[len(leads) :])


def product(amp, ovov, first, x_count, y_count, half, leads, blocks, sizes, origin, after, name):
    rows, depth = amp.shape[3:]
    cols = ovov.shape[2]

    def a_spec(i):
        def index(g, blocks, *_):
            block = blocks[jnp.where(g < x_count, 0, 16) + 8 * half + i]
            return block // 2, g, block % 2, 0, 0

        return pl.BlockSpec((1, 1, 1, rows, depth), index)

    def x_spec(lead):
        return pl.BlockSpec((lead, 1, rows, cols), lambda g, *_: (0, jnp.minimum(g, x_count - 1), 0, 0))

    def y_spec(lead):
        return pl.BlockSpec((lead, 1, rows, cols), lambda g, *_: (0, jnp.maximum(g - x_count, 0), 0, 0))

    shapes = [(lead, count, rows, cols) for count in (x_count, y_count) for lead in leads]
    outs = pl.pallas_call(
        functools.partial(product_kernel, first, x_count, leads),
        grid_spec=pltpu.PrefetchScalarGridSpec(
            num_scalar_prefetch=3,
            grid=(x_count + y_count,),
            in_specs=[a_spec(i) for i in range(8)]
            + [pl.BlockSpec((1, depth, cols), lambda g, *_: (first + g, 0, 0))]
            + [pl.BlockSpec(memory_space=pl.ANY)] * len(after),
            out_specs=[x_spec(lead) for lead in leads] + [y_spec(lead) for lead in leads],
            scratch_shapes=[
                pltpu.VMEM((8 * rows, 3 * depth), jnp.bfloat16),
                pltpu.VMEM((3 * depth, cols), jnp.bfloat16),
            ],
        ),
        out_shape=[jax.ShapeDtypeStruct(shape, jnp.float32) for shape in shapes],
        compiler_params=pltpu.CompilerParams(vmem_limit_bytes=VMEM),
        cost_estimate=LIGHT,
        name=name,
    )(blocks, sizes, origin, *[amp] * 8, ovov, *after)
    return {"x": outs[: len(leads)], "y": outs[len(leads) :]}


def add_kernel(up, down, recv_p, recv_m, *refs):
    refs[-2][...] = up[...] + recv_p[...]
    refs[-1][...] = down[...] + recv_m[...]


def add_far(up, down, recv_p, recv_m, after, name):
    lead, count, rows, cols = up.shape
    spec = pl.BlockSpec((lead, 1, rows, cols), lambda g: (0, g, 0, 0))
    return pl.pallas_call(
        add_kernel,
        grid=(count,),
        in_specs=[spec] * 4 + [pl.BlockSpec(memory_space=pl.ANY)] * len(after),
        out_specs=[spec] * 2,
        out_shape=[jax.ShapeDtypeStruct(up.shape, jnp.float32)] * 2,
        compiler_params=pltpu.CompilerParams(vmem_limit_bytes=VMEM),
        cost_estimate=LIGHT,
        name=name,
    )(up, down, recv_p, recv_m, *after)


def own_kernel(own, p1, m1, p2, m2, *refs):
    outs = refs[-4:]
    outs[0][0] = own[0, 0] + (p2[0, 0] + m1[0, 0])
    outs[1][0] = own[1, 0] + (p2[1, 0] + m1[1, 0])
    outs[2][0] = own[2, 0] + (m2[0, 0] + p1[0, 0])
    outs[3][0] = own[3, 0] + (m2[1, 0] + p1[1, 0])


def add_own(own, p1, m1, p2, m2, at, total, into, name):
    count, rows, cols = own.shape[1:]

    def spec(lead, first):
        return pl.BlockSpec((lead, 1, rows, cols), lambda g: (first, g, 0, 0))

    return pl.pallas_call(
        own_kernel,
        grid=(count,),
        in_specs=[spec(4, 0), spec(2, 1), spec(2, 1), spec(2, 0), spec(2, 0)]
        + [pl.BlockSpec(memory_space=pl.ANY)] * len(into),
        out_specs=[pl.BlockSpec((1, rows, cols), lambda g: (at + g, 0, 0))] * 4,
        out_shape=[jax.ShapeDtypeStruct((total, rows, cols), jnp.float32)] * 4,
        input_output_aliases={5 + i: i for i in range(len(into))},
        compiler_params=pltpu.CompilerParams(vmem_limit_bytes=VMEM),
        cost_estimate=LIGHT,
        name=name,
    )(own, p1, m1, p2, m2, *into)


def finish_kernel(order, sizes, origin, *refs):
    out = refs[-1]
    rows, _, cols = out.shape
    row = origin[0] + lax.broadcasted_iota(jnp.int32, (rows, cols), 0)
    for i, irreps in enumerate(order):
        parts = refs[4 * i : 4 * i + 4]
        for at, g in enumerate(irreps):
            total = (parts[0][at] + parts[1][at]) + (parts[2][at] + parts[3][at])
            out[:, g, :] = jnp.where(row < sizes[g], total, 0.0)


def finish(order, parts, row_sizes, origin, shape):
    rows, irreps, cols = shape
    flat = [p for four in parts for p in four]
    return pl.pallas_call(
        functools.partial(finish_kernel, order),
        grid_spec=pltpu.PrefetchScalarGridSpec(
            num_scalar_prefetch=2,
            grid=(cols // WIDTH,),
            in_specs=[pl.BlockSpec((p.shape[0], rows, WIDTH), lambda c, *_: (0, 0, c)) for p in flat],
            out_specs=pl.BlockSpec((rows, irreps, WIDTH), lambda c, *_: (0, 0, c)),
        ),
        out_shape=jax.ShapeDtypeStruct(shape, jnp.float32),
        compiler_params=pltpu.CompilerParams(vmem_limit_bytes=VMEM),
        cost_estimate=LIGHT,
        name="finish",
    )(row_sizes, origin, *flat)


GROUPS = ((0, 2, 2), (4, 2, 2))


def exchange(amplitudes, first, count, depth):
    rows, _, pairs = amplitudes.shape
    parts = pairs // depth
    mine = amplitudes[:, first : first + count].reshape(rows, count, parts, depth)
    mine = jnp.transpose(mine, (2, 0, 1, 3)).reshape(parts, rows * count, depth)
    mine = lax.all_to_all(mine, "ob", split_axis=0, concat_axis=0, tiled=True)
    return jnp.transpose(mine.reshape(parts * rows, count, depth), (1, 0, 2))


def contract(first_mine, amplitudes, ovov, row_sizes, pair_sizes):
    ob = lax.axis_index("ob")
    vb = lax.axis_index("vb")
    local_rows, irreps, _ = amplitudes.shape
    depth, cols = ovov.shape[1:]
    out_rows = local_rows * lax.axis_size("vb")
    blocks = lax.dynamic_slice(jnp.asarray(BLOCKS), (vb, ob, 0), (1, 1, 32)).reshape(32)
    origin = jnp.stack([ob * depth, vb * cols]).astype(jnp.int32)

    hops_of = {"x": (X_HOPS, Y_HOPS), "y": (Y_HOPS, X_HOPS)}
    order = {axis: [] for axis in hops_of}
    sums = {axis: [] for axis in hops_of}
    gathered = []
    for t, (first, nx, ny) in enumerate(GROUPS):
        mine = exchange(amplitudes, first, nx + ny, depth) if t else first_mine
        order["x"] += range(first, first + nx)
        order["y"] += range(first + nx, first + nx + ny)
        gathered.append(lax.all_gather(mine, "vb", axis=0).reshape(-1, nx + ny, 2, out_rows, depth))

    after, behind = [], []
    for t, (first, nx, ny) in enumerate(GROUPS):
        leads = {"send": (4, 4), "rest": (2, 2, 4)}
        args = (gathered[t], ovov, first, nx, ny)
        send = product(*args, 0, leads["send"], blocks, pair_sizes, origin, after, "send")
        recv = {
            axis: (lax.ppermute(send[axis][0], BOTH, here[1]), lax.ppermute(send[axis][1], BOTH, here[-1]))
            for axis, (here, _) in hops_of.items()
        }
        rest = product(*args, 1, leads["rest"], blocks, pair_sizes, origin, [*send["y"], *behind], "rest")
        after, behind = [], []
        for axis, (here, _) in hops_of.items():
            up, down, own = rest[axis]
            added = add_far(up, down, *recv[axis], [], f"{axis}_add")
            after += added
            handed = lax.ppermute(added[0], BOTH, here[1]), lax.ppermute(added[1], BOTH, here[-1])
            behind += handed
            sums[axis].append((own, *recv[axis], *handed))

    parts = []
    for axis, (_, there) in hops_of.items():
        four, at = [], 0
        for group in sums[axis]:
            four = add_own(*group, at, len(order[axis]), four, f"{axis}_own")
            at += group[0].shape[1]
        parts.append([four[0]] + [lax.ppermute(four[k], BOTH, there[d]) for k, d in ((1, 1), (2, 2), (3, -1))])
    origin = jnp.stack([ob * out_rows, vb * cols]).astype(jnp.int32)
    return finish([order[axis] for axis in hops_of], parts, row_sizes, origin, (out_rows, irreps, cols))


def local(amplitudes, ovov, row_sizes, pair_sizes):
    local_rows, irreps, _ = amplitudes.shape
    depth, cols = ovov.shape[1:]
    first, nx, ny = GROUPS[0]
    mine = exchange(amplitudes, first, nx + ny, depth)
    nothing = jnp.zeros((local_rows * lax.axis_size("vb"), irreps, cols), jnp.float32)
    return lax.cond(
        jnp.max(row_sizes) > 0,
        contract,
        lambda *_: nothing,
        mine, amplitudes, ovov, row_sizes, pair_sizes,
    )


def solution(mesh):
    placed = (P(("vb", "ob"), None, None), P(None, "ob", "vb"), P(), P())
    return jax.shard_map(
        local, mesh=mesh, in_specs=placed, out_specs=P("ob", None, "vb"), check_vma=False
    )
```

time: 234 us -> 248 us (1.060)
  starting transfers between devices: 35.5 us -> 57.4 us
  blocking collectives: 33.4 us -> 14.6 us
  waiting for transfers between devices: 79 us -> 84.5 us
  Pallas kernels: 63.4 us -> 67.9 us
    all_to_all x2 -> x1, blocking collectives: 33.4 us -> 14.6 us  [exchange(): mine = lax.all_to_all(mine, 'ob', split_axis=0, concat_axis=0, tiled=True)]
    ppermute x22, starting transfers between devices: 35.4 us -> 50 us  [the longest x6 24.7 us: contract(): lax.ppermute(four[k], BOTH, there[d])]
    all_gather x2, waiting for transfers between devices: 29.7 us -> 17.1 us  [contract(): lax.all_gather(mine, 'vb', axis=0).reshape(-1, nx + ny, 2, out_rows, depth)]
    all_to_all x0 -> x1, waiting for transfers between devices: none -> 10.6 us  [exchange(): mine = lax.all_to_all(mine, 'ob', split_axis=0, concat_axis=0, tiled=True)]
    ppermute x22, waiting for transfers between devices: 49.2 us -> 56.7 us  [the longest x4 31.1 us: contract(): lax.ppermute(added[1], BOTH, here[-1])]
    all_to_all x0 -> x1, starting transfers between devices: none -> 7.25 us  [exchange(): mine = lax.all_to_all(mine, 'ob', split_axis=0, concat_axis=0, tiled=True)]
    pallas_call x16 -> x12, Pallas kernels: 58.4 us -> 63 us  [the longest x4 41.4 us: product(): pl.pallas_call(functools.partial(product_kernel, first, x_count, leads),...]
  transfers between devices with their start and end apart: 24 -> 25, of which waited for: 14 -> 7; matrix products, arithmetic and copies ran while one was open for 2% -> 2% of each run, Pallas kernels for 25% -> 17%
where the time goes in v6:
time: 248 us; the launch traced here: 247 us
  waiting for transfers between devices  84.5 us (34%)
  Pallas kernels  67.9 us (27%)
  starting transfers between devices  57.4 us (23%)
  blocking collectives  14.6 us (6%)
  between operations  14.1 us (6%)
  local copies, waits for them, and re-layouts  6.23 us (3%)
    pallas_call x4, Pallas kernels, product(): pl.pallas_call(functools.partial(product_kernel, first, x_count, leads),...  41.4 us
    ppermute x4, waiting for transfers between devices, contract(): lax.ppermute(added[1], BOTH, here[-1])  31.1 us
    ppermute x6, starting transfers between devices, contract(): lax.ppermute(four[k], BOTH, there[d])  24.7 us
    all_gather x2, waiting for transfers between devices, contract(): lax.all_gather(mine, 'vb', axis=0).reshape(-1, nx + ny, 2, out_rows, depth)  17.1 us
    all_to_all x1, blocking collectives, exchange(): mine = lax.all_to_all(mine, 'ob', split_axis=0, concat_axis=0, tiled=True)  14.6 us
    pallas_call x4, Pallas kernels, add_own(): pl.pallas_call(own_kernel, grid=(count,), in_specs=[spec(4, 0), spec(2, 1...  11.5 us
    ppermute x4, waiting for transfers between devices, contract(): lax.ppermute(send[axis][0], BOTH, here[1])  11.5 us
    all_to_all x1, waiting for transfers between devices, exchange(): mine = lax.all_to_all(mine, 'ob', split_axis=0, concat_axis=0, tiled=True)  10.6 us
  transfers between devices with their start and end apart: 25, of which 7 were waited for; matrix products, arithmetic and copies ran while one was open for 2% of the time, Pallas kernels for 17%

profile of v6, /device:TPU:0, one launch (start us, length us, event | category | flops | bytes accessed | tf_op | source)
XLA Modules:
  0.0 246.8 jit_solution(13790391667563682878)
XLA Ops:
  6.5 1.1 slice-done
  7.9 1.0 copy.29
  8.9 7.2 %all-to-all-start.1 = ((f32[16,24,384]{2,1,0:T(8,128)}), f32[16,24,384]{2,1,0:T(8,128)S(1)}, u32[]{:S(2)}, u32[]{:S(2)}) async-start(f32[16,24,384]{2,1,0:T(8,128)} %copy.29), calls=%async_computation.1 | async-start | bytes 1179648 | tf_op jit(solution)/shard_map/all_to_all | solution.py:216
  16.2 0.7 reduce_max.9
  17.5 10.6 %all-to-all-done.1 = f32[16,24,384]{2,1,0:T(8,128)S(1)} async-done(((f32[16,24,384]{2,1,0:T(8,128)}), f32[16,24,384]{2,1,0:T(8,128)S(1)}, u32[]{:S(2)}, u32[]{:S(2)}) %all-to-all-start.1) | async-done | bytes 589856 | tf_op jit(solution)/shard_map/all_to_all | solution.py:216
  28.3 211.7 %conditional.1 = (f32[48,8,768]{2,1,0:T(8,128)}) conditional(s32[]{:T(128)} %convert_element_type.3, () %tuple.11, ((), f32[6,8,6144]{2,1,0:T(8,128)S(1)}, f32[4,96,384]{2,0,1:T(4,128)S(1)}, s32[8]{0:T(128)S(1)}, f32[8,384,768]{2,1,0:T(8,128)}, /*index=5*/s32[8]{0:T(128)S(1)}) %tuple.28), branch_computations={%region_1.0_spmd, %region_2.0_spmd} | conditional | flops 18 | bytes 117966312 | solution.py:275
  28.3 0.9 copy.30
  29.4 0.3 reshape.19
  29.9 14.6 %all_to_all.9 = f32[16,24,384]{2,1,0:T(8,128)S(1)} all-to-all(f32[16,24,384]{2,1,0:T(8,128)S(1)} %copy.27), channel_id=1, replica_groups=mesh['vb'=8,'ob'=16] {'ob'}, dimensions={0} | all-to-all | bytes 1179648 | tf_op jit(solution)/shard_map/cond/branch_1_fun/all_to_all | solution.py:216
  44.7 0.9 copy.28
  45.6 0.6 pad_add_fusion.1.origin
  46.2 1.2 dynamic-slice_bitcast_fusion.blocks
  47.4 17.1 %all-gather.7.cloned.1.call-done = f32[32,96,384]{2,1,0:T(8,128)} async-done(((f32[4,96,384]{2,1,0:T(8,128)}), f32[32,96,384]{2,1,0:T(8,128)}) %all-gather.7.cloned.1.call-update) | async-done | bytes 4718608 | tf_op jit(solution)/shard_map/cond/branch_1_fun/all_gather | solution.py:237
  64.5 10.1 %send.2 = (f32[4,2,48,768]{3,2,1,0:T(8,128)}, f32[4,2,48,768]{3,2,1,0:T(8,128)}, f32[4,2,48,768]{3,2,1,0:T(8,128)}, f32[4,2,48,768]{3,2,1,0:T(8,128)}) custom-call(s32[32]{0:T(128)} %dynamic-slice_bitcast_fusion.blocks, s32[8]{0:T(128)S(1)} %get-tuple-element.75.sizes, s32[2]{0:T(128)} %pad_add_fusion.1.origin, f32[8,4,2,48,384]{4,3,2,1,0:T(8,128)} %bitcast.31, ...), custom_call_target="tpu_custom_call" | custom-call | tf_op jit(solution)/shard_map/cond/branch_1_fun/send/pallas_call | solution.py:109
  74.6 1.5 collective-permute-start
  76.1 1.8 collective-permute-start.1
  77.9 1.5 collective-permute-start.2
  79.4 1.8 collective-permute-start.3
  81.1 10.7 %rest.2 = (f32[2,2,48,768]{3,2,1,0:T(8,128)}, f32[2,2,48,768]{3,2,1,0:T(8,128)}, f32[4,2,48,768]{3,2,1,0:T(8,128)}, f32[2,2,48,768]{3,2,1,0:T(8,128)}, f32[2,2,4...) custom-call(s32[32]{0:T(128)} %dynamic-slice_bitcast_fusion.blocks, s32[8]{0:T(128)S(1)} %get-tuple-element.75.sizes, ...), custom_call_target="tpu_custom_call" | custom-call | tf_op jit(solution)/shard_map/cond/branch_1_fun/rest/pallas_call | solution.py:109
  91.8 11.5 %collective-permute-done.recv_p.p1 = f32[4,2,48,768]{3,2,1,0:T(8,128)} collective-permute-done((f32[4,2,48,768]{3,2,1,0:T(8,128)}, f32[4,2,48,768]{3,2,1,0:T(8,128)}, u32[]{:S(2)}, u32[]{:S(2)}) %collective-permute-start) | collective-permute-done | bytes 1179680 | tf_op jit(solution)/shard_map/cond/branch_1_fun/ppermute | solution.py:245
  103.3 2.5 %x_add.2 = (f32[2,2,48,768]{3,2,1,0:T(8,128)}, f32[2,2,48,768]{3,2,1,0:T(8,128)}) custom-call(f32[2,2,48,768]{3,2,1,0:T(8,128)} %get-tuple-element.28.up, f32[2,2,48,768]{3,2,1,0:T(8,128)} %get-tuple-element.29.down, f32[4,2,48,768]{3,2,1,0:T(8,128)} %collective-permute-done.recv_p.p1, f32[4,2,48,768]{3,2,1,0:T(8,128)} %collective-permute-done.1.recv_m.m1), custom_call_target="tpu_custom_call" | custom-call | tf_op jit(solution)/shard_map/cond/branch_1_fun/x_add/pallas_call | solution.py:139
  105.8 1.6 collective-permute-start.4
  107.3 2.2 collective-permute-start.5
  109.5 2.6 %y_add.2 = (f32[2,2,48,768]{3,2,1,0:T(8,128)}, f32[2,2,48,768]{3,2,1,0:T(8,128)}) custom-call(f32[2,2,48,768]{3,2,1,0:T(8,128)} %get-tuple-element.34.up, f32[2,2,48,768]{3,2,1,0:T(8,128)} %get-tuple-element.35.down, f32[4,2,48,768]{3,2,1,0:T(8,128)} %collective-permute-done.2.recv_p.p1, f32[4,2,48,768]{3,2,1,0:T(8,128)} %collective-permute-done.3.recv_m.m1), custom_call_target="tpu_custom_call" | custom-call | tf_op jit(solution)/shard_map/cond/branch_1_fun/y_add/pallas_call | solution.py:139
  112.1 1.5 collective-permute-start.6
  113.6 10.0 %send.3 = (f32[4,2,48,768]{3,2,1,0:T(8,128)}, f32[4,2,48,768]{3,2,1,0:T(8,128)}, f32[4,2,48,768]{3,2,1,0:T(8,128)}, f32[4,2,48,768]{3,2,1,0:T(8,128)}) custom-call(s32[32]{0:T(128)} %dynamic-slice_bitcast_fusion.blocks, s32[8]{0:T(128)S(1)} %get-tuple-element.75.sizes, s32[2]{0:T(128)} %pad_add_fusion.1.origin, f32[8,4,2,48,384]{4,3,2,1,0:T(8,128)} %bitcast.15, ...), custom_call_target="tpu_custom_call" | custom-call | tf_op jit(solution)/shard_map/cond/branch_1_fun/send/pallas_call | solution.py:109
  123.7 3.2 %collective-permute-start.9 = (f32[4,2,48,768]{3,2,1,0:T(8,128)}, f32[4,2,48,768]{3,2,1,0:T(8,128)}, u32[]{:S(2)}, u32[]{:S(2)}) collective-permute-start(f32[4,2,48,768]{3,2,1,0:T(8,128)} %get-tuple-element.42), channel_id=1, source_target_pairs={{0,12},{1,13},{2,14},{3,15},{4,0},{5,1},{6,2},{7,3},{8,4},{9,5},{1... | collective-permute-start | bytes 3538952 | tf_op jit(solution)/shard_map/cond/branch_1_fun/ppermute | solution.py:245
  126.9 1.5 collective-permute-start.15
  128.4 1.7 collective-permute-start.16
  130.2 0.5 collective-permute-start.7
  130.7 30.1 %collective-permute-done.7.refs_14_.m2 = f32[2,2,48,768]{3,2,1,0:T(8,128)} collective-permute-done((f32[2,2,48,768]{3,2,1,0:T(8,128)}, f32[2,2,48,768]{3,2,1,0:T(8,128)}, u32[]{:S(2)}, u32[]{:S(2)}) %collective-permute-start.7) | collective-permute-done | bytes 589856 | tf_op jit(solution)/shard_map/cond/branch_1_fun/ppermute | solution.py:254
  160.8 10.7 %rest.3 = (f32[2,2,48,768]{3,2,1,0:T(8,128)}, f32[2,2,48,768]{3,2,1,0:T(8,128)}, f32[4,2,48,768]{3,2,1,0:T(8,128)}, f32[2,2,48,768]{3,2,1,0:T(8,128)}, f32[2,2,4...) custom-call(s32[32]{0:T(128)} %dynamic-slice_bitcast_fusion.blocks, s32[8]{0:T(128)S(1)} %get-tuple-element.75.sizes, ...), custom_call_target="tpu_custom_call" | custom-call | tf_op jit(solution)/shard_map/cond/branch_1_fun/rest/pallas_call | solution.py:109
  171.6 2.5 %x_add.3 = (f32[2,2,48,768]{3,2,1,0:T(8,128)}, f32[2,2,48,768]{3,2,1,0:T(8,128)}) custom-call(f32[2,2,48,768]{3,2,1,0:T(8,128)} %get-tuple-element.43.up, f32[2,2,48,768]{3,2,1,0:T(8,128)} %get-tuple-element.44.down, f32[4,2,48,768]{3,2,1,0:T(8,128)} %collective-permute-done.8.recv_p.p1, f32[4,2,48,768]{3,2,1,0:T(8,128)} %collective-permute-done.9.recv_m.m1), custom_call_target="tpu_custom_call" | custom-call | tf_op jit(solution)/shard_map/cond/branch_1_fun/x_add/pallas_call | solution.py:139
  174.0 3.2 %collective-permute-start.11 = (f32[2,2,48,768]{3,2,1,0:T(8,128)}, f32[2,2,48,768]{3,2,1,0:T(8,128)}, u32[]{:S(2)}, u32[]{:S(2)}) collective-permute-start(f32[2,2,48,768]{3,2,1,0:T(8,128)} %get-tuple-element.46), channel_id=1, source_target_pairs={{0,12},{1,13},{2,14},{3,15},{4,0},{5,1},{6,2},{7,3},{8,4},{9,5},{1... | collective-permute-start | bytes 1769480 | tf_op jit(solution)/shard_map/cond/branch_1_fun/ppermute | solution.py:254
  177.3 2.5 %y_add.3 = (f32[2,2,48,768]{3,2,1,0:T(8,128)}, f32[2,2,48,768]{3,2,1,0:T(8,128)}) custom-call(f32[2,2,48,768]{3,2,1,0:T(8,128)} %get-tuple-element.57.up, f32[2,2,48,768]{3,2,1,0:T(8,128)} %get-tuple-element.58.down, f32[4,2,48,768]{3,2,1,0:T(8,128)} %collective-permute-done.15.recv_p.p1, f32[4,2,48,768]{3,2,1,0:T(8,128)} %collective-permute-done.16.recv_m.m1), custom_call_target="tpu_custom_call" | custom-call | tf_op jit(solution)/shard_map/cond/branch_1_fun/y_add/pallas_call | solution.py:139
  179.8 3.2 %collective-permute-start.18 = (f32[2,2,48,768]{3,2,1,0:T(8,128)}, f32[2,2,48,768]{3,2,1,0:T(8,128)}, u32[]{:S(2)}, u32[]{:S(2)}) collective-permute-start(f32[2,2,48,768]{3,2,1,0:T(8,128)} %get-tuple-element.60), channel_id=1, source_target_pairs={{0,3},{1,0},{2,1},{3,2},{4,7},{5,4},{6,5},{7,6},{8,11},{9,8},{10,9... | collective-permute-start | bytes 1769480 | tf_op jit(solution)/shard_map/cond/branch_1_fun/ppermute | solution.py:254
  183.0 2.9 %x_own.2 = (f32[4,48,768]{2,1,0:T(8,128)}, f32[4,48,768]{2,1,0:T(8,128)}, f32[4,48,768]{2,1,0:T(8,128)}, f32[4,48,768]{2,1,0:T(8,128)}) custom-call(f32[4,2,48,768]{3,2,1,0:T(8,128)} %get-tuple-element.47.own, f32[4,2,48,768]{3,2,1,0:T(8,128)} %collective-permute-done.recv_p.p1, f32[4,2,48,768]{3,2,1,0:T(8,128)} %collective-permute-done.1.recv_m.m1, ...), custom_call_target="tpu_custom_call" | custom-call | tf_op jit(solution)/shard_map/cond/branch_1_fun/x_own/pallas_call | solution.py:165
  185.9 3.6 %collective-permute-done.10.p2 = f32[2,2,48,768]{3,2,1,0:T(8,128)S(1)} collective-permute-done((f32[2,2,48,768]{3,2,1,0:T(8,128)}, f32[2,2,48,768]{3,2,1,0:T(8,128)S(1)}, u32[]{:S(2)}, u32[]{:S(2)}) %collective-permute-start.10) | collective-permute-done | bytes 589856 | tf_op jit(solution)/shard_map/cond/branch_1_fun/ppermute | solution.py:254
  189.5 1.0 collective-permute-done.11.m2
  190.5 2.9 %x_own.3 = (f32[4,48,768]{2,1,0:T(8,128)}, f32[4,48,768]{2,1,0:T(8,128)}, f32[4,48,768]{2,1,0:T(8,128)}, f32[4,48,768]{2,1,0:T(8,128)}) custom-call(f32[4,2,48,768]{3,2,1,0:T(8,128)} %get-tuple-element.40.own, f32[4,2,48,768]{3,2,1,0:T(8,128)} %collective-permute-done.8.recv_p.p1, ...), custom_call_target="tpu_custom_call", output_to_operand_aliasing={{0}: (5, {}), {1}: (6, {}), {2}: (7, {}), {3}: (8, {})} | custom-call | tf_op jit(solution)/shard_map/cond/branch_1_fun/x_own/pallas_call | solution.py:165
  193.7 2.8 %y_own.2 = (f32[4,48,768]{2,1,0:T(8,128)}, f32[4,48,768]{2,1,0:T(8,128)}, f32[4,48,768]{2,1,0:T(8,128)}, f32[4,48,768]{2,1,0:T(8,128)}) custom-call(f32[4,2,48,768]{3,2,1,0:T(8,128)} %get-tuple-element.61.own, f32[4,2,48,768]{3,2,1,0:T(8,128)} %collective-permute-done.2.recv_p.p1, f32[4,2,48,768]{3,2,1,0:T(8,128)} %collective-permute-done.3.recv_m.m1, ...), custom_call_target="tpu_custom_call" | custom-call | tf_op jit(solution)/shard_map/cond/branch_1_fun/y_own/pallas_call | solution.py:165
  196.5 4.5 %collective-permute-start.13 = (f32[4,48,768]{2,1,0:T(8,128)}, f32[4,48,768]{2,1,0:T(8,128)}, u32[]{:S(2)}, u32[]{:S(2)}) collective-permute-start(f32[4,48,768]{2,1,0:T(8,128)} %get-tuple-element.54), channel_id=1, source_target_pairs={{0,2},{1,3},{2,0},{3,1},{4,6},{5,7},{6,4},{7,5},{8,10},{9,11},{10,... | collective-permute-start | bytes 1769480 | tf_op jit(solution)/shard_map/cond/branch_1_fun/ppermute | solution.py:264
  201.0 2.9 %y_own.3 = (f32[4,48,768]{2,1,0:T(8,128)}, f32[4,48,768]{2,1,0:T(8,128)}, f32[4,48,768]{2,1,0:T(8,128)}, f32[4,48,768]{2,1,0:T(8,128)}) custom-call(f32[4,2,48,768]{3,2,1,0:T(8,128)} %get-tuple-element.56.own, f32[4,2,48,768]{3,2,1,0:T(8,128)} %collective-permute-done.15.recv_p.p1, ...), custom_call_target="tpu_custom_call", output_to_operand_aliasing={{0}: (5, {}), {1}: (6, {}), {2}: (7, {}), {3}: (8, {})} | custom-call | tf_op jit(solution)/shard_map/cond/branch_1_fun/y_own/pallas_call | solution.py:165
  203.9 4.5 %collective-permute-start.20 = (f32[4,48,768]{2,1,0:T(8,128)}, f32[4,48,768]{2,1,0:T(8,128)}, u32[]{:S(2)}, u32[]{:S(2)}) collective-permute-start(f32[4,48,768]{2,1,0:T(8,128)} %get-tuple-element.68), channel_id=1, source_target_pairs={{0,8},{1,9},{2,10},{3,11},{4,12},{5,13},{6,14},{7,15},{8,0},{9,1},... | collective-permute-start | bytes 1769480 | tf_op jit(solution)/shard_map/cond/branch_1_fun/ppermute | solution.py:264
  208.4 15.4 %collective-permute-start.21 = (f32[4,48,768]{2,1,0:T(8,128)}, f32[4,48,768]{2,1,0:T(8,128)}, u32[]{:S(2)}, u32[]{:S(2)}) collective-permute-start(f32[4,48,768]{2,1,0:T(8,128)} %get-tuple-element.69), channel_id=1, source_target_pairs={{0,12},{1,13},{2,14},{3,15},{4,0},{5,1},{6,2},{7,3},{8,4},{9,5},{1... | collective-permute-start | bytes 1769480 | tf_op jit(solution)/shard_map/cond/branch_1_fun/ppermute | solution.py:264
  223.9 0.7 pad_add_fusion.origin
  224.5 10.5 %collective-permute-done.20.refs_6_ = f32[4,48,768]{2,1,0:T(8,128)} collective-permute-done((f32[4,48,768]{2,1,0:T(8,128)}, f32[4,48,768]{2,1,0:T(8,128)}, u32[]{:S(2)}, u32[]{:S(2)}) %collective-permute-start.20) | collective-permute-done | bytes 589856 | tf_op jit(solution)/shard_map/cond/branch_1_fun/ppermute | solution.py:264
  235.0 5.0 %finish.1 = f32[48,8,768]{2,1,0:T(8,128)} custom-call(s32[8]{0:T(128)S(1)} %get-tuple-element.20.sizes, s32[2]{0:T(128)} %pad_add_fusion.origin, f32[4,48,768]{2,1,0:T(8,128)} %get-tuple-element.52.refs_0_, f32[4,48,768]{2,1,0:T(8,128)} %copy-done.2, f32[4,48,768]{2,1,0:T(8,128)} %collective-permute-done.13.refs_2_, ...), custom_call_target="tpu_custom_call" | custom-call | tf_op jit(solution)/shard_map/cond/branch_1_fun/finish/pallas_call | solution.py:193
  (46 shorter events, 1.5 us)
Async XLA Ops:
  6.5 1.1 slice-start
  7.9 8.3 %copy-start.5 = (s32[8]{0:T(128)S(1)}, s32[8]{0:T(128)}, u32[]{:S(2)}) copy-start(s32[8]{0:T(128)} %param.9) | copy-start | bytes 100
  8.9 19.3 %copy-start = (f32[6,8,6144]{2,1,0:T(8,128)S(1)}, f32[6,8,6144]{2,1,0:T(8,128)}, u32[]{:S(2)}) copy-start(f32[6,8,6144]{2,1,0:T(8,128)} %param.7) | copy-start | bytes 3538948
  8.9 19.3 %copy-start.4 = (s32[8]{0:T(128)S(1)}, s32[8]{0:T(128)}, u32[]{:S(2)}) copy-start(s32[8]{0:T(128)} %param.10) | copy-start | bytes 100
  8.9 19.2 %all-to-all-start.1 = ((f32[16,24,384]{2,1,0:T(8,128)}), f32[16,24,384]{2,1,0:T(8,128)S(1)}, u32[]{:S(2)}, u32[]{:S(2)}) async-start(f32[16,24,384]{2,1,0:T(8,128)} %copy.29), calls=%async_computation.1 | async-start | bytes 1179648 | tf_op jit(solution)/shard_map/all_to_all | solution.py:216
  28.3 36.2 %all-gather.7.cloned.1.call-start = ((), (), s32[]{:S(2)}) async-start(), calls=%async_computation.3 | async-start | bytes 5308416 | tf_op jit(solution)/shard_map/cond/branch_1_fun/all_gather | solution.py:237
  29.2 84.4 %all-gather.5.cloned.1.call-start = ((), (), s32[]{:S(2)}) async-start(), calls=%async_computation.2 | async-start | bytes 5308416 | tf_op jit(solution)/shard_map/cond/branch_1_fun/all_gather | solution.py:237
  74.6 28.7 %collective-permute-start = (f32[4,2,48,768]{3,2,1,0:T(8,128)}, f32[4,2,48,768]{3,2,1,0:T(8,128)}, u32[]{:S(2)}, u32[]{:S(2)}) collective-permute-start(f32[4,2,48,768]{3,2,1,0:T(8,128)} %get-tuple-element.30), channel_id=1, source_target_pairs={{0,4},{1,5},{2,6},{3,7},{4,8},{5,9},{6,10},{7,11},{8,12},{9,13},{1... | collective-permute-start | bytes 3538952 | tf_op jit(solution)/shard_map/cond/branch_1_fun/ppermute | solution.py:245
  76.1 27.2 %collective-permute-start.1 = (f32[4,2,48,768]{3,2,1,0:T(8,128)}, f32[4,2,48,768]{3,2,1,0:T(8,128)}, u32[]{:S(2)}, u32[]{:S(2)}) collective-permute-start(f32[4,2,48,768]{3,2,1,0:T(8,128)} %get-tuple-element.31), channel_id=1, source_target_pairs={{0,12},{1,13},{2,14},{3,15},{4,0},{5,1},{6,2},{7,3},{8,4},{9,5},{1... | collective-permute-start | bytes 3538952 | tf_op jit(solution)/shard_map/cond/branch_1_fun/ppermute | solution.py:245
  77.9 31.6 %collective-permute-start.2 = (f32[4,2,48,768]{3,2,1,0:T(8,128)}, f32[4,2,48,768]{3,2,1,0:T(8,128)}, u32[]{:S(2)}, u32[]{:S(2)}) collective-permute-start(f32[4,2,48,768]{3,2,1,0:T(8,128)} %get-tuple-element.26.refs_9_), channel_id=1, source_target_pairs={{0,1},{1,2},{2,3},{3,0},{4,5},{5,6},{6,7},{7,4},{8,9},{9,10},{10,1... | collective-permute-start | bytes 3538952 | tf_op jit(solution)/shard_map/cond/branch_1_fun/ppermute | solution.py:245
  79.4 30.2 %collective-permute-start.3 = (f32[4,2,48,768]{3,2,1,0:T(8,128)}, f32[4,2,48,768]{3,2,1,0:T(8,128)}, u32[]{:S(2)}, u32[]{:S(2)}) collective-permute-start(f32[4,2,48,768]{3,2,1,0:T(8,128)} %get-tuple-element.27.refs_10_), channel_id=1, source_target_pairs={{0,3},{1,0},{2,1},{3,2},{4,7},{5,4},{6,5},{7,6},{8,11},{9,8},{10,9... | collective-permute-start | bytes 3538952 | tf_op jit(solution)/shard_map/cond/branch_1_fun/ppermute | solution.py:245
  105.8 21.2 %collective-permute-start.4 = (f32[2,2,48,768]{3,2,1,0:T(8,128)}, f32[2,2,48,768]{3,2,1,0:T(8,128)}, u32[]{:S(2)}, u32[]{:S(2)}) collective-permute-start(f32[2,2,48,768]{3,2,1,0:T(8,128)} %get-tuple-element.32.refs_9_), channel_id=1, source_target_pairs={{0,4},{1,5},{2,6},{3,7},{4,8},{5,9},{6,10},{7,11},{8,12},{9,13},{1... | collective-permute-start | bytes 1769480 | tf_op jit(solution)/shard_map/cond/branch_1_fun/ppermute | solution.py:254
  107.3 21.1 %collective-permute-start.5 = (f32[2,2,48,768]{3,2,1,0:T(8,128)}, f32[2,2,48,768]{3,2,1,0:T(8,128)}, u32[]{:S(2)}, u32[]{:S(2)}) collective-permute-start(f32[2,2,48,768]{3,2,1,0:T(8,128)} %get-tuple-element.33.refs_10_), channel_id=1, source_target_pairs={{0,12},{1,13},{2,14},{3,15},{4,0},{5,1},{6,2},{7,3},{8,4},{9,5},{1... | collective-permute-start | bytes 1769480 | tf_op jit(solution)/shard_map/cond/branch_1_fun/ppermute | solution.py:254
  112.1 18.1 %collective-permute-start.6 = (f32[2,2,48,768]{3,2,1,0:T(8,128)}, f32[2,2,48,768]{3,2,1,0:T(8,128)S(1)}, u32[]{:S(2)}, u32[]{:S(2)}) collective-permute-start(f32[2,2,48,768]{3,2,1,0:T(8,128)} %get-tuple-element.36.refs_11_), channel_id=1, source_target_pairs={{0,1},{1,2},{2,3},{3,0},{4,5},{5,6},{6,7},{7,4},{8,9},{9,10},{10,1... | collective-permute-start | bytes 1769480 | tf_op jit(solution)/shard_map/cond/branch_1_fun/ppermute | solution.py:254
  123.6 47.9 %collective-permute-start.8 = (f32[4,2,48,768]{3,2,1,0:T(8,128)}, f32[4,2,48,768]{3,2,1,0:T(8,128)}, u32[]{:S(2)}, u32[]{:S(2)}) collective-permute-start(f32[4,2,48,768]{3,2,1,0:T(8,128)} %get-tuple-element.41), channel_id=1, source_target_pairs={{0,4},{1,5},{2,6},{3,7},{4,8},{5,9},{6,10},{7,11},{8,12},{9,13},{1... | collective-permute-start | bytes 3538952 | tf_op jit(solution)/shard_map/cond/branch_1_fun/ppermute | solution.py:245
  123.7 47.8 %collective-permute-start.9 = (f32[4,2,48,768]{3,2,1,0:T(8,128)}, f32[4,2,48,768]{3,2,1,0:T(8,128)}, u32[]{:S(2)}, u32[]{:S(2)}) collective-permute-start(f32[4,2,48,768]{3,2,1,0:T(8,128)} %get-tuple-element.42), channel_id=1, source_target_pairs={{0,12},{1,13},{2,14},{3,15},{4,0},{5,1},{6,2},{7,3},{8,4},{9,5},{1... | collective-permute-start | bytes 3538952 | tf_op jit(solution)/shard_map/cond/branch_1_fun/ppermute | solution.py:245
  126.9 50.4 %collective-permute-start.15 = (f32[4,2,48,768]{3,2,1,0:T(8,128)}, f32[4,2,48,768]{3,2,1,0:T(8,128)}, u32[]{:S(2)}, u32[]{:S(2)}) collective-permute-start(f32[4,2,48,768]{3,2,1,0:T(8,128)} %get-tuple-element.38.refs_9_), channel_id=1, source_target_pairs={{0,1},{1,2},{2,3},{3,0},{4,5},{5,6},{6,7},{7,4},{8,9},{9,10},{10,1... | collective-permute-start | bytes 3538952 | tf_op jit(solution)/shard_map/cond/branch_1_fun/ppermute | solution.py:245
  128.4 48.9 %collective-permute-start.16 = (f32[4,2,48,768]{3,2,1,0:T(8,128)}, f32[4,2,48,768]{3,2,1,0:T(8,128)}, u32[]{:S(2)}, u32[]{:S(2)}) collective-permute-start(f32[4,2,48,768]{3,2,1,0:T(8,128)} %get-tuple-element.39.refs_10_), channel_id=1, source_target_pairs={{0,3},{1,0},{2,1},{3,2},{4,7},{5,4},{6,5},{7,6},{8,11},{9,8},{10,9... | collective-permute-start | bytes 3538952 | tf_op jit(solution)/shard_map/cond/branch_1_fun/ppermute | solution.py:245
  130.2 30.7 %copy-start.1 = (f32[2,2,48,768]{3,2,1,0:T(8,128)}, f32[2,2,48,768]{3,2,1,0:T(8,128)S(1)}, u32[]{:S(2)}) copy-start(f32[2,2,48,768]{3,2,1,0:T(8,128)S(1)} %collective-permute-done.6.refs_13_.p2) | copy-start | bytes 1769476 | tf_op jit(solution)/shard_map/cond
  130.2 30.7 %collective-permute-start.7 = (f32[2,2,48,768]{3,2,1,0:T(8,128)}, f32[2,2,48,768]{3,2,1,0:T(8,128)}, u32[]{:S(2)}, u32[]{:S(2)}) collective-permute-start(f32[2,2,48,768]{3,2,1,0:T(8,128)} %get-tuple-element.37.refs_12_), channel_id=1, source_target_pairs={{0,3},{1,0},{2,1},{3,2},{4,7},{5,4},{6,5},{7,6},{8,11},{9,8},{10,9... | collective-permute-start | bytes 1769480 | tf_op jit(solution)/shard_map/cond/branch_1_fun/ppermute | solution.py:254
  174.0 15.4 %collective-permute-start.10 = (f32[2,2,48,768]{3,2,1,0:T(8,128)}, f32[2,2,48,768]{3,2,1,0:T(8,128)S(1)}, u32[]{:S(2)}, u32[]{:S(2)}) collective-permute-start(f32[2,2,48,768]{3,2,1,0:T(8,128)} %get-tuple-element.45), channel_id=1, source_target_pairs={{0,4},{1,5},{2,6},{3,7},{4,8},{5,9},{6,10},{7,11},{8,12},{9,13},{1... | collective-permute-start | bytes 1769480 | tf_op jit(solution)/shard_map/cond/branch_1_fun/ppermute | solution.py:254
  174.0 16.4 %collective-permute-start.11 = (f32[2,2,48,768]{3,2,1,0:T(8,128)}, f32[2,2,48,768]{3,2,1,0:T(8,128)}, u32[]{:S(2)}, u32[]{:S(2)}) collective-permute-start(f32[2,2,48,768]{3,2,1,0:T(8,128)} %get-tuple-element.46), channel_id=1, source_target_pairs={{0,12},{1,13},{2,14},{3,15},{4,0},{5,1},{6,2},{7,3},{8,4},{9,5},{1... | collective-permute-start | bytes 1769480 | tf_op jit(solution)/shard_map/cond/branch_1_fun/ppermute | solution.py:254
  179.8 21.2 %collective-permute-start.17 = (f32[2,2,48,768]{3,2,1,0:T(8,128)}, f32[2,2,48,768]{3,2,1,0:T(8,128)}, u32[]{:S(2)}, u32[]{:S(2)}) collective-permute-start(f32[2,2,48,768]{3,2,1,0:T(8,128)} %get-tuple-element.59), channel_id=1, source_target_pairs={{0,1},{1,2},{2,3},{3,0},{4,5},{5,6},{6,7},{7,4},{8,9},{9,10},{10,1... | collective-permute-start | bytes 1769480 | tf_op jit(solution)/shard_map/cond/branch_1_fun/ppermute | solution.py:254
  179.8 21.2 %collective-permute-start.18 = (f32[2,2,48,768]{3,2,1,0:T(8,128)}, f32[2,2,48,768]{3,2,1,0:T(8,128)}, u32[]{:S(2)}, u32[]{:S(2)}) collective-permute-start(f32[2,2,48,768]{3,2,1,0:T(8,128)} %get-tuple-element.60), channel_id=1, source_target_pairs={{0,3},{1,0},{2,1},{3,2},{4,7},{5,4},{6,5},{7,6},{8,11},{9,8},{10,9... | collective-permute-start | bytes 1769480 | tf_op jit(solution)/shard_map/cond/branch_1_fun/ppermute | solution.py:254
  189.5 1.0 copy-start.3
  193.4 15.0 %collective-permute-start.12 = (f32[4,48,768]{2,1,0:T(8,128)}, f32[4,48,768]{2,1,0:T(8,128)S(1)}, u32[]{:S(2)}, u32[]{:S(2)}) collective-permute-start(f32[4,48,768]{2,1,0:T(8,128)} %get-tuple-element.53), channel_id=1, source_target_pairs={{0,1},{1,2},{2,3},{3,0},{4,5},{5,6},{6,7},{7,4},{8,9},{9,10},{10,1... | collective-permute-start | bytes 1769480 | tf_op jit(solution)/shard_map/cond/branch_1_fun/ppermute | solution.py:264
  196.5 28.0 %collective-permute-start.13 = (f32[4,48,768]{2,1,0:T(8,128)}, f32[4,48,768]{2,1,0:T(8,128)}, u32[]{:S(2)}, u32[]{:S(2)}) collective-permute-start(f32[4,48,768]{2,1,0:T(8,128)} %get-tuple-element.54), channel_id=1, source_target_pairs={{0,2},{1,3},{2,0},{3,1},{4,6},{5,7},{6,4},{7,5},{8,10},{9,11},{10,... | collective-permute-start | bytes 1769480 | tf_op jit(solution)/shard_map/cond/branch_1_fun/ppermute | solution.py:264
  201.0 23.6 %collective-permute-start.14 = (f32[4,48,768]{2,1,0:T(8,128)}, f32[4,48,768]{2,1,0:T(8,128)}, u32[]{:S(2)}, u32[]{:S(2)}) collective-permute-start(f32[4,48,768]{2,1,0:T(8,128)} %get-tuple-element.55), channel_id=1, source_target_pairs={{0,3},{1,0},{2,1},{3,2},{4,7},{5,4},{6,5},{7,6},{8,11},{9,8},{10,9... | collective-permute-start | bytes 1769480 | tf_op jit(solution)/shard_map/cond/branch_1_fun/ppermute | solution.py:264
  203.9 20.7 %collective-permute-start.19 = (f32[4,48,768]{2,1,0:T(8,128)}, f32[4,48,768]{2,1,0:T(8,128)}, u32[]{:S(2)}, u32[]{:S(2)}) collective-permute-start(f32[4,48,768]{2,1,0:T(8,128)} %get-tuple-element.67), channel_id=1, source_target_pairs={{0,4},{1,5},{2,6},{3,7},{4,8},{5,9},{6,10},{7,11},{8,12},{9,13},{1... | collective-permute-start | bytes 1769480 | tf_op jit(solution)/shard_map/cond/branch_1_fun/ppermute | solution.py:264
  203.9 31.1 %collective-permute-start.20 = (f32[4,48,768]{2,1,0:T(8,128)}, f32[4,48,768]{2,1,0:T(8,128)}, u32[]{:S(2)}, u32[]{:S(2)}) collective-permute-start(f32[4,48,768]{2,1,0:T(8,128)} %get-tuple-element.68), channel_id=1, source_target_pairs={{0,8},{1,9},{2,10},{3,11},{4,12},{5,13},{6,14},{7,15},{8,0},{9,1},... | collective-permute-start | bytes 1769480 | tf_op jit(solution)/shard_map/cond/branch_1_fun/ppermute | solution.py:264
  208.4 26.6 %copy-start.2 = (f32[4,48,768]{2,1,0:T(8,128)}, f32[4,48,768]{2,1,0:T(8,128)S(1)}, u32[]{:S(2)}) copy-start(f32[4,48,768]{2,1,0:T(8,128)S(1)} %collective-permute-done.12.refs_1_) | copy-start | bytes 1769476 | tf_op jit(solution)/shard_map/cond
  208.4 26.6 %collective-permute-start.21 = (f32[4,48,768]{2,1,0:T(8,128)}, f32[4,48,768]{2,1,0:T(8,128)}, u32[]{:S(2)}, u32[]{:S(2)}) collective-permute-start(f32[4,48,768]{2,1,0:T(8,128)} %get-tuple-element.69), channel_id=1, source_target_pairs={{0,12},{1,13},{2,14},{3,15},{4,0},{5,1},{6,2},{7,3},{8,4},{9,5},{1... | collective-permute-start | bytes 1769480 | tf_op jit(solution)/shard_map/cond/branch_1_fun/ppermute | solution.py:264
Sparse Core Ops, SparseCore 0:
  30.8 33.6 all-gather.6
  66.2 34.3 all-gather.4

commit v7 on v6

--- a/solution.py
+++ b/solution.py
@@ -25,6 +25,8 @@
     return [(down if cores(i) else up)[i] for i in range(count)]
 
 
+SWAP = [(i, i ^ 1) for i in range(8)]
+Z_STEPS = [apart(8, 2, d, lambda i: i % 2) for d in (1, -1, 2)]
 X_HOPS = {d: apart(128, SIDE, d, lambda i: i // 16 % 2) for d in (1, 2, -1)}
 Y_HOPS = {d: apart(128, 1, d, lambda i: i // 16 % 2) for d in (1, 2, -1)}
 BOTH = ("vb", "ob")
@@ -34,31 +36,43 @@
 ORDER += [(1, 0), (1, 1)] + [(3, 2), (3, 3)] + [(0, k) for k in range(SIDE)]
 
 
-def block_table():
+SOURCES = [(dz, dc) for dz in (0, -1, 1, 2) for dc in (0, 1)]
+
+
+def place_table():
     table = np.zeros((8, 16, 32), np.int32)
     for vb in range(8):
         for ob in range(16):
             x, y = divmod(ob, SIDE)
             sign = -1 if vb % 2 else 1
-            for i, (near, far) in enumerate(ORDER):
-                table[vb, ob, i] = (x + sign * near) % SIDE * SIDE + (y + sign * far) % SIDE
-                table[vb, ob, 16 + i] = (x + sign * far) % SIDE * SIDE + (y + sign * near) % SIDE
+            for a, (dz, dc) in enumerate(SOURCES):
+                core = (vb % 2) ^ dc
+                source = 2 * ((vb // 2 + (-dz if core else dz)) % SIDE) + core
+                for h in range(2):
+                    to_x, to_y = divmod(2 * source + h, SIDE)
+                    rel_x, rel_y = sign * (to_x - x) % SIDE, sign * (to_y - y) % SIDE
+                    table[vb, ob, 2 * a + h] = ORDER.index((rel_x, rel_y))
+                    table[vb, ob, 16 + 2 * a + h] = ORDER.index((rel_y, rel_x))
     return table
 
 
-BLOCKS = block_table()
-
-
-def product_kernel(first, x_count, leads, blocks, sizes, origin, *refs):
-    pieces, v_ref, outs, (a_all, v_all) = refs[:8], refs[8], refs[-2 - 2 * len(leads) : -2], refs[-2:]
-    rows, depth = pieces[0].shape[3:]
-    for i, piece in enumerate(pieces):
-        block = piece[0, 0, 0]
-        hi = block.astype(jnp.bfloat16)
-        at = slice(rows * i, rows * (i + 1))
-        a_all[at, 0:depth] = hi
-        a_all[at, depth : 2 * depth] = (block - hi.astype(jnp.float32)).astype(jnp.bfloat16)
-        a_all[at, 2 * depth : 3 * depth] = hi
+PLACES = place_table()
+LEADS = (4, 4, 2, 2, 4)
+
+
+def product_kernel(first, x_count, place, sizes, origin, *refs):
+    pieces, v_ref, outs, (a_all, v_all) = refs[:8], refs[8], refs[-12:-2], refs[-2:]
+    rows = pieces[0].shape[1] // 2
+    depth = pieces[0].shape[2]
+    table = jnp.where(pl.program_id(0) < x_count, 0, 16)
+    for a, piece in enumerate(pieces):
+        for h in range(2):
+            block = piece[0, h * rows : (h + 1) * rows]
+            hi = block.astype(jnp.bfloat16)
+            at = pl.ds(pl.multiple_of(place[table + 2 * a + h] * rows, rows), rows)
+            a_all[at, 0:depth] = hi
+            a_all[at, depth : 2 * depth] = (block - hi.astype(jnp.float32)).astype(jnp.bfloat16)
+            a_all[at, 2 * depth : 3 * depth] = hi
     size = sizes[first + pl.program_id(0)]
     shape = v_ref.shape[1:]
     p = origin[0] + lax.broadcasted_iota(jnp.int32, shape, 0)
@@ -71,7 +85,7 @@
 
     def write(targets):
         at = 0
-        for lead, out in zip(leads, targets):
+        for lead, out in zip(LEADS, targets):
             acc = jnp.dot(
                 a_all[rows * at : rows * (at + lead)], v_all[...], preferred_element_type=jnp.float32
             )
@@ -81,23 +95,17 @@
 
     @pl.when(pl.program_id(0) < x_count)
     def _():
-        write(outs[: len(leads)])
+        write(outs[:5])
 
     @pl.when(pl.program_id(0) >= x_count)
     def _():
-        write(outs[len(leads) :])
-
-
-def product(amp, ovov, first, x_count, y_count, half, leads, blocks, sizes, origin, after, name):
-    rows, depth = amp.shape[3:]
+        write(outs[5:])
+
+
+def product(pieces, ovov, first, x_count, y_count, place, sizes, origin, after, name):
+    rows2, depth = pieces[0][0].shape[1:]
+    rows = rows2 // 2
     cols = ovov.shape[2]
-
-    def a_spec(i):
-        def index(g, blocks, *_):
-            block = blocks[jnp.where(g < x_count, 0, 16) + 8 * half + i]
-            return block // 2, g, block % 2, 0, 0
-
-        return pl.BlockSpec((1, 1, 1, rows, depth), index)
 
     def x_spec(lead):
         return pl.BlockSpec((lead, 1, rows, cols), lambda g, *_: (0, jnp.minimum(g, x_count - 1), 0, 0))
@@ -105,18 +113,18 @@
     def y_spec(lead):
         return pl.BlockSpec((lead, 1, rows, cols), lambda g, *_: (0, jnp.maximum(g - x_count, 0), 0, 0))
 
-    shapes = [(lead, count, rows, cols) for count in (x_count, y_count) for lead in leads]
+    shapes = [(lead, count, rows, cols) for count in (x_count, y_count) for lead in LEADS]
     outs = pl.pallas_call(
-        functools.partial(product_kernel, first, x_count, leads),
+        functools.partial(product_kernel, first, x_count),
         grid_spec=pltpu.PrefetchScalarGridSpec(
             num_scalar_prefetch=3,
             grid=(x_count + y_count,),
-            in_specs=[a_spec(i) for i in range(8)]
+            in_specs=[pl.BlockSpec((1, rows2, depth), lambda g, *_, at=at: (at + g, 0, 0)) for _, at in pieces]
             + [pl.BlockSpec((1, depth, cols), lambda g, *_: (first + g, 0, 0))]
             + [pl.BlockSpec(memory_space=pl.ANY)] * len(after),
-            out_specs=[x_spec(lead) for lead in leads] + [y_spec(lead) for lead in leads],
+            out_specs=[x_spec(lead) for lead in LEADS] + [y_spec(lead) for lead in LEADS],
             scratch_shapes=[
-                pltpu.VMEM((8 * rows, 3 * depth), jnp.bfloat16),
+                pltpu.VMEM((16 * rows, 3 * depth), jnp.bfloat16),
                 pltpu.VMEM((3 * depth, cols), jnp.bfloat16),
             ],
         ),
@@ -124,8 +132,26 @@
         compiler_params=pltpu.CompilerParams(vmem_limit_bytes=VMEM),
         cost_estimate=LIGHT,
         name=name,
-    )(blocks, sizes, origin, *[amp] * 8, ovov, *after)
-    return {"x": outs[: len(leads)], "y": outs[len(leads) :]}
+    )(place, sizes, origin, *[piece for piece, _ in pieces], ovov, *after)
+    return {"x": outs[:5], "y": outs[5:]}
+
+
+def tie_kernel(*refs):
+    pass
+
+
+def tie(values, after):
+    anywhere = pl.BlockSpec(memory_space=pl.ANY)
+    return pl.pallas_call(
+        tie_kernel,
+        in_specs=[anywhere] * (len(values) + len(after)),
+        out_specs=[anywhere] * len(values),
+        out_shape=[jax.ShapeDtypeStruct(v.shape, v.dtype) for v in values],
+        input_output_aliases={i: i for i in range(len(values))},
+        compiler_params=pltpu.CompilerParams(vmem_limit_bytes=VMEM),
+        cost_estimate=LIGHT,
+        name="tie",
+    )(*values, *after)
 
 
 def add_kernel(up, down, recv_p, recv_m, *refs):
@@ -208,52 +234,48 @@
 GROUPS = ((0, 2, 2), (4, 2, 2))
 
 
-def exchange(amplitudes, first, count, depth):
-    rows, _, pairs = amplitudes.shape
-    parts = pairs // depth
-    mine = amplitudes[:, first : first + count].reshape(rows, count, parts, depth)
-    mine = jnp.transpose(mine, (2, 0, 1, 3)).reshape(parts, rows * count, depth)
-    mine = lax.all_to_all(mine, "ob", split_axis=0, concat_axis=0, tiled=True)
-    return jnp.transpose(mine.reshape(parts * rows, count, depth), (1, 0, 2))
-
-
-def contract(first_mine, amplitudes, ovov, row_sizes, pair_sizes):
+def local(amplitudes, ovov, row_sizes, pair_sizes):
     ob = lax.axis_index("ob")
     vb = lax.axis_index("vb")
     local_rows, irreps, _ = amplitudes.shape
+    obs = lax.axis_size("ob")
     depth, cols = ovov.shape[1:]
     out_rows = local_rows * lax.axis_size("vb")
-    blocks = lax.dynamic_slice(jnp.asarray(BLOCKS), (vb, ob, 0), (1, 1, 32)).reshape(32)
+    place = lax.dynamic_slice(jnp.asarray(PLACES), (vb, ob, 0), (1, 1, 32)).reshape(32)
     origin = jnp.stack([ob * depth, vb * cols]).astype(jnp.int32)
+
+    mine = jnp.transpose(amplitudes.reshape(local_rows, irreps, obs, depth), (2, 0, 1, 3))
+    mine = mine.reshape(obs, local_rows * irreps, depth)
+    mine = lax.all_to_all(mine, "ob", split_axis=0, concat_axis=0, tiled=True)
+    mine = jnp.transpose(mine.reshape(obs * local_rows, irreps, depth), (1, 0, 2))
+    mine_swapped = lax.ppermute(mine, "vb", SWAP)
 
     hops_of = {"x": (X_HOPS, Y_HOPS), "y": (Y_HOPS, X_HOPS)}
     order = {axis: [] for axis in hops_of}
     sums = {axis: [] for axis in hops_of}
-    gathered = []
+    landed, sent, handed = [], [], []
     for t, (first, nx, ny) in enumerate(GROUPS):
-        mine = exchange(amplitudes, first, nx + ny, depth) if t else first_mine
         order["x"] += range(first, first + nx)
         order["y"] += range(first + nx, first + nx + ny)
-        gathered.append(lax.all_gather(mine, "vb", axis=0).reshape(-1, nx + ny, 2, out_rows, depth))
-
-    after, behind = [], []
-    for t, (first, nx, ny) in enumerate(GROUPS):
-        leads = {"send": (4, 4), "rest": (2, 2, 4)}
-        args = (gathered[t], ovov, first, nx, ny)
-        send = product(*args, 0, leads["send"], blocks, pair_sizes, origin, after, "send")
-        recv = {
-            axis: (lax.ppermute(send[axis][0], BOTH, here[1]), lax.ppermute(send[axis][1], BOTH, here[-1]))
-            for axis, (here, _) in hops_of.items()
-        }
-        rest = product(*args, 1, leads["rest"], blocks, pair_sizes, origin, [*send["y"], *behind], "rest")
-        after, behind = [], []
+        held = mine[first : first + nx + ny]
+        if t:
+            (held,) = tie([held], landed)
+        landed = [lax.ppermute(held, "vb", steps) for steps in Z_STEPS]
+        pieces = [(mine, first), (mine_swapped, first)]
+        for piece in tie(landed, sent) if t else landed:
+            pieces += [(piece, 0), (lax.ppermute(piece, "vb", SWAP), 0)]
+        made = product(pieces, ovov, first, nx, ny, place, pair_sizes, origin, [], "product")
+        sent = []
+        waits, handed = handed, []
         for axis, (here, _) in hops_of.items():
-            up, down, own = rest[axis]
-            added = add_far(up, down, *recv[axis], [], f"{axis}_add")
-            after += added
-            handed = lax.ppermute(added[0], BOTH, here[1]), lax.ppermute(added[1], BOTH, here[-1])
-            behind += handed
-            sums[axis].append((own, *recv[axis], *handed))
+            send_p, send_m, up, down, own = made[axis]
+            p1 = lax.ppermute(send_p, BOTH, here[1])
+            m1 = lax.ppermute(send_m, BOTH, here[-1])
+            added = add_far(up, down, p1, m1, waits, f"{axis}_add")
+            sent += [p1, m1]
+            p2, m2 = lax.ppermute(added[0], BOTH, here[1]), lax.ppermute(added[1], BOTH, here[-1])
+            handed += [p2, m2]
+            sums[axis].append((own, p1, m1, p2, m2))
 
     parts = []
     for axis, (_, there) in hops_of.items():
@@ -266,20 +288,6 @@
     return finish([order[axis] for axis in hops_of], parts, row_sizes, origin, (out_rows, irreps, cols))
 
 
-def local(amplitudes, ovov, row_sizes, pair_sizes):
-    local_rows, irreps, _ = amplitudes.shape
-    depth, cols = ovov.shape[1:]
-    first, nx, ny = GROUPS[0]
-    mine = exchange(amplitudes, first, nx + ny, depth)
-    nothing = jnp.zeros((local_rows * lax.axis_size("vb"), irreps, cols), jnp.float32)
-    return lax.cond(
-        jnp.max(row_sizes) > 0,
-        contract,
-        lambda *_: nothing,
-        mine, amplitudes, ovov, row_sizes, pair_sizes,
-    )
-
-
 def solution(mesh):
     placed = (P(("vb", "ob"), None, None), P(None, "ob", "vb"), P(), P())
     return jax.shard_map(

time: 248 us -> 241 us (0.972)
  waiting for transfers between devices: 84.5 us -> 101 us
  between operations: 14.1 us -> 0.1 us
  Pallas kernels: 67.9 us -> 55.2 us
  blocking collectives: 14.6 us -> 25.4 us
  starting transfers between devices: 57.4 us -> 49.2 us
    ppermute x22 -> x35, waiting for transfers between devices: 56.7 us -> 101 us  [the longest x6 34 us: local(): landed = [lax.ppermute(held, 'vb', steps) for steps in Z_STEPS]]
    all_gather x2 -> x0, waiting for transfers between devices: 17.1 us -> none  [contract(): lax.all_gather(mine, 'vb', axis=0).reshape(-1, nx + ny, 2, out_rows, depth)]
    pallas_call x4, Pallas kernels: 41.4 us -> 28.7 us  [the longest x2 28.7 us: product(): pl.pallas_call(functools.partial(product_kernel, first, x_count), grid_sp...]
    all_to_all x1, blocking collectives: 14.6 us -> 25.4 us  [local(): mine = lax.all_to_all(mine, 'ob', split_axis=0, concat_axis=0, tiled=True)]
    all_to_all x1 -> x0, waiting for transfers between devices: 10.6 us -> none  [exchange(): mine = lax.all_to_all(mine, 'ob', split_axis=0, concat_axis=0, tiled=True)]
    all_to_all x1 -> x0, starting transfers between devices: 7.25 us -> none  [exchange(): mine = lax.all_to_all(mine, 'ob', split_axis=0, concat_axis=0, tiled=True)]
    ppermute x22 -> x35, starting transfers between devices: 50 us -> 49.2 us  [the longest x6 13.4 us: local(): lax.ppermute(four[k], BOTH, there[d])]
  transfers between devices with their start and end apart: 25 -> 35, of which waited for: 7 -> 10; matrix products, arithmetic and copies ran while one was open for 2% -> 1% of each run, Pallas kernels for 17% -> 21%
where the time goes in v7:
time: 241 us; the launch traced here: 239 us
  waiting for transfers between devices  101 us (42%)
  Pallas kernels  55.2 us (23%)
  starting transfers between devices  49.2 us (20%)
  blocking collectives  25.4 us (11%)
  local copies, waits for them, and re-layouts  7.48 us (3%)
    ppermute x6, waiting for transfers between devices, local(): landed = [lax.ppermute(held, 'vb', steps) for steps in Z_STEPS]  34 us
    ppermute x4, waiting for transfers between devices, local(): lax.ppermute(added[1], BOTH, here[-1])  29 us
    pallas_call x2, Pallas kernels, product(): pl.pallas_call(functools.partial(product_kernel, first, x_count), grid_sp...  28.7 us
    all_to_all x1, blocking collectives, local(): mine = lax.all_to_all(mine, 'ob', split_axis=0, concat_axis=0, tiled=True)  25.4 us
    ppermute x6, waiting for transfers between devices, local(): lax.ppermute(four[k], BOTH, there[d])  20.3 us
    ppermute x6, starting transfers between devices, local(): lax.ppermute(four[k], BOTH, there[d])  13.4 us
    ppermute x4, waiting for transfers between devices, local(): p1 = lax.ppermute(send_p, BOTH, here[1])  13.4 us
    ppermute x4, starting transfers between devices, local(): m1 = lax.ppermute(send_m, BOTH, here[-1])  12.1 us
  transfers between devices with their start and end apart: 35, of which 10 were waited for; matrix products, arithmetic and copies ran while one was open for 1% of the time, Pallas kernels for 21%

profile of v7, /device:TPU:0, one launch (start us, length us, event | category | flops | bytes accessed | tf_op | source)
XLA Modules:
  0.0 239.2 jit_solution(13210660502616953251)
XLA Ops:
  0.0 1.5 copy.25
  1.9 25.4 %all_to_all.5 = f32[16,48,384]{2,1,0:T(8,128)S(1)} all-to-all(f32[16,48,384]{2,1,0:T(8,128)S(1)} %bitcast.21), channel_id=1, replica_groups=mesh['vb'=8,'ob'=16] {'ob'}, dimensions={0} | all-to-all | bytes 2359296 | tf_op jit(solution)/shard_map/all_to_all | solution.py:249
  27.2 1.2 copy.26
  28.5 2.2 fusion
  30.7 3.9 %collective-permute-start.3 = (f32[4,96,384]{2,1,0:T(8,128)S(1)}, f32[4,96,384]{2,1,0:T(8,128)}, u32[]{:S(2)}, u32[]{:S(2)}) collective-permute-start(f32[4,96,384]{2,1,0:T(8,128)S(1)} %get-tuple-element.99), channel_id=1, source_target_pairs={{0,64},{16,80},{32,96},{48,112},{64,0},{80,16},{96,32},{112,48},{1... | collective-permute-start | bytes 1769480 | tf_op jit(solution)/shard_map/ppermute | solution.py:263
  34.5 0.7 collective-permute-start.2
  35.3 1.3 collective-permute-start.1
  36.6 12.4 %collective-permute-done.3.refs_3_.refs_6_ = f32[4,96,384]{2,1,0:T(8,128)} collective-permute-done((f32[4,96,384]{2,1,0:T(8,128)S(1)}, f32[4,96,384]{2,1,0:T(8,128)}, u32[]{:S(2)}, u32[]{:S(2)}) %collective-permute-start.3) | collective-permute-done | bytes 589856 | tf_op jit(solution)/shard_map/ppermute | solution.py:263
  48.9 11.1 %collective-permute-done.2.refs_2_.refs_4_ = f32[4,96,384]{2,1,0:T(8,128)} collective-permute-done((f32[4,96,384]{2,1,0:T(8,128)S(1)}, f32[4,96,384]{2,1,0:T(8,128)}, u32[]{:S(2)}, u32[]{:S(2)}) %collective-permute-start.2) | collective-permute-done | bytes 589856 | tf_op jit(solution)/shard_map/ppermute | solution.py:263
  60.5 2.0 collective-permute-start.6
  62.5 0.6 pad_add_fusion.1.origin
  63.1 1.3 dynamic-slice_bitcast_fusion.place
  64.4 1.2 collective-permute-start.5
  65.6 14.3 %product.2 = (f32[4,2,48,768]{3,2,1,0:T(8,128)}, f32[4,2,48,768]{3,2,1,0:T(8,128)}, f32[2,2,48,768]{3,2,1,0:T(8,128)}, f32[2,2,48,768]{3,2,1,0:T(8,128)}, f32[4,...) custom-call(s32[32]{0:T(128)} %dynamic-slice_bitcast_fusion.place, ...), custom_call_target="tpu_custom_call" | custom-call | tf_op jit(solution)/shard_map/product/pallas_call | solution.py:117
  80.4 2.8 %collective-permute-start.11 = (f32[4,2,48,768]{3,2,1,0:T(8,128)}, f32[4,2,48,768]{3,2,1,0:T(8,128)}, u32[]{:S(2)}, u32[]{:S(2)}) collective-permute-start(f32[4,2,48,768]{3,2,1,0:T(8,128)} %get-tuple-element.53), channel_id=1, source_target_pairs={{0,12},{1,13},{2,14},{3,15},{4,0},{5,1},{6,2},{7,3},{8,4},{9,5},{1... | collective-permute-start | bytes 3538952 | tf_op jit(solution)/shard_map/ppermute | solution.py:273
  83.5 3.0 %collective-permute-start.13 = (f32[4,2,48,768]{3,2,1,0:T(8,128)}, f32[4,2,48,768]{3,2,1,0:T(8,128)}, u32[]{:S(2)}, u32[]{:S(2)}) collective-permute-start(f32[4,2,48,768]{3,2,1,0:T(8,128)} %get-tuple-element.55), channel_id=1, source_target_pairs={{0,3},{1,0},{2,1},{3,2},{4,7},{5,4},{6,5},{7,6},{8,11},{9,8},{10,9... | collective-permute-start | bytes 3538952 | tf_op jit(solution)/shard_map/ppermute | solution.py:273
  86.5 0.8 collective-permute-start.4
  87.3 10.6 %collective-permute-done.4.refs_0_ = f32[4,96,384]{2,1,0:T(8,128)} collective-permute-done((f32[4,96,384]{2,1,0:T(8,128)}, f32[4,96,384]{2,1,0:T(8,128)}, u32[]{:S(2)}, u32[]{:S(2)}) %collective-permute-start.4) | collective-permute-done | bytes 589856 | tf_op jit(solution)/shard_map/ppermute | solution.py:263
  97.9 12.0 %collective-permute-done.10.refs_3_.recv_p.p1 = f32[4,2,48,768]{3,2,1,0:T(8,128)} collective-permute-done((f32[4,2,48,768]{3,2,1,0:T(8,128)}, f32[4,2,48,768]{3,2,1,0:T(8,128)}, u32[]{:S(2)}, u32[]{:S(2)}) %collective-permute-start.10) | collective-permute-done | bytes 1179680 | tf_op jit(solution)/shard_map/ppermute | solution.py:272
  109.9 1.4 collective-permute-done.12.refs_5_.recv_p.p1
  111.9 2.5 %x_add.2 = (f32[2,2,48,768]{3,2,1,0:T(8,128)}, f32[2,2,48,768]{3,2,1,0:T(8,128)}) custom-call(f32[2,2,48,768]{3,2,1,0:T(8,128)} %get-tuple-element.64.up, f32[2,2,48,768]{3,2,1,0:T(8,128)} %get-tuple-element.65.down, f32[4,2,48,768]{3,2,1,0:T(8,128)} %collective-permute-done.10.refs_3_.recv_p.p1, f32[4,2,48,768]{3,2,1,0:T(8,128)} %collective-permute-done.11.refs_4_.recv_m.m1), custom_call_target="tpu_custom_call" | custom-call | tf_op jit(solution)/shard_map/x_add/pallas_call | solution.py:165
  114.8 2.8 %collective-permute-start.20 = (f32[2,2,48,768]{3,2,1,0:T(8,128)}, f32[2,2,48,768]{3,2,1,0:T(8,128)}, u32[]{:S(2)}, u32[]{:S(2)}) collective-permute-start(f32[2,2,48,768]{3,2,1,0:T(8,128)} %get-tuple-element.67), channel_id=1, source_target_pairs={{0,12},{1,13},{2,14},{3,15},{4,0},{5,1},{6,2},{7,3},{8,4},{9,5},{1... | collective-permute-start | bytes 1769480 | tf_op jit(solution)/shard_map/ppermute | solution.py:276
  117.6 2.5 %y_add.2 = (f32[2,2,48,768]{3,2,1,0:T(8,128)}, f32[2,2,48,768]{3,2,1,0:T(8,128)}) custom-call(f32[2,2,48,768]{3,2,1,0:T(8,128)} %get-tuple-element.68.up, f32[2,2,48,768]{3,2,1,0:T(8,128)} %get-tuple-element.69.down, f32[4,2,48,768]{3,2,1,0:T(8,128)} %collective-permute-done.12.refs_5_.recv_p.p1, f32[4,2,48,768]{3,2,1,0:T(8,128)} %collective-permute-done.13.refs_6_.recv_m.m1), custom_call_target="tpu_custom_call" | custom-call | tf_op jit(solution)/shard_map/y_add/pallas_call | solution.py:165
  120.1 0.8 copy-done.3
  120.9 14.4 %product.3 = (f32[4,2,48,768]{3,2,1,0:T(8,128)}, f32[4,2,48,768]{3,2,1,0:T(8,128)}, f32[2,2,48,768]{3,2,1,0:T(8,128)}, f32[2,2,48,768]{3,2,1,0:T(8,128)}, f32[4,...) custom-call(s32[32]{0:T(128)} %dynamic-slice_bitcast_fusion.place, ...), custom_call_target="tpu_custom_call" | custom-call | tf_op jit(solution)/shard_map/product/pallas_call | solution.py:117
  135.4 3.2 %collective-permute-start.18 = (f32[4,2,48,768]{3,2,1,0:T(8,128)}, f32[4,2,48,768]{3,2,1,0:T(8,128)}, u32[]{:S(2)}, u32[]{:S(2)}) collective-permute-start(f32[4,2,48,768]{3,2,1,0:T(8,128)} %get-tuple-element.61), channel_id=1, source_target_pairs={{0,12},{1,13},{2,14},{3,15},{4,0},{5,1},{6,2},{7,3},{8,4},{9,5},{1... | collective-permute-start | bytes 3538952 | tf_op jit(solution)/shard_map/ppermute | solution.py:273
  138.8 3.1 %collective-permute-start.29 = (f32[4,2,48,768]{3,2,1,0:T(8,128)}, f32[4,2,48,768]{3,2,1,0:T(8,128)}, u32[]{:S(2)}, u32[]{:S(2)}) collective-permute-start(f32[4,2,48,768]{3,2,1,0:T(8,128)} %get-tuple-element.85), channel_id=1, source_target_pairs={{0,3},{1,0},{2,1},{3,2},{4,7},{5,4},{6,5},{7,6},{8,11},{9,8},{10,9... | collective-permute-start | bytes 3538952 | tf_op jit(solution)/shard_map/ppermute | solution.py:273
  141.9 2.0 collective-permute-start.22
  143.9 28.2 %collective-permute-done.22.refs_3_.m2 = f32[2,2,48,768]{3,2,1,0:T(8,128)} collective-permute-done((f32[2,2,48,768]{3,2,1,0:T(8,128)}, f32[2,2,48,768]{3,2,1,0:T(8,128)}, u32[]{:S(2)}, u32[]{:S(2)}) %collective-permute-start.22) | collective-permute-done | bytes 589856 | tf_op jit(solution)/shard_map/ppermute | solution.py:276
  172.1 2.5 %x_add.3 = (f32[2,2,48,768]{3,2,1,0:T(8,128)}, f32[2,2,48,768]{3,2,1,0:T(8,128)}) custom-call(f32[2,2,48,768]{3,2,1,0:T(8,128)} %get-tuple-element.62.up, f32[2,2,48,768]{3,2,1,0:T(8,128)} %get-tuple-element.63.down, f32[4,2,48,768]{3,2,1,0:T(8,128)} %collective-permute-done.17.recv_p.p1, f32[4,2,48,768]{3,2,1,0:T(8,128)} %collective-permute-done.18.recv_m.m1, ...), custom_call_target="tpu_custom_call" | custom-call | tf_op jit(solution)/shard_map/x_add/pallas_call | solution.py:165
  174.6 3.2 %collective-permute-start.24 = (f32[2,2,48,768]{3,2,1,0:T(8,128)}, f32[2,2,48,768]{3,2,1,0:T(8,128)}, u32[]{:S(2)}, u32[]{:S(2)}) collective-permute-start(f32[2,2,48,768]{3,2,1,0:T(8,128)} %get-tuple-element.73), channel_id=1, source_target_pairs={{0,12},{1,13},{2,14},{3,15},{4,0},{5,1},{6,2},{7,3},{8,4},{9,5},{1... | collective-permute-start | bytes 1769480 | tf_op jit(solution)/shard_map/ppermute | solution.py:276
  177.9 2.5 %y_add.3 = (f32[2,2,48,768]{3,2,1,0:T(8,128)}, f32[2,2,48,768]{3,2,1,0:T(8,128)}) custom-call(f32[2,2,48,768]{3,2,1,0:T(8,128)} %get-tuple-element.86.up, f32[2,2,48,768]{3,2,1,0:T(8,128)} %get-tuple-element.87.down, f32[4,2,48,768]{3,2,1,0:T(8,128)} %collective-permute-done.28.recv_p.p1, f32[4,2,48,768]{3,2,1,0:T(8,128)} %collective-permute-done.29.recv_m.m1, ...), custom_call_target="tpu_custom_call" | custom-call | tf_op jit(solution)/shard_map/y_add/pallas_call | solution.py:165
  180.4 1.1 collective-permute-start.30
  181.5 2.1 collective-permute-start.31
  183.6 2.9 %x_own.2 = (f32[4,48,768]{2,1,0:T(8,128)}, f32[4,48,768]{2,1,0:T(8,128)}, f32[4,48,768]{2,1,0:T(8,128)}, f32[4,48,768]{2,1,0:T(8,128)}) custom-call(f32[4,2,48,768]{3,2,1,0:T(8,128)} %get-tuple-element.74.own, f32[4,2,48,768]{3,2,1,0:T(8,128)} %collective-permute-done.10.refs_3_.recv_p.p1, f32[4,2,48,768]{3,2,1,0:T(8,128)} %collective-permute-done.11.refs_4_.recv_m.m1, ...), custom_call_target="tpu_custom_call" | custom-call | tf_op jit(solution)/shard_map/x_own/pallas_call | solution.py:191
  186.5 3.9 %collective-permute-done.23.p2 = f32[2,2,48,768]{3,2,1,0:T(8,128)S(1)} collective-permute-done((f32[2,2,48,768]{3,2,1,0:T(8,128)}, f32[2,2,48,768]{3,2,1,0:T(8,128)S(1)}, u32[]{:S(2)}, u32[]{:S(2)}) %collective-permute-start.23) | collective-permute-done | bytes 589856 | tf_op jit(solution)/shard_map/ppermute | solution.py:276
  190.4 0.7 collective-permute-done.24.m2
  191.2 2.9 %x_own.3 = (f32[4,48,768]{2,1,0:T(8,128)}, f32[4,48,768]{2,1,0:T(8,128)}, f32[4,48,768]{2,1,0:T(8,128)}, f32[4,48,768]{2,1,0:T(8,128)}) custom-call(f32[4,2,48,768]{3,2,1,0:T(8,128)} %get-tuple-element.59.own, f32[4,2,48,768]{3,2,1,0:T(8,128)} %collective-permute-done.17.recv_p.p1, ...), custom_call_target="tpu_custom_call", output_to_operand_aliasing={{0}: (5, {}), {1}: (6, {}), {2}: (7, {}), {3}: (8, {})} | custom-call | tf_op jit(solution)/shard_map/x_own/pallas_call | solution.py:191
  194.1 2.9 %collective-permute-start.25 = (f32[4,48,768]{2,1,0:T(8,128)}, f32[4,48,768]{2,1,0:T(8,128)S(1)}, u32[]{:S(2)}, u32[]{:S(2)}) collective-permute-start(f32[4,48,768]{2,1,0:T(8,128)} %get-tuple-element.80), channel_id=1, source_target_pairs={{0,1},{1,2},{2,3},{3,0},{4,5},{5,6},{6,7},{7,4},{8,9},{9,10},{10,1... | collective-permute-start | bytes 1769480 | tf_op jit(solution)/shard_map/ppermute | solution.py:286
  197.0 2.9 %y_own.2 = (f32[4,48,768]{2,1,0:T(8,128)}, f32[4,48,768]{2,1,0:T(8,128)}, f32[4,48,768]{2,1,0:T(8,128)}, f32[4,48,768]{2,1,0:T(8,128)}) custom-call(f32[4,2,48,768]{3,2,1,0:T(8,128)} %get-tuple-element.90.own, f32[4,2,48,768]{3,2,1,0:T(8,128)} %collective-permute-done.12.refs_5_.recv_p.p1, f32[4,2,48,768]{3,2,1,0:T(8,128)} %collective-permute-done.13.refs_6_.recv_m.m1, ...), custom_call_target="tpu_custom_call" | custom-call | tf_op jit(solution)/shard_map/y_own/pallas_call | solution.py:191
  199.9 2.7 %collective-permute-start.27 = (f32[4,48,768]{2,1,0:T(8,128)}, f32[4,48,768]{2,1,0:T(8,128)}, u32[]{:S(2)}, u32[]{:S(2)}) collective-permute-start(f32[4,48,768]{2,1,0:T(8,128)} %get-tuple-element.82), channel_id=1, source_target_pairs={{0,3},{1,0},{2,1},{3,2},{4,7},{5,4},{6,5},{7,6},{8,11},{9,8},{10,9... | collective-permute-start | bytes 1769480 | tf_op jit(solution)/shard_map/ppermute | solution.py:286
  202.6 2.9 %y_own.3 = (f32[4,48,768]{2,1,0:T(8,128)}, f32[4,48,768]{2,1,0:T(8,128)}, f32[4,48,768]{2,1,0:T(8,128)}, f32[4,48,768]{2,1,0:T(8,128)}) custom-call(f32[4,2,48,768]{3,2,1,0:T(8,128)} %get-tuple-element.83.own, f32[4,2,48,768]{3,2,1,0:T(8,128)} %collective-permute-done.28.recv_p.p1, ...), custom_call_target="tpu_custom_call", output_to_operand_aliasing={{0}: (5, {}), {1}: (6, {}), {2}: (7, {}), {3}: (8, {})} | custom-call | tf_op jit(solution)/shard_map/y_own/pallas_call | solution.py:191
  205.5 2.5 %collective-permute-start.33 = (f32[4,48,768]{2,1,0:T(8,128)}, f32[4,48,768]{2,1,0:T(8,128)}, u32[]{:S(2)}, u32[]{:S(2)}) collective-permute-start(f32[4,48,768]{2,1,0:T(8,128)} %get-tuple-element.97), channel_id=1, source_target_pairs={{0,8},{1,9},{2,10},{3,11},{4,12},{5,13},{6,14},{7,15},{8,0},{9,1},... | collective-permute-start | bytes 1769480 | tf_op jit(solution)/shard_map/ppermute | solution.py:286
  207.9 11.2 %collective-permute-done.25.refs_1_ = f32[4,48,768]{2,1,0:T(8,128)S(1)} collective-permute-done((f32[4,48,768]{2,1,0:T(8,128)}, f32[4,48,768]{2,1,0:T(8,128)S(1)}, u32[]{:S(2)}, u32[]{:S(2)}) %collective-permute-start.25) | collective-permute-done | bytes 589856 | tf_op jit(solution)/shard_map/ppermute | solution.py:286
  219.2 5.4 %collective-permute-start.34 = (f32[4,48,768]{2,1,0:T(8,128)}, f32[4,48,768]{2,1,0:T(8,128)}, u32[]{:S(2)}, u32[]{:S(2)}) collective-permute-start(f32[4,48,768]{2,1,0:T(8,128)} %get-tuple-element.98), channel_id=1, source_target_pairs={{0,12},{1,13},{2,14},{3,15},{4,0},{5,1},{6,2},{7,3},{8,4},{9,5},{1... | collective-permute-start | bytes 1769480 | tf_op jit(solution)/shard_map/ppermute | solution.py:286
  224.5 0.7 pad_add_fusion.origin
  225.2 9.1 %collective-permute-done.33.refs_6_ = f32[4,48,768]{2,1,0:T(8,128)} collective-permute-done((f32[4,48,768]{2,1,0:T(8,128)}, f32[4,48,768]{2,1,0:T(8,128)}, u32[]{:S(2)}, u32[]{:S(2)}) %collective-permute-start.33) | collective-permute-done | bytes 589856 | tf_op jit(solution)/shard_map/ppermute | solution.py:286
  234.3 5.0 %finish.1 = f32[48,8,768]{2,1,0:T(8,128)} custom-call(s32[8]{0:T(128)} %sizes.5, s32[2]{0:T(128)} %pad_add_fusion.origin, f32[4,48,768]{2,1,0:T(8,128)} %get-tuple-element.79.refs_0_, f32[4,48,768]{2,1,0:T(8,128)} %copy-done.2, f32[4,48,768]{2,1,0:T(8,128)} %collective-permute-done.26.refs_2_, f32[4,48,768]{2,1,0:T(8,128)} %collective-permute-done.27.refs_3_, ...), custom_call_target="tpu_custom_call" | custom-call | tf_op jit(solution)/shard_map/finish/pallas_call | solution.py:219
  (53 shorter events, 3.2 us)
Async XLA Ops:
  30.7 18.3 %collective-permute-start.3 = (f32[4,96,384]{2,1,0:T(8,128)S(1)}, f32[4,96,384]{2,1,0:T(8,128)}, u32[]{:S(2)}, u32[]{:S(2)}) collective-permute-start(f32[4,96,384]{2,1,0:T(8,128)S(1)} %get-tuple-element.99), channel_id=1, source_target_pairs={{0,64},{16,80},{32,96},{48,112},{64,0},{80,16},{96,32},{112,48},{1... | collective-permute-start | bytes 1769480 | tf_op jit(solution)/shard_map/ppermute | solution.py:263
  34.5 29.8 %collective-permute-start = (f32[8,96,384]{2,1,0:T(8,128)}, f32[8,96,384]{2,1,0:T(8,128)}, u32[]{:S(2)}, u32[]{:S(2)}) collective-permute-start(f32[8,96,384]{2,1,0:T(8,128)} %bitcast.19.refs_0_), channel_id=1, source_target_pairs={{0,16},{16,0},{32,48},{48,32},{64,80},{80,64},{96,112},{112,96},{1... | collective-permute-start | bytes 3538952 | tf_op jit(solution)/shard_map/ppermute | solution.py:251
  34.5 25.5 %collective-permute-start.2 = (f32[4,96,384]{2,1,0:T(8,128)S(1)}, f32[4,96,384]{2,1,0:T(8,128)}, u32[]{:S(2)}, u32[]{:S(2)}) collective-permute-start(f32[4,96,384]{2,1,0:T(8,128)S(1)} %get-tuple-element.99), channel_id=1, source_target_pairs={{0,96},{16,48},{32,0},{48,80},{64,32},{80,112},{96,64},{112,16},{1... | collective-permute-start | bytes 1769480 | tf_op jit(solution)/shard_map/ppermute | solution.py:263
  35.3 24.7 %collective-permute-start.1 = (f32[4,96,384]{2,1,0:T(8,128)S(1)}, f32[4,96,384]{2,1,0:T(8,128)}, u32[]{:S(2)}, u32[]{:S(2)}) collective-permute-start(f32[4,96,384]{2,1,0:T(8,128)S(1)} %get-tuple-element.99), channel_id=1, source_target_pairs={{0,32},{16,112},{32,64},{48,16},{64,96},{80,48},{96,0},{112,80},{1... | collective-permute-start | bytes 1769480 | tf_op jit(solution)/shard_map/ppermute | solution.py:263
  48.9 16.7 %collective-permute-start.9 = (f32[4,96,384]{2,1,0:T(8,128)}, f32[4,96,384]{2,1,0:T(8,128)}, u32[]{:S(2)}, u32[]{:S(2)}) collective-permute-start(f32[4,96,384]{2,1,0:T(8,128)} %collective-permute-done.3.refs_3_.refs_6_), channel_id=1, source_target_pairs={{0,16},{16,0},{32,48},{48,32},{64,80},{80,64},{96,112},{112,96},{1... | collective-permute-start | bytes 1769480 | tf_op jit(solution)/shard_map/ppermute | solution.py:266
  60.0 5.6 %collective-permute-start.8 = (f32[4,96,384]{2,1,0:T(8,128)}, f32[4,96,384]{2,1,0:T(8,128)}, u32[]{:S(2)}, u32[]{:S(2)}) collective-permute-start(f32[4,96,384]{2,1,0:T(8,128)} %collective-permute-done.2.refs_2_.refs_4_), channel_id=1, source_target_pairs={{0,16},{16,0},{32,48},{48,32},{64,80},{80,64},{96,112},{112,96},{1... | collective-permute-start | bytes 1769480 | tf_op jit(solution)/shard_map/ppermute | solution.py:266
  60.0 5.6 %collective-permute-start.7 = (f32[4,96,384]{2,1,0:T(8,128)}, f32[4,96,384]{2,1,0:T(8,128)}, u32[]{:S(2)}, u32[]{:S(2)}) collective-permute-start(f32[4,96,384]{2,1,0:T(8,128)} %collective-permute-done.1.refs_1_.refs_2_), channel_id=1, source_target_pairs={{0,16},{16,0},{32,48},{48,32},{64,80},{80,64},{96,112},{112,96},{1... | collective-permute-start | bytes 1769480 | tf_op jit(solution)/shard_map/ppermute | solution.py:266
  60.5 23.0 %collective-permute-start.6 = (f32[4,96,384]{2,1,0:T(8,128)}, f32[4,96,384]{2,1,0:T(8,128)S(1)}, u32[]{:S(2)}, u32[]{:S(2)}) collective-permute-start(f32[4,96,384]{2,1,0:T(8,128)} %tie.2), channel_id=1, source_target_pairs={{0,64},{16,80},{32,96},{48,112},{64,0},{80,16},{96,32},{112,48},{1... | collective-permute-start | bytes 1769480 | tf_op jit(solution)/shard_map/ppermute | solution.py:263
  64.4 22.1 %collective-permute-start.5 = (f32[4,96,384]{2,1,0:T(8,128)}, f32[4,96,384]{2,1,0:T(8,128)}, u32[]{:S(2)}, u32[]{:S(2)}) collective-permute-start(f32[4,96,384]{2,1,0:T(8,128)} %tie.2), channel_id=1, source_target_pairs={{0,96},{16,48},{32,0},{48,80},{64,32},{80,112},{96,64},{112,16},{1... | collective-permute-start | bytes 1769480 | tf_op jit(solution)/shard_map/ppermute | solution.py:263
  79.9 29.9 %collective-permute-start.10 = (f32[4,2,48,768]{3,2,1,0:T(8,128)}, f32[4,2,48,768]{3,2,1,0:T(8,128)}, u32[]{:S(2)}, u32[]{:S(2)}) collective-permute-start(f32[4,2,48,768]{3,2,1,0:T(8,128)} %get-tuple-element.52), channel_id=1, source_target_pairs={{0,4},{1,5},{2,6},{3,7},{4,8},{5,9},{6,10},{7,11},{8,12},{9,13},{1... | collective-permute-start | bytes 3538952 | tf_op jit(solution)/shard_map/ppermute | solution.py:272
  80.4 29.4 %collective-permute-start.11 = (f32[4,2,48,768]{3,2,1,0:T(8,128)}, f32[4,2,48,768]{3,2,1,0:T(8,128)}, u32[]{:S(2)}, u32[]{:S(2)}) collective-permute-start(f32[4,2,48,768]{3,2,1,0:T(8,128)} %get-tuple-element.53), channel_id=1, source_target_pairs={{0,12},{1,13},{2,14},{3,15},{4,0},{5,1},{6,2},{7,3},{8,4},{9,5},{1... | collective-permute-start | bytes 3538952 | tf_op jit(solution)/shard_map/ppermute | solution.py:273
  83.2 28.0 %collective-permute-start.12 = (f32[4,2,48,768]{3,2,1,0:T(8,128)}, f32[4,2,48,768]{3,2,1,0:T(8,128)}, u32[]{:S(2)}, u32[]{:S(2)}) collective-permute-start(f32[4,2,48,768]{3,2,1,0:T(8,128)} %get-tuple-element.54), channel_id=1, source_target_pairs={{0,1},{1,2},{2,3},{3,0},{4,5},{5,6},{6,7},{7,4},{8,9},{9,10},{10,1... | collective-permute-start | bytes 3538952 | tf_op jit(solution)/shard_map/ppermute | solution.py:272
  83.5 27.8 %copy-start.1 = (f32[4,96,384]{2,1,0:T(8,128)}, f32[4,96,384]{2,1,0:T(8,128)S(1)}, u32[]{:S(2)}) copy-start(f32[4,96,384]{2,1,0:T(8,128)S(1)} %collective-permute-done.6.refs_2_) | copy-start | bytes 1769476
  83.5 27.8 %collective-permute-start.13 = (f32[4,2,48,768]{3,2,1,0:T(8,128)}, f32[4,2,48,768]{3,2,1,0:T(8,128)}, u32[]{:S(2)}, u32[]{:S(2)}) collective-permute-start(f32[4,2,48,768]{3,2,1,0:T(8,128)} %get-tuple-element.55), channel_id=1, source_target_pairs={{0,3},{1,0},{2,1},{3,2},{4,7},{5,4},{6,5},{7,6},{8,11},{9,8},{10,9... | collective-permute-start | bytes 3538952 | tf_op jit(solution)/shard_map/ppermute | solution.py:273
  86.5 11.4 %collective-permute-start.4 = (f32[4,96,384]{2,1,0:T(8,128)}, f32[4,96,384]{2,1,0:T(8,128)}, u32[]{:S(2)}, u32[]{:S(2)}) collective-permute-start(f32[4,96,384]{2,1,0:T(8,128)} %tie.2), channel_id=1, source_target_pairs={{0,32},{16,112},{32,64},{48,16},{64,96},{80,48},{96,0},{112,80},{1... | collective-permute-start | bytes 1769480 | tf_op jit(solution)/shard_map/ppermute | solution.py:263
  111.3 8.8 %collective-permute-start.14 = (f32[4,96,384]{2,1,0:T(8,128)}, f32[4,96,384]{2,1,0:T(8,128)S(1)}, u32[]{:S(2)}, u32[]{:S(2)}) collective-permute-start(f32[4,96,384]{2,1,0:T(8,128)} %get-tuple-element.56.refs_2_), channel_id=1, source_target_pairs={{0,16},{16,0},{32,48},{48,32},{64,80},{80,64},{96,112},{112,96},{1... | collective-permute-start | bytes 1769480 | tf_op jit(solution)/shard_map/ppermute | solution.py:266
  111.3 9.6 %collective-permute-start.15 = (f32[4,96,384]{2,1,0:T(8,128)}, f32[4,96,384]{2,1,0:T(8,128)}, u32[]{:S(2)}, u32[]{:S(2)}) collective-permute-start(f32[4,96,384]{2,1,0:T(8,128)} %get-tuple-element.57.refs_4_), channel_id=1, source_target_pairs={{0,16},{16,0},{32,48},{48,32},{64,80},{80,64},{96,112},{112,96},{1... | collective-permute-start | bytes 1769480 | tf_op jit(solution)/shard_map/ppermute | solution.py:266
  111.8 9.1 %collective-permute-start.16 = (f32[4,96,384]{2,1,0:T(8,128)}, f32[4,96,384]{2,1,0:T(8,128)}, u32[]{:S(2)}, u32[]{:S(2)}) collective-permute-start(f32[4,96,384]{2,1,0:T(8,128)} %get-tuple-element.58.refs_6_), channel_id=1, source_target_pairs={{0,16},{16,0},{32,48},{48,32},{64,80},{80,64},{96,112},{112,96},{1... | collective-permute-start | bytes 1769480 | tf_op jit(solution)/shard_map/ppermute | solution.py:266
  114.4 24.2 %collective-permute-start.19 = (f32[2,2,48,768]{3,2,1,0:T(8,128)}, f32[2,2,48,768]{3,2,1,0:T(8,128)}, u32[]{:S(2)}, u32[]{:S(2)}) collective-permute-start(f32[2,2,48,768]{3,2,1,0:T(8,128)} %get-tuple-element.66), channel_id=1, source_target_pairs={{0,4},{1,5},{2,6},{3,7},{4,8},{5,9},{6,10},{7,11},{8,12},{9,13},{1... | collective-permute-start | bytes 1769480 | tf_op jit(solution)/shard_map/ppermute | solution.py:276
  114.8 24.0 %collective-permute-start.20 = (f32[2,2,48,768]{3,2,1,0:T(8,128)}, f32[2,2,48,768]{3,2,1,0:T(8,128)}, u32[]{:S(2)}, u32[]{:S(2)}) collective-permute-start(f32[2,2,48,768]{3,2,1,0:T(8,128)} %get-tuple-element.67), channel_id=1, source_target_pairs={{0,12},{1,13},{2,14},{3,15},{4,0},{5,1},{6,2},{7,3},{8,4},{9,5},{1... | collective-permute-start | bytes 1769480 | tf_op jit(solution)/shard_map/ppermute | solution.py:276
  120.1 0.8 copy-start.3
  120.9 21.0 %collective-permute-start.21 = (f32[2,2,48,768]{3,2,1,0:T(8,128)}, f32[2,2,48,768]{3,2,1,0:T(8,128)S(1)}, u32[]{:S(2)}, u32[]{:S(2)}) collective-permute-start(f32[2,2,48,768]{3,2,1,0:T(8,128)} %get-tuple-element.70), channel_id=1, source_target_pairs={{0,1},{1,2},{2,3},{3,0},{4,5},{5,6},{6,7},{7,4},{8,9},{9,10},{10,1... | collective-permute-start | bytes 1769480 | tf_op jit(solution)/shard_map/ppermute | solution.py:276
  135.3 36.8 %collective-permute-start.17 = (f32[4,2,48,768]{3,2,1,0:T(8,128)}, f32[4,2,48,768]{3,2,1,0:T(8,128)}, u32[]{:S(2)}, u32[]{:S(2)}) collective-permute-start(f32[4,2,48,768]{3,2,1,0:T(8,128)} %get-tuple-element.60), channel_id=1, source_target_pairs={{0,4},{1,5},{2,6},{3,7},{4,8},{5,9},{6,10},{7,11},{8,12},{9,13},{1... | collective-permute-start | bytes 3538952 | tf_op jit(solution)/shard_map/ppermute | solution.py:272
  135.4 36.7 %collective-permute-start.18 = (f32[4,2,48,768]{3,2,1,0:T(8,128)}, f32[4,2,48,768]{3,2,1,0:T(8,128)}, u32[]{:S(2)}, u32[]{:S(2)}) collective-permute-start(f32[4,2,48,768]{3,2,1,0:T(8,128)} %get-tuple-element.61), channel_id=1, source_target_pairs={{0,12},{1,13},{2,14},{3,15},{4,0},{5,1},{6,2},{7,3},{8,4},{9,5},{1... | collective-permute-start | bytes 3538952 | tf_op jit(solution)/shard_map/ppermute | solution.py:273
  138.6 39.3 %collective-permute-start.28 = (f32[4,2,48,768]{3,2,1,0:T(8,128)}, f32[4,2,48,768]{3,2,1,0:T(8,128)}, u32[]{:S(2)}, u32[]{:S(2)}) collective-permute-start(f32[4,2,48,768]{3,2,1,0:T(8,128)} %get-tuple-element.84), channel_id=1, source_target_pairs={{0,1},{1,2},{2,3},{3,0},{4,5},{5,6},{6,7},{7,4},{8,9},{9,10},{10,1... | collective-permute-start | bytes 3538952 | tf_op jit(solution)/shard_map/ppermute | solution.py:272
  138.8 39.1 %collective-permute-start.29 = (f32[4,2,48,768]{3,2,1,0:T(8,128)}, f32[4,2,48,768]{3,2,1,0:T(8,128)}, u32[]{:S(2)}, u32[]{:S(2)}) collective-permute-start(f32[4,2,48,768]{3,2,1,0:T(8,128)} %get-tuple-element.85), channel_id=1, source_target_pairs={{0,3},{1,0},{2,1},{3,2},{4,7},{5,4},{6,5},{7,6},{8,11},{9,8},{10,9... | collective-permute-start | bytes 3538952 | tf_op jit(solution)/shard_map/ppermute | solution.py:273
  141.9 30.2 %copy-start = (f32[2,2,48,768]{3,2,1,0:T(8,128)}, f32[2,2,48,768]{3,2,1,0:T(8,128)S(1)}, u32[]{:S(2)}) copy-start(f32[2,2,48,768]{3,2,1,0:T(8,128)S(1)} %collective-permute-done.21.refs_2_.p2) | copy-start | bytes 1769476
  141.9 30.2 %collective-permute-start.22 = (f32[2,2,48,768]{3,2,1,0:T(8,128)}, f32[2,2,48,768]{3,2,1,0:T(8,128)}, u32[]{:S(2)}, u32[]{:S(2)}) collective-permute-start(f32[2,2,48,768]{3,2,1,0:T(8,128)} %get-tuple-element.71), channel_id=1, source_target_pairs={{0,3},{1,0},{2,1},{3,2},{4,7},{5,4},{6,5},{7,6},{8,11},{9,8},{10,9... | collective-permute-start | bytes 1769480 | tf_op jit(solution)/shard_map/ppermute | solution.py:276
  174.6 15.8 %collective-permute-start.23 = (f32[2,2,48,768]{3,2,1,0:T(8,128)}, f32[2,2,48,768]{3,2,1,0:T(8,128)S(1)}, u32[]{:S(2)}, u32[]{:S(2)}) collective-permute-start(f32[2,2,48,768]{3,2,1,0:T(8,128)} %get-tuple-element.72), channel_id=1, source_target_pairs={{0,4},{1,5},{2,6},{3,7},{4,8},{5,9},{6,10},{7,11},{8,12},{9,13},{1... | collective-permute-start | bytes 1769480 | tf_op jit(solution)/shard_map/ppermute | solution.py:276
  174.6 16.5 %collective-permute-start.24 = (f32[2,2,48,768]{3,2,1,0:T(8,128)}, f32[2,2,48,768]{3,2,1,0:T(8,128)}, u32[]{:S(2)}, u32[]{:S(2)}) collective-permute-start(f32[2,2,48,768]{3,2,1,0:T(8,128)} %get-tuple-element.73), channel_id=1, source_target_pairs={{0,12},{1,13},{2,14},{3,15},{4,0},{5,1},{6,2},{7,3},{8,4},{9,5},{1... | collective-permute-start | bytes 1769480 | tf_op jit(solution)/shard_map/ppermute | solution.py:276
  180.4 22.2 %collective-permute-start.30 = (f32[2,2,48,768]{3,2,1,0:T(8,128)}, f32[2,2,48,768]{3,2,1,0:T(8,128)}, u32[]{:S(2)}, u32[]{:S(2)}) collective-permute-start(f32[2,2,48,768]{3,2,1,0:T(8,128)} %get-tuple-element.88), channel_id=1, source_target_pairs={{0,1},{1,2},{2,3},{3,0},{4,5},{5,6},{6,7},{7,4},{8,9},{9,10},{10,1... | collective-permute-start | bytes 1769480 | tf_op jit(solution)/shard_map/ppermute | solution.py:276
  181.5 21.1 %collective-permute-start.31 = (f32[2,2,48,768]{3,2,1,0:T(8,128)}, f32[2,2,48,768]{3,2,1,0:T(8,128)}, u32[]{:S(2)}, u32[]{:S(2)}) collective-permute-start(f32[2,2,48,768]{3,2,1,0:T(8,128)} %get-tuple-element.89), channel_id=1, source_target_pairs={{0,3},{1,0},{2,1},{3,2},{4,7},{5,4},{6,5},{7,6},{8,11},{9,8},{10,9... | collective-permute-start | bytes 1769480 | tf_op jit(solution)/shard_map/ppermute | solution.py:276
  190.4 0.8 copy-start.4
  194.1 25.1 %collective-permute-start.25 = (f32[4,48,768]{2,1,0:T(8,128)}, f32[4,48,768]{2,1,0:T(8,128)S(1)}, u32[]{:S(2)}, u32[]{:S(2)}) collective-permute-start(f32[4,48,768]{2,1,0:T(8,128)} %get-tuple-element.80), channel_id=1, source_target_pairs={{0,1},{1,2},{2,3},{3,0},{4,5},{5,6},{6,7},{7,4},{8,9},{9,10},{10,1... | collective-permute-start | bytes 1769480 | tf_op jit(solution)/shard_map/ppermute | solution.py:286
  199.9 25.3 %collective-permute-start.26 = (f32[4,48,768]{2,1,0:T(8,128)}, f32[4,48,768]{2,1,0:T(8,128)}, u32[]{:S(2)}, u32[]{:S(2)}) collective-permute-start(f32[4,48,768]{2,1,0:T(8,128)} %get-tuple-element.81), channel_id=1, source_target_pairs={{0,2},{1,3},{2,0},{3,1},{4,6},{5,7},{6,4},{7,5},{8,10},{9,11},{10,... | collective-permute-start | bytes 1769480 | tf_op jit(solution)/shard_map/ppermute | solution.py:286
  199.9 25.3 %collective-permute-start.27 = (f32[4,48,768]{2,1,0:T(8,128)}, f32[4,48,768]{2,1,0:T(8,128)}, u32[]{:S(2)}, u32[]{:S(2)}) collective-permute-start(f32[4,48,768]{2,1,0:T(8,128)} %get-tuple-element.82), channel_id=1, source_target_pairs={{0,3},{1,0},{2,1},{3,2},{4,7},{5,4},{6,5},{7,6},{8,11},{9,8},{10,9... | collective-permute-start | bytes 1769480 | tf_op jit(solution)/shard_map/ppermute | solution.py:286
  205.5 19.7 %collective-permute-start.32 = (f32[4,48,768]{2,1,0:T(8,128)}, f32[4,48,768]{2,1,0:T(8,128)}, u32[]{:S(2)}, u32[]{:S(2)}) collective-permute-start(f32[4,48,768]{2,1,0:T(8,128)} %get-tuple-element.96), channel_id=1, source_target_pairs={{0,4},{1,5},{2,6},{3,7},{4,8},{5,9},{6,10},{7,11},{8,12},{9,13},{1... | collective-permute-start | bytes 1769480 | tf_op jit(solution)/shard_map/ppermute | solution.py:286
  205.5 28.8 %collective-permute-start.33 = (f32[4,48,768]{2,1,0:T(8,128)}, f32[4,48,768]{2,1,0:T(8,128)}, u32[]{:S(2)}, u32[]{:S(2)}) collective-permute-start(f32[4,48,768]{2,1,0:T(8,128)} %get-tuple-element.97), channel_id=1, source_target_pairs={{0,8},{1,9},{2,10},{3,11},{4,12},{5,13},{6,14},{7,15},{8,0},{9,1},... | collective-permute-start | bytes 1769480 | tf_op jit(solution)/shard_map/ppermute | solution.py:286
  219.2 15.1 %copy-start.2 = (f32[4,48,768]{2,1,0:T(8,128)}, f32[4,48,768]{2,1,0:T(8,128)S(1)}, u32[]{:S(2)}) copy-start(f32[4,48,768]{2,1,0:T(8,128)S(1)} %collective-permute-done.25.refs_1_) | copy-start | bytes 1769476
  219.2 15.1 %collective-permute-start.34 = (f32[4,48,768]{2,1,0:T(8,128)}, f32[4,48,768]{2,1,0:T(8,128)}, u32[]{:S(2)}, u32[]{:S(2)}) collective-permute-start(f32[4,48,768]{2,1,0:T(8,128)} %get-tuple-element.98), channel_id=1, source_target_pairs={{0,12},{1,13},{2,14},{3,15},{4,0},{5,1},{6,2},{7,3},{8,4},{9,5},{1... | collective-permute-start | bytes 1769480 | tf_op jit(solution)/shard_map/ppermute | solution.py:286

commit v8 on v7

v8 whole, which is shorter than its diff:
```python
import functools

import jax
import jax.numpy as jnp
import numpy as np
from jax import lax
from jax.experimental import pallas as pl
from jax.experimental.pallas import tpu as pltpu
from jax.sharding import PartitionSpec as P

SIDE = 4
VMEM = 64 * 1024 * 1024 - 256 * 1024
WIDTH = 256
LIGHT = pl.CostEstimate(flops=0, bytes_accessed=0, transcendentals=0)
def hops(count, steps):
    pairs = []
    for i in range(count):
        stride, delta = steps(i)
        at = (i // stride) % SIDE
        pairs.append((i, i + ((at + delta) % SIDE - at) * stride))
    return pairs


Z_STEPS = [hops(8, lambda i, d=d: (2, -d if i % 2 else d)) for d in (1, -1, 2)]
SWAP = [(i, i ^ 1) for i in range(8)]
BOTH = ("vb", "ob")
NEAR = {d: hops(128, lambda i, d=d: (1 if i // 16 % 2 else SIDE, d)) for d in (1, -1)}
FAR = {d: hops(128, lambda i, d=d: (SIDE if i // 16 % 2 else 1, d)) for d in (1, 2, -1)}


ORDER = [(2, 0), (2, 1)] + [(2, 2), (2, 3)] + [(1, 2), (1, 3)] + [(3, 0), (3, 1)]
ORDER += [(1, 0), (1, 1)] + [(3, 2), (3, 3)] + [(0, k) for k in range(SIDE)]


SOURCES = [(dz, dc) for dz in (0, -1, 1, 2) for dc in (0, 1)]


def place_table():
    table = np.zeros((8, 16, 16), np.int32)
    for vb in range(8):
        for ob in range(16):
            for a, (dz, dc) in enumerate(SOURCES):
                core = (vb % 2) ^ dc
                source = 2 * ((vb // 2 + (-dz if core else dz)) % SIDE) + core
                for h in range(2):
                    to = 2 * source + h
                    rel = (to // SIDE - ob // SIDE) % SIDE, (to - ob) % SIDE
                    table[vb, ob, 2 * a + h] = ORDER.index(rel[::-1] if vb % 2 else rel)
    return table


PLACES = place_table()
LEADS = (2, 2, 2, 2, 2, 2, 4)


def product_kernel(first, place, sizes, origin, *refs):
    pieces, v_ref, outs, (a_all, v_all) = refs[:8], refs[8], refs[-9:-2], refs[-2:]
    rows = pieces[0].shape[1] // 2
    depth = pieces[0].shape[2]
    for a, piece in enumerate(pieces):
        for h in range(2):
            block = piece[0, h * rows : (h + 1) * rows]
            hi = block.astype(jnp.bfloat16)
            at = pl.ds(pl.multiple_of(place[2 * a + h] * rows, rows), rows)
            a_all[at, 0:depth] = hi
            a_all[at, depth : 2 * depth] = (block - hi.astype(jnp.float32)).astype(jnp.bfloat16)
            a_all[at, 2 * depth : 3 * depth] = hi
    size = sizes[first + pl.program_id(0)]
    shape = v_ref.shape[1:]
    p = origin[0] + lax.broadcasted_iota(jnp.int32, shape, 0)
    q = origin[1] + lax.broadcasted_iota(jnp.int32, shape, 1)
    v = jnp.where((p < size) & (q < size), v_ref[0], 0.0)
    hi = v.astype(jnp.bfloat16)
    v_all[0:depth] = hi
    v_all[depth : 2 * depth] = hi
    v_all[2 * depth : 3 * depth] = (v - hi.astype(jnp.float32)).astype(jnp.bfloat16)
    blocks = [(out, k) for lead, out in zip(LEADS, outs) for k in range(lead)]
    for at in range(0, len(blocks), SIDE):
        acc = jnp.dot(a_all[rows * at : rows * (at + SIDE)], v_all[...], preferred_element_type=jnp.float32)
        for i, (out, k) in enumerate(blocks[at : at + SIDE]):
            out[k, 0] = acc[rows * i : rows * (i + 1)]


def product(pieces, ovov, first, count, place, sizes, origin, after):
    rows2, depth = pieces[0][0].shape[1:]
    rows = rows2 // 2
    cols = ovov.shape[2]
    return pl.pallas_call(
        functools.partial(product_kernel, first),
        grid_spec=pltpu.PrefetchScalarGridSpec(
            num_scalar_prefetch=3,
            grid=(count,),
            in_specs=[pl.BlockSpec((1, rows2, depth), lambda g, *_, at=at: (at + g, 0, 0)) for _, at in pieces]
            + [pl.BlockSpec((1, depth, cols), lambda g, *_: (first + g, 0, 0))]
            + [pl.BlockSpec(memory_space=pl.ANY)] * len(after),
            out_specs=[pl.BlockSpec((lead, 1, rows, cols), lambda g, *_: (0, g, 0, 0)) for lead in LEADS],
            scratch_shapes=[
                pltpu.VMEM((16 * rows, 3 * depth), jnp.bfloat16),
                pltpu.VMEM((3 * depth, cols), jnp.bfloat16),
            ],
        ),
        out_shape=[jax.ShapeDtypeStruct((lead, count, rows, cols), jnp.float32) for lead in LEADS],
        compiler_params=pltpu.CompilerParams(vmem_limit_bytes=VMEM),
        cost_estimate=LIGHT,
        name="product",
    )(place, sizes, origin, *[piece for piece, _ in pieces], ovov, *after)


def tie_kernel(*refs):
    pass


def tie(values, after):
    anywhere = pl.BlockSpec(memory_space=pl.ANY)
    return pl.pallas_call(
        tie_kernel,
        in_specs=[anywhere] * (len(values) + len(after)),
        out_specs=[anywhere] * len(values),
        out_shape=[jax.ShapeDtypeStruct(v.shape, v.dtype) for v in values],
        input_output_aliases={i: i for i in range(len(values))},
        compiler_params=pltpu.CompilerParams(vmem_limit_bytes=VMEM),
        cost_estimate=LIGHT,
        name="tie",
    )(*values, *after)


def add_kernel(up, down, recv_p, recv_m, *refs):
    refs[-2][...] = up[...] + recv_p[...]
    refs[-1][...] = down[...] + recv_m[...]


def add_far(up, down, recv_p, recv_m, after):
    lead, count, rows, cols = up.shape
    spec = pl.BlockSpec((lead, 1, rows, cols), lambda g: (0, g, 0, 0))
    return pl.pallas_call(
        add_kernel,
        grid=(count,),
        in_specs=[spec] * 4 + [pl.BlockSpec(memory_space=pl.ANY)] * len(after),
        out_specs=[spec] * 2,
        out_shape=[jax.ShapeDtypeStruct(up.shape, jnp.float32)] * 2,
        compiler_params=pltpu.CompilerParams(vmem_limit_bytes=VMEM),
        cost_estimate=LIGHT,
        name="add_far",
    )(up, down, recv_p, recv_m, *after)


def own_kernel(own, n1, n2, p2, m2, *refs):
    outs = refs[-4:]
    outs[0][0] = own[0, 0] + (p2[0, 0] + n2[0, 0])
    outs[1][0] = own[1, 0] + (p2[1, 0] + n2[1, 0])
    outs[2][0] = own[2, 0] + (m2[0, 0] + n1[0, 0])
    outs[3][0] = own[3, 0] + (m2[1, 0] + n1[1, 0])


def add_own(own, n1, n2, p2, m2, at, total, into):
    count, rows, cols = own.shape[1:]

    def spec(lead):
        return pl.BlockSpec((lead, 1, rows, cols), lambda g: (0, g, 0, 0))

    return pl.pallas_call(
        own_kernel,
        grid=(count,),
        in_specs=[spec(4)] + [spec(2)] * 4
        + [pl.BlockSpec(memory_space=pl.ANY)] * len(into),
        out_specs=[pl.BlockSpec((1, rows, cols), lambda g: (at + g, 0, 0))] * 4,
        out_shape=[jax.ShapeDtypeStruct((total, rows, cols), jnp.float32)] * 4,
        input_output_aliases={5 + i: i for i in range(len(into))},
        compiler_params=pltpu.CompilerParams(vmem_limit_bytes=VMEM),
        cost_estimate=LIGHT,
        name="add_own",
    )(own, n1, n2, p2, m2, *into)


def finish_kernel(sizes, origin, a, b, c, d, out):
    rows, irreps, cols = out.shape
    row = origin[0] + lax.broadcasted_iota(jnp.int32, (rows, cols), 0)
    for g in range(irreps):
        out[:, g, :] = jnp.where(row < sizes[g], (a[g] + b[g]) + (c[g] + d[g]), 0.0)


def finish(parts, row_sizes, origin):
    irreps, rows, cols = parts[0].shape
    part = pl.BlockSpec((irreps, rows, WIDTH), lambda c, *_: (0, 0, c))
    return pl.pallas_call(
        finish_kernel,
        grid_spec=pltpu.PrefetchScalarGridSpec(
            num_scalar_prefetch=2,
            grid=(cols // WIDTH,),
            in_specs=[part] * 4,
            out_specs=pl.BlockSpec((rows, irreps, WIDTH), lambda c, *_: (0, 0, c)),
        ),
        out_shape=jax.ShapeDtypeStruct((rows, irreps, cols), jnp.float32),
        compiler_params=pltpu.CompilerParams(vmem_limit_bytes=VMEM),
        cost_estimate=LIGHT,
        name="finish",
    )(row_sizes, origin, *parts)


GROUPS = ((0, 4), (4, 4))


def local(amplitudes, ovov, row_sizes, pair_sizes):
    ob = lax.axis_index("ob")
    vb = lax.axis_index("vb")
    local_rows, irreps, _ = amplitudes.shape
    obs = lax.axis_size("ob")
    depth, cols = ovov.shape[1:]
    out_rows = local_rows * lax.axis_size("vb")
    place = lax.dynamic_slice(jnp.asarray(PLACES), (vb, ob, 0), (1, 1, 16)).reshape(16)
    origin = jnp.stack([ob * depth, vb * cols]).astype(jnp.int32)

    mine = jnp.transpose(amplitudes.reshape(local_rows, irreps, obs, depth), (2, 0, 1, 3))
    mine = mine.reshape(obs, local_rows * irreps, depth)
    mine = lax.all_to_all(mine, "ob", split_axis=0, concat_axis=0, tiled=True)
    mine = jnp.transpose(mine.reshape(obs * local_rows, irreps, depth), (1, 0, 2))
    mine_swapped = lax.ppermute(mine, "vb", SWAP)

    gathered, landed = [], []
    for first, count in GROUPS:
        held = mine[first : first + count]
        if landed:
            (held,) = tie([held], landed)
        landed = [lax.ppermute(held, "vb", steps) for steps in Z_STEPS]
        pieces = [(mine, first), (mine_swapped, first)]
        for piece in landed:
            pieces += [(piece, 0), (lax.ppermute(piece, "vb", SWAP), 0)]
        gathered.append(pieces)

    swapped = [piece for piece, _ in gathered[-1][3::2]]
    sums, added = [], []
    for (first, count), pieces in zip(GROUPS, gathered):
        far_p, far_m, near_p, near_m, up, down, own = product(
            pieces, ovov, first, count, place, pair_sizes, origin, added
        )
        far_p = lax.ppermute(far_p, BOTH, NEAR[1])
        far_m = lax.ppermute(far_m, BOTH, NEAR[-1])
        near_p = lax.ppermute(near_p, BOTH, NEAR[1])
        near_m = lax.ppermute(near_m, BOTH, NEAR[-1])
        added = add_far(up, down, far_p, far_m, sums[-1][1:] if sums else swapped)
        sums.append((own, near_p, near_m, lax.ppermute(added[0], BOTH, NEAR[1]), lax.ppermute(added[1], BOTH, NEAR[-1])))

    four = []
    for (first, _), group in zip(GROUPS, sums):
        four = add_own(*group, first, irreps, four)
    parts = [four[0]] + [lax.ppermute(four[k], BOTH, FAR[d]) for k, d in ((1, 1), (2, 2), (3, -1))]
    origin = jnp.stack([ob * out_rows, vb * cols]).astype(jnp.int32)
    return finish(parts, row_sizes, origin)


def solution(mesh):
    placed = (P(("vb", "ob"), None, None), P(None, "ob", "vb"), P(), P())
    return jax.shard_map(
        local, mesh=mesh, in_specs=placed, out_specs=P("ob", None, "vb"), check_vma=False
    )
```

time: 241 us -> 226 us (0.938)
  starting transfers between devices: 49.2 us -> 31.6 us
  waiting for transfers between devices: 101 us -> 112 us
  Pallas kernels: 55.2 us -> 48.2 us
    ppermute x22 -> x15, starting transfers between devices: 38.2 us -> 21.3 us  [the longest x2 5.16 us: local(): near_m = lax.ppermute(near_m, BOTH, NEAR[-1])]
    ppermute x22 -> x15, waiting for transfers between devices: 66.5 us -> 72.6 us  [the longest x3 26.5 us: local(): lax.ppermute(four[k], BOTH, FAR[d])]
    pallas_call x7 -> x5, Pallas kernels: 45.2 us -> 39.6 us  [the longest x2 24.9 us: product(): pl.pallas_call(functools.partial(product_kernel, first), grid_spec=pltpu....]
    ppermute x6, waiting for transfers between devices: 34 us -> 37.6 us  [local(): landed = [lax.ppermute(held, 'vb', steps) for steps in Z_STEPS]]
    pallas_call x4 -> x2, Pallas kernels: 10 us -> 8.62 us  [add_far(): pl.pallas_call(add_kernel, grid=(count,), in_specs=[spec] * 4 + [pl.Block...]
  transfers between devices with their start and end apart: 35 -> 28, of which waited for: 10 -> 14; matrix products, arithmetic and copies ran while one was open for 1% -> 2% of each run, Pallas kernels for 21% -> 17%
where the time goes in v8:
time: 226 us; the launch traced here: 225 us
  waiting for transfers between devices  112 us (50%)
  Pallas kernels  48.2 us (21%)
  starting transfers between devices  31.6 us (14%)
  blocking collectives  25.4 us (11%)
  local copies, waits for them, and re-layouts  6.45 us (3%)
    ppermute x6, waiting for transfers between devices, local(): landed = [lax.ppermute(held, 'vb', steps) for steps in Z_STEPS]  37.6 us
    ppermute x3, waiting for transfers between devices, local(): lax.ppermute(four[k], BOTH, FAR[d])  26.5 us
    all_to_all x1, blocking collectives, local(): mine = lax.all_to_all(mine, 'ob', split_axis=0, concat_axis=0, tiled=True)  25.4 us
    pallas_call x2, Pallas kernels, product(): pl.pallas_call(functools.partial(product_kernel, first), grid_spec=pltpu....  24.9 us
    ppermute x2, waiting for transfers between devices, local(): lax.ppermute(added[0], BOTH, NEAR[1])  21.9 us
    ppermute x2, waiting for transfers between devices, local(): far_p = lax.ppermute(far_p, BOTH, NEAR[1])  21.2 us
    pallas_call x2, Pallas kernels, add_own(): pl.pallas_call(own_kernel, grid=(count,), in_specs=[spec(4)] + [spec(2)]...  9.78 us
    pallas_call x2, Pallas kernels, add_far(): pl.pallas_call(add_kernel, grid=(count,), in_specs=[spec] * 4 + [pl.Block...  8.62 us
  transfers between devices with their start and end apart: 28, of which 14 were waited for; matrix products, arithmetic and copies ran while one was open for 2% of the time, Pallas kernels for 17%

profile of v8, /device:TPU:0, one launch (start us, length us, event | category | flops | bytes accessed | tf_op | source)
XLA Modules:
  0.0 225.0 jit_solution(15229074310494436227)
XLA Ops:
  0.0 1.5 copy.18
  1.5 0.4 copy.20
  1.9 25.4 %all_to_all.5 = f32[16,48,384]{2,1,0:T(8,128)S(1)} all-to-all(f32[16,48,384]{2,1,0:T(8,128)S(1)} %bitcast.21), channel_id=1, replica_groups=mesh['vb'=8,'ob'=16] {'ob'}, dimensions={0} | all-to-all | bytes 2359296 | tf_op jit(solution)/shard_map/all_to_all | solution.py:215
  27.2 1.2 copy.19
  28.5 2.1 fusion
  30.6 1.9 collective-permute-start.1
  32.5 2.1 collective-permute-start.2
  34.7 1.9 collective-permute-start.3
  36.5 9.9 %collective-permute-done.1.refs_1_.refs_2_ = f32[4,96,384]{2,1,0:T(8,128)} collective-permute-done((f32[4,96,384]{2,1,0:T(8,128)S(1)}, f32[4,96,384]{2,1,0:T(8,128)}, u32[]{:S(2)}, u32[]{:S(2)}) %collective-permute-start.1) | collective-permute-done | bytes 589856 | tf_op jit(solution)/shard_map/ppermute | solution.py:224
  46.4 14.2 %collective-permute-done.2.refs_2_.refs_4_ = f32[4,96,384]{2,1,0:T(8,128)} collective-permute-done((f32[4,96,384]{2,1,0:T(8,128)S(1)}, f32[4,96,384]{2,1,0:T(8,128)}, u32[]{:S(2)}, u32[]{:S(2)}) %collective-permute-start.2) | collective-permute-done | bytes 589856 | tf_op jit(solution)/shard_map/ppermute | solution.py:224
  60.5 2.1 collective-permute-done.3.refs_3_.refs_6_
  62.7 1.2 collective-permute-start.10
  63.9 0.5 collective-permute-start.12
  64.4 2.1 collective-permute-start.6
  66.5 0.6 pad_add_fusion.1.origin
  67.1 1.2 dynamic-slice_bitcast_fusion.place
  68.3 11.5 %collective-permute-done.4.refs_2_ = f32[4,96,384]{2,1,0:T(8,128)} collective-permute-done((f32[4,96,384]{2,1,0:T(8,128)}, f32[4,96,384]{2,1,0:T(8,128)}, u32[]{:S(2)}, u32[]{:S(2)}) %collective-permute-start.4) | collective-permute-done | bytes 589856 | tf_op jit(solution)/shard_map/ppermute | solution.py:224
  79.8 12.4 %product.2 = (f32[2,4,48,768]{3,2,1,0:T(8,128)}, f32[2,4,48,768]{3,2,1,0:T(8,128)}, f32[2,4,48,768]{3,2,1,0:T(8,128)}, f32[2,4,48,768]{3,2,1,0:T(8,128)}, f32[2,...) custom-call(s32[16]{0:T(128)} %dynamic-slice_bitcast_fusion.place, s32[8]{0:T(128)} %sizes.4, ...), custom_call_target="tpu_custom_call" | custom-call | tf_op jit(solution)/shard_map/product/pallas_call | solution.py:88
  92.2 0.6 collective-permute-start.13
  92.8 2.7 %collective-permute-start.14 = (f32[2,4,48,768]{3,2,1,0:T(8,128)}, f32[2,4,48,768]{3,2,1,0:T(8,128)}, u32[]{:S(2)}, u32[]{:S(2)}) collective-permute-start(f32[2,4,48,768]{3,2,1,0:T(8,128)} %get-tuple-element.34), channel_id=1, source_target_pairs={{0,12},{1,13},{2,14},{3,15},{4,0},{5,1},{6,2},{7,3},{8,4},{9,5},{1... | collective-permute-start | bytes 3538952 | tf_op jit(solution)/shard_map/ppermute | solution.py:237
  95.6 0.5 collective-permute-start.9
  96.1 1.8 collective-permute-done.7.refs_1_.refs_5_
  98.0 3.2 %collective-permute-start.20 = (f32[2,4,48,768]{3,2,1,0:T(8,128)}, f32[2,4,48,768]{3,2,1,0:T(8,128)}, u32[]{:S(2)}, u32[]{:S(2)}) collective-permute-start(f32[2,4,48,768]{3,2,1,0:T(8,128)} %get-tuple-element.45), channel_id=1, source_target_pairs={{0,12},{1,13},{2,14},{3,15},{4,0},{5,1},{6,2},{7,3},{8,4},{9,5},{1... | collective-permute-start | bytes 3538952 | tf_op jit(solution)/shard_map/ppermute | solution.py:239
  101.1 8.9 %collective-permute-done.13.recv_p = f32[2,4,48,768]{3,2,1,0:T(8,128)} collective-permute-done((f32[2,4,48,768]{3,2,1,0:T(8,128)}, f32[2,4,48,768]{3,2,1,0:T(8,128)}, u32[]{:S(2)}, u32[]{:S(2)}) %collective-permute-start.13) | collective-permute-done | bytes 1179680 | tf_op jit(solution)/shard_map/ppermute | solution.py:236
  110.0 4.3 %add_far.2 = (f32[2,4,48,768]{3,2,1,0:T(8,128)}, f32[2,4,48,768]{3,2,1,0:T(8,128)}) custom-call(f32[2,4,48,768]{3,2,1,0:T(8,128)} %get-tuple-element.31.up, f32[2,4,48,768]{3,2,1,0:T(8,128)} %get-tuple-element.32.down, f32[2,4,48,768]{3,2,1,0:T(8,128)} %collective-permute-done.13.recv_p, f32[2,4,48,768]{3,2,1,0:T(8,128)} %collective-permute-done.14.recv_m, ...), custom_call_target="tpu_custom_call" | custom-call | tf_op jit(solution)/shard_map/add_far/pallas_call | solution.py:135
  114.3 12.4 %product.3 = (f32[2,4,48,768]{3,2,1,0:T(8,128)}, f32[2,4,48,768]{3,2,1,0:T(8,128)}, f32[2,4,48,768]{3,2,1,0:T(8,128)}, f32[2,4,48,768]{3,2,1,0:T(8,128)}, f32[2,...) custom-call(s32[16]{0:T(128)} %dynamic-slice_bitcast_fusion.place, s32[8]{0:T(128)} %sizes.4, ...), custom_call_target="tpu_custom_call" | custom-call | tf_op jit(solution)/shard_map/product/pallas_call | solution.py:88
  126.9 1.3 collective-permute-start.21
  128.3 2.0 collective-permute-start.18
  130.2 1.9 collective-permute-start.22
  132.3 12.3 %collective-permute-done.17.recv_p = f32[2,4,48,768]{3,2,1,0:T(8,128)} collective-permute-done((f32[2,4,48,768]{3,2,1,0:T(8,128)}, f32[2,4,48,768]{3,2,1,0:T(8,128)}, u32[]{:S(2)}, u32[]{:S(2)}) %collective-permute-start.17) | collective-permute-done | bytes 1179680 | tf_op jit(solution)/shard_map/ppermute | solution.py:236
  144.6 2.0 collective-permute-start.16
  146.6 10.6 %collective-permute-done.21.refs_2_.p2 = f32[2,4,48,768]{3,2,1,0:T(8,128)} collective-permute-done((f32[2,4,48,768]{3,2,1,0:T(8,128)}, f32[2,4,48,768]{3,2,1,0:T(8,128)}, u32[]{:S(2)}, u32[]{:S(2)}) %collective-permute-start.21) | collective-permute-done | bytes 1179680 | tf_op jit(solution)/shard_map/ppermute | solution.py:241
  157.2 1.4 collective-permute-done.22.refs_3_.m2
  158.6 4.3 %add_far.3 = (f32[2,4,48,768]{3,2,1,0:T(8,128)}, f32[2,4,48,768]{3,2,1,0:T(8,128)}) custom-call(f32[2,4,48,768]{3,2,1,0:T(8,128)} %get-tuple-element.40.up, f32[2,4,48,768]{3,2,1,0:T(8,128)} %get-tuple-element.41.down, f32[2,4,48,768]{3,2,1,0:T(8,128)} %collective-permute-done.17.recv_p, f32[2,4,48,768]{3,2,1,0:T(8,128)} %collective-permute-done.18.recv_m, ...), custom_call_target="tpu_custom_call" | custom-call | tf_op jit(solution)/shard_map/add_far/pallas_call | solution.py:135
  162.9 2.0 collective-permute-start.23
  164.9 1.2 collective-permute-start.24
  166.2 4.9 %add_own.2 = (f32[8,48,768]{2,1,0:T(8,128)}, f32[8,48,768]{2,1,0:T(8,128)}, f32[8,48,768]{2,1,0:T(8,128)}, f32[8,48,768]{2,1,0:T(8,128)}) custom-call(f32[4,4,48,768]{3,2,1,0:T(8,128)} %get-tuple-element.48.own, f32[2,4,48,768]{3,2,1,0:T(8,128)} %collective-permute-done.19.refs_0_.n1, f32[2,4,48,768]{3,2,1,0:T(8,128)} %collective-permute-done.20.refs_1_.n2, ...), custom_call_target="tpu_custom_call" | custom-call | tf_op jit(solution)/shard_map/add_own/pallas_call | solution.py:161
  171.1 0.2 collective-permute-done.16.n2
  171.3 11.2 %collective-permute-done.23.p2 = f32[2,4,48,768]{3,2,1,0:T(8,128)} collective-permute-done((f32[2,4,48,768]{3,2,1,0:T(8,128)}, f32[2,4,48,768]{3,2,1,0:T(8,128)}, u32[]{:S(2)}, u32[]{:S(2)}) %collective-permute-start.23) | collective-permute-done | bytes 1179680 | tf_op jit(solution)/shard_map/ppermute | solution.py:241
  182.5 1.4 collective-permute-done.24.m2
  183.9 4.9 %add_own.3 = (f32[8,48,768]{2,1,0:T(8,128)}, f32[8,48,768]{2,1,0:T(8,128)}, f32[8,48,768]{2,1,0:T(8,128)}, f32[8,48,768]{2,1,0:T(8,128)}) custom-call(f32[4,4,48,768]{3,2,1,0:T(8,128)} %get-tuple-element.37.own, f32[2,4,48,768]{3,2,1,0:T(8,128)} %collective-permute-done.15.n1, ...), custom_call_target="tpu_custom_call", output_to_operand_aliasing={{0}: (5, {}), {1}: (6, {}), {2}: (7, {}), {3}: (8, {})} | custom-call | tf_op jit(solution)/shard_map/add_own/pallas_call | solution.py:161
  188.8 0.5 collective-permute-start.25
  189.3 2.3 %collective-permute-start.26 = (f32[8,48,768]{2,1,0:T(8,128)}, f32[8,48,768]{2,1,0:T(8,128)}, u32[]{:S(2)}, u32[]{:S(2)}) collective-permute-start(f32[8,48,768]{2,1,0:T(8,128)} %get-tuple-element.55), channel_id=1, source_target_pairs={{0,2},{1,3},{2,0},{3,1},{4,6},{5,7},{6,4},{7,5},{8,10},{9,11},{10,... | collective-permute-start | bytes 3538952 | tf_op jit(solution)/shard_map/ppermute | solution.py:246
  191.6 1.4 collective-permute-start.27
  192.9 0.6 pad_add_fusion.origin
  193.5 25.6 %collective-permute-done.25.b = f32[8,48,768]{2,1,0:T(8,128)} collective-permute-done((f32[8,48,768]{2,1,0:T(8,128)}, f32[8,48,768]{2,1,0:T(8,128)}, u32[]{:S(2)}, u32[]{:S(2)}) %collective-permute-start.25) | collective-permute-done | bytes 1179680 | tf_op jit(solution)/shard_map/ppermute | solution.py:246
  219.2 0.9 collective-permute-done.27.d
  220.1 5.0 %finish.1 = f32[48,8,768]{2,1,0:T(8,128)} custom-call(s32[8]{0:T(128)} %sizes.5, s32[2]{0:T(128)} %pad_add_fusion.origin, f32[8,48,768]{2,1,0:T(8,128)} %get-tuple-element.53.a, f32[8,48,768]{2,1,0:T(8,128)} %collective-permute-done.25.b, f32[8,48,768]{2,1,0:T(8,128)} %collective-permute-done.26.c, f32[8,48,768]{2,1,0:T(8,128)} %collective-permute-done.27.d), custom_call_target="tpu_custom_call" | custom-call | tf_op jit(solution)/shard_map/finish/pallas_call | solution.py:185
  (24 shorter events, 0.4 us)
Async XLA Ops:
  28.5 35.9 %collective-permute-start = (f32[8,96,384]{2,1,0:T(8,128)}, f32[8,96,384]{2,1,0:T(8,128)}, u32[]{:S(2)}, u32[]{:S(2)}) collective-permute-start(f32[8,96,384]{2,1,0:T(8,128)} %bitcast.19.refs_0_), channel_id=1, source_target_pairs={{0,16},{16,0},{32,48},{48,32},{64,80},{80,64},{96,112},{112,96},{1... | collective-permute-start | bytes 3538952 | tf_op jit(solution)/shard_map/ppermute | solution.py:217
  30.6 15.8 %collective-permute-start.1 = (f32[4,96,384]{2,1,0:T(8,128)S(1)}, f32[4,96,384]{2,1,0:T(8,128)}, u32[]{:S(2)}, u32[]{:S(2)}) collective-permute-start(f32[4,96,384]{2,1,0:T(8,128)S(1)} %get-tuple-element.57), channel_id=1, source_target_pairs={{0,32},{16,112},{32,64},{48,16},{64,96},{80,48},{96,0},{112,80},{1... | collective-permute-start | bytes 1769480 | tf_op jit(solution)/shard_map/ppermute | solution.py:224
  32.5 28.0 %collective-permute-start.2 = (f32[4,96,384]{2,1,0:T(8,128)S(1)}, f32[4,96,384]{2,1,0:T(8,128)}, u32[]{:S(2)}, u32[]{:S(2)}) collective-permute-start(f32[4,96,384]{2,1,0:T(8,128)S(1)} %get-tuple-element.57), channel_id=1, source_target_pairs={{0,96},{16,48},{32,0},{48,80},{64,32},{80,112},{96,64},{112,16},{1... | collective-permute-start | bytes 1769480 | tf_op jit(solution)/shard_map/ppermute | solution.py:224
  34.7 28.0 %collective-permute-start.3 = (f32[4,96,384]{2,1,0:T(8,128)S(1)}, f32[4,96,384]{2,1,0:T(8,128)}, u32[]{:S(2)}, u32[]{:S(2)}) collective-permute-start(f32[4,96,384]{2,1,0:T(8,128)S(1)} %get-tuple-element.57), channel_id=1, source_target_pairs={{0,64},{16,80},{32,96},{48,112},{64,0},{80,16},{96,32},{112,48},{1... | collective-permute-start | bytes 1769480 | tf_op jit(solution)/shard_map/ppermute | solution.py:224
  62.7 17.1 %collective-permute-start.4 = (f32[4,96,384]{2,1,0:T(8,128)}, f32[4,96,384]{2,1,0:T(8,128)}, u32[]{:S(2)}, u32[]{:S(2)}) collective-permute-start(f32[4,96,384]{2,1,0:T(8,128)} %tie.1), channel_id=1, source_target_pairs={{0,32},{16,112},{32,64},{48,16},{64,96},{80,48},{96,0},{112,80},{1... | collective-permute-start | bytes 1769480 | tf_op jit(solution)/shard_map/ppermute | solution.py:224
  62.7 17.1 %collective-permute-start.10 = (f32[4,96,384]{2,1,0:T(8,128)}, f32[4,96,384]{2,1,0:T(8,128)}, u32[]{:S(2)}, u32[]{:S(2)}) collective-permute-start(f32[4,96,384]{2,1,0:T(8,128)} %collective-permute-done.1.refs_1_.refs_2_), channel_id=1, source_target_pairs={{0,16},{16,0},{32,48},{48,32},{64,80},{80,64},{96,112},{112,96},{1... | collective-permute-start | bytes 1769480 | tf_op jit(solution)/shard_map/ppermute | solution.py:227
  63.9 15.9 %collective-permute-start.11 = (f32[4,96,384]{2,1,0:T(8,128)}, f32[4,96,384]{2,1,0:T(8,128)}, u32[]{:S(2)}, u32[]{:S(2)}) collective-permute-start(f32[4,96,384]{2,1,0:T(8,128)} %collective-permute-done.2.refs_2_.refs_4_), channel_id=1, source_target_pairs={{0,16},{16,0},{32,48},{48,32},{64,80},{80,64},{96,112},{112,96},{1... | collective-permute-start | bytes 1769480 | tf_op jit(solution)/shard_map/ppermute | solution.py:227
  63.9 15.9 %collective-permute-start.12 = (f32[4,96,384]{2,1,0:T(8,128)}, f32[4,96,384]{2,1,0:T(8,128)}, u32[]{:S(2)}, u32[]{:S(2)}) collective-permute-start(f32[4,96,384]{2,1,0:T(8,128)} %collective-permute-done.3.refs_3_.refs_6_), channel_id=1, source_target_pairs={{0,16},{16,0},{32,48},{48,32},{64,80},{80,64},{96,112},{112,96},{1... | collective-permute-start | bytes 1769480 | tf_op jit(solution)/shard_map/ppermute | solution.py:227
  64.4 31.2 %collective-permute-start.6 = (f32[4,96,384]{2,1,0:T(8,128)}, f32[4,96,384]{2,1,0:T(8,128)}, u32[]{:S(2)}, u32[]{:S(2)}) collective-permute-start(f32[4,96,384]{2,1,0:T(8,128)} %tie.1), channel_id=1, source_target_pairs={{0,96},{16,48},{32,0},{48,80},{64,32},{80,112},{96,64},{112,16},{1... | collective-permute-start | bytes 1769480 | tf_op jit(solution)/shard_map/ppermute | solution.py:224
  79.8 15.8 %collective-permute-start.8 = (f32[4,96,384]{2,1,0:T(8,128)}, f32[4,96,384]{2,1,0:T(8,128)}, u32[]{:S(2)}, u32[]{:S(2)}) collective-permute-start(f32[4,96,384]{2,1,0:T(8,128)} %tie.1), channel_id=1, source_target_pairs={{0,64},{16,80},{32,96},{48,112},{64,0},{80,16},{96,32},{112,48},{1... | collective-permute-start | bytes 1769480 | tf_op jit(solution)/shard_map/ppermute | solution.py:224
  79.8 15.9 %collective-permute-start.5 = (f32[4,96,384]{2,1,0:T(8,128)}, f32[4,96,384]{2,1,0:T(8,128)}, u32[]{:S(2)}, u32[]{:S(2)}) collective-permute-start(f32[4,96,384]{2,1,0:T(8,128)} %collective-permute-done.4.refs_2_), channel_id=1, source_target_pairs={{0,16},{16,0},{32,48},{48,32},{64,80},{80,64},{96,112},{112,96},{1... | collective-permute-start | bytes 1769480 | tf_op jit(solution)/shard_map/ppermute | solution.py:227
  92.2 17.8 %collective-permute-start.13 = (f32[2,4,48,768]{3,2,1,0:T(8,128)}, f32[2,4,48,768]{3,2,1,0:T(8,128)}, u32[]{:S(2)}, u32[]{:S(2)}) collective-permute-start(f32[2,4,48,768]{3,2,1,0:T(8,128)} %get-tuple-element.33), channel_id=1, source_target_pairs={{0,4},{1,5},{2,6},{3,7},{4,8},{5,9},{6,10},{7,11},{8,12},{9,13},{1... | collective-permute-start | bytes 3538952 | tf_op jit(solution)/shard_map/ppermute | solution.py:236
  92.8 17.2 %collective-permute-start.14 = (f32[2,4,48,768]{3,2,1,0:T(8,128)}, f32[2,4,48,768]{3,2,1,0:T(8,128)}, u32[]{:S(2)}, u32[]{:S(2)}) collective-permute-start(f32[2,4,48,768]{3,2,1,0:T(8,128)} %get-tuple-element.34), channel_id=1, source_target_pairs={{0,12},{1,13},{2,14},{3,15},{4,0},{5,1},{6,2},{7,3},{8,4},{9,5},{1... | collective-permute-start | bytes 3538952 | tf_op jit(solution)/shard_map/ppermute | solution.py:237
  95.5 34.7 %collective-permute-start.19 = (f32[2,4,48,768]{3,2,1,0:T(8,128)}, f32[2,4,48,768]{3,2,1,0:T(8,128)}, u32[]{:S(2)}, u32[]{:S(2)}) collective-permute-start(f32[2,4,48,768]{3,2,1,0:T(8,128)} %get-tuple-element.44), channel_id=1, source_target_pairs={{0,4},{1,5},{2,6},{3,7},{4,8},{5,9},{6,10},{7,11},{8,12},{9,13},{1... | collective-permute-start | bytes 3538952 | tf_op jit(solution)/shard_map/ppermute | solution.py:238
  95.5 2.4 %collective-permute-start.7 = (f32[4,96,384]{2,1,0:T(8,128)}, f32[4,96,384]{2,1,0:T(8,128)}, u32[]{:S(2)}, u32[]{:S(2)}) collective-permute-start(f32[4,96,384]{2,1,0:T(8,128)} %collective-permute-done.6.refs_4_), channel_id=1, source_target_pairs={{0,16},{16,0},{32,48},{48,32},{64,80},{80,64},{96,112},{112,96},{1... | collective-permute-start | bytes 1769480 | tf_op jit(solution)/shard_map/ppermute | solution.py:227
  95.6 5.5 %collective-permute-start.9 = (f32[4,96,384]{2,1,0:T(8,128)}, f32[4,96,384]{2,1,0:T(8,128)}, u32[]{:S(2)}, u32[]{:S(2)}) collective-permute-start(f32[4,96,384]{2,1,0:T(8,128)} %collective-permute-done.8.refs_6_), channel_id=1, source_target_pairs={{0,16},{16,0},{32,48},{48,32},{64,80},{80,64},{96,112},{112,96},{1... | collective-permute-start | bytes 1769480 | tf_op jit(solution)/shard_map/ppermute | solution.py:227
  98.0 34.2 %collective-permute-start.20 = (f32[2,4,48,768]{3,2,1,0:T(8,128)}, f32[2,4,48,768]{3,2,1,0:T(8,128)}, u32[]{:S(2)}, u32[]{:S(2)}) collective-permute-start(f32[2,4,48,768]{3,2,1,0:T(8,128)} %get-tuple-element.45), channel_id=1, source_target_pairs={{0,12},{1,13},{2,14},{3,15},{4,0},{5,1},{6,2},{7,3},{8,4},{9,5},{1... | collective-permute-start | bytes 3538952 | tf_op jit(solution)/shard_map/ppermute | solution.py:239
  126.8 17.8 %collective-permute-start.17 = (f32[2,4,48,768]{3,2,1,0:T(8,128)}, f32[2,4,48,768]{3,2,1,0:T(8,128)}, u32[]{:S(2)}, u32[]{:S(2)}) collective-permute-start(f32[2,4,48,768]{3,2,1,0:T(8,128)} %get-tuple-element.42), channel_id=1, source_target_pairs={{0,4},{1,5},{2,6},{3,7},{4,8},{5,9},{6,10},{7,11},{8,12},{9,13},{1... | collective-permute-start | bytes 3538952 | tf_op jit(solution)/shard_map/ppermute | solution.py:236
  126.9 30.3 %collective-permute-start.21 = (f32[2,4,48,768]{3,2,1,0:T(8,128)}, f32[2,4,48,768]{3,2,1,0:T(8,128)}, u32[]{:S(2)}, u32[]{:S(2)}) collective-permute-start(f32[2,4,48,768]{3,2,1,0:T(8,128)} %get-tuple-element.35.refs_9_), channel_id=1, source_target_pairs={{0,4},{1,5},{2,6},{3,7},{4,8},{5,9},{6,10},{7,11},{8,12},{9,13},{1... | collective-permute-start | bytes 3538952 | tf_op jit(solution)/shard_map/ppermute | solution.py:241
  128.3 18.3 %collective-permute-start.18 = (f32[2,4,48,768]{3,2,1,0:T(8,128)}, f32[2,4,48,768]{3,2,1,0:T(8,128)}, u32[]{:S(2)}, u32[]{:S(2)}) collective-permute-start(f32[2,4,48,768]{3,2,1,0:T(8,128)} %get-tuple-element.43), channel_id=1, source_target_pairs={{0,12},{1,13},{2,14},{3,15},{4,0},{5,1},{6,2},{7,3},{8,4},{9,5},{1... | collective-permute-start | bytes 3538952 | tf_op jit(solution)/shard_map/ppermute | solution.py:237
  130.2 28.4 %collective-permute-start.22 = (f32[2,4,48,768]{3,2,1,0:T(8,128)}, f32[2,4,48,768]{3,2,1,0:T(8,128)}, u32[]{:S(2)}, u32[]{:S(2)}) collective-permute-start(f32[2,4,48,768]{3,2,1,0:T(8,128)} %get-tuple-element.36.refs_10_), channel_id=1, source_target_pairs={{0,12},{1,13},{2,14},{3,15},{4,0},{5,1},{6,2},{7,3},{8,4},{9,5},{1... | collective-permute-start | bytes 3538952 | tf_op jit(solution)/shard_map/ppermute | solution.py:241
  132.2 38.9 %collective-permute-start.15 = (f32[2,4,48,768]{3,2,1,0:T(8,128)}, f32[2,4,48,768]{3,2,1,0:T(8,128)}, u32[]{:S(2)}, u32[]{:S(2)}) collective-permute-start(f32[2,4,48,768]{3,2,1,0:T(8,128)} %get-tuple-element.38), channel_id=1, source_target_pairs={{0,4},{1,5},{2,6},{3,7},{4,8},{5,9},{6,10},{7,11},{8,12},{9,13},{1... | collective-permute-start | bytes 3538952 | tf_op jit(solution)/shard_map/ppermute | solution.py:238
  144.6 26.7 %collective-permute-start.16 = (f32[2,4,48,768]{3,2,1,0:T(8,128)}, f32[2,4,48,768]{3,2,1,0:T(8,128)}, u32[]{:S(2)}, u32[]{:S(2)}) collective-permute-start(f32[2,4,48,768]{3,2,1,0:T(8,128)} %get-tuple-element.39), channel_id=1, source_target_pairs={{0,12},{1,13},{2,14},{3,15},{4,0},{5,1},{6,2},{7,3},{8,4},{9,5},{1... | collective-permute-start | bytes 3538952 | tf_op jit(solution)/shard_map/ppermute | solution.py:239
  162.9 19.6 %collective-permute-start.23 = (f32[2,4,48,768]{3,2,1,0:T(8,128)}, f32[2,4,48,768]{3,2,1,0:T(8,128)}, u32[]{:S(2)}, u32[]{:S(2)}) collective-permute-start(f32[2,4,48,768]{3,2,1,0:T(8,128)} %get-tuple-element.46), channel_id=1, source_target_pairs={{0,4},{1,5},{2,6},{3,7},{4,8},{5,9},{6,10},{7,11},{8,12},{9,13},{1... | collective-permute-start | bytes 3538952 | tf_op jit(solution)/shard_map/ppermute | solution.py:241
  164.9 19.0 %collective-permute-start.24 = (f32[2,4,48,768]{3,2,1,0:T(8,128)}, f32[2,4,48,768]{3,2,1,0:T(8,128)}, u32[]{:S(2)}, u32[]{:S(2)}) collective-permute-start(f32[2,4,48,768]{3,2,1,0:T(8,128)} %get-tuple-element.47), channel_id=1, source_target_pairs={{0,12},{1,13},{2,14},{3,15},{4,0},{5,1},{6,2},{7,3},{8,4},{9,5},{1... | collective-permute-start | bytes 3538952 | tf_op jit(solution)/shard_map/ppermute | solution.py:241
  188.8 30.4 %collective-permute-start.25 = (f32[8,48,768]{2,1,0:T(8,128)}, f32[8,48,768]{2,1,0:T(8,128)}, u32[]{:S(2)}, u32[]{:S(2)}) collective-permute-start(f32[8,48,768]{2,1,0:T(8,128)} %get-tuple-element.54), channel_id=1, source_target_pairs={{0,1},{1,2},{2,3},{3,0},{4,5},{5,6},{6,7},{7,4},{8,9},{9,10},{10,1... | collective-permute-start | bytes 3538952 | tf_op jit(solution)/shard_map/ppermute | solution.py:246
  189.3 29.9 %collective-permute-start.26 = (f32[8,48,768]{2,1,0:T(8,128)}, f32[8,48,768]{2,1,0:T(8,128)}, u32[]{:S(2)}, u32[]{:S(2)}) collective-permute-start(f32[8,48,768]{2,1,0:T(8,128)} %get-tuple-element.55), channel_id=1, source_target_pairs={{0,2},{1,3},{2,0},{3,1},{4,6},{5,7},{6,4},{7,5},{8,10},{9,11},{10,... | collective-permute-start | bytes 3538952 | tf_op jit(solution)/shard_map/ppermute | solution.py:246
  191.6 28.5 %collective-permute-start.27 = (f32[8,48,768]{2,1,0:T(8,128)}, f32[8,48,768]{2,1,0:T(8,128)}, u32[]{:S(2)}, u32[]{:S(2)}) collective-permute-start(f32[8,48,768]{2,1,0:T(8,128)} %get-tuple-element.56), channel_id=1, source_target_pairs={{0,3},{1,0},{2,1},{3,2},{4,7},{5,4},{6,5},{7,6},{8,11},{9,8},{10,9... | collective-permute-start | bytes 3538952 | tf_op jit(solution)/shard_map/ppermute | solution.py:246

commit v9 on v8

--- a/solution.py
+++ b/solution.py
@@ -152,7 +152,7 @@
     outs[3][0] = own[3, 0] + (m2[1, 0] + n1[1, 0])
 
 
-def add_own(own, n1, n2, p2, m2, at, total, into):
+def add_own(own, n1, n2, p2, m2, after):
     count, rows, cols = own.shape[1:]
 
     def spec(lead):
@@ -161,33 +161,36 @@
     return pl.pallas_call(
         own_kernel,
         grid=(count,),
-        in_specs=[spec(4)] + [spec(2)] * 4
-        + [pl.BlockSpec(memory_space=pl.ANY)] * len(into),
-        out_specs=[pl.BlockSpec((1, rows, cols), lambda g: (at + g, 0, 0))] * 4,
-        out_shape=[jax.ShapeDtypeStruct((total, rows, cols), jnp.float32)] * 4,
-        input_output_aliases={5 + i: i for i in range(len(into))},
+        in_specs=[spec(4)] + [spec(2)] * 4 + [pl.BlockSpec(memory_space=pl.ANY)] * len(after),
+        out_specs=[pl.BlockSpec((1, rows, cols), lambda g: (g, 0, 0))] * 4,
+        out_shape=[jax.ShapeDtypeStruct((count, rows, cols), jnp.float32)] * 4,
         compiler_params=pltpu.CompilerParams(vmem_limit_bytes=VMEM),
         cost_estimate=LIGHT,
         name="add_own",
-    )(own, n1, n2, p2, m2, *into)
-
-
-def finish_kernel(sizes, origin, a, b, c, d, out):
+    )(own, n1, n2, p2, m2, *after)
+
+
+def finish_kernel(sizes, origin, *refs):
+    out = refs[-1]
     rows, irreps, cols = out.shape
     row = origin[0] + lax.broadcasted_iota(jnp.int32, (rows, cols), 0)
-    for g in range(irreps):
-        out[:, g, :] = jnp.where(row < sizes[g], (a[g] + b[g]) + (c[g] + d[g]), 0.0)
-
-
-def finish(parts, row_sizes, origin):
-    irreps, rows, cols = parts[0].shape
-    part = pl.BlockSpec((irreps, rows, WIDTH), lambda c, *_: (0, 0, c))
+    g = 0
+    for i in range(0, len(refs) - 1, 4):
+        a, b, c, d = refs[i : i + 4]
+        for k in range(a.shape[0]):
+            out[:, g, :] = jnp.where(row < sizes[g], (a[k] + b[k]) + (c[k] + d[k]), 0.0)
+            g += 1
+
+
+def finish(groups, row_sizes, origin, irreps):
+    parts = [part for group in groups for part in group]
+    _, rows, cols = parts[0].shape
     return pl.pallas_call(
         finish_kernel,
         grid_spec=pltpu.PrefetchScalarGridSpec(
             num_scalar_prefetch=2,
             grid=(cols // WIDTH,),
-            in_specs=[part] * 4,
+            in_specs=[pl.BlockSpec((part.shape[0], rows, WIDTH), lambda c, *_: (0, 0, c)) for part in parts],
             out_specs=pl.BlockSpec((rows, irreps, WIDTH), lambda c, *_: (0, 0, c)),
         ),
         out_shape=jax.ShapeDtypeStruct((rows, irreps, cols), jnp.float32),
@@ -197,7 +200,7 @@
     )(row_sizes, origin, *parts)
 
 
-GROUPS = ((0, 4), (4, 4))
+SPLIT = 4
 
 
 def local(amplitudes, ovov, row_sizes, pair_sizes):
@@ -213,39 +216,39 @@
     mine = jnp.transpose(amplitudes.reshape(local_rows, irreps, obs, depth), (2, 0, 1, 3))
     mine = mine.reshape(obs, local_rows * irreps, depth)
     mine = lax.all_to_all(mine, "ob", split_axis=0, concat_axis=0, tiled=True)
-    mine = jnp.transpose(mine.reshape(obs * local_rows, irreps, depth), (1, 0, 2))
-    mine_swapped = lax.ppermute(mine, "vb", SWAP)
-
-    gathered, landed = [], []
-    for first, count in GROUPS:
-        held = mine[first : first + count]
-        if landed:
-            (held,) = tie([held], landed)
-        landed = [lax.ppermute(held, "vb", steps) for steps in Z_STEPS]
-        pieces = [(mine, first), (mine_swapped, first)]
-        for piece in landed:
-            pieces += [(piece, 0), (lax.ppermute(piece, "vb", SWAP), 0)]
-        gathered.append(pieces)
-
-    swapped = [piece for piece, _ in gathered[-1][3::2]]
-    sums, added = [], []
-    for (first, count), pieces in zip(GROUPS, gathered):
-        far_p, far_m, near_p, near_m, up, down, own = product(
-            pieces, ovov, first, count, place, pair_sizes, origin, added
-        )
-        far_p = lax.ppermute(far_p, BOTH, NEAR[1])
-        far_m = lax.ppermute(far_m, BOTH, NEAR[-1])
-        near_p = lax.ppermute(near_p, BOTH, NEAR[1])
-        near_m = lax.ppermute(near_m, BOTH, NEAR[-1])
-        added = add_far(up, down, far_p, far_m, sums[-1][1:] if sums else swapped)
-        sums.append((own, near_p, near_m, lax.ppermute(added[0], BOTH, NEAR[1]), lax.ppermute(added[1], BOTH, NEAR[-1])))
-
-    four = []
-    for (first, _), group in zip(GROUPS, sums):
-        four = add_own(*group, first, irreps, four)
-    parts = [four[0]] + [lax.ppermute(four[k], BOTH, FAR[d]) for k, d in ((1, 1), (2, 2), (3, -1))]
+    mine = mine.reshape(obs * local_rows, irreps, depth)
+    early, late = jnp.transpose(mine[:, :SPLIT], (1, 0, 2)), jnp.transpose(mine[:, SPLIT:], (1, 0, 2))
+
+    def swap(piece):
+        return lax.ppermute(piece, "vb", SWAP)
+
+    def along_z(held):
+        return [lax.ppermute(held, "vb", steps) for steps in Z_STEPS]
+
+    def multiply(held, moved, first):
+        pieces = [(piece, 0) for whole in (held, *moved) for piece in (whole, swap(whole))]
+        return product(pieces, ovov, first, held.shape[0], place, pair_sizes, origin, [])
+
+    def to_neighbours(p, m):
+        return lax.ppermute(p, BOTH, NEAR[1]), lax.ppermute(m, BOTH, NEAR[-1])
+
+    def across(four):
+        return [four[0]] + [lax.ppermute(four[k], BOTH, FAR[d]) for k, d in ((1, 1), (2, 2), (3, -1))]
+
+    moved = along_z(early)
+    (late,) = tie([late], moved)
+    far_p, far_m, near_p, near_m, up, down, own = multiply(early, moved, 0)
+    moved = tie(along_z(late), [far_p])
+    late_far_p, late_far_m, late_near_p, late_near_m, late_up, late_down, late_own = multiply(late, moved, SPLIT)
+
+    far, near = to_neighbours(far_p, far_m), to_neighbours(near_p, near_m)
+    handed = to_neighbours(*add_far(up, down, *far, [late_far_p]))
+    late_far, late_near = to_neighbours(late_far_p, late_far_m), to_neighbours(late_near_p, late_near_m)
+    late_handed = to_neighbours(*add_far(late_up, late_down, *late_far, []))
+    sums = across(add_own(own, *near, *handed, []))
+    late_sums = across(add_own(late_own, *late_near, *late_handed, sums[1:]))
     origin = jnp.stack([ob * out_rows, vb * cols]).astype(jnp.int32)
-    return finish(parts, row_sizes, origin)
+    return finish([sums, late_sums], row_sizes, origin, irreps)
 
 
 def solution(mesh):

time: 226 us -> 215 us (0.951)
  waiting for transfers between devices: 112 us -> 103 us
    ppermute x28 -> x32, waiting for transfers between devices: 112 us -> 103 us  [the longest x6 35 us: along_z(): return [lax.ppermute(held, 'vb', steps) for steps in Z_STEPS]]
    ppermute x28 -> x32, starting transfers between devices: 31.6 us -> 29.7 us  [the longest x12 10.7 us: to_neighbours(): return (lax.ppermute(p, BOTH, NEAR[1]), lax.ppermute(m, BOTH, NEAR[-1]))]
  transfers between devices with their start and end apart: 28 -> 32, of which waited for: 14 -> 18; matrix products, arithmetic and copies ran while one was open for 2% -> 2% of each run, Pallas kernels for 17% -> 18%
where the time goes in v9:
time: 215 us; the launch traced here: 213 us
  waiting for transfers between devices  103 us (48%)
  Pallas kernels  48.2 us (22%)
  starting transfers between devices  29.7 us (14%)
  blocking collectives  25.4 us (12%)
  local copies, waits for them, and re-layouts  4.96 us (2%)
    ppermute x6, waiting for transfers between devices, along_z(): return [lax.ppermute(held, 'vb', steps) for steps in Z_STEPS]  35 us
    ppermute x12, waiting for transfers between devices, to_neighbours(): return (lax.ppermute(p, BOTH, NEAR[1]), lax.ppermute(m, BOTH, NEAR[-1]))  35 us
    ppermute x6, waiting for transfers between devices, across(): lax.ppermute(four[k], BOTH, FAR[d])  32.4 us
    all_to_all x1, blocking collectives, local(): mine = lax.all_to_all(mine, 'ob', split_axis=0, concat_axis=0, tiled=True)  25.4 us
    pallas_call x2, Pallas kernels, product(): pl.pallas_call(functools.partial(product_kernel, first), grid_spec=pltpu....  24.8 us
    ppermute x12, starting transfers between devices, to_neighbours(): return (lax.ppermute(p, BOTH, NEAR[1]), lax.ppermute(m, BOTH, NEAR[-1]))  10.7 us
    pallas_call x2, Pallas kernels, add_own(): pl.pallas_call(own_kernel, grid=(count,), in_specs=[spec(4)] + [spec(2)]...  9.7 us
    ppermute x6, starting transfers between devices, along_z(): return [lax.ppermute(held, 'vb', steps) for steps in Z_STEPS]  9.46 us
  transfers between devices with their start and end apart: 32, of which 18 were waited for; matrix products, arithmetic and copies ran while one was open for 2% of the time, Pallas kernels for 18%

profile of v9, /device:TPU:0, one launch (start us, length us, event | category | flops | bytes accessed | tf_op | source)
XLA Modules:
  0.0 213.0 jit_solution(8757214417440455300)
XLA Ops:
  0.0 1.5 copy.22
  1.9 25.4 %all_to_all.5 = f32[16,48,384]{2,1,0:T(8,128)S(1)} all-to-all(f32[16,48,384]{2,1,0:T(8,128)S(1)} %bitcast.26), channel_id=1, replica_groups=mesh['vb'=8,'ob'=16] {'ob'}, dimensions={0} | all-to-all | bytes 2359296 | tf_op jit(solution)/shard_map/all_to_all | solution.py:218
  27.4 0.9 copy.25
  28.3 3.9 %collective-permute-start.5 = (f32[4,96,384]{2,1,0:T(8,128)}, f32[4,96,384]{2,1,0:T(8,128)}, u32[]{:S(2)}, u32[]{:S(2)}) collective-permute-start(f32[4,96,384]{2,1,0:T(8,128)} %bitcast.23.refs_0_), channel_id=1, source_target_pairs={{0,64},{16,80},{32,96},{48,112},{64,0},{80,16},{96,32},{112,48},{1... | collective-permute-start | bytes 1769480 | tf_op jit(solution)/shard_map/ppermute | solution.py:226
  32.2 0.7 collective-permute-start.3
  32.9 1.3 collective-permute-start.1
  34.2 12.6 %collective-permute-done.5.refs_6_.refs_3_ = f32[4,96,384]{2,1,0:T(8,128)} collective-permute-done((f32[4,96,384]{2,1,0:T(8,128)}, f32[4,96,384]{2,1,0:T(8,128)}, u32[]{:S(2)}, u32[]{:S(2)}) %collective-permute-start.5) | collective-permute-done | bytes 589856 | tf_op jit(solution)/shard_map/ppermute | solution.py:226
  46.8 11.1 %collective-permute-done.3.refs_4_.refs_2_ = f32[4,96,384]{2,1,0:T(8,128)} collective-permute-done((f32[4,96,384]{2,1,0:T(8,128)}, f32[4,96,384]{2,1,0:T(8,128)}, u32[]{:S(2)}, u32[]{:S(2)}) %collective-permute-start.3) | collective-permute-done | bytes 589856 | tf_op jit(solution)/shard_map/ppermute | solution.py:226
  57.8 0.9 copy.24
  58.7 0.5 collective-permute-start.2
  59.2 1.2 collective-permute-start.14
  60.4 2.0 collective-permute-start.13
  62.8 0.4 collective-permute-start.11
  63.2 0.7 pad_add_fusion.1.origin
  63.9 1.2 dynamic-slice_bitcast_fusion.place
  65.1 12.4 %product.2 = (f32[2,4,48,768]{3,2,1,0:T(8,128)}, f32[2,4,48,768]{3,2,1,0:T(8,128)}, f32[2,4,48,768]{3,2,1,0:T(8,128)}, f32[2,4,48,768]{3,2,1,0:T(8,128)}, f32[2,...) custom-call(s32[16]{0:T(128)} %dynamic-slice_bitcast_fusion.place, s32[8]{0:T(128)} %sizes.4, ...), custom_call_target="tpu_custom_call" | custom-call | tf_op jit(solution)/shard_map/product/pallas_call | solution.py:88
  77.5 11.4 %collective-permute-done.13.refs_1_ = f32[4,96,384]{2,1,0:T(8,128)} collective-permute-done((f32[4,96,384]{2,1,0:T(8,128)}, f32[4,96,384]{2,1,0:T(8,128)}, u32[]{:S(2)}, u32[]{:S(2)}) %collective-permute-start.13) | collective-permute-done | bytes 589856 | tf_op jit(solution)/shard_map/ppermute | solution.py:226
  88.9 0.5 collective-permute-start.16
  89.5 1.1 collective-permute-start.10
  90.6 1.0 collective-permute-start.9
  91.5 0.4 collective-permute-start.7
  92.1 0.8 collective-permute-done.17.refs_7_
  93.0 12.4 %product.3 = (f32[2,4,48,768]{3,2,1,0:T(8,128)}, f32[2,4,48,768]{3,2,1,0:T(8,128)}, f32[2,4,48,768]{3,2,1,0:T(8,128)}, f32[2,4,48,768]{3,2,1,0:T(8,128)}, f32[2,...) custom-call(s32[16]{0:T(128)} %dynamic-slice_bitcast_fusion.place, s32[8]{0:T(128)} %sizes.4, ...), custom_call_target="tpu_custom_call" | custom-call | tf_op jit(solution)/shard_map/product/pallas_call | solution.py:88
  105.4 1.9 collective-permute-start.26
  107.5 3.0 %collective-permute-start.8 = (f32[2,4,48,768]{3,2,1,0:T(8,128)}, f32[2,4,48,768]{3,2,1,0:T(8,128)}, u32[]{:S(2)}, u32[]{:S(2)}) collective-permute-start(f32[2,4,48,768]{3,2,1,0:T(8,128)} %get-tuple-element.36), channel_id=1, source_target_pairs={{0,12},{1,13},{2,14},{3,15},{4,0},{5,1},{6,2},{7,3},{8,4},{9,5},{1... | collective-permute-start | bytes 3538952 | tf_op jit(solution)/shard_map/ppermute | solution.py:233
  110.5 4.3 %add_far.2 = (f32[2,4,48,768]{3,2,1,0:T(8,128)}, f32[2,4,48,768]{3,2,1,0:T(8,128)}) custom-call(f32[2,4,48,768]{3,2,1,0:T(8,128)} %get-tuple-element.37.up, f32[2,4,48,768]{3,2,1,0:T(8,128)} %get-tuple-element.38.down, f32[2,4,48,768]{3,2,1,0:T(8,128)} %collective-permute-done.9.recv_p, f32[2,4,48,768]{3,2,1,0:T(8,128)} %collective-permute-done.10.recv_m, ...), custom_call_target="tpu_custom_call" | custom-call | tf_op jit(solution)/shard_map/add_far/pallas_call | solution.py:135
  114.8 6.1 %collective-permute-done.7.n1 = f32[2,4,48,768]{3,2,1,0:T(8,128)} collective-permute-done((f32[2,4,48,768]{3,2,1,0:T(8,128)}, f32[2,4,48,768]{3,2,1,0:T(8,128)}, u32[]{:S(2)}, u32[]{:S(2)}) %collective-permute-start.7) | collective-permute-done | bytes 1179680 | tf_op jit(solution)/shard_map/ppermute | solution.py:233
  120.9 1.0 collective-permute-done.26.recv_m
  121.9 1.0 collective-permute-start.23
  123.0 10.6 %collective-permute-done.25.recv_p = f32[2,4,48,768]{3,2,1,0:T(8,128)} collective-permute-done((f32[2,4,48,768]{3,2,1,0:T(8,128)}, f32[2,4,48,768]{3,2,1,0:T(8,128)}, u32[]{:S(2)}, u32[]{:S(2)}) %collective-permute-start.25) | collective-permute-done | bytes 1179680 | tf_op jit(solution)/shard_map/ppermute | solution.py:233
  133.6 4.3 %add_far.3 = (f32[2,4,48,768]{3,2,1,0:T(8,128)}, f32[2,4,48,768]{3,2,1,0:T(8,128)}) custom-call(f32[2,4,48,768]{3,2,1,0:T(8,128)} %get-tuple-element.54.up, f32[2,4,48,768]{3,2,1,0:T(8,128)} %get-tuple-element.55.down, f32[2,4,48,768]{3,2,1,0:T(8,128)} %collective-permute-done.25.recv_p, f32[2,4,48,768]{3,2,1,0:T(8,128)} %collective-permute-done.26.recv_m), custom_call_target="tpu_custom_call" | custom-call | tf_op jit(solution)/shard_map/add_far/pallas_call | solution.py:135
  137.9 2.1 collective-permute-start.27
  140.0 6.2 %collective-permute-done.18.p2 = f32[2,4,48,768]{3,2,1,0:T(8,128)} collective-permute-done((f32[2,4,48,768]{3,2,1,0:T(8,128)}, f32[2,4,48,768]{3,2,1,0:T(8,128)}, u32[]{:S(2)}, u32[]{:S(2)}) %collective-permute-start.18) | collective-permute-done | bytes 1179680 | tf_op jit(solution)/shard_map/ppermute | solution.py:233
  146.2 1.0 collective-permute-done.19.m2
  147.2 4.8 %add_own.2 = (f32[4,48,768]{2,1,0:T(8,128)}, f32[4,48,768]{2,1,0:T(8,128)}, f32[4,48,768]{2,1,0:T(8,128)}, f32[4,48,768]{2,1,0:T(8,128)}) custom-call(f32[4,4,48,768]{3,2,1,0:T(8,128)} %get-tuple-element.34.own, f32[2,4,48,768]{3,2,1,0:T(8,128)} %collective-permute-done.7.n1, f32[2,4,48,768]{3,2,1,0:T(8,128)} %collective-permute-done.8.n2, ...), custom_call_target="tpu_custom_call" | custom-call | tf_op jit(solution)/shard_map/add_own/pallas_call | solution.py:161
  152.3 9.8 %collective-permute-done.23.n1 = f32[2,4,48,768]{3,2,1,0:T(8,128)} collective-permute-done((f32[2,4,48,768]{3,2,1,0:T(8,128)}, f32[2,4,48,768]{3,2,1,0:T(8,128)}, u32[]{:S(2)}, u32[]{:S(2)}) %collective-permute-start.23) | collective-permute-done | bytes 1179680 | tf_op jit(solution)/shard_map/ppermute | solution.py:233
  162.2 1.4 collective-permute-start.21
  163.6 2.0 collective-permute-start.22
  165.5 5.1 %collective-permute-done.20.refs_0_.refs_1_ = f32[4,48,768]{2,1,0:T(8,128)} collective-permute-done((f32[4,48,768]{2,1,0:T(8,128)}, f32[4,48,768]{2,1,0:T(8,128)}, u32[]{:S(2)}, u32[]{:S(2)}) %collective-permute-start.20) | collective-permute-done | bytes 589856 | tf_op jit(solution)/shard_map/ppermute | solution.py:236
  170.6 11.2 %collective-permute-done.21.refs_1_.refs_2_ = f32[4,48,768]{2,1,0:T(8,128)} collective-permute-done((f32[4,48,768]{2,1,0:T(8,128)}, f32[4,48,768]{2,1,0:T(8,128)}, u32[]{:S(2)}, u32[]{:S(2)}) %collective-permute-start.21) | collective-permute-done | bytes 589856 | tf_op jit(solution)/shard_map/ppermute | solution.py:236
  181.8 2.5 %collective-permute-done.22.refs_2_.refs_3_ = f32[4,48,768]{2,1,0:T(8,128)} collective-permute-done((f32[4,48,768]{2,1,0:T(8,128)}, f32[4,48,768]{2,1,0:T(8,128)}, u32[]{:S(2)}, u32[]{:S(2)}) %collective-permute-start.22) | collective-permute-done | bytes 589856 | tf_op jit(solution)/shard_map/ppermute | solution.py:236
  184.5 4.9 %add_own.3 = (f32[4,48,768]{2,1,0:T(8,128)}, f32[4,48,768]{2,1,0:T(8,128)}, f32[4,48,768]{2,1,0:T(8,128)}, f32[4,48,768]{2,1,0:T(8,128)}) custom-call(f32[4,4,48,768]{3,2,1,0:T(8,128)} %get-tuple-element.51.own, f32[2,4,48,768]{3,2,1,0:T(8,128)} %collective-permute-done.23.n1, f32[2,4,48,768]{3,2,1,0:T(8,128)} %collective-permute-done.24.n2, ...), custom_call_target="tpu_custom_call" | custom-call | tf_op jit(solution)/shard_map/add_own/pallas_call | solution.py:161
  189.7 3.4 %collective-permute-start.30 = (f32[4,48,768]{2,1,0:T(8,128)}, f32[4,48,768]{2,1,0:T(8,128)}, u32[]{:S(2)}, u32[]{:S(2)}) collective-permute-start(f32[4,48,768]{2,1,0:T(8,128)} %get-tuple-element.61), channel_id=1, source_target_pairs={{0,2},{1,3},{2,0},{3,1},{4,6},{5,7},{6,4},{7,5},{8,10},{9,11},{10,... | collective-permute-start | bytes 1769480 | tf_op jit(solution)/shard_map/ppermute | solution.py:236
  193.1 0.6 collective-permute-start.31
  193.8 0.6 pad_add_fusion.origin
  194.4 6.4 %collective-permute-done.29.refs_5_ = f32[4,48,768]{2,1,0:T(8,128)} collective-permute-done((f32[4,48,768]{2,1,0:T(8,128)}, f32[4,48,768]{2,1,0:T(8,128)}, u32[]{:S(2)}, u32[]{:S(2)}) %collective-permute-start.29) | collective-permute-done | bytes 589856 | tf_op jit(solution)/shard_map/ppermute | solution.py:236
  200.8 6.9 %collective-permute-done.30.refs_6_ = f32[4,48,768]{2,1,0:T(8,128)} collective-permute-done((f32[4,48,768]{2,1,0:T(8,128)}, f32[4,48,768]{2,1,0:T(8,128)}, u32[]{:S(2)}, u32[]{:S(2)}) %collective-permute-start.30) | collective-permute-done | bytes 589856 | tf_op jit(solution)/shard_map/ppermute | solution.py:236
  208.0 5.0 %finish.1 = f32[48,8,768]{2,1,0:T(8,128)} custom-call(s32[8]{0:T(128)} %sizes.5, s32[2]{0:T(128)} %pad_add_fusion.origin, f32[4,48,768]{2,1,0:T(8,128)} %get-tuple-element.47.refs_0_, f32[4,48,768]{2,1,0:T(8,128)} %collective-permute-done.20.refs_0_.refs_1_, f32[4,48,768]{2,1,0:T(8,128)} %collective-permute-done.21.refs_1_.refs_2_, ...), custom_call_target="tpu_custom_call" | custom-call | tf_op jit(solution)/shard_map/finish/pallas_call | solution.py:188
  (34 shorter events, 2.6 us)
Async XLA Ops:
  28.3 18.5 %collective-permute-start.5 = (f32[4,96,384]{2,1,0:T(8,128)}, f32[4,96,384]{2,1,0:T(8,128)}, u32[]{:S(2)}, u32[]{:S(2)}) collective-permute-start(f32[4,96,384]{2,1,0:T(8,128)} %bitcast.23.refs_0_), channel_id=1, source_target_pairs={{0,64},{16,80},{32,96},{48,112},{64,0},{80,16},{96,32},{112,48},{1... | collective-permute-start | bytes 1769480 | tf_op jit(solution)/shard_map/ppermute | solution.py:226
  32.2 25.7 %collective-permute-start.3 = (f32[4,96,384]{2,1,0:T(8,128)}, f32[4,96,384]{2,1,0:T(8,128)}, u32[]{:S(2)}, u32[]{:S(2)}) collective-permute-start(f32[4,96,384]{2,1,0:T(8,128)} %bitcast.23.refs_0_), channel_id=1, source_target_pairs={{0,96},{16,48},{32,0},{48,80},{64,32},{80,112},{96,64},{112,16},{1... | collective-permute-start | bytes 1769480 | tf_op jit(solution)/shard_map/ppermute | solution.py:226
  32.9 25.8 %collective-permute-start.1 = (f32[4,96,384]{2,1,0:T(8,128)}, f32[4,96,384]{2,1,0:T(8,128)}, u32[]{:S(2)}, u32[]{:S(2)}) collective-permute-start(f32[4,96,384]{2,1,0:T(8,128)} %bitcast.23.refs_0_), channel_id=1, source_target_pairs={{0,32},{16,112},{32,64},{48,16},{64,96},{80,48},{96,0},{112,80},{1... | collective-permute-start | bytes 1769480 | tf_op jit(solution)/shard_map/ppermute | solution.py:226
  34.2 26.2 %collective-permute-start = (f32[4,96,384]{2,1,0:T(8,128)}, f32[4,96,384]{2,1,0:T(8,128)}, u32[]{:S(2)}, u32[]{:S(2)}) collective-permute-start(f32[4,96,384]{2,1,0:T(8,128)} %bitcast.23.refs_0_), channel_id=1, source_target_pairs={{0,16},{16,0},{32,48},{48,32},{64,80},{80,64},{96,112},{112,96},{1... | collective-permute-start | bytes 1769480 | tf_op jit(solution)/shard_map/ppermute | solution.py:223
  46.8 15.6 %collective-permute-start.6 = (f32[4,96,384]{2,1,0:T(8,128)}, f32[4,96,384]{2,1,0:T(8,128)}, u32[]{:S(2)}, u32[]{:S(2)}) collective-permute-start(f32[4,96,384]{2,1,0:T(8,128)} %collective-permute-done.5.refs_6_.refs_3_), channel_id=1, source_target_pairs={{0,16},{16,0},{32,48},{48,32},{64,80},{80,64},{96,112},{112,96},{1... | collective-permute-start | bytes 1769480 | tf_op jit(solution)/shard_map/ppermute | solution.py:223
  57.8 5.0 %collective-permute-start.4 = (f32[4,96,384]{2,1,0:T(8,128)}, f32[4,96,384]{2,1,0:T(8,128)}, u32[]{:S(2)}, u32[]{:S(2)}) collective-permute-start(f32[4,96,384]{2,1,0:T(8,128)} %collective-permute-done.3.refs_4_.refs_2_), channel_id=1, source_target_pairs={{0,16},{16,0},{32,48},{48,32},{64,80},{80,64},{96,112},{112,96},{1... | collective-permute-start | bytes 1769480 | tf_op jit(solution)/shard_map/ppermute | solution.py:223
  58.7 6.4 %collective-permute-start.2 = (f32[4,96,384]{2,1,0:T(8,128)}, f32[4,96,384]{2,1,0:T(8,128)}, u32[]{:S(2)}, u32[]{:S(2)}) collective-permute-start(f32[4,96,384]{2,1,0:T(8,128)} %collective-permute-done.1.refs_2_.refs_1_), channel_id=1, source_target_pairs={{0,16},{16,0},{32,48},{48,32},{64,80},{80,64},{96,112},{112,96},{1... | collective-permute-start | bytes 1769480 | tf_op jit(solution)/shard_map/ppermute | solution.py:223
  59.2 18.3 %collective-permute-start.14 = (f32[4,96,384]{2,1,0:T(8,128)}, f32[4,96,384]{2,1,0:T(8,128)}, u32[]{:S(2)}, u32[]{:S(2)}) collective-permute-start(f32[4,96,384]{2,1,0:T(8,128)} %tie.2.refs_0_), channel_id=1, source_target_pairs={{0,64},{16,80},{32,96},{48,112},{64,0},{80,16},{96,32},{112,48},{1... | collective-permute-start | bytes 1769480 | tf_op jit(solution)/shard_map/ppermute | solution.py:226
  60.4 28.5 %collective-permute-start.13 = (f32[4,96,384]{2,1,0:T(8,128)}, f32[4,96,384]{2,1,0:T(8,128)}, u32[]{:S(2)}, u32[]{:S(2)}) collective-permute-start(f32[4,96,384]{2,1,0:T(8,128)} %tie.2.refs_0_), channel_id=1, source_target_pairs={{0,96},{16,48},{32,0},{48,80},{64,32},{80,112},{96,64},{112,16},{1... | collective-permute-start | bytes 1769480 | tf_op jit(solution)/shard_map/ppermute | solution.py:226
  62.4 26.5 %collective-permute-start.12 = (f32[4,96,384]{2,1,0:T(8,128)}, f32[4,96,384]{2,1,0:T(8,128)}, u32[]{:S(2)}, u32[]{:S(2)}) collective-permute-start(f32[4,96,384]{2,1,0:T(8,128)} %tie.2.refs_0_), channel_id=1, source_target_pairs={{0,32},{16,112},{32,64},{48,16},{64,96},{80,48},{96,0},{112,80},{1... | collective-permute-start | bytes 1769480 | tf_op jit(solution)/shard_map/ppermute | solution.py:226
  62.8 27.8 %collective-permute-start.11 = (f32[4,96,384]{2,1,0:T(8,128)}, f32[4,96,384]{2,1,0:T(8,128)}, u32[]{:S(2)}, u32[]{:S(2)}) collective-permute-start(f32[4,96,384]{2,1,0:T(8,128)} %tie.2.refs_0_), channel_id=1, source_target_pairs={{0,16},{16,0},{32,48},{48,32},{64,80},{80,64},{96,112},{112,96},{1... | collective-permute-start | bytes 1769480 | tf_op jit(solution)/shard_map/ppermute | solution.py:223
  88.9 2.6 %collective-permute-start.15 = (f32[4,96,384]{2,1,0:T(8,128)}, f32[4,96,384]{2,1,0:T(8,128)}, u32[]{:S(2)}, u32[]{:S(2)}) collective-permute-start(f32[4,96,384]{2,1,0:T(8,128)} %get-tuple-element.41.refs_2_), channel_id=1, source_target_pairs={{0,16},{16,0},{32,48},{48,32},{64,80},{80,64},{96,112},{112,96},{1... | collective-permute-start | bytes 1769480 | tf_op jit(solution)/shard_map/ppermute | solution.py:223
  88.9 3.2 %collective-permute-start.16 = (f32[4,96,384]{2,1,0:T(8,128)}, f32[4,96,384]{2,1,0:T(8,128)}, u32[]{:S(2)}, u32[]{:S(2)}) collective-permute-start(f32[4,96,384]{2,1,0:T(8,128)} %get-tuple-element.42.refs_4_), channel_id=1, source_target_pairs={{0,16},{16,0},{32,48},{48,32},{64,80},{80,64},{96,112},{112,96},{1... | collective-permute-start | bytes 1769480 | tf_op jit(solution)/shard_map/ppermute | solution.py:223
  89.4 3.5 %collective-permute-start.17 = (f32[4,96,384]{2,1,0:T(8,128)}, f32[4,96,384]{2,1,0:T(8,128)}, u32[]{:S(2)}, u32[]{:S(2)}) collective-permute-start(f32[4,96,384]{2,1,0:T(8,128)} %get-tuple-element.43.refs_6_), channel_id=1, source_target_pairs={{0,16},{16,0},{32,48},{48,32},{64,80},{80,64},{96,112},{112,96},{1... | collective-permute-start | bytes 1769480 | tf_op jit(solution)/shard_map/ppermute | solution.py:223
  89.5 17.9 %collective-permute-start.10 = (f32[2,4,48,768]{3,2,1,0:T(8,128)}, f32[2,4,48,768]{3,2,1,0:T(8,128)}, u32[]{:S(2)}, u32[]{:S(2)}) collective-permute-start(f32[2,4,48,768]{3,2,1,0:T(8,128)} %get-tuple-element.40), channel_id=1, source_target_pairs={{0,12},{1,13},{2,14},{3,15},{4,0},{5,1},{6,2},{7,3},{8,4},{9,5},{1... | collective-permute-start | bytes 3538952 | tf_op jit(solution)/shard_map/ppermute | solution.py:233
  90.6 19.9 %collective-permute-start.9 = (f32[2,4,48,768]{3,2,1,0:T(8,128)}, f32[2,4,48,768]{3,2,1,0:T(8,128)}, u32[]{:S(2)}, u32[]{:S(2)}) collective-permute-start(f32[2,4,48,768]{3,2,1,0:T(8,128)} %get-tuple-element.39.refs_3_), channel_id=1, source_target_pairs={{0,4},{1,5},{2,6},{3,7},{4,8},{5,9},{6,10},{7,11},{8,12},{9,13},{1... | collective-permute-start | bytes 3538952 | tf_op jit(solution)/shard_map/ppermute | solution.py:233
  91.5 29.4 %collective-permute-start.7 = (f32[2,4,48,768]{3,2,1,0:T(8,128)}, f32[2,4,48,768]{3,2,1,0:T(8,128)}, u32[]{:S(2)}, u32[]{:S(2)}) collective-permute-start(f32[2,4,48,768]{3,2,1,0:T(8,128)} %get-tuple-element.35), channel_id=1, source_target_pairs={{0,4},{1,5},{2,6},{3,7},{4,8},{5,9},{6,10},{7,11},{8,12},{9,13},{1... | collective-permute-start | bytes 3538952 | tf_op jit(solution)/shard_map/ppermute | solution.py:233
  105.4 16.6 %collective-permute-start.26 = (f32[2,4,48,768]{3,2,1,0:T(8,128)}, f32[2,4,48,768]{3,2,1,0:T(8,128)}, u32[]{:S(2)}, u32[]{:S(2)}) collective-permute-start(f32[2,4,48,768]{3,2,1,0:T(8,128)} %get-tuple-element.56), channel_id=1, source_target_pairs={{0,12},{1,13},{2,14},{3,15},{4,0},{5,1},{6,2},{7,3},{8,4},{9,5},{1... | collective-permute-start | bytes 3538952 | tf_op jit(solution)/shard_map/ppermute | solution.py:233
  107.3 26.3 %collective-permute-start.25 = (f32[2,4,48,768]{3,2,1,0:T(8,128)}, f32[2,4,48,768]{3,2,1,0:T(8,128)}, u32[]{:S(2)}, u32[]{:S(2)}) collective-permute-start(f32[2,4,48,768]{3,2,1,0:T(8,128)} %get-tuple-element.44.refs_0_), channel_id=1, source_target_pairs={{0,4},{1,5},{2,6},{3,7},{4,8},{5,9},{6,10},{7,11},{8,12},{9,13},{1... | collective-permute-start | bytes 3538952 | tf_op jit(solution)/shard_map/ppermute | solution.py:233
  107.5 30.4 %collective-permute-start.8 = (f32[2,4,48,768]{3,2,1,0:T(8,128)}, f32[2,4,48,768]{3,2,1,0:T(8,128)}, u32[]{:S(2)}, u32[]{:S(2)}) collective-permute-start(f32[2,4,48,768]{3,2,1,0:T(8,128)} %get-tuple-element.36), channel_id=1, source_target_pairs={{0,12},{1,13},{2,14},{3,15},{4,0},{5,1},{6,2},{7,3},{8,4},{9,5},{1... | collective-permute-start | bytes 3538952 | tf_op jit(solution)/shard_map/ppermute | solution.py:233
  114.8 31.4 %collective-permute-start.18 = (f32[2,4,48,768]{3,2,1,0:T(8,128)}, f32[2,4,48,768]{3,2,1,0:T(8,128)}, u32[]{:S(2)}, u32[]{:S(2)}) collective-permute-start(f32[2,4,48,768]{3,2,1,0:T(8,128)} %get-tuple-element.45), channel_id=1, source_target_pairs={{0,4},{1,5},{2,6},{3,7},{4,8},{5,9},{6,10},{7,11},{8,12},{9,13},{1... | collective-permute-start | bytes 3538952 | tf_op jit(solution)/shard_map/ppermute | solution.py:233
  120.9 26.3 %collective-permute-start.19 = (f32[2,4,48,768]{3,2,1,0:T(8,128)}, f32[2,4,48,768]{3,2,1,0:T(8,128)}, u32[]{:S(2)}, u32[]{:S(2)}) collective-permute-start(f32[2,4,48,768]{3,2,1,0:T(8,128)} %get-tuple-element.46), channel_id=1, source_target_pairs={{0,12},{1,13},{2,14},{3,15},{4,0},{5,1},{6,2},{7,3},{8,4},{9,5},{1... | collective-permute-start | bytes 3538952 | tf_op jit(solution)/shard_map/ppermute | solution.py:233
  121.9 40.2 %collective-permute-start.23 = (f32[2,4,48,768]{3,2,1,0:T(8,128)}, f32[2,4,48,768]{3,2,1,0:T(8,128)}, u32[]{:S(2)}, u32[]{:S(2)}) collective-permute-start(f32[2,4,48,768]{3,2,1,0:T(8,128)} %get-tuple-element.52), channel_id=1, source_target_pairs={{0,4},{1,5},{2,6},{3,7},{4,8},{5,9},{6,10},{7,11},{8,12},{9,13},{1... | collective-permute-start | bytes 3538952 | tf_op jit(solution)/shard_map/ppermute | solution.py:233
  133.6 30.0 %collective-permute-start.24 = (f32[2,4,48,768]{3,2,1,0:T(8,128)}, f32[2,4,48,768]{3,2,1,0:T(8,128)}, u32[]{:S(2)}, u32[]{:S(2)}) collective-permute-start(f32[2,4,48,768]{3,2,1,0:T(8,128)} %get-tuple-element.53), channel_id=1, source_target_pairs={{0,12},{1,13},{2,14},{3,15},{4,0},{5,1},{6,2},{7,3},{8,4},{9,5},{1... | collective-permute-start | bytes 3538952 | tf_op jit(solution)/shard_map/ppermute | solution.py:233
  137.9 46.4 %collective-permute-start.27 = (f32[2,4,48,768]{3,2,1,0:T(8,128)}, f32[2,4,48,768]{3,2,1,0:T(8,128)}, u32[]{:S(2)}, u32[]{:S(2)}) collective-permute-start(f32[2,4,48,768]{3,2,1,0:T(8,128)} %get-tuple-element.57), channel_id=1, source_target_pairs={{0,4},{1,5},{2,6},{3,7},{4,8},{5,9},{6,10},{7,11},{8,12},{9,13},{1... | collective-permute-start | bytes 3538952 | tf_op jit(solution)/shard_map/ppermute | solution.py:233
  146.2 38.3 %collective-permute-start.28 = (f32[2,4,48,768]{3,2,1,0:T(8,128)}, f32[2,4,48,768]{3,2,1,0:T(8,128)}, u32[]{:S(2)}, u32[]{:S(2)}) collective-permute-start(f32[2,4,48,768]{3,2,1,0:T(8,128)} %get-tuple-element.58), channel_id=1, source_target_pairs={{0,12},{1,13},{2,14},{3,15},{4,0},{5,1},{6,2},{7,3},{8,4},{9,5},{1... | collective-permute-start | bytes 3538952 | tf_op jit(solution)/shard_map/ppermute | solution.py:233
  152.1 18.5 %collective-permute-start.20 = (f32[4,48,768]{2,1,0:T(8,128)}, f32[4,48,768]{2,1,0:T(8,128)}, u32[]{:S(2)}, u32[]{:S(2)}) collective-permute-start(f32[4,48,768]{2,1,0:T(8,128)} %get-tuple-element.48), channel_id=1, source_target_pairs={{0,1},{1,2},{2,3},{3,0},{4,5},{5,6},{6,7},{7,4},{8,9},{9,10},{10,1... | collective-permute-start | bytes 1769480 | tf_op jit(solution)/shard_map/ppermute | solution.py:236
  162.2 19.6 %collective-permute-start.21 = (f32[4,48,768]{2,1,0:T(8,128)}, f32[4,48,768]{2,1,0:T(8,128)}, u32[]{:S(2)}, u32[]{:S(2)}) collective-permute-start(f32[4,48,768]{2,1,0:T(8,128)} %get-tuple-element.49), channel_id=1, source_target_pairs={{0,2},{1,3},{2,0},{3,1},{4,6},{5,7},{6,4},{7,5},{8,10},{9,11},{10,... | collective-permute-start | bytes 1769480 | tf_op jit(solution)/shard_map/ppermute | solution.py:236
  163.6 20.8 %collective-permute-start.22 = (f32[4,48,768]{2,1,0:T(8,128)}, f32[4,48,768]{2,1,0:T(8,128)}, u32[]{:S(2)}, u32[]{:S(2)}) collective-permute-start(f32[4,48,768]{2,1,0:T(8,128)} %get-tuple-element.50), channel_id=1, source_target_pairs={{0,3},{1,0},{2,1},{3,2},{4,7},{5,4},{6,5},{7,6},{8,11},{9,8},{10,9... | collective-permute-start | bytes 1769480 | tf_op jit(solution)/shard_map/ppermute | solution.py:236
  189.3 11.4 %collective-permute-start.29 = (f32[4,48,768]{2,1,0:T(8,128)}, f32[4,48,768]{2,1,0:T(8,128)}, u32[]{:S(2)}, u32[]{:S(2)}) collective-permute-start(f32[4,48,768]{2,1,0:T(8,128)} %get-tuple-element.60), channel_id=1, source_target_pairs={{0,1},{1,2},{2,3},{3,0},{4,5},{5,6},{6,7},{7,4},{8,9},{9,10},{10,1... | collective-permute-start | bytes 1769480 | tf_op jit(solution)/shard_map/ppermute | solution.py:236
  189.7 17.9 %collective-permute-start.30 = (f32[4,48,768]{2,1,0:T(8,128)}, f32[4,48,768]{2,1,0:T(8,128)}, u32[]{:S(2)}, u32[]{:S(2)}) collective-permute-start(f32[4,48,768]{2,1,0:T(8,128)} %get-tuple-element.61), channel_id=1, source_target_pairs={{0,2},{1,3},{2,0},{3,1},{4,6},{5,7},{6,4},{7,5},{8,10},{9,11},{10,... | collective-permute-start | bytes 1769480 | tf_op jit(solution)/shard_map/ppermute | solution.py:236
  193.1 14.8 %collective-permute-start.31 = (f32[4,48,768]{2,1,0:T(8,128)}, f32[4,48,768]{2,1,0:T(8,128)}, u32[]{:S(2)}, u32[]{:S(2)}) collective-permute-start(f32[4,48,768]{2,1,0:T(8,128)} %get-tuple-element.62), channel_id=1, source_target_pairs={{0,3},{1,0},{2,1},{3,2},{4,7},{5,4},{6,5},{7,6},{8,11},{9,8},{10,9... | collective-permute-start | bytes 1769480 | tf_op jit(solution)/shard_map/ppermute | solution.py:236

commit v10 on v9

--- a/solution.py
+++ b/solution.py
@@ -10,7 +10,7 @@
 
 SIDE = 4
 VMEM = 64 * 1024 * 1024 - 256 * 1024
-WIDTH = 256
+HEIGHT = 16
 LIGHT = pl.CostEstimate(flops=0, bytes_accessed=0, transcendentals=0)
 def hops(count, steps):
     pairs = []
@@ -28,7 +28,7 @@
 FAR = {d: hops(128, lambda i, d=d: (SIDE if i // 16 % 2 else 1, d)) for d in (1, 2, -1)}
 
 
-ORDER = [(2, 0), (2, 1)] + [(2, 2), (2, 3)] + [(1, 2), (1, 3)] + [(3, 0), (3, 1)]
+ORDER = [(2, 0), (2, 1), (1, 2), (1, 3)] + [(2, 2), (2, 3), (3, 0), (3, 1)]
 ORDER += [(1, 0), (1, 1)] + [(3, 2), (3, 3)] + [(0, k) for k in range(SIDE)]
 
 
@@ -50,11 +50,11 @@
 
 
 PLACES = place_table()
-LEADS = (2, 2, 2, 2, 2, 2, 4)
+LEADS = (4, 4, 2, 2, 4)
 
 
 def product_kernel(first, place, sizes, origin, *refs):
-    pieces, v_ref, outs, (a_all, v_all) = refs[:8], refs[8], refs[-9:-2], refs[-2:]
+    pieces, v_ref, outs, (a_all, v_all) = refs[:8], refs[8], refs[-7:-2], refs[-2:]
     rows = pieces[0].shape[1] // 2
     depth = pieces[0].shape[2]
     for a, piece in enumerate(pieces):
@@ -144,36 +144,36 @@
     )(up, down, recv_p, recv_m, *after)
 
 
-def own_kernel(own, n1, n2, p2, m2, *refs):
+def own_kernel(own, p1, m1, p2, m2, *refs):
     outs = refs[-4:]
-    outs[0][0] = own[0, 0] + (p2[0, 0] + n2[0, 0])
-    outs[1][0] = own[1, 0] + (p2[1, 0] + n2[1, 0])
-    outs[2][0] = own[2, 0] + (m2[0, 0] + n1[0, 0])
-    outs[3][0] = own[3, 0] + (m2[1, 0] + n1[1, 0])
-
-
-def add_own(own, n1, n2, p2, m2, after):
+    outs[0][0] = own[0, 0] + (p2[0, 0] + m1[0, 0])
+    outs[1][0] = own[1, 0] + (p2[1, 0] + m1[1, 0])
+    outs[2][0] = own[2, 0] + (m2[0, 0] + p1[0, 0])
+    outs[3][0] = own[3, 0] + (m2[1, 0] + p1[1, 0])
+
+
+def add_own(own, p1, m1, p2, m2, after):
     count, rows, cols = own.shape[1:]
 
-    def spec(lead):
-        return pl.BlockSpec((lead, 1, rows, cols), lambda g: (0, g, 0, 0))
+    def spec(lead, at=0):
+        return pl.BlockSpec((lead, 1, rows, cols), lambda g: (at, g, 0, 0))
 
     return pl.pallas_call(
         own_kernel,
         grid=(count,),
-        in_specs=[spec(4)] + [spec(2)] * 4 + [pl.BlockSpec(memory_space=pl.ANY)] * len(after),
+        in_specs=[spec(4), spec(2, 1), spec(2, 1), spec(2), spec(2)] + [pl.BlockSpec(memory_space=pl.ANY)] * len(after),
         out_specs=[pl.BlockSpec((1, rows, cols), lambda g: (g, 0, 0))] * 4,
         out_shape=[jax.ShapeDtypeStruct((count, rows, cols), jnp.float32)] * 4,
         compiler_params=pltpu.CompilerParams(vmem_limit_bytes=VMEM),
         cost_estimate=LIGHT,
         name="add_own",
-    )(own, n1, n2, p2, m2, *after)
+    )(own, p1, m1, p2, m2, *after)
 
 
 def finish_kernel(sizes, origin, *refs):
     out = refs[-1]
     rows, irreps, cols = out.shape
-    row = origin[0] + lax.broadcasted_iota(jnp.int32, (rows, cols), 0)
+    row = origin[0] + pl.program_id(0) * HEIGHT + lax.broadcasted_iota(jnp.int32, (rows, cols), 0)
     g = 0
     for i in range(0, len(refs) - 1, 4):
         a, b, c, d = refs[i : i + 4]
@@ -189,9 +189,9 @@
         finish_kernel,
         grid_spec=pltpu.PrefetchScalarGridSpec(
             num_scalar_prefetch=2,
-            grid=(cols // WIDTH,),
-            in_specs=[pl.BlockSpec((part.shape[0], rows, WIDTH), lambda c, *_: (0, 0, c)) for part in parts],
-            out_specs=pl.BlockSpec((rows, irreps, WIDTH), lambda c, *_: (0, 0, c)),
+            grid=(rows // HEIGHT,),
+            in_specs=[pl.BlockSpec((part.shape[0], HEIGHT, cols), lambda r, *_: (0, r, 0)) for part in parts],
+            out_specs=pl.BlockSpec((HEIGHT, irreps, cols), lambda r, *_: (r, 0, 0)),
         ),
         out_shape=jax.ShapeDtypeStruct((rows, irreps, cols), jnp.float32),
         compiler_params=pltpu.CompilerParams(vmem_limit_bytes=VMEM),
@@ -225,9 +225,9 @@
     def along_z(held):
         return [lax.ppermute(held, "vb", steps) for steps in Z_STEPS]
 
-    def multiply(held, moved, first):
+    def multiply(held, moved, first, after):
         pieces = [(piece, 0) for whole in (held, *moved) for piece in (whole, swap(whole))]
-        return product(pieces, ovov, first, held.shape[0], place, pair_sizes, origin, [])
+        return product(pieces, ovov, first, held.shape[0], place, pair_sizes, origin, after)
 
     def to_neighbours(p, m):
         return lax.ppermute(p, BOTH, NEAR[1]), lax.ppermute(m, BOTH, NEAR[-1])
@@ -237,16 +237,16 @@
 
     moved = along_z(early)
     (late,) = tie([late], moved)
-    far_p, far_m, near_p, near_m, up, down, own = multiply(early, moved, 0)
-    moved = tie(along_z(late), [far_p])
-    late_far_p, late_far_m, late_near_p, late_near_m, late_up, late_down, late_own = multiply(late, moved, SPLIT)
-
-    far, near = to_neighbours(far_p, far_m), to_neighbours(near_p, near_m)
-    handed = to_neighbours(*add_far(up, down, *far, [late_far_p]))
-    late_far, late_near = to_neighbours(late_far_p, late_far_m), to_neighbours(late_near_p, late_near_m)
-    late_handed = to_neighbours(*add_far(late_up, late_down, *late_far, []))
-    sums = across(add_own(own, *near, *handed, []))
-    late_sums = across(add_own(late_own, *late_near, *late_handed, sums[1:]))
+    send_p, send_m, up, down, own = multiply(early, moved, 0, [])
+    late, *moved = tie([late, *along_z(late)], [send_p])
+    late_send_p, late_send_m, late_up, late_down, late_own = multiply(late, moved, SPLIT, [])
+
+    got = to_neighbours(send_p, send_m)
+    handed = to_neighbours(*add_far(up, down, *got, [late_send_p]))
+    late_got = to_neighbours(late_send_p, late_send_m)
+    late_handed = to_neighbours(*add_far(late_up, late_down, *late_got, []))
+    sums = across(add_own(own, *got, *handed, []))
+    late_sums = across(add_own(late_own, *late_got, *late_handed, sums[1:2]))
     origin = jnp.stack([ob * out_rows, vb * cols]).astype(jnp.int32)
     return finish([sums, late_sums], row_sizes, origin, irreps)
 

time: 215 us -> 211 us (0.981)
  waiting for transfers between devices: 103 us -> 98.9 us
    ppermute x12 -> x8, waiting for transfers between devices: 35 us -> 31.3 us  [to_neighbours(): return (lax.ppermute(p, BOTH, NEAR[1]), lax.ppermute(m, BOTH, NEAR[-1]))]
    ppermute x12 -> x8, starting transfers between devices: 10.7 us -> 13.1 us  [to_neighbours(): return (lax.ppermute(p, BOTH, NEAR[1]), lax.ppermute(m, BOTH, NEAR[-1]))]
  transfers between devices with their start and end apart: 32 -> 28, of which waited for: 18 -> 13; matrix products, arithmetic and copies ran while one was open for 2% -> 2% of each run, Pallas kernels for 18% -> 21%
where the time goes in v10:
time: 211 us; the launch traced here: 210 us
  waiting for transfers between devices  98.9 us (47%)
  Pallas kernels  48.4 us (23%)
  starting transfers between devices  30.9 us (15%)
  blocking collectives  25.4 us (12%)
  local copies, waits for them, and re-layouts  4.95 us (2%)
    ppermute x6, waiting for transfers between devices, along_z(): return [lax.ppermute(held, 'vb', steps) for steps in Z_STEPS]  34.7 us
    ppermute x8, waiting for transfers between devices, to_neighbours(): return (lax.ppermute(p, BOTH, NEAR[1]), lax.ppermute(m, BOTH, NEAR[-1]))  31.3 us
    ppermute x6, waiting for transfers between devices, across(): lax.ppermute(four[k], BOTH, FAR[d])  30.6 us
    all_to_all x1, blocking collectives, local(): mine = lax.all_to_all(mine, 'ob', split_axis=0, concat_axis=0, tiled=True)  25.4 us
    pallas_call x2, Pallas kernels, product(): pl.pallas_call(functools.partial(product_kernel, first), grid_spec=pltpu....  24.9 us
    ppermute x8, starting transfers between devices, to_neighbours(): return (lax.ppermute(p, BOTH, NEAR[1]), lax.ppermute(m, BOTH, NEAR[-1]))  13.1 us
    pallas_call x2, Pallas kernels, add_own(): pl.pallas_call(own_kernel, grid=(count,), in_specs=[spec(4), spec(2, 1),...  9.79 us
    ppermute x6, starting transfers between devices, along_z(): return [lax.ppermute(held, 'vb', steps) for steps in Z_STEPS]  9.48 us
  transfers between devices with their start and end apart: 28, of which 13 were waited for; matrix products, arithmetic and copies ran while one was open for 2% of the time, Pallas kernels for 21%

profile of v10, /device:TPU:0, one launch (start us, length us, event | category | flops | bytes accessed | tf_op | source)
XLA Modules:
  0.0 209.7 jit_solution(6530609442818310930)
XLA Ops:
  0.0 1.5 copy.23
  1.5 0.4 copy.24
  1.9 25.4 %all_to_all.5 = f32[16,48,384]{2,1,0:T(8,128)S(1)} all-to-all(f32[16,48,384]{2,1,0:T(8,128)S(1)} %bitcast.26), channel_id=1, replica_groups=mesh['vb'=8,'ob'=16] {'ob'}, dimensions={0} | all-to-all | bytes 2359296 | tf_op jit(solution)/shard_map/all_to_all | solution.py:218
  27.4 0.9 copy.26
  28.3 3.9 %collective-permute-start.5 = (f32[4,96,384]{2,1,0:T(8,128)}, f32[4,96,384]{2,1,0:T(8,128)}, u32[]{:S(2)}, u32[]{:S(2)}) collective-permute-start(f32[4,96,384]{2,1,0:T(8,128)} %bitcast.23.refs_0_), channel_id=1, source_target_pairs={{0,64},{16,80},{32,96},{48,112},{64,0},{80,16},{96,32},{112,48},{1... | collective-permute-start | bytes 1769480 | tf_op jit(solution)/shard_map/ppermute | solution.py:226
  32.2 0.7 collective-permute-start.3
  32.9 1.3 collective-permute-start.1
  34.2 12.6 %collective-permute-done.5.refs_6_.refs_3_ = f32[4,96,384]{2,1,0:T(8,128)} collective-permute-done((f32[4,96,384]{2,1,0:T(8,128)}, f32[4,96,384]{2,1,0:T(8,128)}, u32[]{:S(2)}, u32[]{:S(2)}) %collective-permute-start.5) | collective-permute-done | bytes 589856 | tf_op jit(solution)/shard_map/ppermute | solution.py:226
  46.8 0.9 copy.25
  47.6 10.2 %collective-permute-done.3.refs_4_.refs_2_ = f32[4,96,384]{2,1,0:T(8,128)} collective-permute-done((f32[4,96,384]{2,1,0:T(8,128)}, f32[4,96,384]{2,1,0:T(8,128)}, u32[]{:S(2)}, u32[]{:S(2)}) %collective-permute-start.3) | collective-permute-done | bytes 589856 | tf_op jit(solution)/shard_map/ppermute | solution.py:226
  57.8 0.5 collective-permute-start.2
  58.3 1.5 collective-permute-start.11
  59.9 1.6 collective-permute-start.10
  61.5 0.4 collective-permute-start.9
  61.9 0.6 pad_add_fusion.1.origin
  62.5 1.2 dynamic-slice_bitcast_fusion.place
  63.7 12.4 %product.2 = (f32[4,4,48,768]{3,2,1,0:T(8,128)}, f32[4,4,48,768]{3,2,1,0:T(8,128)}, f32[2,4,48,768]{3,2,1,0:T(8,128)}, f32[2,4,48,768]{3,2,1,0:T(8,128)}, f32[4,4,48,768]{3,2,1,0:T(8,128)}) custom-call(s32[16]{0:T(128)} %dynamic-slice_bitcast_fusion.place, s32[8]{0:T(128)} %sizes.4, s32[2]{0:T(128)} %pad_add_fusion.1.origin, f32[4,96,384]{2,1,0:T(8,128)} %bitcast.23.refs_0_, ...), custom_call_target="tpu_custom_call" | custom-call | tf_op jit(solution)/shard_map/product/pallas_call | solution.py:88
  76.1 0.3 collective-permute-done.11.refs_3_
  76.4 11.6 %collective-permute-done.10.refs_2_ = f32[4,96,384]{2,1,0:T(8,128)} collective-permute-done((f32[4,96,384]{2,1,0:T(8,128)}, f32[4,96,384]{2,1,0:T(8,128)}, u32[]{:S(2)}, u32[]{:S(2)}) %collective-permute-start.10) | collective-permute-done | bytes 589856 | tf_op jit(solution)/shard_map/ppermute | solution.py:226
  88.1 0.5 collective-permute-start.7
  88.6 0.5 collective-permute-start.14
  89.1 2.8 %collective-permute-start.8 = (f32[4,4,48,768]{3,2,1,0:T(8,128)}, f32[4,4,48,768]{3,2,1,0:T(8,128)}, u32[]{:S(2)}, u32[]{:S(2)}) collective-permute-start(f32[4,4,48,768]{3,2,1,0:T(8,128)} %get-tuple-element.33), channel_id=1, source_target_pairs={{0,12},{1,13},{2,14},{3,15},{4,0},{5,1},{6,2},{7,3},{8,4},{9,5},{1... | collective-permute-start | bytes 7077896 | tf_op jit(solution)/shard_map/ppermute | solution.py:233
  91.9 0.2 collective-permute-done.14.refs_5_
  92.1 2.1 %collective-permute-done.15.refs_7_ = f32[4,96,384]{2,1,0:T(8,128)} collective-permute-done((f32[4,96,384]{2,1,0:T(8,128)}, f32[4,96,384]{2,1,0:T(8,128)}, u32[]{:S(2)}, u32[]{:S(2)}) %collective-permute-start.15) | collective-permute-done | bytes 589856 | tf_op jit(solution)/shard_map/ppermute | solution.py:223
  94.2 12.5 %product.3 = (f32[4,4,48,768]{3,2,1,0:T(8,128)}, f32[4,4,48,768]{3,2,1,0:T(8,128)}, f32[2,4,48,768]{3,2,1,0:T(8,128)}, f32[2,4,48,768]{3,2,1,0:T(8,128)}, f32[4,4,48,768]{3,2,1,0:T(8,128)}) custom-call(s32[16]{0:T(128)} %dynamic-slice_bitcast_fusion.place, s32[8]{0:T(128)} %sizes.4, s32[2]{0:T(128)} %pad_add_fusion.1.origin, ...), custom_call_target="tpu_custom_call" | custom-call | tf_op jit(solution)/shard_map/product/pallas_call | solution.py:88
  106.7 1.2 collective-permute-start.22
  107.9 0.9 collective-permute-start.21
  108.8 9.7 %collective-permute-done.8.recv_m.m1 = f32[4,4,48,768]{3,2,1,0:T(8,128)} collective-permute-done((f32[4,4,48,768]{3,2,1,0:T(8,128)}, f32[4,4,48,768]{3,2,1,0:T(8,128)}, u32[]{:S(2)}, u32[]{:S(2)}) %collective-permute-start.8) | collective-permute-done | bytes 2359328 | tf_op jit(solution)/shard_map/ppermute | solution.py:233
  118.5 4.4 %add_far.2 = (f32[2,4,48,768]{3,2,1,0:T(8,128)}, f32[2,4,48,768]{3,2,1,0:T(8,128)}) custom-call(f32[2,4,48,768]{3,2,1,0:T(8,128)} %get-tuple-element.34.up, f32[2,4,48,768]{3,2,1,0:T(8,128)} %get-tuple-element.35.down, f32[4,4,48,768]{3,2,1,0:T(8,128)} %collective-permute-done.7.recv_p.p1, f32[4,4,48,768]{3,2,1,0:T(8,128)} %collective-permute-done.8.recv_m.m1, ...), custom_call_target="tpu_custom_call" | custom-call | tf_op jit(solution)/shard_map/add_far/pallas_call | solution.py:135
  122.9 0.6 collective-permute-start.16
  123.5 3.2 %collective-permute-start.17 = (f32[2,4,48,768]{3,2,1,0:T(8,128)}, f32[2,4,48,768]{3,2,1,0:T(8,128)}, u32[]{:S(2)}, u32[]{:S(2)}) collective-permute-start(f32[2,4,48,768]{3,2,1,0:T(8,128)} %get-tuple-element.42), channel_id=1, source_target_pairs={{0,12},{1,13},{2,14},{3,15},{4,0},{5,1},{6,2},{7,3},{8,4},{9,5},{1... | collective-permute-start | bytes 3538952 | tf_op jit(solution)/shard_map/ppermute | solution.py:233
  126.7 17.2 %collective-permute-done.22.recv_m.m1 = f32[4,4,48,768]{3,2,1,0:T(8,128)} collective-permute-done((f32[4,4,48,768]{3,2,1,0:T(8,128)}, f32[4,4,48,768]{3,2,1,0:T(8,128)}, u32[]{:S(2)}, u32[]{:S(2)}) %collective-permute-start.22) | collective-permute-done | bytes 2359328 | tf_op jit(solution)/shard_map/ppermute | solution.py:233
  143.8 4.3 %add_far.3 = (f32[2,4,48,768]{3,2,1,0:T(8,128)}, f32[2,4,48,768]{3,2,1,0:T(8,128)}) custom-call(f32[2,4,48,768]{3,2,1,0:T(8,128)} %get-tuple-element.49.up, f32[2,4,48,768]{3,2,1,0:T(8,128)} %get-tuple-element.50.down, f32[4,4,48,768]{3,2,1,0:T(8,128)} %collective-permute-done.21.recv_p.p1, f32[4,4,48,768]{3,2,1,0:T(8,128)} %collective-permute-done.22.recv_m.m1), custom_call_target="tpu_custom_call" | custom-call | tf_op jit(solution)/shard_map/add_far/pallas_call | solution.py:135
  148.1 0.6 collective-permute-start.23
  148.7 3.3 %collective-permute-start.24 = (f32[2,4,48,768]{3,2,1,0:T(8,128)}, f32[2,4,48,768]{3,2,1,0:T(8,128)}, u32[]{:S(2)}, u32[]{:S(2)}) collective-permute-start(f32[2,4,48,768]{3,2,1,0:T(8,128)} %get-tuple-element.52), channel_id=1, source_target_pairs={{0,12},{1,13},{2,14},{3,15},{4,0},{5,1},{6,2},{7,3},{8,4},{9,5},{1... | collective-permute-start | bytes 3538952 | tf_op jit(solution)/shard_map/ppermute | solution.py:233
  152.1 4.3 %collective-permute-done.16.p2 = f32[2,4,48,768]{3,2,1,0:T(8,128)} collective-permute-done((f32[2,4,48,768]{3,2,1,0:T(8,128)}, f32[2,4,48,768]{3,2,1,0:T(8,128)}, u32[]{:S(2)}, u32[]{:S(2)}) %collective-permute-start.16) | collective-permute-done | bytes 1179680 | tf_op jit(solution)/shard_map/ppermute | solution.py:233
  156.5 4.9 %add_own.2 = (f32[4,48,768]{2,1,0:T(8,128)}, f32[4,48,768]{2,1,0:T(8,128)}, f32[4,48,768]{2,1,0:T(8,128)}, f32[4,48,768]{2,1,0:T(8,128)}) custom-call(f32[4,4,48,768]{3,2,1,0:T(8,128)} %get-tuple-element.31.own, f32[4,4,48,768]{3,2,1,0:T(8,128)} %collective-permute-done.7.recv_p.p1, f32[4,4,48,768]{3,2,1,0:T(8,128)} %collective-permute-done.8.recv_m.m1, ...), custom_call_target="tpu_custom_call" | custom-call | tf_op jit(solution)/shard_map/add_own/pallas_call | solution.py:161
  161.4 0.3 collective-permute-start.18
  161.7 3.3 %collective-permute-start.19 = (f32[4,48,768]{2,1,0:T(8,128)}, f32[4,48,768]{2,1,0:T(8,128)}, u32[]{:S(2)}, u32[]{:S(2)}) collective-permute-start(f32[4,48,768]{2,1,0:T(8,128)} %get-tuple-element.45), channel_id=1, source_target_pairs={{0,2},{1,3},{2,0},{3,1},{4,6},{5,7},{6,4},{7,5},{8,10},{9,11},{10,... | collective-permute-start | bytes 1769480 | tf_op jit(solution)/shard_map/ppermute | solution.py:236
  165.0 0.4 collective-permute-start.20
  165.4 15.7 %collective-permute-done.18.refs_0_.refs_1_ = f32[4,48,768]{2,1,0:T(8,128)} collective-permute-done((f32[4,48,768]{2,1,0:T(8,128)}, f32[4,48,768]{2,1,0:T(8,128)}, u32[]{:S(2)}, u32[]{:S(2)}) %collective-permute-start.18) | collective-permute-done | bytes 589856 | tf_op jit(solution)/shard_map/ppermute | solution.py:236
  181.2 4.9 %add_own.3 = (f32[4,48,768]{2,1,0:T(8,128)}, f32[4,48,768]{2,1,0:T(8,128)}, f32[4,48,768]{2,1,0:T(8,128)}, f32[4,48,768]{2,1,0:T(8,128)}) custom-call(f32[4,4,48,768]{3,2,1,0:T(8,128)} %get-tuple-element.47.own, f32[4,4,48,768]{3,2,1,0:T(8,128)} %collective-permute-done.21.recv_p.p1, f32[4,4,48,768]{3,2,1,0:T(8,128)} %collective-permute-done.22.recv_m.m1, ...), custom_call_target="tpu_custom_call" | custom-call | tf_op jit(solution)/shard_map/add_own/pallas_call | solution.py:161
  186.0 1.0 collective-permute-start.26
  187.1 2.2 %collective-permute-start.27 = (f32[4,48,768]{2,1,0:T(8,128)}, f32[4,48,768]{2,1,0:T(8,128)}, u32[]{:S(2)}, u32[]{:S(2)}) collective-permute-start(f32[4,48,768]{2,1,0:T(8,128)} %get-tuple-element.56), channel_id=1, source_target_pairs={{0,3},{1,0},{2,1},{3,2},{4,7},{5,4},{6,5},{7,6},{8,11},{9,8},{10,9... | collective-permute-start | bytes 1769480 | tf_op jit(solution)/shard_map/ppermute | solution.py:236
  189.3 0.6 pad_add_fusion.origin
  189.8 13.9 %collective-permute-done.25.refs_5_ = f32[4,48,768]{2,1,0:T(8,128)} collective-permute-done((f32[4,48,768]{2,1,0:T(8,128)}, f32[4,48,768]{2,1,0:T(8,128)}, u32[]{:S(2)}, u32[]{:S(2)}) %collective-permute-start.25) | collective-permute-done | bytes 589856 | tf_op jit(solution)/shard_map/ppermute | solution.py:236
  203.8 0.9 collective-permute-done.27.refs_7_
  204.7 5.0 %finish.1 = f32[48,8,768]{2,1,0:T(8,128)} custom-call(s32[8]{0:T(128)} %sizes.5, s32[2]{0:T(128)} %pad_add_fusion.origin, f32[4,48,768]{2,1,0:T(8,128)} %get-tuple-element.43.refs_0_, f32[4,48,768]{2,1,0:T(8,128)} %collective-permute-done.18.refs_0_.refs_1_, f32[4,48,768]{2,1,0:T(8,128)} %collective-permute-done.19.refs_2_, ...), custom_call_target="tpu_custom_call" | custom-call | tf_op jit(solution)/shard_map/finish/pallas_call | solution.py:188
  (26 shorter events, 0.3 us)
Async XLA Ops:
  28.3 18.5 %collective-permute-start.5 = (f32[4,96,384]{2,1,0:T(8,128)}, f32[4,96,384]{2,1,0:T(8,128)}, u32[]{:S(2)}, u32[]{:S(2)}) collective-permute-start(f32[4,96,384]{2,1,0:T(8,128)} %bitcast.23.refs_0_), channel_id=1, source_target_pairs={{0,64},{16,80},{32,96},{48,112},{64,0},{80,16},{96,32},{112,48},{1... | collective-permute-start | bytes 1769480 | tf_op jit(solution)/shard_map/ppermute | solution.py:226
  32.2 25.7 %collective-permute-start.3 = (f32[4,96,384]{2,1,0:T(8,128)}, f32[4,96,384]{2,1,0:T(8,128)}, u32[]{:S(2)}, u32[]{:S(2)}) collective-permute-start(f32[4,96,384]{2,1,0:T(8,128)} %bitcast.23.refs_0_), channel_id=1, source_target_pairs={{0,96},{16,48},{32,0},{48,80},{64,32},{80,112},{96,64},{112,16},{1... | collective-permute-start | bytes 1769480 | tf_op jit(solution)/shard_map/ppermute | solution.py:226
  32.9 25.0 %collective-permute-start.1 = (f32[4,96,384]{2,1,0:T(8,128)}, f32[4,96,384]{2,1,0:T(8,128)}, u32[]{:S(2)}, u32[]{:S(2)}) collective-permute-start(f32[4,96,384]{2,1,0:T(8,128)} %bitcast.23.refs_0_), channel_id=1, source_target_pairs={{0,32},{16,112},{32,64},{48,16},{64,96},{80,48},{96,0},{112,80},{1... | collective-permute-start | bytes 1769480 | tf_op jit(solution)/shard_map/ppermute | solution.py:226
  34.2 25.7 %collective-permute-start = (f32[4,96,384]{2,1,0:T(8,128)}, f32[4,96,384]{2,1,0:T(8,128)}, u32[]{:S(2)}, u32[]{:S(2)}) collective-permute-start(f32[4,96,384]{2,1,0:T(8,128)} %bitcast.23.refs_0_), channel_id=1, source_target_pairs={{0,16},{16,0},{32,48},{48,32},{64,80},{80,64},{96,112},{112,96},{1... | collective-permute-start | bytes 1769480 | tf_op jit(solution)/shard_map/ppermute | solution.py:223
  46.8 14.8 %collective-permute-start.6 = (f32[4,96,384]{2,1,0:T(8,128)}, f32[4,96,384]{2,1,0:T(8,128)}, u32[]{:S(2)}, u32[]{:S(2)}) collective-permute-start(f32[4,96,384]{2,1,0:T(8,128)} %collective-permute-done.5.refs_6_.refs_3_), channel_id=1, source_target_pairs={{0,16},{16,0},{32,48},{48,32},{64,80},{80,64},{96,112},{112,96},{1... | collective-permute-start | bytes 1769480 | tf_op jit(solution)/shard_map/ppermute | solution.py:223
  57.8 5.9 %collective-permute-start.4 = (f32[4,96,384]{2,1,0:T(8,128)}, f32[4,96,384]{2,1,0:T(8,128)}, u32[]{:S(2)}, u32[]{:S(2)}) collective-permute-start(f32[4,96,384]{2,1,0:T(8,128)} %collective-permute-done.3.refs_4_.refs_2_), channel_id=1, source_target_pairs={{0,16},{16,0},{32,48},{48,32},{64,80},{80,64},{96,112},{112,96},{1... | collective-permute-start | bytes 1769480 | tf_op jit(solution)/shard_map/ppermute | solution.py:223
  57.8 5.9 %collective-permute-start.2 = (f32[4,96,384]{2,1,0:T(8,128)}, f32[4,96,384]{2,1,0:T(8,128)}, u32[]{:S(2)}, u32[]{:S(2)}) collective-permute-start(f32[4,96,384]{2,1,0:T(8,128)} %collective-permute-done.1.refs_2_.refs_1_), channel_id=1, source_target_pairs={{0,16},{16,0},{32,48},{48,32},{64,80},{80,64},{96,112},{112,96},{1... | collective-permute-start | bytes 1769480 | tf_op jit(solution)/shard_map/ppermute | solution.py:223
  58.3 18.1 %collective-permute-start.11 = (f32[4,96,384]{2,1,0:T(8,128)}, f32[4,96,384]{2,1,0:T(8,128)}, u32[]{:S(2)}, u32[]{:S(2)}) collective-permute-start(f32[4,96,384]{2,1,0:T(8,128)} %tie.2.refs_0_), channel_id=1, source_target_pairs={{0,64},{16,80},{32,96},{48,112},{64,0},{80,16},{96,32},{112,48},{1... | collective-permute-start | bytes 1769480 | tf_op jit(solution)/shard_map/ppermute | solution.py:226
  59.9 28.1 %collective-permute-start.10 = (f32[4,96,384]{2,1,0:T(8,128)}, f32[4,96,384]{2,1,0:T(8,128)}, u32[]{:S(2)}, u32[]{:S(2)}) collective-permute-start(f32[4,96,384]{2,1,0:T(8,128)} %tie.2.refs_0_), channel_id=1, source_target_pairs={{0,96},{16,48},{32,0},{48,80},{64,32},{80,112},{96,64},{112,16},{1... | collective-permute-start | bytes 1769480 | tf_op jit(solution)/shard_map/ppermute | solution.py:226
  61.5 26.5 %collective-permute-start.9 = (f32[4,96,384]{2,1,0:T(8,128)}, f32[4,96,384]{2,1,0:T(8,128)}, u32[]{:S(2)}, u32[]{:S(2)}) collective-permute-start(f32[4,96,384]{2,1,0:T(8,128)} %tie.2.refs_0_), channel_id=1, source_target_pairs={{0,32},{16,112},{32,64},{48,16},{64,96},{80,48},{96,0},{112,80},{1... | collective-permute-start | bytes 1769480 | tf_op jit(solution)/shard_map/ppermute | solution.py:226
  88.0 3.8 %collective-permute-start.12 = (f32[4,96,384]{2,1,0:T(8,128)}, f32[4,96,384]{2,1,0:T(8,128)}, u32[]{:S(2)}, u32[]{:S(2)}) collective-permute-start(f32[4,96,384]{2,1,0:T(8,128)} %get-tuple-element.36.refs_0_), channel_id=1, source_target_pairs={{0,16},{16,0},{32,48},{48,32},{64,80},{80,64},{96,112},{112,96},{1... | collective-permute-start | bytes 1769480 | tf_op jit(solution)/shard_map/ppermute | solution.py:223
  88.1 30.5 %collective-permute-start.7 = (f32[4,4,48,768]{3,2,1,0:T(8,128)}, f32[4,4,48,768]{3,2,1,0:T(8,128)}, u32[]{:S(2)}, u32[]{:S(2)}) collective-permute-start(f32[4,4,48,768]{3,2,1,0:T(8,128)} %get-tuple-element.32.refs_4_), channel_id=1, source_target_pairs={{0,4},{1,5},{2,6},{3,7},{4,8},{5,9},{6,10},{7,11},{8,12},{9,13},{1... | collective-permute-start | bytes 7077896 | tf_op jit(solution)/shard_map/ppermute | solution.py:233
  88.5 3.3 %collective-permute-start.13 = (f32[4,96,384]{2,1,0:T(8,128)}, f32[4,96,384]{2,1,0:T(8,128)}, u32[]{:S(2)}, u32[]{:S(2)}) collective-permute-start(f32[4,96,384]{2,1,0:T(8,128)} %get-tuple-element.37.refs_2_), channel_id=1, source_target_pairs={{0,16},{16,0},{32,48},{48,32},{64,80},{80,64},{96,112},{112,96},{1... | collective-permute-start | bytes 1769480 | tf_op jit(solution)/shard_map/ppermute | solution.py:223
  88.6 3.5 %collective-permute-start.14 = (f32[4,96,384]{2,1,0:T(8,128)}, f32[4,96,384]{2,1,0:T(8,128)}, u32[]{:S(2)}, u32[]{:S(2)}) collective-permute-start(f32[4,96,384]{2,1,0:T(8,128)} %get-tuple-element.38.refs_4_), channel_id=1, source_target_pairs={{0,16},{16,0},{32,48},{48,32},{64,80},{80,64},{96,112},{112,96},{1... | collective-permute-start | bytes 1769480 | tf_op jit(solution)/shard_map/ppermute | solution.py:223
  89.1 29.5 %collective-permute-start.8 = (f32[4,4,48,768]{3,2,1,0:T(8,128)}, f32[4,4,48,768]{3,2,1,0:T(8,128)}, u32[]{:S(2)}, u32[]{:S(2)}) collective-permute-start(f32[4,4,48,768]{3,2,1,0:T(8,128)} %get-tuple-element.33), channel_id=1, source_target_pairs={{0,12},{1,13},{2,14},{3,15},{4,0},{5,1},{6,2},{7,3},{8,4},{9,5},{1... | collective-permute-start | bytes 7077896 | tf_op jit(solution)/shard_map/ppermute | solution.py:233
  91.9 2.3 %collective-permute-start.15 = (f32[4,96,384]{2,1,0:T(8,128)}, f32[4,96,384]{2,1,0:T(8,128)}, u32[]{:S(2)}, u32[]{:S(2)}) collective-permute-start(f32[4,96,384]{2,1,0:T(8,128)} %get-tuple-element.39.refs_6_), channel_id=1, source_target_pairs={{0,16},{16,0},{32,48},{48,32},{64,80},{80,64},{96,112},{112,96},{1... | collective-permute-start | bytes 1769480 | tf_op jit(solution)/shard_map/ppermute | solution.py:223
  106.7 37.1 %collective-permute-start.22 = (f32[4,4,48,768]{3,2,1,0:T(8,128)}, f32[4,4,48,768]{3,2,1,0:T(8,128)}, u32[]{:S(2)}, u32[]{:S(2)}) collective-permute-start(f32[4,4,48,768]{3,2,1,0:T(8,128)} %get-tuple-element.48), channel_id=1, source_target_pairs={{0,12},{1,13},{2,14},{3,15},{4,0},{5,1},{6,2},{7,3},{8,4},{9,5},{1... | collective-permute-start | bytes 7077896 | tf_op jit(solution)/shard_map/ppermute | solution.py:233
  107.9 35.9 %collective-permute-start.21 = (f32[4,4,48,768]{3,2,1,0:T(8,128)}, f32[4,4,48,768]{3,2,1,0:T(8,128)}, u32[]{:S(2)}, u32[]{:S(2)}) collective-permute-start(f32[4,4,48,768]{3,2,1,0:T(8,128)} %get-tuple-element.40.refs_0_), channel_id=1, source_target_pairs={{0,4},{1,5},{2,6},{3,7},{4,8},{5,9},{6,10},{7,11},{8,12},{9,13},{1... | collective-permute-start | bytes 7077896 | tf_op jit(solution)/shard_map/ppermute | solution.py:233
  122.9 33.5 %collective-permute-start.16 = (f32[2,4,48,768]{3,2,1,0:T(8,128)}, f32[2,4,48,768]{3,2,1,0:T(8,128)}, u32[]{:S(2)}, u32[]{:S(2)}) collective-permute-start(f32[2,4,48,768]{3,2,1,0:T(8,128)} %get-tuple-element.41), channel_id=1, source_target_pairs={{0,4},{1,5},{2,6},{3,7},{4,8},{5,9},{6,10},{7,11},{8,12},{9,13},{1... | collective-permute-start | bytes 3538952 | tf_op jit(solution)/shard_map/ppermute | solution.py:233
  123.5 33.0 %collective-permute-start.17 = (f32[2,4,48,768]{3,2,1,0:T(8,128)}, f32[2,4,48,768]{3,2,1,0:T(8,128)}, u32[]{:S(2)}, u32[]{:S(2)}) collective-permute-start(f32[2,4,48,768]{3,2,1,0:T(8,128)} %get-tuple-element.42), channel_id=1, source_target_pairs={{0,12},{1,13},{2,14},{3,15},{4,0},{5,1},{6,2},{7,3},{8,4},{9,5},{1... | collective-permute-start | bytes 3538952 | tf_op jit(solution)/shard_map/ppermute | solution.py:233
  148.1 33.0 %collective-permute-start.23 = (f32[2,4,48,768]{3,2,1,0:T(8,128)}, f32[2,4,48,768]{3,2,1,0:T(8,128)}, u32[]{:S(2)}, u32[]{:S(2)}) collective-permute-start(f32[2,4,48,768]{3,2,1,0:T(8,128)} %get-tuple-element.51), channel_id=1, source_target_pairs={{0,4},{1,5},{2,6},{3,7},{4,8},{5,9},{6,10},{7,11},{8,12},{9,13},{1... | collective-permute-start | bytes 3538952 | tf_op jit(solution)/shard_map/ppermute | solution.py:233
  148.7 32.4 %collective-permute-start.24 = (f32[2,4,48,768]{3,2,1,0:T(8,128)}, f32[2,4,48,768]{3,2,1,0:T(8,128)}, u32[]{:S(2)}, u32[]{:S(2)}) collective-permute-start(f32[2,4,48,768]{3,2,1,0:T(8,128)} %get-tuple-element.52), channel_id=1, source_target_pairs={{0,12},{1,13},{2,14},{3,15},{4,0},{5,1},{6,2},{7,3},{8,4},{9,5},{1... | collective-permute-start | bytes 3538952 | tf_op jit(solution)/shard_map/ppermute | solution.py:233
  161.4 19.8 %collective-permute-start.18 = (f32[4,48,768]{2,1,0:T(8,128)}, f32[4,48,768]{2,1,0:T(8,128)}, u32[]{:S(2)}, u32[]{:S(2)}) collective-permute-start(f32[4,48,768]{2,1,0:T(8,128)} %get-tuple-element.44), channel_id=1, source_target_pairs={{0,1},{1,2},{2,3},{3,0},{4,5},{5,6},{6,7},{7,4},{8,9},{9,10},{10,1... | collective-permute-start | bytes 1769480 | tf_op jit(solution)/shard_map/ppermute | solution.py:236
  161.7 28.2 %collective-permute-start.19 = (f32[4,48,768]{2,1,0:T(8,128)}, f32[4,48,768]{2,1,0:T(8,128)}, u32[]{:S(2)}, u32[]{:S(2)}) collective-permute-start(f32[4,48,768]{2,1,0:T(8,128)} %get-tuple-element.45), channel_id=1, source_target_pairs={{0,2},{1,3},{2,0},{3,1},{4,6},{5,7},{6,4},{7,5},{8,10},{9,11},{10,... | collective-permute-start | bytes 1769480 | tf_op jit(solution)/shard_map/ppermute | solution.py:236
  165.0 24.8 %collective-permute-start.20 = (f32[4,48,768]{2,1,0:T(8,128)}, f32[4,48,768]{2,1,0:T(8,128)}, u32[]{:S(2)}, u32[]{:S(2)}) collective-permute-start(f32[4,48,768]{2,1,0:T(8,128)} %get-tuple-element.46), channel_id=1, source_target_pairs={{0,3},{1,0},{2,1},{3,2},{4,7},{5,4},{6,5},{7,6},{8,11},{9,8},{10,9... | collective-permute-start | bytes 1769480 | tf_op jit(solution)/shard_map/ppermute | solution.py:236
  186.0 17.7 %collective-permute-start.25 = (f32[4,48,768]{2,1,0:T(8,128)}, f32[4,48,768]{2,1,0:T(8,128)}, u32[]{:S(2)}, u32[]{:S(2)}) collective-permute-start(f32[4,48,768]{2,1,0:T(8,128)} %get-tuple-element.54), channel_id=1, source_target_pairs={{0,1},{1,2},{2,3},{3,0},{4,5},{5,6},{6,7},{7,4},{8,9},{9,10},{10,1... | collective-permute-start | bytes 1769480 | tf_op jit(solution)/shard_map/ppermute | solution.py:236
  186.0 17.7 %collective-permute-start.26 = (f32[4,48,768]{2,1,0:T(8,128)}, f32[4,48,768]{2,1,0:T(8,128)}, u32[]{:S(2)}, u32[]{:S(2)}) collective-permute-start(f32[4,48,768]{2,1,0:T(8,128)} %get-tuple-element.55), channel_id=1, source_target_pairs={{0,2},{1,3},{2,0},{3,1},{4,6},{5,7},{6,4},{7,5},{8,10},{9,11},{10,... | collective-permute-start | bytes 1769480 | tf_op jit(solution)/shard_map/ppermute | solution.py:236
  187.1 17.6 %collective-permute-start.27 = (f32[4,48,768]{2,1,0:T(8,128)}, f32[4,48,768]{2,1,0:T(8,128)}, u32[]{:S(2)}, u32[]{:S(2)}) collective-permute-start(f32[4,48,768]{2,1,0:T(8,128)} %get-tuple-element.56), channel_id=1, source_target_pairs={{0,3},{1,0},{2,1},{3,2},{4,7},{5,4},{6,5},{7,6},{8,11},{9,8},{10,9... | collective-permute-start | bytes 1769480 | tf_op jit(solution)/shard_map/ppermute | solution.py:236

commit v11 on v9

--- a/solution.py
+++ b/solution.py
@@ -10,7 +10,7 @@
 
 SIDE = 4
 VMEM = 64 * 1024 * 1024 - 256 * 1024
-WIDTH = 256
+STEP = 2
 LIGHT = pl.CostEstimate(flops=0, bytes_accessed=0, transcendentals=0)
 def hops(count, steps):
     pairs = []
@@ -131,10 +131,10 @@
 
 def add_far(up, down, recv_p, recv_m, after):
     lead, count, rows, cols = up.shape
-    spec = pl.BlockSpec((lead, 1, rows, cols), lambda g: (0, g, 0, 0))
+    spec = pl.BlockSpec((lead, STEP, rows, cols), lambda g: (0, g, 0, 0))
     return pl.pallas_call(
         add_kernel,
-        grid=(count,),
+        grid=(count // STEP,),
         in_specs=[spec] * 4 + [pl.BlockSpec(memory_space=pl.ANY)] * len(after),
         out_specs=[spec] * 2,
         out_shape=[jax.ShapeDtypeStruct(up.shape, jnp.float32)] * 2,
@@ -146,23 +146,23 @@
 
 def own_kernel(own, n1, n2, p2, m2, *refs):
     outs = refs[-4:]
-    outs[0][0] = own[0, 0] + (p2[0, 0] + n2[0, 0])
-    outs[1][0] = own[1, 0] + (p2[1, 0] + n2[1, 0])
-    outs[2][0] = own[2, 0] + (m2[0, 0] + n1[0, 0])
-    outs[3][0] = own[3, 0] + (m2[1, 0] + n1[1, 0])
+    outs[0][...] = own[0] + (p2[0] + n2[0])
+    outs[1][...] = own[1] + (p2[1] + n2[1])
+    outs[2][...] = own[2] + (m2[0] + n1[0])
+    outs[3][...] = own[3] + (m2[1] + n1[1])
 
 
 def add_own(own, n1, n2, p2, m2, after):
     count, rows, cols = own.shape[1:]
 
     def spec(lead):
-        return pl.BlockSpec((lead, 1, rows, cols), lambda g: (0, g, 0, 0))
+        return pl.BlockSpec((lead, STEP, rows, cols), lambda g: (0, g, 0, 0))
 
     return pl.pallas_call(
         own_kernel,
-        grid=(count,),
+        grid=(count // STEP,),
         in_specs=[spec(4)] + [spec(2)] * 4 + [pl.BlockSpec(memory_space=pl.ANY)] * len(after),
-        out_specs=[pl.BlockSpec((1, rows, cols), lambda g: (g, 0, 0))] * 4,
+        out_specs=[pl.BlockSpec((STEP, rows, cols), lambda g: (g, 0, 0))] * 4,
         out_shape=[jax.ShapeDtypeStruct((count, rows, cols), jnp.float32)] * 4,
         compiler_params=pltpu.CompilerParams(vmem_limit_bytes=VMEM),
         cost_estimate=LIGHT,
@@ -189,9 +189,9 @@
         finish_kernel,
         grid_spec=pltpu.PrefetchScalarGridSpec(
             num_scalar_prefetch=2,
-            grid=(cols // WIDTH,),
-            in_specs=[pl.BlockSpec((part.shape[0], rows, WIDTH), lambda c, *_: (0, 0, c)) for part in parts],
-            out_specs=pl.BlockSpec((rows, irreps, WIDTH), lambda c, *_: (0, 0, c)),
+            grid=(1,),
+            in_specs=[pl.BlockSpec(part.shape, lambda r, *_: (0, 0, 0)) for part in parts],
+            out_specs=pl.BlockSpec((rows, irreps, cols), lambda r, *_: (0, 0, 0)),
         ),
         out_shape=jax.ShapeDtypeStruct((rows, irreps, cols), jnp.float32),
         compiler_params=pltpu.CompilerParams(vmem_limit_bytes=VMEM),
@@ -225,9 +225,9 @@
     def along_z(held):
         return [lax.ppermute(held, "vb", steps) for steps in Z_STEPS]
 
-    def multiply(held, moved, first):
-        pieces = [(piece, 0) for whole in (held, *moved) for piece in (whole, swap(whole))]
-        return product(pieces, ovov, first, held.shape[0], place, pair_sizes, origin, [])
+    def multiply(held, swapped, moved, moved_swapped, first, after):
+        pieces = [(held, 0), (swapped, 0)] + [(piece, 0) for pair in zip(moved, moved_swapped) for piece in pair]
+        return product(pieces, ovov, first, held.shape[0], place, pair_sizes, origin, after)
 
     def to_neighbours(p, m):
         return lax.ppermute(p, BOTH, NEAR[1]), lax.ppermute(m, BOTH, NEAR[-1])
@@ -235,18 +235,24 @@
     def across(four):
         return [four[0]] + [lax.ppermute(four[k], BOTH, FAR[d]) for k, d in ((1, 1), (2, 2), (3, -1))]
 
+    late_swapped = swap(late)
     moved = along_z(early)
     (late,) = tie([late], moved)
-    far_p, far_m, near_p, near_m, up, down, own = multiply(early, moved, 0)
-    moved = tie(along_z(late), [far_p])
-    late_far_p, late_far_m, late_near_p, late_near_m, late_up, late_down, late_own = multiply(late, moved, SPLIT)
-
+    far_p, far_m, near_p, near_m, up, down, own = multiply(early, swap(early), moved, [swap(piece) for piece in moved], 0, [late_swapped])
     far, near = to_neighbours(far_p, far_m), to_neighbours(near_p, near_m)
-    handed = to_neighbours(*add_far(up, down, *far, [late_far_p]))
+    up_z, down_z, far_z = along_z(late)
+    down_z, far_z = tie([down_z, far_z], [far_p])
+    down_swapped, far_swapped = swap(down_z), swap(far_z)
+    (up_z,) = tie([up_z], [*far, down_swapped])
+    late_far_p, late_far_m, late_near_p, late_near_m, late_up, late_down, late_own = multiply(
+        late, late_swapped, (up_z, down_z, far_z), (swap(up_z), down_swapped, far_swapped), SPLIT, []
+    )
+
+    handed = to_neighbours(*add_far(up, down, *far, [late_far_p, *near]))
     late_far, late_near = to_neighbours(late_far_p, late_far_m), to_neighbours(late_near_p, late_near_m)
     late_handed = to_neighbours(*add_far(late_up, late_down, *late_far, []))
     sums = across(add_own(own, *near, *handed, []))
-    late_sums = across(add_own(late_own, *late_near, *late_handed, sums[1:]))
+    late_sums = across(add_own(late_own, *late_near, *late_handed, sums[1:2]))
     origin = jnp.stack([ob * out_rows, vb * cols]).astype(jnp.int32)
     return finish([sums, late_sums], row_sizes, origin, irreps)
 

time: 215 us -> 206 us (0.958)
  waiting for transfers between devices: 103 us -> 99.4 us
  Pallas kernels: 48.2 us -> 44.8 us
    ppermute x6, waiting for transfers between devices: 32.4 us -> 17 us  [across(): lax.ppermute(four[k], BOTH, FAR[d])]
    ppermute x12, waiting for transfers between devices: 35 us -> 46.7 us  [to_neighbours(): return (lax.ppermute(p, BOTH, NEAR[1]), lax.ppermute(m, BOTH, NEAR[-1]))]
    pallas_call x4, Pallas kernels: 18.4 us -> 15.4 us  [the longest x2 8.45 us: add_own(): pl.pallas_call(own_kernel, grid=(count // STEP,), in_specs=[spec(4)] + [s...]
  transfers between devices with their start and end apart: 32 -> 32, of which waited for: 18 -> 15; matrix products, arithmetic and copies ran while one was open for 2% -> 1% of each run, Pallas kernels for 18% -> 20%
where the time goes in v11:
time: 206 us; the launch traced here: 205 us
  waiting for transfers between devices  99.4 us (48%)
  Pallas kernels  44.8 us (22%)
  starting transfers between devices  29.4 us (14%)
  blocking collectives  25.4 us (12%)
  local copies, waits for them, and re-layouts  5 us (2%)
    ppermute x12, waiting for transfers between devices, to_neighbours(): return (lax.ppermute(p, BOTH, NEAR[1]), lax.ppermute(m, BOTH, NEAR[-1]))  46.7 us
    ppermute x6, waiting for transfers between devices, along_z(): return [lax.ppermute(held, 'vb', steps) for steps in Z_STEPS]  33.3 us
    all_to_all x1, blocking collectives, local(): mine = lax.all_to_all(mine, 'ob', split_axis=0, concat_axis=0, tiled=True)  25.4 us
    pallas_call x2, Pallas kernels, product(): pl.pallas_call(functools.partial(product_kernel, first), grid_spec=pltpu....  24.9 us
    ppermute x6, waiting for transfers between devices, across(): lax.ppermute(four[k], BOTH, FAR[d])  17 us
    ppermute x12, starting transfers between devices, to_neighbours(): return (lax.ppermute(p, BOTH, NEAR[1]), lax.ppermute(m, BOTH, NEAR[-1]))  11.5 us
    ppermute x6, starting transfers between devices, along_z(): return [lax.ppermute(held, 'vb', steps) for steps in Z_STEPS]  9.48 us
    pallas_call x2, Pallas kernels, add_own(): pl.pallas_call(own_kernel, grid=(count // STEP,), in_specs=[spec(4)] + [s...  8.45 us
  transfers between devices with their start and end apart: 32, of which 15 were waited for; matrix products, arithmetic and copies ran while one was open for 1% of the time, Pallas kernels for 20%

profile of v11, /device:TPU:0, one launch (start us, length us, event | category | flops | bytes accessed | tf_op | source)
XLA Modules:
  0.0 205.2 jit_solution(1100421294116091915)
XLA Ops:
  0.0 1.5 copy.22
  1.9 25.4 %all_to_all.5 = f32[16,48,384]{2,1,0:T(8,128)S(1)} all-to-all(f32[16,48,384]{2,1,0:T(8,128)S(1)} %bitcast.27), channel_id=1, replica_groups=mesh['vb'=8,'ob'=16] {'ob'}, dimensions={0} | all-to-all | bytes 2359296 | tf_op jit(solution)/shard_map/all_to_all | solution.py:218
  27.4 0.9 copy.25
  28.3 3.9 %collective-permute-start.5 = (f32[4,96,384]{2,1,0:T(8,128)}, f32[4,96,384]{2,1,0:T(8,128)}, u32[]{:S(2)}, u32[]{:S(2)}) collective-permute-start(f32[4,96,384]{2,1,0:T(8,128)} %bitcast.23.refs_0_), channel_id=1, source_target_pairs={{0,64},{16,80},{32,96},{48,112},{64,0},{80,16},{96,32},{112,48},{1... | collective-permute-start | bytes 1769480 | tf_op jit(solution)/shard_map/ppermute | solution.py:226
  32.2 0.7 collective-permute-start.3
  32.9 1.3 collective-permute-start.1
  34.3 0.9 copy-done
  35.1 0.5 collective-permute-start
  35.6 11.1 %collective-permute-done.5.refs_6_.refs_3_ = f32[4,96,384]{2,1,0:T(8,128)} collective-permute-done((f32[4,96,384]{2,1,0:T(8,128)}, f32[4,96,384]{2,1,0:T(8,128)}, u32[]{:S(2)}, u32[]{:S(2)}) %collective-permute-start.5) | collective-permute-done | bytes 589856 | tf_op jit(solution)/shard_map/ppermute | solution.py:226
  46.8 11.1 %collective-permute-done.3.refs_4_.refs_2_ = f32[4,96,384]{2,1,0:T(8,128)} collective-permute-done((f32[4,96,384]{2,1,0:T(8,128)}, f32[4,96,384]{2,1,0:T(8,128)}, u32[]{:S(2)}, u32[]{:S(2)}) %collective-permute-start.3) | collective-permute-done | bytes 589856 | tf_op jit(solution)/shard_map/ppermute | solution.py:226
  57.8 0.5 collective-permute-start.2
  58.3 0.6 pad_add_fusion.1.origin
  58.9 1.2 dynamic-slice_bitcast_fusion.place
  60.1 1.6 collective-permute-start.14
  61.7 1.6 collective-permute-start.13
  63.3 12.4 %product.2 = (f32[2,4,48,768]{3,2,1,0:T(8,128)}, f32[2,4,48,768]{3,2,1,0:T(8,128)}, f32[2,4,48,768]{3,2,1,0:T(8,128)}, f32[2,4,48,768]{3,2,1,0:T(8,128)}, f32[2,...) custom-call(s32[16]{0:T(128)} %dynamic-slice_bitcast_fusion.place, s32[8]{0:T(128)} %sizes.4, ...), custom_call_target="tpu_custom_call" | custom-call | tf_op jit(solution)/shard_map/product/pallas_call | solution.py:88
  75.8 1.1 collective-permute-start.11
  76.9 1.0 collective-permute-start.10
  78.2 8.7 %collective-permute-done.13.refs_0_ = f32[4,96,384]{2,1,0:T(8,128)} collective-permute-done((f32[4,96,384]{2,1,0:T(8,128)}, f32[4,96,384]{2,1,0:T(8,128)}, u32[]{:S(2)}, u32[]{:S(2)}) %collective-permute-start.13) | collective-permute-done | bytes 589856 | tf_op jit(solution)/shard_map/ppermute | solution.py:226
  87.0 0.4 collective-permute-start.8
  87.4 2.4 %collective-permute-done.12.refs_0_ = f32[4,96,384]{2,1,0:T(8,128)} collective-permute-done((f32[4,96,384]{2,1,0:T(8,128)}, f32[4,96,384]{2,1,0:T(8,128)}, u32[]{:S(2)}, u32[]{:S(2)}) %collective-permute-start.12) | collective-permute-done | bytes 589856 | tf_op jit(solution)/shard_map/ppermute | solution.py:226
  89.8 1.7 collective-permute-start.9
  91.5 0.8 collective-permute-done.11.refs_2_.recv_m
  92.3 2.3 %collective-permute-done.10.refs_1_.recv_p = f32[2,4,48,768]{3,2,1,0:T(8,128)} collective-permute-done((f32[2,4,48,768]{3,2,1,0:T(8,128)}, f32[2,4,48,768]{3,2,1,0:T(8,128)}, u32[]{:S(2)}, u32[]{:S(2)}) %collective-permute-start.10) | collective-permute-done | bytes 1179680 | tf_op jit(solution)/shard_map/ppermute | solution.py:233
  94.6 2.3 %collective-permute-done.16.refs_3_ = f32[4,96,384]{2,1,0:T(8,128)} collective-permute-done((f32[4,96,384]{2,1,0:T(8,128)}, f32[4,96,384]{2,1,0:T(8,128)}, u32[]{:S(2)}, u32[]{:S(2)}) %collective-permute-start.16) | collective-permute-done | bytes 589856 | tf_op jit(solution)/shard_map/ppermute | solution.py:223
  97.0 12.4 %product.3 = (f32[2,4,48,768]{3,2,1,0:T(8,128)}, f32[2,4,48,768]{3,2,1,0:T(8,128)}, f32[2,4,48,768]{3,2,1,0:T(8,128)}, f32[2,4,48,768]{3,2,1,0:T(8,128)}, f32[2,...) custom-call(s32[16]{0:T(128)} %dynamic-slice_bitcast_fusion.place, s32[8]{0:T(128)} %sizes.4, ...), custom_call_target="tpu_custom_call" | custom-call | tf_op jit(solution)/shard_map/product/pallas_call | solution.py:88
  109.5 2.0 collective-permute-start.25
  111.5 3.5 %add_far.2 = (f32[2,4,48,768]{3,2,1,0:T(8,128)}, f32[2,4,48,768]{3,2,1,0:T(8,128)}) custom-call(f32[2,4,48,768]{3,2,1,0:T(8,128)} %get-tuple-element.36.up, f32[2,4,48,768]{3,2,1,0:T(8,128)} %get-tuple-element.37.down, f32[2,4,48,768]{3,2,1,0:T(8,128)} %collective-permute-done.10.refs_1_.recv_p, f32[2,4,48,768]{3,2,1,0:T(8,128)} %collective-permute-done.11.refs_2_.recv_m, ...), custom_call_target="tpu_custom_call" | custom-call | tf_op jit(solution)/shard_map/add_far/pallas_call | solution.py:135
  115.0 3.2 %collective-permute-start.19 = (f32[2,4,48,768]{3,2,1,0:T(8,128)}, f32[2,4,48,768]{3,2,1,0:T(8,128)}, u32[]{:S(2)}, u32[]{:S(2)}) collective-permute-start(f32[2,4,48,768]{3,2,1,0:T(8,128)} %get-tuple-element.44), channel_id=1, source_target_pairs={{0,12},{1,13},{2,14},{3,15},{4,0},{5,1},{6,2},{7,3},{8,4},{9,5},{1... | collective-permute-start | bytes 3538952 | tf_op jit(solution)/shard_map/ppermute | solution.py:233
  118.2 7.8 %collective-permute-done.26.recv_m = f32[2,4,48,768]{3,2,1,0:T(8,128)} collective-permute-done((f32[2,4,48,768]{3,2,1,0:T(8,128)}, f32[2,4,48,768]{3,2,1,0:T(8,128)}, u32[]{:S(2)}, u32[]{:S(2)}) %collective-permute-start.26) | collective-permute-done | bytes 1179680 | tf_op jit(solution)/shard_map/ppermute | solution.py:233
  126.0 1.2 collective-permute-start.24
  127.3 3.5 %add_far.3 = (f32[2,4,48,768]{3,2,1,0:T(8,128)}, f32[2,4,48,768]{3,2,1,0:T(8,128)}) custom-call(f32[2,4,48,768]{3,2,1,0:T(8,128)} %get-tuple-element.52.up, f32[2,4,48,768]{3,2,1,0:T(8,128)} %get-tuple-element.53.down, f32[2,4,48,768]{3,2,1,0:T(8,128)} %collective-permute-done.25.recv_p, f32[2,4,48,768]{3,2,1,0:T(8,128)} %collective-permute-done.26.recv_m), custom_call_target="tpu_custom_call" | custom-call | tf_op jit(solution)/shard_map/add_far/pallas_call | solution.py:135
  130.7 0.8 collective-permute-start.27
  131.5 8.4 %collective-permute-done.18.p2 = f32[2,4,48,768]{3,2,1,0:T(8,128)} collective-permute-done((f32[2,4,48,768]{3,2,1,0:T(8,128)}, f32[2,4,48,768]{3,2,1,0:T(8,128)}, u32[]{:S(2)}, u32[]{:S(2)}) %collective-permute-start.18) | collective-permute-done | bytes 1179680 | tf_op jit(solution)/shard_map/ppermute | solution.py:233
  139.9 4.2 %add_own.2 = (f32[4,48,768]{2,1,0:T(8,128)}, f32[4,48,768]{2,1,0:T(8,128)}, f32[4,48,768]{2,1,0:T(8,128)}, f32[4,48,768]{2,1,0:T(8,128)}) custom-call(f32[4,4,48,768]{3,2,1,0:T(8,128)} %get-tuple-element.33.own, f32[2,4,48,768]{3,2,1,0:T(8,128)} %collective-permute-done.8.refs_1_.n1, f32[2,4,48,768]{3,2,1,0:T(8,128)} %collective-permute-done.9.refs_2_.n2, ...), custom_call_target="tpu_custom_call" | custom-call | tf_op jit(solution)/shard_map/add_own/pallas_call | solution.py:161
  144.2 0.7 collective-permute-start.20
  144.9 11.5 %collective-permute-done.23.n1 = f32[2,4,48,768]{3,2,1,0:T(8,128)} collective-permute-done((f32[2,4,48,768]{3,2,1,0:T(8,128)}, f32[2,4,48,768]{3,2,1,0:T(8,128)}, u32[]{:S(2)}, u32[]{:S(2)}) %collective-permute-start.23) | collective-permute-done | bytes 1179680 | tf_op jit(solution)/shard_map/ppermute | solution.py:233
  156.4 2.0 collective-permute-start.21
  158.8 3.2 %collective-permute-done.20.refs_0_.refs_1_ = f32[4,48,768]{2,1,0:T(8,128)} collective-permute-done((f32[4,48,768]{2,1,0:T(8,128)}, f32[4,48,768]{2,1,0:T(8,128)}, u32[]{:S(2)}, u32[]{:S(2)}) %collective-permute-start.20) | collective-permute-done | bytes 589856 | tf_op jit(solution)/shard_map/ppermute | solution.py:236
  162.0 15.8 %collective-permute-done.27.p2 = f32[2,4,48,768]{3,2,1,0:T(8,128)} collective-permute-done((f32[2,4,48,768]{3,2,1,0:T(8,128)}, f32[2,4,48,768]{3,2,1,0:T(8,128)}, u32[]{:S(2)}, u32[]{:S(2)}) %collective-permute-start.27) | collective-permute-done | bytes 1179680 | tf_op jit(solution)/shard_map/ppermute | solution.py:233
  177.8 4.2 %add_own.3 = (f32[4,48,768]{2,1,0:T(8,128)}, f32[4,48,768]{2,1,0:T(8,128)}, f32[4,48,768]{2,1,0:T(8,128)}, f32[4,48,768]{2,1,0:T(8,128)}) custom-call(f32[4,4,48,768]{3,2,1,0:T(8,128)} %get-tuple-element.49.own, f32[2,4,48,768]{3,2,1,0:T(8,128)} %collective-permute-done.23.n1, f32[2,4,48,768]{3,2,1,0:T(8,128)} %collective-permute-done.24.n2, ...), custom_call_target="tpu_custom_call" | custom-call | tf_op jit(solution)/shard_map/add_own/pallas_call | solution.py:161
  182.0 0.7 collective-permute-start.29
  182.8 2.2 %collective-permute-start.30 = (f32[4,48,768]{2,1,0:T(8,128)}, f32[4,48,768]{2,1,0:T(8,128)}, u32[]{:S(2)}, u32[]{:S(2)}) collective-permute-start(f32[4,48,768]{2,1,0:T(8,128)} %get-tuple-element.59), channel_id=1, source_target_pairs={{0,2},{1,3},{2,0},{3,1},{4,6},{5,7},{6,4},{7,5},{8,10},{9,11},{10,... | collective-permute-start | bytes 1769480 | tf_op jit(solution)/shard_map/ppermute | solution.py:236
  184.9 1.3 collective-permute-start.31
  186.2 0.6 pad_add_fusion.origin
  186.9 12.9 %collective-permute-done.29.refs_5_ = f32[4,48,768]{2,1,0:T(8,128)} collective-permute-done((f32[4,48,768]{2,1,0:T(8,128)}, f32[4,48,768]{2,1,0:T(8,128)}, u32[]{:S(2)}, u32[]{:S(2)}) %collective-permute-start.29) | collective-permute-done | bytes 589856 | tf_op jit(solution)/shard_map/ppermute | solution.py:236
  199.8 0.9 collective-permute-done.31.refs_7_
  200.7 4.6 %finish.1 = f32[48,8,768]{2,1,0:T(8,128)} custom-call(s32[8]{0:T(128)} %sizes.5, s32[2]{0:T(128)} %pad_add_fusion.origin, f32[4,48,768]{2,1,0:T(8,128)} %get-tuple-element.45.refs_0_, f32[4,48,768]{2,1,0:T(8,128)} %collective-permute-done.20.refs_0_.refs_1_, f32[4,48,768]{2,1,0:T(8,128)} %collective-permute-done.21.refs_2_, ...), custom_call_target="tpu_custom_call" | custom-call | tf_op jit(solution)/shard_map/finish/pallas_call | solution.py:188
  (37 shorter events, 1.6 us)
Async XLA Ops:
  28.3 18.5 %collective-permute-start.5 = (f32[4,96,384]{2,1,0:T(8,128)}, f32[4,96,384]{2,1,0:T(8,128)}, u32[]{:S(2)}, u32[]{:S(2)}) collective-permute-start(f32[4,96,384]{2,1,0:T(8,128)} %bitcast.23.refs_0_), channel_id=1, source_target_pairs={{0,64},{16,80},{32,96},{48,112},{64,0},{80,16},{96,32},{112,48},{1... | collective-permute-start | bytes 1769480 | tf_op jit(solution)/shard_map/ppermute | solution.py:226
  32.2 25.7 %collective-permute-start.3 = (f32[4,96,384]{2,1,0:T(8,128)}, f32[4,96,384]{2,1,0:T(8,128)}, u32[]{:S(2)}, u32[]{:S(2)}) collective-permute-start(f32[4,96,384]{2,1,0:T(8,128)} %bitcast.23.refs_0_), channel_id=1, source_target_pairs={{0,96},{16,48},{32,0},{48,80},{64,32},{80,112},{96,64},{112,16},{1... | collective-permute-start | bytes 1769480 | tf_op jit(solution)/shard_map/ppermute | solution.py:226
  32.9 25.0 %collective-permute-start.1 = (f32[4,96,384]{2,1,0:T(8,128)}, f32[4,96,384]{2,1,0:T(8,128)}, u32[]{:S(2)}, u32[]{:S(2)}) collective-permute-start(f32[4,96,384]{2,1,0:T(8,128)} %bitcast.23.refs_0_), channel_id=1, source_target_pairs={{0,32},{16,112},{32,64},{48,16},{64,96},{80,48},{96,0},{112,80},{1... | collective-permute-start | bytes 1769480 | tf_op jit(solution)/shard_map/ppermute | solution.py:226
  34.2 0.9 copy-start
  35.1 25.0 %collective-permute-start.7 = (f32[4,96,384]{2,1,0:T(8,128)S(1)}, f32[4,96,384]{2,1,0:T(8,128)}, u32[]{:S(2)}, u32[]{:S(2)}) collective-permute-start(f32[4,96,384]{2,1,0:T(8,128)S(1)} %bitcast.24), channel_id=1, source_target_pairs={{0,16},{16,0},{32,48},{48,32},{64,80},{80,64},{96,112},{112,96},{1... | collective-permute-start | bytes 1769480 | tf_op jit(solution)/shard_map/ppermute | solution.py:223
  35.1 26.5 %collective-permute-start = (f32[4,96,384]{2,1,0:T(8,128)}, f32[4,96,384]{2,1,0:T(8,128)}, u32[]{:S(2)}, u32[]{:S(2)}) collective-permute-start(f32[4,96,384]{2,1,0:T(8,128)} %bitcast.23.refs_0_), channel_id=1, source_target_pairs={{0,16},{16,0},{32,48},{48,32},{64,80},{80,64},{96,112},{112,96},{1... | collective-permute-start | bytes 1769480 | tf_op jit(solution)/shard_map/ppermute | solution.py:223
  46.8 16.5 %collective-permute-start.6 = (f32[4,96,384]{2,1,0:T(8,128)}, f32[4,96,384]{2,1,0:T(8,128)}, u32[]{:S(2)}, u32[]{:S(2)}) collective-permute-start(f32[4,96,384]{2,1,0:T(8,128)} %collective-permute-done.5.refs_6_.refs_3_), channel_id=1, source_target_pairs={{0,16},{16,0},{32,48},{48,32},{64,80},{80,64},{96,112},{112,96},{1... | collective-permute-start | bytes 1769480 | tf_op jit(solution)/shard_map/ppermute | solution.py:223
  57.8 5.5 %collective-permute-start.4 = (f32[4,96,384]{2,1,0:T(8,128)}, f32[4,96,384]{2,1,0:T(8,128)}, u32[]{:S(2)}, u32[]{:S(2)}) collective-permute-start(f32[4,96,384]{2,1,0:T(8,128)} %collective-permute-done.3.refs_4_.refs_2_), channel_id=1, source_target_pairs={{0,16},{16,0},{32,48},{48,32},{64,80},{80,64},{96,112},{112,96},{1... | collective-permute-start | bytes 1769480 | tf_op jit(solution)/shard_map/ppermute | solution.py:223
  57.8 5.5 %collective-permute-start.2 = (f32[4,96,384]{2,1,0:T(8,128)}, f32[4,96,384]{2,1,0:T(8,128)}, u32[]{:S(2)}, u32[]{:S(2)}) collective-permute-start(f32[4,96,384]{2,1,0:T(8,128)} %collective-permute-done.1.refs_2_.refs_1_), channel_id=1, source_target_pairs={{0,16},{16,0},{32,48},{48,32},{64,80},{80,64},{96,112},{112,96},{1... | collective-permute-start | bytes 1769480 | tf_op jit(solution)/shard_map/ppermute | solution.py:223
  60.1 18.1 %collective-permute-start.14 = (f32[4,96,384]{2,1,0:T(8,128)}, f32[4,96,384]{2,1,0:T(8,128)}, u32[]{:S(2)}, u32[]{:S(2)}) collective-permute-start(f32[4,96,384]{2,1,0:T(8,128)} %tie.3.refs_0_), channel_id=1, source_target_pairs={{0,64},{16,80},{32,96},{48,112},{64,0},{80,16},{96,32},{112,48},{1... | collective-permute-start | bytes 1769480 | tf_op jit(solution)/shard_map/ppermute | solution.py:226
  61.7 25.3 %collective-permute-start.13 = (f32[4,96,384]{2,1,0:T(8,128)}, f32[4,96,384]{2,1,0:T(8,128)}, u32[]{:S(2)}, u32[]{:S(2)}) collective-permute-start(f32[4,96,384]{2,1,0:T(8,128)} %tie.3.refs_0_), channel_id=1, source_target_pairs={{0,96},{16,48},{32,0},{48,80},{64,32},{80,112},{96,64},{112,16},{1... | collective-permute-start | bytes 1769480 | tf_op jit(solution)/shard_map/ppermute | solution.py:226
  75.8 16.6 %collective-permute-start.11 = (f32[2,4,48,768]{3,2,1,0:T(8,128)}, f32[2,4,48,768]{3,2,1,0:T(8,128)}, u32[]{:S(2)}, u32[]{:S(2)}) collective-permute-start(f32[2,4,48,768]{3,2,1,0:T(8,128)} %get-tuple-element.39), channel_id=1, source_target_pairs={{0,12},{1,13},{2,14},{3,15},{4,0},{5,1},{6,2},{7,3},{8,4},{9,5},{1... | collective-permute-start | bytes 3538952 | tf_op jit(solution)/shard_map/ppermute | solution.py:233
  76.9 17.7 %collective-permute-start.10 = (f32[2,4,48,768]{3,2,1,0:T(8,128)}, f32[2,4,48,768]{3,2,1,0:T(8,128)}, u32[]{:S(2)}, u32[]{:S(2)}) collective-permute-start(f32[2,4,48,768]{3,2,1,0:T(8,128)} %get-tuple-element.38.refs_2_), channel_id=1, source_target_pairs={{0,4},{1,5},{2,6},{3,7},{4,8},{5,9},{6,10},{7,11},{8,12},{9,13},{1... | collective-permute-start | bytes 3538952 | tf_op jit(solution)/shard_map/ppermute | solution.py:233
  77.9 12.0 %collective-permute-start.12 = (f32[4,96,384]{2,1,0:T(8,128)}, f32[4,96,384]{2,1,0:T(8,128)}, u32[]{:S(2)}, u32[]{:S(2)}) collective-permute-start(f32[4,96,384]{2,1,0:T(8,128)} %tie.3.refs_0_), channel_id=1, source_target_pairs={{0,32},{16,112},{32,64},{48,16},{64,96},{80,48},{96,0},{112,80},{1... | collective-permute-start | bytes 1769480 | tf_op jit(solution)/shard_map/ppermute | solution.py:226
  87.0 4.6 %collective-permute-start.15 = (f32[4,96,384]{2,1,0:T(8,128)}, f32[4,96,384]{2,1,0:T(8,128)}, u32[]{:S(2)}, u32[]{:S(2)}) collective-permute-start(f32[4,96,384]{2,1,0:T(8,128)} %get-tuple-element.40.refs_4_), channel_id=1, source_target_pairs={{0,16},{16,0},{32,48},{48,32},{64,80},{80,64},{96,112},{112,96},{1... | collective-permute-start | bytes 1769480 | tf_op jit(solution)/shard_map/ppermute | solution.py:223
  87.0 24.5 %collective-permute-start.8 = (f32[2,4,48,768]{3,2,1,0:T(8,128)}, f32[2,4,48,768]{3,2,1,0:T(8,128)}, u32[]{:S(2)}, u32[]{:S(2)}) collective-permute-start(f32[2,4,48,768]{3,2,1,0:T(8,128)} %get-tuple-element.34), channel_id=1, source_target_pairs={{0,4},{1,5},{2,6},{3,7},{4,8},{5,9},{6,10},{7,11},{8,12},{9,13},{1... | collective-permute-start | bytes 3538952 | tf_op jit(solution)/shard_map/ppermute | solution.py:233
  89.8 21.7 %collective-permute-start.9 = (f32[2,4,48,768]{3,2,1,0:T(8,128)}, f32[2,4,48,768]{3,2,1,0:T(8,128)}, u32[]{:S(2)}, u32[]{:S(2)}) collective-permute-start(f32[2,4,48,768]{3,2,1,0:T(8,128)} %get-tuple-element.35), channel_id=1, source_target_pairs={{0,12},{1,13},{2,14},{3,15},{4,0},{5,1},{6,2},{7,3},{8,4},{9,5},{1... | collective-permute-start | bytes 3538952 | tf_op jit(solution)/shard_map/ppermute | solution.py:233
  91.5 3.1 %collective-permute-start.17 = (f32[4,96,384]{2,1,0:T(8,128)}, f32[4,96,384]{2,1,0:T(8,128)}, u32[]{:S(2)}, u32[]{:S(2)}) collective-permute-start(f32[4,96,384]{2,1,0:T(8,128)} %get-tuple-element.41.refs_6_), channel_id=1, source_target_pairs={{0,16},{16,0},{32,48},{48,32},{64,80},{80,64},{96,112},{112,96},{1... | collective-permute-start | bytes 1769480 | tf_op jit(solution)/shard_map/ppermute | solution.py:223
  94.6 2.3 %collective-permute-start.16 = (f32[4,96,384]{2,1,0:T(8,128)}, f32[4,96,384]{2,1,0:T(8,128)}, u32[]{:S(2)}, u32[]{:S(2)}) collective-permute-start(f32[4,96,384]{2,1,0:T(8,128)} %tie.5.refs_2_), channel_id=1, source_target_pairs={{0,16},{16,0},{32,48},{48,32},{64,80},{80,64},{96,112},{112,96},{1... | collective-permute-start | bytes 1769480 | tf_op jit(solution)/shard_map/ppermute | solution.py:223
  109.4 16.6 %collective-permute-start.26 = (f32[2,4,48,768]{3,2,1,0:T(8,128)}, f32[2,4,48,768]{3,2,1,0:T(8,128)}, u32[]{:S(2)}, u32[]{:S(2)}) collective-permute-start(f32[2,4,48,768]{3,2,1,0:T(8,128)} %get-tuple-element.54), channel_id=1, source_target_pairs={{0,12},{1,13},{2,14},{3,15},{4,0},{5,1},{6,2},{7,3},{8,4},{9,5},{1... | collective-permute-start | bytes 3538952 | tf_op jit(solution)/shard_map/ppermute | solution.py:233
  109.5 17.8 %collective-permute-start.25 = (f32[2,4,48,768]{3,2,1,0:T(8,128)}, f32[2,4,48,768]{3,2,1,0:T(8,128)}, u32[]{:S(2)}, u32[]{:S(2)}) collective-permute-start(f32[2,4,48,768]{3,2,1,0:T(8,128)} %get-tuple-element.42.refs_0_), channel_id=1, source_target_pairs={{0,4},{1,5},{2,6},{3,7},{4,8},{5,9},{6,10},{7,11},{8,12},{9,13},{1... | collective-permute-start | bytes 3538952 | tf_op jit(solution)/shard_map/ppermute | solution.py:233
  115.0 24.9 %collective-permute-start.18 = (f32[2,4,48,768]{3,2,1,0:T(8,128)}, f32[2,4,48,768]{3,2,1,0:T(8,128)}, u32[]{:S(2)}, u32[]{:S(2)}) collective-permute-start(f32[2,4,48,768]{3,2,1,0:T(8,128)} %get-tuple-element.43), channel_id=1, source_target_pairs={{0,4},{1,5},{2,6},{3,7},{4,8},{5,9},{6,10},{7,11},{8,12},{9,13},{1... | collective-permute-start | bytes 3538952 | tf_op jit(solution)/shard_map/ppermute | solution.py:233
  115.0 24.9 %collective-permute-start.19 = (f32[2,4,48,768]{3,2,1,0:T(8,128)}, f32[2,4,48,768]{3,2,1,0:T(8,128)}, u32[]{:S(2)}, u32[]{:S(2)}) collective-permute-start(f32[2,4,48,768]{3,2,1,0:T(8,128)} %get-tuple-element.44), channel_id=1, source_target_pairs={{0,12},{1,13},{2,14},{3,15},{4,0},{5,1},{6,2},{7,3},{8,4},{9,5},{1... | collective-permute-start | bytes 3538952 | tf_op jit(solution)/shard_map/ppermute | solution.py:233
  118.2 38.2 %collective-permute-start.23 = (f32[2,4,48,768]{3,2,1,0:T(8,128)}, f32[2,4,48,768]{3,2,1,0:T(8,128)}, u32[]{:S(2)}, u32[]{:S(2)}) collective-permute-start(f32[2,4,48,768]{3,2,1,0:T(8,128)} %get-tuple-element.50), channel_id=1, source_target_pairs={{0,4},{1,5},{2,6},{3,7},{4,8},{5,9},{6,10},{7,11},{8,12},{9,13},{1... | collective-permute-start | bytes 3538952 | tf_op jit(solution)/shard_map/ppermute | solution.py:233
  126.0 32.4 %collective-permute-start.24 = (f32[2,4,48,768]{3,2,1,0:T(8,128)}, f32[2,4,48,768]{3,2,1,0:T(8,128)}, u32[]{:S(2)}, u32[]{:S(2)}) collective-permute-start(f32[2,4,48,768]{3,2,1,0:T(8,128)} %get-tuple-element.51), channel_id=1, source_target_pairs={{0,12},{1,13},{2,14},{3,15},{4,0},{5,1},{6,2},{7,3},{8,4},{9,5},{1... | collective-permute-start | bytes 3538952 | tf_op jit(solution)/shard_map/ppermute | solution.py:233
  130.7 47.1 %collective-permute-start.27 = (f32[2,4,48,768]{3,2,1,0:T(8,128)}, f32[2,4,48,768]{3,2,1,0:T(8,128)}, u32[]{:S(2)}, u32[]{:S(2)}) collective-permute-start(f32[2,4,48,768]{3,2,1,0:T(8,128)} %get-tuple-element.55), channel_id=1, source_target_pairs={{0,4},{1,5},{2,6},{3,7},{4,8},{5,9},{6,10},{7,11},{8,12},{9,13},{1... | collective-permute-start | bytes 3538952 | tf_op jit(solution)/shard_map/ppermute | solution.py:233
  139.9 37.9 %collective-permute-start.28 = (f32[2,4,48,768]{3,2,1,0:T(8,128)}, f32[2,4,48,768]{3,2,1,0:T(8,128)}, u32[]{:S(2)}, u32[]{:S(2)}) collective-permute-start(f32[2,4,48,768]{3,2,1,0:T(8,128)} %get-tuple-element.56), channel_id=1, source_target_pairs={{0,12},{1,13},{2,14},{3,15},{4,0},{5,1},{6,2},{7,3},{8,4},{9,5},{1... | collective-permute-start | bytes 3538952 | tf_op jit(solution)/shard_map/ppermute | solution.py:233
  144.2 17.9 %collective-permute-start.20 = (f32[4,48,768]{2,1,0:T(8,128)}, f32[4,48,768]{2,1,0:T(8,128)}, u32[]{:S(2)}, u32[]{:S(2)}) collective-permute-start(f32[4,48,768]{2,1,0:T(8,128)} %get-tuple-element.46), channel_id=1, source_target_pairs={{0,1},{1,2},{2,3},{3,0},{4,5},{5,6},{6,7},{7,4},{8,9},{9,10},{10,1... | collective-permute-start | bytes 1769480 | tf_op jit(solution)/shard_map/ppermute | solution.py:236
  156.4 30.5 %collective-permute-start.21 = (f32[4,48,768]{2,1,0:T(8,128)}, f32[4,48,768]{2,1,0:T(8,128)}, u32[]{:S(2)}, u32[]{:S(2)}) collective-permute-start(f32[4,48,768]{2,1,0:T(8,128)} %get-tuple-element.47), channel_id=1, source_target_pairs={{0,2},{1,3},{2,0},{3,1},{4,6},{5,7},{6,4},{7,5},{8,10},{9,11},{10,... | collective-permute-start | bytes 1769480 | tf_op jit(solution)/shard_map/ppermute | solution.py:236
  158.4 28.5 %collective-permute-start.22 = (f32[4,48,768]{2,1,0:T(8,128)}, f32[4,48,768]{2,1,0:T(8,128)}, u32[]{:S(2)}, u32[]{:S(2)}) collective-permute-start(f32[4,48,768]{2,1,0:T(8,128)} %get-tuple-element.48), channel_id=1, source_target_pairs={{0,3},{1,0},{2,1},{3,2},{4,7},{5,4},{6,5},{7,6},{8,11},{9,8},{10,9... | collective-permute-start | bytes 1769480 | tf_op jit(solution)/shard_map/ppermute | solution.py:236
  182.0 17.7 %collective-permute-start.29 = (f32[4,48,768]{2,1,0:T(8,128)}, f32[4,48,768]{2,1,0:T(8,128)}, u32[]{:S(2)}, u32[]{:S(2)}) collective-permute-start(f32[4,48,768]{2,1,0:T(8,128)} %get-tuple-element.58), channel_id=1, source_target_pairs={{0,1},{1,2},{2,3},{3,0},{4,5},{5,6},{6,7},{7,4},{8,9},{9,10},{10,1... | collective-permute-start | bytes 1769480 | tf_op jit(solution)/shard_map/ppermute | solution.py:236
  182.8 17.0 %collective-permute-start.30 = (f32[4,48,768]{2,1,0:T(8,128)}, f32[4,48,768]{2,1,0:T(8,128)}, u32[]{:S(2)}, u32[]{:S(2)}) collective-permute-start(f32[4,48,768]{2,1,0:T(8,128)} %get-tuple-element.59), channel_id=1, source_target_pairs={{0,2},{1,3},{2,0},{3,1},{4,6},{5,7},{6,4},{7,5},{8,10},{9,11},{10,... | collective-permute-start | bytes 1769480 | tf_op jit(solution)/shard_map/ppermute | solution.py:236
  184.9 15.8 %collective-permute-start.31 = (f32[4,48,768]{2,1,0:T(8,128)}, f32[4,48,768]{2,1,0:T(8,128)}, u32[]{:S(2)}, u32[]{:S(2)}) collective-permute-start(f32[4,48,768]{2,1,0:T(8,128)} %get-tuple-element.60), channel_id=1, source_target_pairs={{0,3},{1,0},{2,1},{3,2},{4,7},{5,4},{6,5},{7,6},{8,11},{9,8},{10,9... | collective-permute-start | bytes 1769480 | tf_op jit(solution)/shard_map/ppermute | solution.py:236

commit v12 on v11

--- a/solution.py
+++ b/solution.py
@@ -10,7 +10,6 @@
 
 SIDE = 4
 VMEM = 64 * 1024 * 1024 - 256 * 1024
-STEP = 2
 LIGHT = pl.CostEstimate(flops=0, bytes_accessed=0, transcendentals=0)
 def hops(count, steps):
     pairs = []
@@ -21,7 +20,7 @@
     return pairs
 
 
-Z_STEPS = [hops(8, lambda i, d=d: (2, -d if i % 2 else d)) for d in (1, -1, 2)]
+Z_stepS = [hops(8, lambda i, d=d: (2, -d if i % 2 else d)) for d in (1, -1, 2)]
 SWAP = [(i, i ^ 1) for i in range(8)]
 BOTH = ("vb", "ob")
 NEAR = {d: hops(128, lambda i, d=d: (1 if i // 16 % 2 else SIDE, d)) for d in (1, -1)}
@@ -131,10 +130,11 @@
 
 def add_far(up, down, recv_p, recv_m, after):
     lead, count, rows, cols = up.shape
-    spec = pl.BlockSpec((lead, STEP, rows, cols), lambda g: (0, g, 0, 0))
+    step = 1 if count % 2 else 2
+    spec = pl.BlockSpec((lead, step, rows, cols), lambda g: (0, g, 0, 0))
     return pl.pallas_call(
         add_kernel,
-        grid=(count // STEP,),
+        grid=(count // step,),
         in_specs=[spec] * 4 + [pl.BlockSpec(memory_space=pl.ANY)] * len(after),
         out_specs=[spec] * 2,
         out_shape=[jax.ShapeDtypeStruct(up.shape, jnp.float32)] * 2,
@@ -154,15 +154,16 @@
 
 def add_own(own, n1, n2, p2, m2, after):
     count, rows, cols = own.shape[1:]
+    step = 1 if count % 2 else 2
 
     def spec(lead):
-        return pl.BlockSpec((lead, STEP, rows, cols), lambda g: (0, g, 0, 0))
+        return pl.BlockSpec((lead, step, rows, cols), lambda g: (0, g, 0, 0))
 
     return pl.pallas_call(
         own_kernel,
-        grid=(count // STEP,),
+        grid=(count // step,),
         in_specs=[spec(4)] + [spec(2)] * 4 + [pl.BlockSpec(memory_space=pl.ANY)] * len(after),
-        out_specs=[pl.BlockSpec((STEP, rows, cols), lambda g: (g, 0, 0))] * 4,
+        out_specs=[pl.BlockSpec((step, rows, cols), lambda g: (g, 0, 0))] * 4,
         out_shape=[jax.ShapeDtypeStruct((count, rows, cols), jnp.float32)] * 4,
         compiler_params=pltpu.CompilerParams(vmem_limit_bytes=VMEM),
         cost_estimate=LIGHT,
@@ -213,17 +214,20 @@
     place = lax.dynamic_slice(jnp.asarray(PLACES), (vb, ob, 0), (1, 1, 16)).reshape(16)
     origin = jnp.stack([ob * depth, vb * cols]).astype(jnp.int32)
 
-    mine = jnp.transpose(amplitudes.reshape(local_rows, irreps, obs, depth), (2, 0, 1, 3))
-    mine = mine.reshape(obs, local_rows * irreps, depth)
-    mine = lax.all_to_all(mine, "ob", split_axis=0, concat_axis=0, tiled=True)
-    mine = mine.reshape(obs * local_rows, irreps, depth)
-    early, late = jnp.transpose(mine[:, :SPLIT], (1, 0, 2)), jnp.transpose(mine[:, SPLIT:], (1, 0, 2))
+    def exchange(part):
+        count = part.shape[1]
+        part = jnp.transpose(part.reshape(local_rows, count, obs, depth), (2, 0, 1, 3))
+        part = part.reshape(obs, local_rows * count, depth)
+        part = lax.all_to_all(part, "ob", split_axis=0, concat_axis=0, tiled=True)
+        return jnp.transpose(part.reshape(obs * local_rows, count, depth), (1, 0, 2))
+
+    early, late = exchange(amplitudes[:, :SPLIT]), exchange(amplitudes[:, SPLIT:])
 
     def swap(piece):
         return lax.ppermute(piece, "vb", SWAP)
 
     def along_z(held):
-        return [lax.ppermute(held, "vb", steps) for steps in Z_STEPS]
+        return [lax.ppermute(held, "vb", steps) for steps in Z_stepS]
 
     def multiply(held, swapped, moved, moved_swapped, first, after):
         pieces = [(held, 0), (swapped, 0)] + [(piece, 0) for pair in zip(moved, moved_swapped) for piece in pair]
@@ -251,8 +255,8 @@
     handed = to_neighbours(*add_far(up, down, *far, [late_far_p, *near]))
     late_far, late_near = to_neighbours(late_far_p, late_far_m), to_neighbours(late_near_p, late_near_m)
     late_handed = to_neighbours(*add_far(late_up, late_down, *late_far, []))
-    sums = across(add_own(own, *near, *handed, []))
-    late_sums = across(add_own(late_own, *late_near, *late_handed, sums[1:2]))
+    sums = across(add_own(own, *near, *handed, late_handed))
+    late_sums = across(add_own(late_own, *late_near, *late_handed, []))
     origin = jnp.stack([ob * out_rows, vb * cols]).astype(jnp.int32)
     return finish([sums, late_sums], row_sizes, origin, irreps)
 

time: 206 us -> 198 us (0.961)
  waiting for transfers between devices: 99.4 us -> 72 us
  starting transfers between devices: 29.4 us -> 38.4 us
  blocking collectives: 25.4 us -> 33.8 us
    ppermute x6, waiting for transfers between devices: 33.3 us -> 17.8 us  [along_z(): return [lax.ppermute(held, 'vb', steps) for steps in Z_stepS]]
    ppermute x6, starting transfers between devices: 7.33 us -> 16 us  [across(): lax.ppermute(four[k], BOTH, FAR[d])]
    all_to_all x1 -> x2, blocking collectives: 25.4 us -> 33.8 us  [exchange(): part = lax.all_to_all(part, 'ob', split_axis=0, concat_axis=0, tiled=True)]
    ppermute x12, waiting for transfers between devices: 46.7 us -> 40.7 us  [to_neighbours(): return (lax.ppermute(p, BOTH, NEAR[1]), lax.ppermute(m, BOTH, NEAR[-1]))]
    ppermute x6, waiting for transfers between devices: 17 us -> 11.2 us  [across(): lax.ppermute(four[k], BOTH, FAR[d])]
    unnamed x5 -> x2, local copies, waits for them, and re-layouts: 3.26 us -> 0.81 us
    reshape x0 -> x8, local copies, waits for them, and re-layouts: none -> 2.23 us  [the longest x4 1.24 us: exchange(): part.reshape(obs * local_rows, count, depth)]
  transfers between devices with their start and end apart: 32 -> 32, of which waited for: 15 -> 13; matrix products, arithmetic and copies ran while one was open for 1% -> 2% of each run, Pallas kernels for 20% -> 20%
where the time goes in v12:
time: 198 us; the launch traced here: 196 us
  waiting for transfers between devices  72 us (36%)
  Pallas kernels  44.8 us (23%)
  starting transfers between devices  38.4 us (19%)
  blocking collectives  33.8 us (17%)
  local copies, waits for them, and re-layouts  6.07 us (3%)
    ppermute x12, waiting for transfers between devices, to_neighbours(): return (lax.ppermute(p, BOTH, NEAR[1]), lax.ppermute(m, BOTH, NEAR[-1]))  40.7 us
    all_to_all x2, blocking collectives, exchange(): part = lax.all_to_all(part, 'ob', split_axis=0, concat_axis=0, tiled=True)  33.8 us
    pallas_call x2, Pallas kernels, product(): pl.pallas_call(functools.partial(product_kernel, first), grid_spec=pltpu....  24.9 us
    ppermute x6, waiting for transfers between devices, along_z(): return [lax.ppermute(held, 'vb', steps) for steps in Z_stepS]  17.8 us
    ppermute x6, starting transfers between devices, across(): lax.ppermute(four[k], BOTH, FAR[d])  16 us
    ppermute x12, starting transfers between devices, to_neighbours(): return (lax.ppermute(p, BOTH, NEAR[1]), lax.ppermute(m, BOTH, NEAR[-1]))  11.4 us
    ppermute x6, waiting for transfers between devices, across(): lax.ppermute(four[k], BOTH, FAR[d])  11.2 us
    ppermute x6, starting transfers between devices, along_z(): return [lax.ppermute(held, 'vb', steps) for steps in Z_stepS]  9.48 us
  transfers between devices with their start and end apart: 32, of which 13 were waited for; matrix products, arithmetic and copies ran while one was open for 2% of the time, Pallas kernels for 20%

profile of v12, /device:TPU:0, one launch (start us, length us, event | category | flops | bytes accessed | tf_op | source)
XLA Modules:
  0.0 196.5 jit_solution(4659823886990098716)
XLA Ops:
  0.0 1.9 fusion
  2.4 19.1 %all_to_all.10 = f32[16,24,384]{2,1,0:T(8,128)S(1)} all-to-all(f32[16,24,384]{2,1,0:T(8,128)S(1)} %copy.10), channel_id=1, replica_groups=mesh['vb'=8,'ob'=16] {'ob'}, dimensions={0} | all-to-all | bytes 1179648 | tf_op jit(solution)/shard_map/all_to_all | solution.py:221
  21.7 0.9 copy.17
  22.6 3.9 %collective-permute-start.5 = (f32[4,96,384]{2,1,0:T(8,128)}, f32[4,96,384]{2,1,0:T(8,128)}, u32[]{:S(2)}, u32[]{:S(2)}) collective-permute-start(f32[4,96,384]{2,1,0:T(8,128)} %bitcast.16.refs_0_), channel_id=1, source_target_pairs={{0,64},{16,80},{32,96},{48,112},{64,0},{80,16},{96,32},{112,48},{1... | collective-permute-start | bytes 1769480 | tf_op jit(solution)/shard_map/ppermute | solution.py:230
  26.4 0.7 collective-permute-start.3
  27.1 1.3 collective-permute-start.1
  29.0 14.7 %all_to_all.11 = f32[16,24,384]{2,1,0:T(8,128)S(1)} all-to-all(f32[16,24,384]{2,1,0:T(8,128)S(1)} %copy.12), channel_id=1, replica_groups=mesh['vb'=8,'ob'=16] {'ob'}, dimensions={0} | all-to-all | bytes 1179648 | tf_op jit(solution)/shard_map/all_to_all | solution.py:221
  43.9 0.8 copy-done
  45.2 6.8 %collective-permute-done.3.refs_4_.refs_2_ = f32[4,96,384]{2,1,0:T(8,128)} collective-permute-done((f32[4,96,384]{2,1,0:T(8,128)}, f32[4,96,384]{2,1,0:T(8,128)}, u32[]{:S(2)}, u32[]{:S(2)}) %collective-permute-start.3) | collective-permute-done | bytes 589856 | tf_op jit(solution)/shard_map/ppermute | solution.py:230
  52.0 0.5 collective-permute-start.2
  52.5 0.6 pad_add_fusion.1.origin
  53.1 1.2 dynamic-slice_bitcast_fusion.place
  54.2 1.6 collective-permute-start.14
  55.8 1.6 collective-permute-start.13
  57.4 12.4 %product.2 = (f32[2,4,48,768]{3,2,1,0:T(8,128)}, f32[2,4,48,768]{3,2,1,0:T(8,128)}, f32[2,4,48,768]{3,2,1,0:T(8,128)}, f32[2,4,48,768]{3,2,1,0:T(8,128)}, f32[2,...) custom-call(s32[16]{0:T(128)} %dynamic-slice_bitcast_fusion.place, s32[8]{0:T(128)} %sizes.4, ...), custom_call_target="tpu_custom_call" | custom-call | tf_op jit(solution)/shard_map/product/pallas_call | solution.py:87
  69.9 1.3 collective-permute-start.11
  71.2 0.8 collective-permute-start.10
  72.4 8.7 %collective-permute-done.13.refs_0_ = f32[4,96,384]{2,1,0:T(8,128)} collective-permute-done((f32[4,96,384]{2,1,0:T(8,128)}, f32[4,96,384]{2,1,0:T(8,128)}, u32[]{:S(2)}, u32[]{:S(2)}) %collective-permute-start.13) | collective-permute-done | bytes 589856 | tf_op jit(solution)/shard_map/ppermute | solution.py:230
  81.1 0.5 collective-permute-start.17
  81.6 2.3 %collective-permute-done.12.refs_0_ = f32[4,96,384]{2,1,0:T(8,128)} collective-permute-done((f32[4,96,384]{2,1,0:T(8,128)}, f32[4,96,384]{2,1,0:T(8,128)}, u32[]{:S(2)}, u32[]{:S(2)}) %collective-permute-start.12) | collective-permute-done | bytes 589856 | tf_op jit(solution)/shard_map/ppermute | solution.py:230
  83.9 0.7 collective-permute-start.8
  84.6 1.9 collective-permute-done.11.refs_2_.recv_m
  86.5 2.4 %collective-permute-done.10.refs_1_.recv_p = f32[2,4,48,768]{3,2,1,0:T(8,128)} collective-permute-done((f32[2,4,48,768]{3,2,1,0:T(8,128)}, f32[2,4,48,768]{3,2,1,0:T(8,128)}, u32[]{:S(2)}, u32[]{:S(2)}) %collective-permute-start.10) | collective-permute-done | bytes 1179680 | tf_op jit(solution)/shard_map/ppermute | solution.py:237
  89.0 2.3 %collective-permute-done.16.refs_3_ = f32[4,96,384]{2,1,0:T(8,128)} collective-permute-done((f32[4,96,384]{2,1,0:T(8,128)}, f32[4,96,384]{2,1,0:T(8,128)}, u32[]{:S(2)}, u32[]{:S(2)}) %collective-permute-start.16) | collective-permute-done | bytes 589856 | tf_op jit(solution)/shard_map/ppermute | solution.py:227
  91.2 12.4 %product.3 = (f32[2,4,48,768]{3,2,1,0:T(8,128)}, f32[2,4,48,768]{3,2,1,0:T(8,128)}, f32[2,4,48,768]{3,2,1,0:T(8,128)}, f32[2,4,48,768]{3,2,1,0:T(8,128)}, f32[2,...) custom-call(s32[16]{0:T(128)} %dynamic-slice_bitcast_fusion.place, s32[8]{0:T(128)} %sizes.4, ...), custom_call_target="tpu_custom_call" | custom-call | tf_op jit(solution)/shard_map/product/pallas_call | solution.py:87
  103.7 2.0 %collective-permute-start.20 = (f32[2,4,48,768]{3,2,1,0:T(8,128)}, f32[2,4,48,768]{3,2,1,0:T(8,128)}, u32[]{:S(2)}, u32[]{:S(2)}) collective-permute-start(f32[2,4,48,768]{3,2,1,0:T(8,128)} %get-tuple-element.42.refs_0_), channel_id=1, source_target_pairs={{0,4},{1,5},{2,6},{3,7},{4,8},{5,9},{6,10},{7,11},{8,12},{9,13},{1... | collective-permute-start | bytes 3538952 | tf_op jit(solution)/shard_map/ppermute | solution.py:237
  105.8 3.5 %add_far.2 = (f32[2,4,48,768]{3,2,1,0:T(8,128)}, f32[2,4,48,768]{3,2,1,0:T(8,128)}) custom-call(f32[2,4,48,768]{3,2,1,0:T(8,128)} %get-tuple-element.36.up, f32[2,4,48,768]{3,2,1,0:T(8,128)} %get-tuple-element.37.down, f32[2,4,48,768]{3,2,1,0:T(8,128)} %collective-permute-done.10.refs_1_.recv_p, f32[2,4,48,768]{3,2,1,0:T(8,128)} %collective-permute-done.11.refs_2_.recv_m, ...), custom_call_target="tpu_custom_call" | custom-call | tf_op jit(solution)/shard_map/add_far/pallas_call | solution.py:135
  109.2 3.2 %collective-permute-start.19 = (f32[2,4,48,768]{3,2,1,0:T(8,128)}, f32[2,4,48,768]{3,2,1,0:T(8,128)}, u32[]{:S(2)}, u32[]{:S(2)}) collective-permute-start(f32[2,4,48,768]{3,2,1,0:T(8,128)} %get-tuple-element.44), channel_id=1, source_target_pairs={{0,12},{1,13},{2,14},{3,15},{4,0},{5,1},{6,2},{7,3},{8,4},{9,5},{1... | collective-permute-start | bytes 3538952 | tf_op jit(solution)/shard_map/ppermute | solution.py:237
  112.5 7.8 %collective-permute-done.21.recv_m = f32[2,4,48,768]{3,2,1,0:T(8,128)} collective-permute-done((f32[2,4,48,768]{3,2,1,0:T(8,128)}, f32[2,4,48,768]{3,2,1,0:T(8,128)}, u32[]{:S(2)}, u32[]{:S(2)}) %collective-permute-start.21) | collective-permute-done | bytes 1179680 | tf_op jit(solution)/shard_map/ppermute | solution.py:237
  120.2 1.5 collective-permute-done.20.recv_p
  121.7 3.5 %add_far.3 = (f32[2,4,48,768]{3,2,1,0:T(8,128)}, f32[2,4,48,768]{3,2,1,0:T(8,128)}) custom-call(f32[2,4,48,768]{3,2,1,0:T(8,128)} %get-tuple-element.45.up, f32[2,4,48,768]{3,2,1,0:T(8,128)} %get-tuple-element.46.down, f32[2,4,48,768]{3,2,1,0:T(8,128)} %collective-permute-done.20.recv_p, f32[2,4,48,768]{3,2,1,0:T(8,128)} %collective-permute-done.21.recv_m), custom_call_target="tpu_custom_call" | custom-call | tf_op jit(solution)/shard_map/add_far/pallas_call | solution.py:135
  125.2 0.6 collective-permute-start.22
  125.8 2.7 %collective-permute-start.23 = (f32[2,4,48,768]{3,2,1,0:T(8,128)}, f32[2,4,48,768]{3,2,1,0:T(8,128)}, u32[]{:S(2)}, u32[]{:S(2)}) collective-permute-start(f32[2,4,48,768]{3,2,1,0:T(8,128)} %get-tuple-element.49), channel_id=1, source_target_pairs={{0,12},{1,13},{2,14},{3,15},{4,0},{5,1},{6,2},{7,3},{8,4},{9,5},{1... | collective-permute-start | bytes 3538952 | tf_op jit(solution)/shard_map/ppermute | solution.py:237
  128.5 5.9 %collective-permute-done.18.p2 = f32[2,4,48,768]{3,2,1,0:T(8,128)} collective-permute-done((f32[2,4,48,768]{3,2,1,0:T(8,128)}, f32[2,4,48,768]{3,2,1,0:T(8,128)}, u32[]{:S(2)}, u32[]{:S(2)}) %collective-permute-start.18) | collective-permute-done | bytes 1179680 | tf_op jit(solution)/shard_map/ppermute | solution.py:237
  134.4 12.6 %collective-permute-done.22.refs_0_.p2 = f32[2,4,48,768]{3,2,1,0:T(8,128)} collective-permute-done((f32[2,4,48,768]{3,2,1,0:T(8,128)}, f32[2,4,48,768]{3,2,1,0:T(8,128)}, u32[]{:S(2)}, u32[]{:S(2)}) %collective-permute-start.22) | collective-permute-done | bytes 1179680 | tf_op jit(solution)/shard_map/ppermute | solution.py:237
  147.0 4.2 %add_own.2 = (f32[4,48,768]{2,1,0:T(8,128)}, f32[4,48,768]{2,1,0:T(8,128)}, f32[4,48,768]{2,1,0:T(8,128)}, f32[4,48,768]{2,1,0:T(8,128)}) custom-call(f32[4,4,48,768]{3,2,1,0:T(8,128)} %get-tuple-element.33.own, f32[2,4,48,768]{3,2,1,0:T(8,128)} %collective-permute-done.8.refs_1_.n1, f32[2,4,48,768]{3,2,1,0:T(8,128)} %collective-permute-done.9.refs_2_.n2, ...), custom_call_target="tpu_custom_call" | custom-call | tf_op jit(solution)/shard_map/add_own/pallas_call | solution.py:162
  151.2 0.5 collective-permute-start.24
  151.7 2.1 %collective-permute-start.25 = (f32[4,48,768]{2,1,0:T(8,128)}, f32[4,48,768]{2,1,0:T(8,128)}, u32[]{:S(2)}, u32[]{:S(2)}) collective-permute-start(f32[4,48,768]{2,1,0:T(8,128)} %get-tuple-element.52), channel_id=1, source_target_pairs={{0,2},{1,3},{2,0},{3,1},{4,6},{5,7},{6,4},{7,5},{8,10},{9,11},{10,... | collective-permute-start | bytes 1769480 | tf_op jit(solution)/shard_map/ppermute | solution.py:240
  153.9 1.5 collective-permute-start.26
  155.4 8.6 %collective-permute-done.27.n1 = f32[2,4,48,768]{3,2,1,0:T(8,128)} collective-permute-done((f32[2,4,48,768]{3,2,1,0:T(8,128)}, f32[2,4,48,768]{3,2,1,0:T(8,128)}, u32[]{:S(2)}, u32[]{:S(2)}) %collective-permute-start.27) | collective-permute-done | bytes 1179680 | tf_op jit(solution)/shard_map/ppermute | solution.py:237
  163.9 4.3 %add_own.3 = (f32[4,48,768]{2,1,0:T(8,128)}, f32[4,48,768]{2,1,0:T(8,128)}, f32[4,48,768]{2,1,0:T(8,128)}, f32[4,48,768]{2,1,0:T(8,128)}) custom-call(f32[4,4,48,768]{3,2,1,0:T(8,128)} %get-tuple-element.54.own, f32[2,4,48,768]{3,2,1,0:T(8,128)} %collective-permute-done.27.n1, f32[2,4,48,768]{3,2,1,0:T(8,128)} %collective-permute-done.28.n2, ...), custom_call_target="tpu_custom_call" | custom-call | tf_op jit(solution)/shard_map/add_own/pallas_call | solution.py:162
  168.2 7.8 %collective-permute-start.29 = (f32[4,48,768]{2,1,0:T(8,128)}, f32[4,48,768]{2,1,0:T(8,128)}, u32[]{:S(2)}, u32[]{:S(2)}) collective-permute-start(f32[4,48,768]{2,1,0:T(8,128)} %get-tuple-element.58), channel_id=1, source_target_pairs={{0,1},{1,2},{2,3},{3,0},{4,5},{5,6},{6,7},{7,4},{8,9},{9,10},{10,1... | collective-permute-start | bytes 1769480 | tf_op jit(solution)/shard_map/ppermute | solution.py:240
  176.0 1.5 collective-permute-start.30
  177.5 2.5 %collective-permute-start.31 = (f32[4,48,768]{2,1,0:T(8,128)}, f32[4,48,768]{2,1,0:T(8,128)}, u32[]{:S(2)}, u32[]{:S(2)}) collective-permute-start(f32[4,48,768]{2,1,0:T(8,128)} %get-tuple-element.60), channel_id=1, source_target_pairs={{0,3},{1,0},{2,1},{3,2},{4,7},{5,4},{6,5},{7,6},{8,11},{9,8},{10,9... | collective-permute-start | bytes 1769480 | tf_op jit(solution)/shard_map/ppermute | solution.py:240
  180.1 0.6 pad_add_fusion.origin
  180.7 3.0 %collective-permute-done.29.refs_5_ = f32[4,48,768]{2,1,0:T(8,128)} collective-permute-done((f32[4,48,768]{2,1,0:T(8,128)}, f32[4,48,768]{2,1,0:T(8,128)}, u32[]{:S(2)}, u32[]{:S(2)}) %collective-permute-start.29) | collective-permute-done | bytes 589856 | tf_op jit(solution)/shard_map/ppermute | solution.py:240
  183.7 8.2 %collective-permute-done.30.refs_6_ = f32[4,48,768]{2,1,0:T(8,128)} collective-permute-done((f32[4,48,768]{2,1,0:T(8,128)}, f32[4,48,768]{2,1,0:T(8,128)}, u32[]{:S(2)}, u32[]{:S(2)}) %collective-permute-start.30) | collective-permute-done | bytes 589856 | tf_op jit(solution)/shard_map/ppermute | solution.py:240
  191.9 4.6 %finish.1 = f32[48,8,768]{2,1,0:T(8,128)} custom-call(s32[8]{0:T(128)} %sizes.5, s32[2]{0:T(128)} %pad_add_fusion.origin, f32[4,48,768]{2,1,0:T(8,128)} %get-tuple-element.50.refs_0_, f32[4,48,768]{2,1,0:T(8,128)} %collective-permute-done.24.refs_1_, f32[4,48,768]{2,1,0:T(8,128)} %collective-permute-done.25.refs_2_, ...), custom_call_target="tpu_custom_call" | custom-call | tf_op jit(solution)/shard_map/finish/pallas_call | solution.py:189
  (42 shorter events, 2.5 us)
Async XLA Ops:
  22.6 22.6 %collective-permute-start.5 = (f32[4,96,384]{2,1,0:T(8,128)}, f32[4,96,384]{2,1,0:T(8,128)}, u32[]{:S(2)}, u32[]{:S(2)}) collective-permute-start(f32[4,96,384]{2,1,0:T(8,128)} %bitcast.16.refs_0_), channel_id=1, source_target_pairs={{0,64},{16,80},{32,96},{48,112},{64,0},{80,16},{96,32},{112,48},{1... | collective-permute-start | bytes 1769480 | tf_op jit(solution)/shard_map/ppermute | solution.py:230
  26.4 25.5 %collective-permute-start.3 = (f32[4,96,384]{2,1,0:T(8,128)}, f32[4,96,384]{2,1,0:T(8,128)}, u32[]{:S(2)}, u32[]{:S(2)}) collective-permute-start(f32[4,96,384]{2,1,0:T(8,128)} %bitcast.16.refs_0_), channel_id=1, source_target_pairs={{0,96},{16,48},{32,0},{48,80},{64,32},{80,112},{96,64},{112,16},{1... | collective-permute-start | bytes 1769480 | tf_op jit(solution)/shard_map/ppermute | solution.py:230
  27.1 24.8 %collective-permute-start.1 = (f32[4,96,384]{2,1,0:T(8,128)}, f32[4,96,384]{2,1,0:T(8,128)}, u32[]{:S(2)}, u32[]{:S(2)}) collective-permute-start(f32[4,96,384]{2,1,0:T(8,128)} %bitcast.16.refs_0_), channel_id=1, source_target_pairs={{0,32},{16,112},{32,64},{48,16},{64,96},{80,48},{96,0},{112,80},{1... | collective-permute-start | bytes 1769480 | tf_op jit(solution)/shard_map/ppermute | solution.py:230
  43.8 0.8 copy-start
  44.7 9.6 %collective-permute-start.7 = (f32[4,96,384]{2,1,0:T(8,128)S(1)}, f32[4,96,384]{2,1,0:T(8,128)}, u32[]{:S(2)}, u32[]{:S(2)}) collective-permute-start(f32[4,96,384]{2,1,0:T(8,128)S(1)} %bitcast.17), channel_id=1, source_target_pairs={{0,16},{16,0},{32,48},{48,32},{64,80},{80,64},{96,112},{112,96},{1... | collective-permute-start | bytes 1769480 | tf_op jit(solution)/shard_map/ppermute | solution.py:227
  44.7 11.1 %collective-permute-start = (f32[4,96,384]{2,1,0:T(8,128)}, f32[4,96,384]{2,1,0:T(8,128)}, u32[]{:S(2)}, u32[]{:S(2)}) collective-permute-start(f32[4,96,384]{2,1,0:T(8,128)} %bitcast.16.refs_0_), channel_id=1, source_target_pairs={{0,16},{16,0},{32,48},{48,32},{64,80},{80,64},{96,112},{112,96},{1... | collective-permute-start | bytes 1769480 | tf_op jit(solution)/shard_map/ppermute | solution.py:227
  45.2 12.3 %collective-permute-start.6 = (f32[4,96,384]{2,1,0:T(8,128)}, f32[4,96,384]{2,1,0:T(8,128)}, u32[]{:S(2)}, u32[]{:S(2)}) collective-permute-start(f32[4,96,384]{2,1,0:T(8,128)} %collective-permute-done.5.refs_6_.refs_3_), channel_id=1, source_target_pairs={{0,16},{16,0},{32,48},{48,32},{64,80},{80,64},{96,112},{112,96},{1... | collective-permute-start | bytes 1769480 | tf_op jit(solution)/shard_map/ppermute | solution.py:227
  52.0 5.5 %collective-permute-start.4 = (f32[4,96,384]{2,1,0:T(8,128)}, f32[4,96,384]{2,1,0:T(8,128)}, u32[]{:S(2)}, u32[]{:S(2)}) collective-permute-start(f32[4,96,384]{2,1,0:T(8,128)} %collective-permute-done.3.refs_4_.refs_2_), channel_id=1, source_target_pairs={{0,16},{16,0},{32,48},{48,32},{64,80},{80,64},{96,112},{112,96},{1... | collective-permute-start | bytes 1769480 | tf_op jit(solution)/shard_map/ppermute | solution.py:227
  52.0 5.5 %collective-permute-start.2 = (f32[4,96,384]{2,1,0:T(8,128)}, f32[4,96,384]{2,1,0:T(8,128)}, u32[]{:S(2)}, u32[]{:S(2)}) collective-permute-start(f32[4,96,384]{2,1,0:T(8,128)} %collective-permute-done.1.refs_2_.refs_1_), channel_id=1, source_target_pairs={{0,16},{16,0},{32,48},{48,32},{64,80},{80,64},{96,112},{112,96},{1... | collective-permute-start | bytes 1769480 | tf_op jit(solution)/shard_map/ppermute | solution.py:227
  54.2 18.1 %collective-permute-start.14 = (f32[4,96,384]{2,1,0:T(8,128)}, f32[4,96,384]{2,1,0:T(8,128)}, u32[]{:S(2)}, u32[]{:S(2)}) collective-permute-start(f32[4,96,384]{2,1,0:T(8,128)} %tie.3.refs_0_), channel_id=1, source_target_pairs={{0,64},{16,80},{32,96},{48,112},{64,0},{80,16},{96,32},{112,48},{1... | collective-permute-start | bytes 1769480 | tf_op jit(solution)/shard_map/ppermute | solution.py:230
  55.8 25.3 %collective-permute-start.13 = (f32[4,96,384]{2,1,0:T(8,128)}, f32[4,96,384]{2,1,0:T(8,128)}, u32[]{:S(2)}, u32[]{:S(2)}) collective-permute-start(f32[4,96,384]{2,1,0:T(8,128)} %tie.3.refs_0_), channel_id=1, source_target_pairs={{0,96},{16,48},{32,0},{48,80},{64,32},{80,112},{96,64},{112,16},{1... | collective-permute-start | bytes 1769480 | tf_op jit(solution)/shard_map/ppermute | solution.py:230
  69.9 16.6 %collective-permute-start.11 = (f32[2,4,48,768]{3,2,1,0:T(8,128)}, f32[2,4,48,768]{3,2,1,0:T(8,128)}, u32[]{:S(2)}, u32[]{:S(2)}) collective-permute-start(f32[2,4,48,768]{3,2,1,0:T(8,128)} %get-tuple-element.39), channel_id=1, source_target_pairs={{0,12},{1,13},{2,14},{3,15},{4,0},{5,1},{6,2},{7,3},{8,4},{9,5},{1... | collective-permute-start | bytes 3538952 | tf_op jit(solution)/shard_map/ppermute | solution.py:237
  71.2 17.7 %collective-permute-start.10 = (f32[2,4,48,768]{3,2,1,0:T(8,128)}, f32[2,4,48,768]{3,2,1,0:T(8,128)}, u32[]{:S(2)}, u32[]{:S(2)}) collective-permute-start(f32[2,4,48,768]{3,2,1,0:T(8,128)} %get-tuple-element.38.refs_2_), channel_id=1, source_target_pairs={{0,4},{1,5},{2,6},{3,7},{4,8},{5,9},{6,10},{7,11},{8,12},{9,13},{1... | collective-permute-start | bytes 3538952 | tf_op jit(solution)/shard_map/ppermute | solution.py:237
  72.0 12.0 %collective-permute-start.12 = (f32[4,96,384]{2,1,0:T(8,128)}, f32[4,96,384]{2,1,0:T(8,128)}, u32[]{:S(2)}, u32[]{:S(2)}) collective-permute-start(f32[4,96,384]{2,1,0:T(8,128)} %tie.3.refs_0_), channel_id=1, source_target_pairs={{0,32},{16,112},{32,64},{48,16},{64,96},{80,48},{96,0},{112,80},{1... | collective-permute-start | bytes 1769480 | tf_op jit(solution)/shard_map/ppermute | solution.py:230
  81.1 3.5 %collective-permute-start.15 = (f32[4,96,384]{2,1,0:T(8,128)}, f32[4,96,384]{2,1,0:T(8,128)}, u32[]{:S(2)}, u32[]{:S(2)}) collective-permute-start(f32[4,96,384]{2,1,0:T(8,128)} %get-tuple-element.40.refs_4_), channel_id=1, source_target_pairs={{0,16},{16,0},{32,48},{48,32},{64,80},{80,64},{96,112},{112,96},{1... | collective-permute-start | bytes 1769480 | tf_op jit(solution)/shard_map/ppermute | solution.py:227
  81.1 7.9 %collective-permute-start.17 = (f32[4,96,384]{2,1,0:T(8,128)}, f32[4,96,384]{2,1,0:T(8,128)}, u32[]{:S(2)}, u32[]{:S(2)}) collective-permute-start(f32[4,96,384]{2,1,0:T(8,128)} %get-tuple-element.41.refs_6_), channel_id=1, source_target_pairs={{0,16},{16,0},{32,48},{48,32},{64,80},{80,64},{96,112},{112,96},{1... | collective-permute-start | bytes 1769480 | tf_op jit(solution)/shard_map/ppermute | solution.py:227
  83.9 21.8 %collective-permute-start.8 = (f32[2,4,48,768]{3,2,1,0:T(8,128)}, f32[2,4,48,768]{3,2,1,0:T(8,128)}, u32[]{:S(2)}, u32[]{:S(2)}) collective-permute-start(f32[2,4,48,768]{3,2,1,0:T(8,128)} %get-tuple-element.34), channel_id=1, source_target_pairs={{0,4},{1,5},{2,6},{3,7},{4,8},{5,9},{6,10},{7,11},{8,12},{9,13},{1... | collective-permute-start | bytes 3538952 | tf_op jit(solution)/shard_map/ppermute | solution.py:237
  88.9 2.3 %collective-permute-start.16 = (f32[4,96,384]{2,1,0:T(8,128)}, f32[4,96,384]{2,1,0:T(8,128)}, u32[]{:S(2)}, u32[]{:S(2)}) collective-permute-start(f32[4,96,384]{2,1,0:T(8,128)} %tie.5.refs_2_), channel_id=1, source_target_pairs={{0,16},{16,0},{32,48},{48,32},{64,80},{80,64},{96,112},{112,96},{1... | collective-permute-start | bytes 1769480 | tf_op jit(solution)/shard_map/ppermute | solution.py:227
  88.9 16.9 %collective-permute-start.9 = (f32[2,4,48,768]{3,2,1,0:T(8,128)}, f32[2,4,48,768]{3,2,1,0:T(8,128)}, u32[]{:S(2)}, u32[]{:S(2)}) collective-permute-start(f32[2,4,48,768]{3,2,1,0:T(8,128)} %get-tuple-element.35), channel_id=1, source_target_pairs={{0,12},{1,13},{2,14},{3,15},{4,0},{5,1},{6,2},{7,3},{8,4},{9,5},{1... | collective-permute-start | bytes 3538952 | tf_op jit(solution)/shard_map/ppermute | solution.py:237
  103.7 16.6 %collective-permute-start.21 = (f32[2,4,48,768]{3,2,1,0:T(8,128)}, f32[2,4,48,768]{3,2,1,0:T(8,128)}, u32[]{:S(2)}, u32[]{:S(2)}) collective-permute-start(f32[2,4,48,768]{3,2,1,0:T(8,128)} %get-tuple-element.47), channel_id=1, source_target_pairs={{0,12},{1,13},{2,14},{3,15},{4,0},{5,1},{6,2},{7,3},{8,4},{9,5},{1... | collective-permute-start | bytes 3538952 | tf_op jit(solution)/shard_map/ppermute | solution.py:237
  103.7 18.0 %collective-permute-start.20 = (f32[2,4,48,768]{3,2,1,0:T(8,128)}, f32[2,4,48,768]{3,2,1,0:T(8,128)}, u32[]{:S(2)}, u32[]{:S(2)}) collective-permute-start(f32[2,4,48,768]{3,2,1,0:T(8,128)} %get-tuple-element.42.refs_0_), channel_id=1, source_target_pairs={{0,4},{1,5},{2,6},{3,7},{4,8},{5,9},{6,10},{7,11},{8,12},{9,13},{1... | collective-permute-start | bytes 3538952 | tf_op jit(solution)/shard_map/ppermute | solution.py:237
  109.2 25.1 %collective-permute-start.18 = (f32[2,4,48,768]{3,2,1,0:T(8,128)}, f32[2,4,48,768]{3,2,1,0:T(8,128)}, u32[]{:S(2)}, u32[]{:S(2)}) collective-permute-start(f32[2,4,48,768]{3,2,1,0:T(8,128)} %get-tuple-element.43), channel_id=1, source_target_pairs={{0,4},{1,5},{2,6},{3,7},{4,8},{5,9},{6,10},{7,11},{8,12},{9,13},{1... | collective-permute-start | bytes 3538952 | tf_op jit(solution)/shard_map/ppermute | solution.py:237
  109.2 25.1 %collective-permute-start.19 = (f32[2,4,48,768]{3,2,1,0:T(8,128)}, f32[2,4,48,768]{3,2,1,0:T(8,128)}, u32[]{:S(2)}, u32[]{:S(2)}) collective-permute-start(f32[2,4,48,768]{3,2,1,0:T(8,128)} %get-tuple-element.44), channel_id=1, source_target_pairs={{0,12},{1,13},{2,14},{3,15},{4,0},{5,1},{6,2},{7,3},{8,4},{9,5},{1... | collective-permute-start | bytes 3538952 | tf_op jit(solution)/shard_map/ppermute | solution.py:237
  125.2 21.8 %collective-permute-start.22 = (f32[2,4,48,768]{3,2,1,0:T(8,128)}, f32[2,4,48,768]{3,2,1,0:T(8,128)}, u32[]{:S(2)}, u32[]{:S(2)}) collective-permute-start(f32[2,4,48,768]{3,2,1,0:T(8,128)} %get-tuple-element.48), channel_id=1, source_target_pairs={{0,4},{1,5},{2,6},{3,7},{4,8},{5,9},{6,10},{7,11},{8,12},{9,13},{1... | collective-permute-start | bytes 3538952 | tf_op jit(solution)/shard_map/ppermute | solution.py:237
  125.8 21.2 %collective-permute-start.23 = (f32[2,4,48,768]{3,2,1,0:T(8,128)}, f32[2,4,48,768]{3,2,1,0:T(8,128)}, u32[]{:S(2)}, u32[]{:S(2)}) collective-permute-start(f32[2,4,48,768]{3,2,1,0:T(8,128)} %get-tuple-element.49), channel_id=1, source_target_pairs={{0,12},{1,13},{2,14},{3,15},{4,0},{5,1},{6,2},{7,3},{8,4},{9,5},{1... | collective-permute-start | bytes 3538952 | tf_op jit(solution)/shard_map/ppermute | solution.py:237
  128.5 35.5 %collective-permute-start.27 = (f32[2,4,48,768]{3,2,1,0:T(8,128)}, f32[2,4,48,768]{3,2,1,0:T(8,128)}, u32[]{:S(2)}, u32[]{:S(2)}) collective-permute-start(f32[2,4,48,768]{3,2,1,0:T(8,128)} %get-tuple-element.55), channel_id=1, source_target_pairs={{0,4},{1,5},{2,6},{3,7},{4,8},{5,9},{6,10},{7,11},{8,12},{9,13},{1... | collective-permute-start | bytes 3538952 | tf_op jit(solution)/shard_map/ppermute | solution.py:237
  134.4 29.6 %collective-permute-start.28 = (f32[2,4,48,768]{3,2,1,0:T(8,128)}, f32[2,4,48,768]{3,2,1,0:T(8,128)}, u32[]{:S(2)}, u32[]{:S(2)}) collective-permute-start(f32[2,4,48,768]{3,2,1,0:T(8,128)} %get-tuple-element.56), channel_id=1, source_target_pairs={{0,12},{1,13},{2,14},{3,15},{4,0},{5,1},{6,2},{7,3},{8,4},{9,5},{1... | collective-permute-start | bytes 3538952 | tf_op jit(solution)/shard_map/ppermute | solution.py:237
  151.2 26.3 %collective-permute-start.24 = (f32[4,48,768]{2,1,0:T(8,128)}, f32[4,48,768]{2,1,0:T(8,128)}, u32[]{:S(2)}, u32[]{:S(2)}) collective-permute-start(f32[4,48,768]{2,1,0:T(8,128)} %get-tuple-element.51), channel_id=1, source_target_pairs={{0,1},{1,2},{2,3},{3,0},{4,5},{5,6},{6,7},{7,4},{8,9},{9,10},{10,1... | collective-permute-start | bytes 1769480 | tf_op jit(solution)/shard_map/ppermute | solution.py:240
  151.7 28.9 %collective-permute-start.25 = (f32[4,48,768]{2,1,0:T(8,128)}, f32[4,48,768]{2,1,0:T(8,128)}, u32[]{:S(2)}, u32[]{:S(2)}) collective-permute-start(f32[4,48,768]{2,1,0:T(8,128)} %get-tuple-element.52), channel_id=1, source_target_pairs={{0,2},{1,3},{2,0},{3,1},{4,6},{5,7},{6,4},{7,5},{8,10},{9,11},{10,... | collective-permute-start | bytes 1769480 | tf_op jit(solution)/shard_map/ppermute | solution.py:240
  153.9 26.8 %collective-permute-start.26 = (f32[4,48,768]{2,1,0:T(8,128)}, f32[4,48,768]{2,1,0:T(8,128)}, u32[]{:S(2)}, u32[]{:S(2)}) collective-permute-start(f32[4,48,768]{2,1,0:T(8,128)} %get-tuple-element.53), channel_id=1, source_target_pairs={{0,3},{1,0},{2,1},{3,2},{4,7},{5,4},{6,5},{7,6},{8,11},{9,8},{10,9... | collective-permute-start | bytes 1769480 | tf_op jit(solution)/shard_map/ppermute | solution.py:240
  168.2 15.5 %collective-permute-start.29 = (f32[4,48,768]{2,1,0:T(8,128)}, f32[4,48,768]{2,1,0:T(8,128)}, u32[]{:S(2)}, u32[]{:S(2)}) collective-permute-start(f32[4,48,768]{2,1,0:T(8,128)} %get-tuple-element.58), channel_id=1, source_target_pairs={{0,1},{1,2},{2,3},{3,0},{4,5},{5,6},{6,7},{7,4},{8,9},{9,10},{10,1... | collective-permute-start | bytes 1769480 | tf_op jit(solution)/shard_map/ppermute | solution.py:240
  176.0 16.0 %collective-permute-start.30 = (f32[4,48,768]{2,1,0:T(8,128)}, f32[4,48,768]{2,1,0:T(8,128)}, u32[]{:S(2)}, u32[]{:S(2)}) collective-permute-start(f32[4,48,768]{2,1,0:T(8,128)} %get-tuple-element.59), channel_id=1, source_target_pairs={{0,2},{1,3},{2,0},{3,1},{4,6},{5,7},{6,4},{7,5},{8,10},{9,11},{10,... | collective-permute-start | bytes 1769480 | tf_op jit(solution)/shard_map/ppermute | solution.py:240
  177.5 14.4 %collective-permute-start.31 = (f32[4,48,768]{2,1,0:T(8,128)}, f32[4,48,768]{2,1,0:T(8,128)}, u32[]{:S(2)}, u32[]{:S(2)}) collective-permute-start(f32[4,48,768]{2,1,0:T(8,128)} %get-tuple-element.60), channel_id=1, source_target_pairs={{0,3},{1,0},{2,1},{3,2},{4,7},{5,4},{6,5},{7,6},{8,11},{9,8},{10,9... | collective-permute-start | bytes 1769480 | tf_op jit(solution)/shard_map/ppermute | solution.py:240

commit v13 on v12

--- a/solution.py
+++ b/solution.py
@@ -9,7 +9,8 @@
 from jax.sharding import PartitionSpec as P
 
 SIDE = 4
-VMEM = 64 * 1024 * 1024 - 256 * 1024
+VMEM = 16 * 1024 * 1024
+ROOMS = (40 * 1024 * 1024, 16 * 1024 * 1024)
 LIGHT = pl.CostEstimate(flops=0, bytes_accessed=0, transcendentals=0)
 def hops(count, steps):
     pairs = []
@@ -80,7 +81,7 @@
             out[k, 0] = acc[rows * i : rows * (i + 1)]
 
 
-def product(pieces, ovov, first, count, place, sizes, origin, after):
+def product(pieces, ovov, room, first, count, place, sizes, origin, after):
     rows2, depth = pieces[0][0].shape[1:]
     rows = rows2 // 2
     cols = ovov.shape[2]
@@ -99,7 +100,7 @@
             ],
         ),
         out_shape=[jax.ShapeDtypeStruct((lead, count, rows, cols), jnp.float32) for lead in LEADS],
-        compiler_params=pltpu.CompilerParams(vmem_limit_bytes=VMEM),
+        compiler_params=pltpu.CompilerParams(vmem_limit_bytes=room),
         cost_estimate=LIGHT,
         name="product",
     )(place, sizes, origin, *[piece for piece, _ in pieces], ovov, *after)
@@ -231,7 +232,7 @@
 
     def multiply(held, swapped, moved, moved_swapped, first, after):
         pieces = [(held, 0), (swapped, 0)] + [(piece, 0) for pair in zip(moved, moved_swapped) for piece in pair]
-        return product(pieces, ovov, first, held.shape[0], place, pair_sizes, origin, after)
+        return product(pieces, ovov, ROOMS[first > 0], first, held.shape[0], place, pair_sizes, origin, after)
 
     def to_neighbours(p, m):
         return lax.ppermute(p, BOTH, NEAR[1]), lax.ppermute(m, BOTH, NEAR[-1])

time: 198 us -> 189 us (0.955)
  waiting for transfers between devices: 72 us -> 90.7 us
  Pallas kernels: 44.8 us -> 28.9 us
  starting transfers between devices: 38.4 us -> 31.2 us
  local copies, waits for them, and re-layouts: 6.07 us -> 3.98 us
    ppermute x12, waiting for transfers between devices: 40.7 us -> 55.5 us  [to_neighbours(): return (lax.ppermute(p, BOTH, NEAR[1]), lax.ppermute(m, BOTH, NEAR[-1]))]
    ppermute x6, starting transfers between devices: 16 us -> 8.34 us  [across(): lax.ppermute(four[k], BOTH, FAR[d])]
    pallas_call x2, Pallas kernels: 6.95 us -> 1.55 us  [add_far(): pl.pallas_call(add_kernel, grid=(count // step,), in_specs=[spec] * 4 + [...]
    pallas_call x2, Pallas kernels: 8.46 us -> 3.54 us  [add_own(): pl.pallas_call(own_kernel, grid=(count // step,), in_specs=[spec(4)] + [s...]
    pallas_call x2, Pallas kernels: 24.9 us -> 20.4 us  [product(): pl.pallas_call(functools.partial(product_kernel, first), grid_spec=pltpu....]
    ppermute x6, waiting for transfers between devices: 11.2 us -> 14.4 us  [across(): lax.ppermute(four[k], BOTH, FAR[d])]
  transfers between devices with their start and end apart: 32 -> 32, of which waited for: 13 -> 17; matrix products, arithmetic and copies ran while one was open for 2% -> 1% of each run, Pallas kernels for 20% -> 13%
where the time goes in v13:
time: 189 us
  waiting for transfers between devices  90.7 us (48%)
  blocking collectives  33.8 us (18%)
  starting transfers between devices  31.2 us (17%)
  Pallas kernels  28.9 us (15%)
  local copies, waits for them, and re-layouts  3.98 us (2%)
    ppermute x12, waiting for transfers between devices, to_neighbours(): return (lax.ppermute(p, BOTH, NEAR[1]), lax.ppermute(m, BOTH, NEAR[-1]))  55.5 us
    all_to_all x2, blocking collectives, exchange(): part = lax.all_to_all(part, 'ob', split_axis=0, concat_axis=0, tiled=True)  33.8 us
    pallas_call x2, Pallas kernels, product(): pl.pallas_call(functools.partial(product_kernel, first), grid_spec=pltpu....  20.4 us
    ppermute x6, waiting for transfers between devices, along_z(): return [lax.ppermute(held, 'vb', steps) for steps in Z_stepS]  18.8 us
    ppermute x6, waiting for transfers between devices, across(): lax.ppermute(four[k], BOTH, FAR[d])  14.4 us
    ppermute x12, starting transfers between devices, to_neighbours(): return (lax.ppermute(p, BOTH, NEAR[1]), lax.ppermute(m, BOTH, NEAR[-1]))  11.5 us
    ppermute x6, starting transfers between devices, along_z(): return [lax.ppermute(held, 'vb', steps) for steps in Z_stepS]  9.71 us
    ppermute x6, starting transfers between devices, across(): lax.ppermute(four[k], BOTH, FAR[d])  8.34 us
  transfers between devices with their start and end apart: 32, of which 17 were waited for; matrix products, arithmetic and copies ran while one was open for 1% of the time, Pallas kernels for 13%

profile of v13, /device:TPU:0, one launch (start us, length us, event | category | flops | bytes accessed | tf_op | source)
XLA Modules:
  0.0 188.9 jit_solution(7702865959960293395)
XLA Ops:
  0.0 1.9 fusion
  2.4 19.1 %all_to_all.10 = f32[16,24,384]{2,1,0:T(8,128)S(1)} all-to-all(f32[16,24,384]{2,1,0:T(8,128)S(1)} %copy.10), channel_id=1, replica_groups=mesh['vb'=8,'ob'=16] {'ob'}, dimensions={0} | all-to-all | bytes 1179648 | tf_op jit(solution)/shard_map/all_to_all | solution.py:222
  21.7 4.0 %collective-permute-start.5 = (f32[4,96,384]{2,1,0:T(8,128)S(1)}, f32[4,96,384]{2,1,0:T(8,128)S(1)}, u32[]{:S(2)}, u32[]{:S(2)}) collective-permute-start(f32[4,96,384]{2,1,0:T(8,128)S(1)} %bitcast.21), channel_id=1, source_target_pairs={{0,64},{16,80},{32,96},{48,112},{64,0},{80,16},{96,32},{112,48},{1... | collective-permute-start | bytes 1769480 | tf_op jit(solution)/shard_map/ppermute | solution.py:231
  25.7 0.7 collective-permute-start.3
  26.4 1.3 collective-permute-start.1
  28.2 14.7 %all_to_all.11 = f32[16,24,384]{2,1,0:T(8,128)S(1)} all-to-all(f32[16,24,384]{2,1,0:T(8,128)S(1)} %copy.12), channel_id=1, replica_groups=mesh['vb'=8,'ob'=16] {'ob'}, dimensions={0} | all-to-all | bytes 1179648 | tf_op jit(solution)/shard_map/all_to_all | solution.py:222
  43.2 0.5 collective-permute-start
  43.8 7.1 %collective-permute-done.3.refs_4_.refs_2_ = f32[4,96,384]{2,1,0:T(8,128)S(1)} collective-permute-done((f32[4,96,384]{2,1,0:T(8,128)S(1)}, f32[4,96,384]{2,1,0:T(8,128)S(1)}, u32[]{:S(2)}, u32[]{:S(2)}) %collective-permute-start.3) | collective-permute-done | bytes 589856 | tf_op jit(solution)/shard_map/ppermute | solution.py:231
  50.9 0.5 collective-permute-start.2
  51.5 0.7 dynamic-slice_bitcast_fusion.place
  52.2 1.7 collective-permute-start.14
  53.9 1.7 collective-permute-start.13
  55.6 11.4 %product.2 = (f32[2,4,48,768]{3,2,1,0:T(8,128)S(1)}, f32[2,4,48,768]{3,2,1,0:T(8,128)S(1)}, f32[2,4,48,768]{3,2,1,0:T(8,128)S(1)}, f32[2,4,48,768]{3,2,1,0:T(8,1...) custom-call(s32[16]{0:T(128)S(1)} %dynamic-slice_bitcast_fusion.place, ...), custom_call_target="tpu_custom_call" | custom-call | tf_op jit(solution)/shard_map/product/pallas_call | solution.py:88
  67.0 1.2 collective-permute-start.11
  68.3 0.8 collective-permute-start.10
  69.1 0.4 collective-permute-start.12
  69.5 0.6 collective-permute-done.14.refs_1_
  70.1 9.9 %collective-permute-done.13.refs_0_ = f32[4,96,384]{2,1,0:T(8,128)S(1)} collective-permute-done((f32[4,96,384]{2,1,0:T(8,128)S(1)}, f32[4,96,384]{2,1,0:T(8,128)S(1)}, u32[]{:S(2)}, u32[]{:S(2)}) %collective-permute-start.13) | collective-permute-done | bytes 589856 | tf_op jit(solution)/shard_map/ppermute | solution.py:231
  79.9 0.5 collective-permute-start.17
  80.4 1.3 collective-permute-done.12.refs_0_
  81.7 0.7 collective-permute-start.8
  82.4 0.9 collective-permute-done.11.refs_2_.recv_m
  83.3 2.4 %collective-permute-done.10.refs_1_.recv_p = f32[2,4,48,768]{3,2,1,0:T(8,128)S(1)} collective-permute-done((f32[2,4,48,768]{3,2,1,0:T(8,128)S(1)}, f32[2,4,48,768]{3,2,1,0:T(8,128)S(1)}, u32[]{:S(2)}, u32[]{:S(2)}) %collective-permute-start.10) | collective-permute-done | bytes 1179680 | tf_op jit(solution)/shard_map/ppermute | solution.py:238
  85.8 1.9 %collective-permute-done.16.refs_3_ = f32[4,96,384]{2,1,0:T(8,128)S(1)} collective-permute-done((f32[4,96,384]{2,1,0:T(8,128)S(1)}, f32[4,96,384]{2,1,0:T(8,128)S(1)}, u32[]{:S(2)}, u32[]{:S(2)}) %collective-permute-start.16) | collective-permute-done | bytes 589856 | tf_op jit(solution)/shard_map/ppermute | solution.py:228
  87.7 9.0 %product.3 = (f32[2,4,48,768]{3,2,1,0:T(8,128)S(1)}, f32[2,4,48,768]{3,2,1,0:T(8,128)S(1)}, f32[2,4,48,768]{3,2,1,0:T(8,128)S(1)}, f32[2,4,48,768]{3,2,1,0:T(8,1...) custom-call(s32[16]{0:T(128)S(1)} %dynamic-slice_bitcast_fusion.place, ...), custom_call_target="tpu_custom_call" | custom-call | tf_op jit(solution)/shard_map/product/pallas_call | solution.py:88
  96.8 2.0 %collective-permute-start.20 = (f32[2,4,48,768]{3,2,1,0:T(8,128)S(1)}, f32[2,4,48,768]{3,2,1,0:T(8,128)S(1)}, u32[]{:S(2)}, u32[]{:S(2)}) collective-permute-start(f32[2,4,48,768]{3,2,1,0:T(8,128)S(1)} %get-tuple-element.42.refs_0_), channel_id=1, source_target_pairs={{0,4},{1,5},{2,6},{3,7},{4,8},{5,9},{6,10},{7,11},{8,12},{9,13},{1... | collective-permute-start | bytes 3538952 | tf_op jit(solution)/shard_map/ppermute | solution.py:238
  98.8 0.3 collective-permute-done.8.refs_1_.n1
  99.1 2.8 %collective-permute-done.9.refs_2_.n2 = f32[2,4,48,768]{3,2,1,0:T(8,128)S(1)} collective-permute-done((f32[2,4,48,768]{3,2,1,0:T(8,128)S(1)}, f32[2,4,48,768]{3,2,1,0:T(8,128)S(1)}, u32[]{:S(2)}, u32[]{:S(2)}) %collective-permute-start.9) | collective-permute-done | bytes 1179680 | tf_op jit(solution)/shard_map/ppermute | solution.py:238
  101.9 0.8 add_far.2
  102.8 3.2 %collective-permute-start.19 = (f32[2,4,48,768]{3,2,1,0:T(8,128)S(1)}, f32[2,4,48,768]{3,2,1,0:T(8,128)S(1)}, u32[]{:S(2)}, u32[]{:S(2)}) collective-permute-start(f32[2,4,48,768]{3,2,1,0:T(8,128)S(1)} %get-tuple-element.44), channel_id=1, source_target_pairs={{0,12},{1,13},{2,14},{3,15},{4,0},{5,1},{6,2},{7,3},{8,4},{9,5},{1... | collective-permute-start | bytes 3538952 | tf_op jit(solution)/shard_map/ppermute | solution.py:238
  106.0 8.6 %collective-permute-done.21.recv_m = f32[2,4,48,768]{3,2,1,0:T(8,128)S(1)} collective-permute-done((f32[2,4,48,768]{3,2,1,0:T(8,128)S(1)}, f32[2,4,48,768]{3,2,1,0:T(8,128)S(1)}, u32[]{:S(2)}, u32[]{:S(2)}) %collective-permute-start.21) | collective-permute-done | bytes 1179680 | tf_op jit(solution)/shard_map/ppermute | solution.py:238
  114.5 0.8 add_far.3
  115.3 0.5 collective-permute-start.22
  115.8 2.8 %collective-permute-start.23 = (f32[2,4,48,768]{3,2,1,0:T(8,128)S(1)}, f32[2,4,48,768]{3,2,1,0:T(8,128)S(1)}, u32[]{:S(2)}, u32[]{:S(2)}) collective-permute-start(f32[2,4,48,768]{3,2,1,0:T(8,128)S(1)} %get-tuple-element.49), channel_id=1, source_target_pairs={{0,12},{1,13},{2,14},{3,15},{4,0},{5,1},{6,2},{7,3},{8,4},{9,5},{1... | collective-permute-start | bytes 3538952 | tf_op jit(solution)/shard_map/ppermute | solution.py:238
  118.6 8.4 %collective-permute-done.18.p2 = f32[2,4,48,768]{3,2,1,0:T(8,128)S(1)} collective-permute-done((f32[2,4,48,768]{3,2,1,0:T(8,128)S(1)}, f32[2,4,48,768]{3,2,1,0:T(8,128)S(1)}, u32[]{:S(2)}, u32[]{:S(2)}) %collective-permute-start.18) | collective-permute-done | bytes 1179680 | tf_op jit(solution)/shard_map/ppermute | solution.py:238
  127.2 12.5 %collective-permute-done.22.refs_0_.p2 = f32[2,4,48,768]{3,2,1,0:T(8,128)S(1)} collective-permute-done((f32[2,4,48,768]{3,2,1,0:T(8,128)S(1)}, f32[2,4,48,768]{3,2,1,0:T(8,128)S(1)}, u32[]{:S(2)}, u32[]{:S(2)}) %collective-permute-start.22) | collective-permute-done | bytes 1179680 | tf_op jit(solution)/shard_map/ppermute | solution.py:238
  139.8 1.7 add_own.2
  141.5 0.5 collective-permute-start.24
  142.0 2.1 %collective-permute-start.25 = (f32[4,48,768]{2,1,0:T(8,128)}, f32[4,48,768]{2,1,0:T(8,128)S(1)}, u32[]{:S(2)}, u32[]{:S(2)}) collective-permute-start(f32[4,48,768]{2,1,0:T(8,128)} %get-tuple-element.52), channel_id=1, source_target_pairs={{0,2},{1,3},{2,0},{3,1},{4,6},{5,7},{6,4},{7,5},{8,10},{9,11},{10,... | collective-permute-start | bytes 1769480 | tf_op jit(solution)/shard_map/ppermute | solution.py:241
  144.1 1.5 collective-permute-start.26
  145.6 19.3 %collective-permute-done.27.n1 = f32[2,4,48,768]{3,2,1,0:T(8,128)S(1)} collective-permute-done((f32[2,4,48,768]{3,2,1,0:T(8,128)S(1)}, f32[2,4,48,768]{3,2,1,0:T(8,128)S(1)}, u32[]{:S(2)}, u32[]{:S(2)}) %collective-permute-start.27) | collective-permute-done | bytes 1179680 | tf_op jit(solution)/shard_map/ppermute | solution.py:238
  165.0 1.9 add_own.3
  166.9 0.5 collective-permute-start.29
  167.4 2.0 %collective-permute-start.30 = (f32[4,48,768]{2,1,0:T(8,128)}, f32[4,48,768]{2,1,0:T(8,128)}, u32[]{:S(2)}, u32[]{:S(2)}) collective-permute-start(f32[4,48,768]{2,1,0:T(8,128)} %get-tuple-element.59), channel_id=1, source_target_pairs={{0,2},{1,3},{2,0},{3,1},{4,6},{5,7},{6,4},{7,5},{8,10},{9,11},{10,... | collective-permute-start | bytes 1769480 | tf_op jit(solution)/shard_map/ppermute | solution.py:241
  169.4 1.7 collective-permute-start.31
  171.1 13.4 %collective-permute-done.29.refs_5_ = f32[4,48,768]{2,1,0:T(8,128)S(1)} collective-permute-done((f32[4,48,768]{2,1,0:T(8,128)}, f32[4,48,768]{2,1,0:T(8,128)S(1)}, u32[]{:S(2)}, u32[]{:S(2)}) %collective-permute-start.29) | collective-permute-done | bytes 589856 | tf_op jit(solution)/shard_map/ppermute | solution.py:241
  184.5 1.0 collective-permute-done.31.refs_7_
  185.5 3.4 %finish.1 = f32[48,8,768]{2,1,0:T(8,128)} custom-call(s32[8]{0:T(128)S(1)} %copy-done.2, s32[2]{0:T(128)S(1)} %pad_add_fusion.origin, f32[4,48,768]{2,1,0:T(8,128)S(1)} %get-tuple-element.50.refs_0_, f32[4,48,768]{2,1,0:T(8,128)S(1)} %collective-permute-done.24.refs_1_, f32[4,48,768]{2,1,0:T(8,128)S(1)} %collective-permute-done.25.refs_2_, ...), custom_call_target="tpu_custom_call" | custom-call | tf_op jit(solution)/shard_map/finish/pallas_call | solution.py:190
  (53 shorter events, 2.3 us)
Async XLA Ops:
  21.7 22.0 %collective-permute-start.5 = (f32[4,96,384]{2,1,0:T(8,128)S(1)}, f32[4,96,384]{2,1,0:T(8,128)S(1)}, u32[]{:S(2)}, u32[]{:S(2)}) collective-permute-start(f32[4,96,384]{2,1,0:T(8,128)S(1)} %bitcast.21), channel_id=1, source_target_pairs={{0,64},{16,80},{32,96},{48,112},{64,0},{80,16},{96,32},{112,48},{1... | collective-permute-start | bytes 1769480 | tf_op jit(solution)/shard_map/ppermute | solution.py:231
  25.7 25.2 %collective-permute-start.3 = (f32[4,96,384]{2,1,0:T(8,128)S(1)}, f32[4,96,384]{2,1,0:T(8,128)S(1)}, u32[]{:S(2)}, u32[]{:S(2)}) collective-permute-start(f32[4,96,384]{2,1,0:T(8,128)S(1)} %bitcast.22), channel_id=1, source_target_pairs={{0,96},{16,48},{32,0},{48,80},{64,32},{80,112},{96,64},{112,16},{1... | collective-permute-start | bytes 1769480 | tf_op jit(solution)/shard_map/ppermute | solution.py:231
  26.4 24.5 %collective-permute-start.1 = (f32[4,96,384]{2,1,0:T(8,128)S(1)}, f32[4,96,384]{2,1,0:T(8,128)}, u32[]{:S(2)}, u32[]{:S(2)}) collective-permute-start(f32[4,96,384]{2,1,0:T(8,128)S(1)} %bitcast.23), channel_id=1, source_target_pairs={{0,32},{16,112},{32,64},{48,16},{64,96},{80,48},{96,0},{112,80},{1... | collective-permute-start | bytes 1769480 | tf_op jit(solution)/shard_map/ppermute | solution.py:231
  43.1 9.1 %collective-permute-start.7 = (f32[4,96,384]{2,1,0:T(8,128)S(1)}, f32[4,96,384]{2,1,0:T(8,128)S(1)}, u32[]{:S(2)}, u32[]{:S(2)}) collective-permute-start(f32[4,96,384]{2,1,0:T(8,128)S(1)} %bitcast.19), channel_id=1, source_target_pairs={{0,16},{16,0},{32,48},{48,32},{64,80},{80,64},{96,112},{112,96},{1... | collective-permute-start | bytes 1769480 | tf_op jit(solution)/shard_map/ppermute | solution.py:228
  43.2 10.7 %collective-permute-start = (f32[4,96,384]{2,1,0:T(8,128)S(1)}, f32[4,96,384]{2,1,0:T(8,128)}, u32[]{:S(2)}, u32[]{:S(2)}) collective-permute-start(f32[4,96,384]{2,1,0:T(8,128)S(1)} %bitcast.24), channel_id=1, source_target_pairs={{0,16},{16,0},{32,48},{48,32},{64,80},{80,64},{96,112},{112,96},{1... | collective-permute-start | bytes 1769480 | tf_op jit(solution)/shard_map/ppermute | solution.py:228
  43.7 11.9 %collective-permute-start.6 = (f32[4,96,384]{2,1,0:T(8,128)S(1)}, f32[4,96,384]{2,1,0:T(8,128)}, u32[]{:S(2)}, u32[]{:S(2)}) collective-permute-start(f32[4,96,384]{2,1,0:T(8,128)S(1)} %collective-permute-done.5.refs_6_.refs_3_), channel_id=1, source_target_pairs={{0,16},{16,0},{32,48},{48,32},{64,80},{80,64},{96,112},{112,96},{1... | collective-permute-start | bytes 1769480 | tf_op jit(solution)/shard_map/ppermute | solution.py:228
  50.9 4.7 %collective-permute-start.4 = (f32[4,96,384]{2,1,0:T(8,128)S(1)}, f32[4,96,384]{2,1,0:T(8,128)}, u32[]{:S(2)}, u32[]{:S(2)}) collective-permute-start(f32[4,96,384]{2,1,0:T(8,128)S(1)} %collective-permute-done.3.refs_4_.refs_2_), channel_id=1, source_target_pairs={{0,16},{16,0},{32,48},{48,32},{64,80},{80,64},{96,112},{112,96},{1... | collective-permute-start | bytes 1769480 | tf_op jit(solution)/shard_map/ppermute | solution.py:228
  50.9 4.7 %collective-permute-start.2 = (f32[4,96,384]{2,1,0:T(8,128)}, f32[4,96,384]{2,1,0:T(8,128)}, u32[]{:S(2)}, u32[]{:S(2)}) collective-permute-start(f32[4,96,384]{2,1,0:T(8,128)} %collective-permute-done.1.refs_2_.refs_1_), channel_id=1, source_target_pairs={{0,16},{16,0},{32,48},{48,32},{64,80},{80,64},{96,112},{112,96},{1... | collective-permute-start | bytes 1769480 | tf_op jit(solution)/shard_map/ppermute | solution.py:228
  52.2 3.4 %copy-start.1 = (s32[8]{0:T(128)S(1)}, s32[8]{0:T(128)}, u32[]{:S(2)}) copy-start(s32[8]{0:T(128)} %sizes.4) | copy-start | bytes 100
  52.2 35.5 %slice-start = ((s8[9437184]{0:T(1024)(128)(4,1)}), s8[4194304]{0:T(1024)(128)(4,1)S(1)}, s32[]{:S(2)}) async-start(s8[9437184]{0:T(1024)(128)(4,1)} %bitcast.17), calls=%async_computation.2 | async-start | bytes 8388608
  52.2 35.5 %slice-start.1 = ((s8[9437184]{0:T(1024)(128)(4,1)}), s8[4194304]{0:T(1024)(128)(4,1)S(1)}, s32[]{:S(2)}) async-start(s8[9437184]{0:T(1024)(128)(4,1)} %bitcast.17), calls=%async_computation.3 | async-start | bytes 8388608
  52.2 35.5 %slice-start.2 = ((s8[9437184]{0:T(1024)(128)(4,1)}), s8[1048576]{0:T(1024)(128)(4,1)S(1)}, s32[]{:S(2)}) async-start(s8[9437184]{0:T(1024)(128)(4,1)} %bitcast.17), calls=%async_computation.4 | async-start | bytes 2097152
  52.2 17.8 %collective-permute-start.14 = (f32[4,96,384]{2,1,0:T(8,128)S(1)}, f32[4,96,384]{2,1,0:T(8,128)S(1)}, u32[]{:S(2)}, u32[]{:S(2)}) collective-permute-start(f32[4,96,384]{2,1,0:T(8,128)S(1)} %tie.3.refs_0_), channel_id=1, source_target_pairs={{0,64},{16,80},{32,96},{48,112},{64,0},{80,16},{96,32},{112,48},{1... | collective-permute-start | bytes 1769480 | tf_op jit(solution)/shard_map/ppermute | solution.py:231
  53.9 26.0 %collective-permute-start.13 = (f32[4,96,384]{2,1,0:T(8,128)S(1)}, f32[4,96,384]{2,1,0:T(8,128)S(1)}, u32[]{:S(2)}, u32[]{:S(2)}) collective-permute-start(f32[4,96,384]{2,1,0:T(8,128)S(1)} %tie.3.refs_0_), channel_id=1, source_target_pairs={{0,96},{16,48},{32,0},{48,80},{64,32},{80,112},{96,64},{112,16},{1... | collective-permute-start | bytes 1769480 | tf_op jit(solution)/shard_map/ppermute | solution.py:231
  67.0 16.2 %collective-permute-start.11 = (f32[2,4,48,768]{3,2,1,0:T(8,128)S(1)}, f32[2,4,48,768]{3,2,1,0:T(8,128)S(1)}, u32[]{:S(2)}, u32[]{:S(2)}) collective-permute-start(f32[2,4,48,768]{3,2,1,0:T(8,128)S(1)} %get-tuple-element.39), channel_id=1, source_target_pairs={{0,12},{1,13},{2,14},{3,15},{4,0},{5,1},{6,2},{7,3},{8,4},{9,5},{1... | collective-permute-start | bytes 3538952 | tf_op jit(solution)/shard_map/ppermute | solution.py:238
  68.3 17.4 %collective-permute-start.10 = (f32[2,4,48,768]{3,2,1,0:T(8,128)S(1)}, f32[2,4,48,768]{3,2,1,0:T(8,128)S(1)}, u32[]{:S(2)}, u32[]{:S(2)}) collective-permute-start(f32[2,4,48,768]{3,2,1,0:T(8,128)S(1)} %get-tuple-element.38.refs_2_), channel_id=1, source_target_pairs={{0,4},{1,5},{2,6},{3,7},{4,8},{5,9},{6,10},{7,11},{8,12},{9,13},{1... | collective-permute-start | bytes 3538952 | tf_op jit(solution)/shard_map/ppermute | solution.py:238
  69.1 12.6 %collective-permute-start.12 = (f32[4,96,384]{2,1,0:T(8,128)S(1)}, f32[4,96,384]{2,1,0:T(8,128)S(1)}, u32[]{:S(2)}, u32[]{:S(2)}) collective-permute-start(f32[4,96,384]{2,1,0:T(8,128)S(1)} %tie.3.refs_0_), channel_id=1, source_target_pairs={{0,32},{16,112},{32,64},{48,16},{64,96},{80,48},{96,0},{112,80},{1... | collective-permute-start | bytes 1769480 | tf_op jit(solution)/shard_map/ppermute | solution.py:231
  79.9 2.4 %collective-permute-start.15 = (f32[4,96,384]{2,1,0:T(8,128)S(1)}, f32[4,96,384]{2,1,0:T(8,128)S(1)}, u32[]{:S(2)}, u32[]{:S(2)}) collective-permute-start(f32[4,96,384]{2,1,0:T(8,128)S(1)} %get-tuple-element.40.refs_4_), channel_id=1, source_target_pairs={{0,16},{16,0},{32,48},{48,32},{64,80},{80,64},{96,112},{112,96},{1... | collective-permute-start | bytes 1769480 | tf_op jit(solution)/shard_map/ppermute | solution.py:228
  79.9 5.8 %collective-permute-start.17 = (f32[4,96,384]{2,1,0:T(8,128)S(1)}, f32[4,96,384]{2,1,0:T(8,128)S(1)}, u32[]{:S(2)}, u32[]{:S(2)}) collective-permute-start(f32[4,96,384]{2,1,0:T(8,128)S(1)} %get-tuple-element.41.refs_6_), channel_id=1, source_target_pairs={{0,16},{16,0},{32,48},{48,32},{64,80},{80,64},{96,112},{112,96},{1... | collective-permute-start | bytes 1769480 | tf_op jit(solution)/shard_map/ppermute | solution.py:228
  81.7 17.4 %collective-permute-start.8 = (f32[2,4,48,768]{3,2,1,0:T(8,128)S(1)}, f32[2,4,48,768]{3,2,1,0:T(8,128)S(1)}, u32[]{:S(2)}, u32[]{:S(2)}) collective-permute-start(f32[2,4,48,768]{3,2,1,0:T(8,128)S(1)} %get-tuple-element.34), channel_id=1, source_target_pairs={{0,4},{1,5},{2,6},{3,7},{4,8},{5,9},{6,10},{7,11},{8,12},{9,13},{1... | collective-permute-start | bytes 3538952 | tf_op jit(solution)/shard_map/ppermute | solution.py:238
  85.7 2.0 %collective-permute-start.16 = (f32[4,96,384]{2,1,0:T(8,128)S(1)}, f32[4,96,384]{2,1,0:T(8,128)S(1)}, u32[]{:S(2)}, u32[]{:S(2)}) collective-permute-start(f32[4,96,384]{2,1,0:T(8,128)S(1)} %tie.5.refs_2_), channel_id=1, source_target_pairs={{0,16},{16,0},{32,48},{48,32},{64,80},{80,64},{96,112},{112,96},{1... | collective-permute-start | bytes 1769480 | tf_op jit(solution)/shard_map/ppermute | solution.py:228
  85.7 16.2 %collective-permute-start.9 = (f32[2,4,48,768]{3,2,1,0:T(8,128)S(1)}, f32[2,4,48,768]{3,2,1,0:T(8,128)S(1)}, u32[]{:S(2)}, u32[]{:S(2)}) collective-permute-start(f32[2,4,48,768]{3,2,1,0:T(8,128)S(1)} %get-tuple-element.35), channel_id=1, source_target_pairs={{0,12},{1,13},{2,14},{3,15},{4,0},{5,1},{6,2},{7,3},{8,4},{9,5},{1... | collective-permute-start | bytes 3538952 | tf_op jit(solution)/shard_map/ppermute | solution.py:238
  96.7 17.8 %collective-permute-start.21 = (f32[2,4,48,768]{3,2,1,0:T(8,128)S(1)}, f32[2,4,48,768]{3,2,1,0:T(8,128)S(1)}, u32[]{:S(2)}, u32[]{:S(2)}) collective-permute-start(f32[2,4,48,768]{3,2,1,0:T(8,128)S(1)} %get-tuple-element.47), channel_id=1, source_target_pairs={{0,12},{1,13},{2,14},{3,15},{4,0},{5,1},{6,2},{7,3},{8,4},{9,5},{1... | collective-permute-start | bytes 3538952 | tf_op jit(solution)/shard_map/ppermute | solution.py:238
  96.8 17.7 %collective-permute-start.20 = (f32[2,4,48,768]{3,2,1,0:T(8,128)S(1)}, f32[2,4,48,768]{3,2,1,0:T(8,128)S(1)}, u32[]{:S(2)}, u32[]{:S(2)}) collective-permute-start(f32[2,4,48,768]{3,2,1,0:T(8,128)S(1)} %get-tuple-element.42.refs_0_), channel_id=1, source_target_pairs={{0,4},{1,5},{2,6},{3,7},{4,8},{5,9},{6,10},{7,11},{8,12},{9,13},{1... | collective-permute-start | bytes 3538952 | tf_op jit(solution)/shard_map/ppermute | solution.py:238
  102.7 24.4 %collective-permute-start.18 = (f32[2,4,48,768]{3,2,1,0:T(8,128)S(1)}, f32[2,4,48,768]{3,2,1,0:T(8,128)S(1)}, u32[]{:S(2)}, u32[]{:S(2)}) collective-permute-start(f32[2,4,48,768]{3,2,1,0:T(8,128)S(1)} %get-tuple-element.43), channel_id=1, source_target_pairs={{0,4},{1,5},{2,6},{3,7},{4,8},{5,9},{6,10},{7,11},{8,12},{9,13},{1... | collective-permute-start | bytes 3538952 | tf_op jit(solution)/shard_map/ppermute | solution.py:238
  102.8 24.4 %collective-permute-start.19 = (f32[2,4,48,768]{3,2,1,0:T(8,128)S(1)}, f32[2,4,48,768]{3,2,1,0:T(8,128)S(1)}, u32[]{:S(2)}, u32[]{:S(2)}) collective-permute-start(f32[2,4,48,768]{3,2,1,0:T(8,128)S(1)} %get-tuple-element.44), channel_id=1, source_target_pairs={{0,12},{1,13},{2,14},{3,15},{4,0},{5,1},{6,2},{7,3},{8,4},{9,5},{1... | collective-permute-start | bytes 3538952 | tf_op jit(solution)/shard_map/ppermute | solution.py:238
  114.5 25.3 %copy-start = (f32[4,4,48,768]{3,2,1,0:T(8,128)S(1)}, f32[4,4,48,768]{3,2,1,0:T(8,128)}, u32[]{:S(2)}) copy-start(f32[4,4,48,768]{3,2,1,0:T(8,128)} %get-tuple-element.33.own) | copy-start | bytes 7077892
  115.3 24.4 %collective-permute-start.22 = (f32[2,4,48,768]{3,2,1,0:T(8,128)S(1)}, f32[2,4,48,768]{3,2,1,0:T(8,128)S(1)}, u32[]{:S(2)}, u32[]{:S(2)}) collective-permute-start(f32[2,4,48,768]{3,2,1,0:T(8,128)S(1)} %get-tuple-element.48), channel_id=1, source_target_pairs={{0,4},{1,5},{2,6},{3,7},{4,8},{5,9},{6,10},{7,11},{8,12},{9,13},{1... | collective-permute-start | bytes 3538952 | tf_op jit(solution)/shard_map/ppermute | solution.py:238
  115.8 24.0 %collective-permute-start.23 = (f32[2,4,48,768]{3,2,1,0:T(8,128)S(1)}, f32[2,4,48,768]{3,2,1,0:T(8,128)S(1)}, u32[]{:S(2)}, u32[]{:S(2)}) collective-permute-start(f32[2,4,48,768]{3,2,1,0:T(8,128)S(1)} %get-tuple-element.49), channel_id=1, source_target_pairs={{0,12},{1,13},{2,14},{3,15},{4,0},{5,1},{6,2},{7,3},{8,4},{9,5},{1... | collective-permute-start | bytes 3538952 | tf_op jit(solution)/shard_map/ppermute | solution.py:238
  118.6 46.4 %collective-permute-start.27 = (f32[2,4,48,768]{3,2,1,0:T(8,128)S(1)}, f32[2,4,48,768]{3,2,1,0:T(8,128)S(1)}, u32[]{:S(2)}, u32[]{:S(2)}) collective-permute-start(f32[2,4,48,768]{3,2,1,0:T(8,128)S(1)} %get-tuple-element.55), channel_id=1, source_target_pairs={{0,4},{1,5},{2,6},{3,7},{4,8},{5,9},{6,10},{7,11},{8,12},{9,13},{1... | collective-permute-start | bytes 3538952 | tf_op jit(solution)/shard_map/ppermute | solution.py:238
  127.1 37.9 %collective-permute-start.28 = (f32[2,4,48,768]{3,2,1,0:T(8,128)S(1)}, f32[2,4,48,768]{3,2,1,0:T(8,128)S(1)}, u32[]{:S(2)}, u32[]{:S(2)}) collective-permute-start(f32[2,4,48,768]{3,2,1,0:T(8,128)S(1)} %get-tuple-element.56), channel_id=1, source_target_pairs={{0,12},{1,13},{2,14},{3,15},{4,0},{5,1},{6,2},{7,3},{8,4},{9,5},{1... | collective-permute-start | bytes 3538952 | tf_op jit(solution)/shard_map/ppermute | solution.py:238
  141.5 27.9 %collective-permute-start.24 = (f32[4,48,768]{2,1,0:T(8,128)S(1)}, f32[4,48,768]{2,1,0:T(8,128)S(1)}, u32[]{:S(2)}, u32[]{:S(2)}) collective-permute-start(f32[4,48,768]{2,1,0:T(8,128)S(1)} %get-tuple-element.51), channel_id=1, source_target_pairs={{0,1},{1,2},{2,3},{3,0},{4,5},{5,6},{6,7},{7,4},{8,9},{9,10},{10,1... | collective-permute-start | bytes 1769480 | tf_op jit(solution)/shard_map/ppermute | solution.py:241
  142.0 29.1 %collective-permute-start.25 = (f32[4,48,768]{2,1,0:T(8,128)}, f32[4,48,768]{2,1,0:T(8,128)S(1)}, u32[]{:S(2)}, u32[]{:S(2)}) collective-permute-start(f32[4,48,768]{2,1,0:T(8,128)} %get-tuple-element.52), channel_id=1, source_target_pairs={{0,2},{1,3},{2,0},{3,1},{4,6},{5,7},{6,4},{7,5},{8,10},{9,11},{10,... | collective-permute-start | bytes 1769480 | tf_op jit(solution)/shard_map/ppermute | solution.py:241
  144.1 27.0 %collective-permute-start.26 = (f32[4,48,768]{2,1,0:T(8,128)}, f32[4,48,768]{2,1,0:T(8,128)S(1)}, u32[]{:S(2)}, u32[]{:S(2)}) collective-permute-start(f32[4,48,768]{2,1,0:T(8,128)} %get-tuple-element.53), channel_id=1, source_target_pairs={{0,3},{1,0},{2,1},{3,2},{4,7},{5,4},{6,5},{7,6},{8,11},{9,8},{10,9... | collective-permute-start | bytes 1769480 | tf_op jit(solution)/shard_map/ppermute | solution.py:241
  165.0 20.5 %copy-start.2 = (s32[8]{0:T(128)S(1)}, s32[8]{0:T(128)}, u32[]{:S(2)}) copy-start(s32[8]{0:T(128)} %sizes.5) | copy-start | bytes 100
  166.9 17.6 %collective-permute-start.29 = (f32[4,48,768]{2,1,0:T(8,128)}, f32[4,48,768]{2,1,0:T(8,128)S(1)}, u32[]{:S(2)}, u32[]{:S(2)}) collective-permute-start(f32[4,48,768]{2,1,0:T(8,128)} %get-tuple-element.58), channel_id=1, source_target_pairs={{0,1},{1,2},{2,3},{3,0},{4,5},{5,6},{6,7},{7,4},{8,9},{9,10},{10,1... | collective-permute-start | bytes 1769480 | tf_op jit(solution)/shard_map/ppermute | solution.py:241
  167.4 17.1 %collective-permute-start.30 = (f32[4,48,768]{2,1,0:T(8,128)}, f32[4,48,768]{2,1,0:T(8,128)}, u32[]{:S(2)}, u32[]{:S(2)}) collective-permute-start(f32[4,48,768]{2,1,0:T(8,128)} %get-tuple-element.59), channel_id=1, source_target_pairs={{0,2},{1,3},{2,0},{3,1},{4,6},{5,7},{6,4},{7,5},{8,10},{9,11},{10,... | collective-permute-start | bytes 1769480 | tf_op jit(solution)/shard_map/ppermute | solution.py:241
  169.4 16.1 %collective-permute-start.31 = (f32[4,48,768]{2,1,0:T(8,128)}, f32[4,48,768]{2,1,0:T(8,128)}, u32[]{:S(2)}, u32[]{:S(2)}) collective-permute-start(f32[4,48,768]{2,1,0:T(8,128)} %get-tuple-element.60), channel_id=1, source_target_pairs={{0,3},{1,0},{2,1},{3,2},{4,7},{5,4},{6,5},{7,6},{8,11},{9,8},{10,9... | collective-permute-start | bytes 1769480 | tf_op jit(solution)/shard_map/ppermute | solution.py:241

commit v14 on v13

--- a/solution.py
+++ b/solution.py
@@ -12,6 +12,9 @@
 VMEM = 16 * 1024 * 1024
 ROOMS = (40 * 1024 * 1024, 16 * 1024 * 1024)
 LIGHT = pl.CostEstimate(flops=0, bytes_accessed=0, transcendentals=0)
+SPLIT = 4
+
+
 def hops(count, steps):
     pairs = []
     for i in range(count):
@@ -21,7 +24,7 @@
     return pairs
 
 
-Z_stepS = [hops(8, lambda i, d=d: (2, -d if i % 2 else d)) for d in (1, -1, 2)]
+Z_STEPS = [hops(8, lambda i, d=d: (2, -d if i % 2 else d)) for d in (1, -1, 2)]
 SWAP = [(i, i ^ 1) for i in range(8)]
 BOTH = ("vb", "ob")
 NEAR = {d: hops(128, lambda i, d=d: (1 if i // 16 % 2 else SIDE, d)) for d in (1, -1)}
@@ -202,9 +205,6 @@
     )(row_sizes, origin, *parts)
 
 
-SPLIT = 4
-
-
 def local(amplitudes, ovov, row_sizes, pair_sizes):
     ob = lax.axis_index("ob")
     vb = lax.axis_index("vb")
@@ -228,7 +228,7 @@
         return lax.ppermute(piece, "vb", SWAP)
 
     def along_z(held):
-        return [lax.ppermute(held, "vb", steps) for steps in Z_stepS]
+        return [lax.ppermute(held, "vb", steps) for steps in Z_STEPS]
 
     def multiply(held, swapped, moved, moved_swapped, first, after):
         pieces = [(held, 0), (swapped, 0)] + [(piece, 0) for pair in zip(moved, moved_swapped) for piece in pair]
@@ -243,7 +243,9 @@
     late_swapped = swap(late)
     moved = along_z(early)
     (late,) = tie([late], moved)
-    far_p, far_m, near_p, near_m, up, down, own = multiply(early, swap(early), moved, [swap(piece) for piece in moved], 0, [late_swapped])
+    far_p, far_m, near_p, near_m, up, down, own = multiply(
+        early, swap(early), moved, [swap(piece) for piece in moved], 0, [late_swapped]
+    )
     far, near = to_neighbours(far_p, far_m), to_neighbours(near_p, near_m)
     up_z, down_z, far_z = along_z(late)
     down_z, far_z = tie([down_z, far_z], [far_p])

time: 189 us -> 189 us (level)
  no operation moved by 1% of the time
where the time goes in v14:
time: 189 us
  waiting for transfers between devices  90.7 us (48%)
  blocking collectives  33.8 us (18%)
  starting transfers between devices  31.2 us (17%)
  Pallas kernels  28.9 us (15%)
  local copies, waits for them, and re-layouts  3.98 us (2%)
    ppermute x12, waiting for transfers between devices, to_neighbours(): return (lax.ppermute(p, BOTH, NEAR[1]), lax.ppermute(m, BOTH, NEAR[-1]))  55.5 us
    all_to_all x2, blocking collectives, exchange(): part = lax.all_to_all(part, 'ob', split_axis=0, concat_axis=0, tiled=True)  33.8 us
    pallas_call x2, Pallas kernels, product(): pl.pallas_call(functools.partial(product_kernel, first), grid_spec=pltpu....  20.4 us
    ppermute x6, waiting for transfers between devices, along_z(): return [lax.ppermute(held, 'vb', steps) for steps in Z_STEPS]  18.8 us
    ppermute x6, waiting for transfers between devices, across(): lax.ppermute(four[k], BOTH, FAR[d])  14.4 us
    ppermute x12, starting transfers between devices, to_neighbours(): return (lax.ppermute(p, BOTH, NEAR[1]), lax.ppermute(m, BOTH, NEAR[-1]))  11.5 us
    ppermute x6, starting transfers between devices, along_z(): return [lax.ppermute(held, 'vb', steps) for steps in Z_STEPS]  9.71 us
    ppermute x6, starting transfers between devices, across(): lax.ppermute(four[k], BOTH, FAR[d])  8.34 us
  transfers between devices with their start and end apart: 32, of which 17 were waited for; matrix products, arithmetic and copies ran while one was open for 1% of the time, Pallas kernels for 13%

profile of v14, /device:TPU:0, one launch (start us, length us, event | category | flops | bytes accessed | tf_op | source)
XLA Modules:
  0.0 188.9 jit_solution(7702865959960293395)
XLA Ops:
  0.0 1.9 fusion
  2.4 19.1 %all_to_all.10 = f32[16,24,384]{2,1,0:T(8,128)S(1)} all-to-all(f32[16,24,384]{2,1,0:T(8,128)S(1)} %copy.10), channel_id=1, replica_groups=mesh['vb'=8,'ob'=16] {'ob'}, dimensions={0} | all-to-all | bytes 1179648 | tf_op jit(solution)/shard_map/all_to_all | solution.py:222
  21.7 4.0 %collective-permute-start.5 = (f32[4,96,384]{2,1,0:T(8,128)S(1)}, f32[4,96,384]{2,1,0:T(8,128)S(1)}, u32[]{:S(2)}, u32[]{:S(2)}) collective-permute-start(f32[4,96,384]{2,1,0:T(8,128)S(1)} %bitcast.21), channel_id=1, source_target_pairs={{0,64},{16,80},{32,96},{48,112},{64,0},{80,16},{96,32},{112,48},{1... | collective-permute-start | bytes 1769480 | tf_op jit(solution)/shard_map/ppermute | solution.py:231
  25.7 0.7 collective-permute-start.3
  26.4 1.3 collective-permute-start.1
  28.2 14.7 %all_to_all.11 = f32[16,24,384]{2,1,0:T(8,128)S(1)} all-to-all(f32[16,24,384]{2,1,0:T(8,128)S(1)} %copy.12), channel_id=1, replica_groups=mesh['vb'=8,'ob'=16] {'ob'}, dimensions={0} | all-to-all | bytes 1179648 | tf_op jit(solution)/shard_map/all_to_all | solution.py:222
  43.2 0.5 collective-permute-start
  43.8 7.1 %collective-permute-done.3.refs_4_.refs_2_ = f32[4,96,384]{2,1,0:T(8,128)S(1)} collective-permute-done((f32[4,96,384]{2,1,0:T(8,128)S(1)}, f32[4,96,384]{2,1,0:T(8,128)S(1)}, u32[]{:S(2)}, u32[]{:S(2)}) %collective-permute-start.3) | collective-permute-done | bytes 589856 | tf_op jit(solution)/shard_map/ppermute | solution.py:231
  50.9 0.5 collective-permute-start.2
  51.5 0.7 dynamic-slice_bitcast_fusion.place
  52.2 1.7 collective-permute-start.14
  53.9 1.7 collective-permute-start.13
  55.6 11.4 %product.2 = (f32[2,4,48,768]{3,2,1,0:T(8,128)S(1)}, f32[2,4,48,768]{3,2,1,0:T(8,128)S(1)}, f32[2,4,48,768]{3,2,1,0:T(8,128)S(1)}, f32[2,4,48,768]{3,2,1,0:T(8,1...) custom-call(s32[16]{0:T(128)S(1)} %dynamic-slice_bitcast_fusion.place, ...), custom_call_target="tpu_custom_call" | custom-call | tf_op jit(solution)/shard_map/product/pallas_call | solution.py:91
  67.0 1.2 collective-permute-start.11
  68.3 0.8 collective-permute-start.10
  69.1 0.4 collective-permute-start.12
  69.5 0.6 collective-permute-done.14.refs_1_
  70.1 9.9 %collective-permute-done.13.refs_0_ = f32[4,96,384]{2,1,0:T(8,128)S(1)} collective-permute-done((f32[4,96,384]{2,1,0:T(8,128)S(1)}, f32[4,96,384]{2,1,0:T(8,128)S(1)}, u32[]{:S(2)}, u32[]{:S(2)}) %collective-permute-start.13) | collective-permute-done | bytes 589856 | tf_op jit(solution)/shard_map/ppermute | solution.py:231
  79.9 0.5 collective-permute-start.17
  80.4 1.3 collective-permute-done.12.refs_0_
  81.7 0.7 collective-permute-start.8
  82.4 0.9 collective-permute-done.11.refs_2_.recv_m
  83.3 2.4 %collective-permute-done.10.refs_1_.recv_p = f32[2,4,48,768]{3,2,1,0:T(8,128)S(1)} collective-permute-done((f32[2,4,48,768]{3,2,1,0:T(8,128)S(1)}, f32[2,4,48,768]{3,2,1,0:T(8,128)S(1)}, u32[]{:S(2)}, u32[]{:S(2)}) %collective-permute-start.10) | collective-permute-done | bytes 1179680 | tf_op jit(solution)/shard_map/ppermute | solution.py:238
  85.8 1.9 %collective-permute-done.16.refs_3_ = f32[4,96,384]{2,1,0:T(8,128)S(1)} collective-permute-done((f32[4,96,384]{2,1,0:T(8,128)S(1)}, f32[4,96,384]{2,1,0:T(8,128)S(1)}, u32[]{:S(2)}, u32[]{:S(2)}) %collective-permute-start.16) | collective-permute-done | bytes 589856 | tf_op jit(solution)/shard_map/ppermute | solution.py:228
  87.7 9.0 %product.3 = (f32[2,4,48,768]{3,2,1,0:T(8,128)S(1)}, f32[2,4,48,768]{3,2,1,0:T(8,128)S(1)}, f32[2,4,48,768]{3,2,1,0:T(8,128)S(1)}, f32[2,4,48,768]{3,2,1,0:T(8,1...) custom-call(s32[16]{0:T(128)S(1)} %dynamic-slice_bitcast_fusion.place, ...), custom_call_target="tpu_custom_call" | custom-call | tf_op jit(solution)/shard_map/product/pallas_call | solution.py:91
  96.8 2.0 %collective-permute-start.20 = (f32[2,4,48,768]{3,2,1,0:T(8,128)S(1)}, f32[2,4,48,768]{3,2,1,0:T(8,128)S(1)}, u32[]{:S(2)}, u32[]{:S(2)}) collective-permute-start(f32[2,4,48,768]{3,2,1,0:T(8,128)S(1)} %get-tuple-element.42.refs_0_), channel_id=1, source_target_pairs={{0,4},{1,5},{2,6},{3,7},{4,8},{5,9},{6,10},{7,11},{8,12},{9,13},{1... | collective-permute-start | bytes 3538952 | tf_op jit(solution)/shard_map/ppermute | solution.py:238
  98.8 0.3 collective-permute-done.8.refs_1_.n1
  99.1 2.8 %collective-permute-done.9.refs_2_.n2 = f32[2,4,48,768]{3,2,1,0:T(8,128)S(1)} collective-permute-done((f32[2,4,48,768]{3,2,1,0:T(8,128)S(1)}, f32[2,4,48,768]{3,2,1,0:T(8,128)S(1)}, u32[]{:S(2)}, u32[]{:S(2)}) %collective-permute-start.9) | collective-permute-done | bytes 1179680 | tf_op jit(solution)/shard_map/ppermute | solution.py:238
  101.9 0.8 add_far.2
  102.8 3.2 %collective-permute-start.19 = (f32[2,4,48,768]{3,2,1,0:T(8,128)S(1)}, f32[2,4,48,768]{3,2,1,0:T(8,128)S(1)}, u32[]{:S(2)}, u32[]{:S(2)}) collective-permute-start(f32[2,4,48,768]{3,2,1,0:T(8,128)S(1)} %get-tuple-element.44), channel_id=1, source_target_pairs={{0,12},{1,13},{2,14},{3,15},{4,0},{5,1},{6,2},{7,3},{8,4},{9,5},{1... | collective-permute-start | bytes 3538952 | tf_op jit(solution)/shard_map/ppermute | solution.py:238
  106.0 8.6 %collective-permute-done.21.recv_m = f32[2,4,48,768]{3,2,1,0:T(8,128)S(1)} collective-permute-done((f32[2,4,48,768]{3,2,1,0:T(8,128)S(1)}, f32[2,4,48,768]{3,2,1,0:T(8,128)S(1)}, u32[]{:S(2)}, u32[]{:S(2)}) %collective-permute-start.21) | collective-permute-done | bytes 1179680 | tf_op jit(solution)/shard_map/ppermute | solution.py:238
  114.5 0.8 add_far.3
  115.3 0.5 collective-permute-start.22
  115.8 2.8 %collective-permute-start.23 = (f32[2,4,48,768]{3,2,1,0:T(8,128)S(1)}, f32[2,4,48,768]{3,2,1,0:T(8,128)S(1)}, u32[]{:S(2)}, u32[]{:S(2)}) collective-permute-start(f32[2,4,48,768]{3,2,1,0:T(8,128)S(1)} %get-tuple-element.49), channel_id=1, source_target_pairs={{0,12},{1,13},{2,14},{3,15},{4,0},{5,1},{6,2},{7,3},{8,4},{9,5},{1... | collective-permute-start | bytes 3538952 | tf_op jit(solution)/shard_map/ppermute | solution.py:238
  118.6 8.4 %collective-permute-done.18.p2 = f32[2,4,48,768]{3,2,1,0:T(8,128)S(1)} collective-permute-done((f32[2,4,48,768]{3,2,1,0:T(8,128)S(1)}, f32[2,4,48,768]{3,2,1,0:T(8,128)S(1)}, u32[]{:S(2)}, u32[]{:S(2)}) %collective-permute-start.18) | collective-permute-done | bytes 1179680 | tf_op jit(solution)/shard_map/ppermute | solution.py:238
  127.2 12.5 %collective-permute-done.22.refs_0_.p2 = f32[2,4,48,768]{3,2,1,0:T(8,128)S(1)} collective-permute-done((f32[2,4,48,768]{3,2,1,0:T(8,128)S(1)}, f32[2,4,48,768]{3,2,1,0:T(8,128)S(1)}, u32[]{:S(2)}, u32[]{:S(2)}) %collective-permute-start.22) | collective-permute-done | bytes 1179680 | tf_op jit(solution)/shard_map/ppermute | solution.py:238
  139.8 1.7 add_own.2
  141.5 0.5 collective-permute-start.24
  142.0 2.1 %collective-permute-start.25 = (f32[4,48,768]{2,1,0:T(8,128)}, f32[4,48,768]{2,1,0:T(8,128)S(1)}, u32[]{:S(2)}, u32[]{:S(2)}) collective-permute-start(f32[4,48,768]{2,1,0:T(8,128)} %get-tuple-element.52), channel_id=1, source_target_pairs={{0,2},{1,3},{2,0},{3,1},{4,6},{5,7},{6,4},{7,5},{8,10},{9,11},{10,... | collective-permute-start | bytes 1769480 | tf_op jit(solution)/shard_map/ppermute | solution.py:241
  144.1 1.5 collective-permute-start.26
  145.6 19.3 %collective-permute-done.27.n1 = f32[2,4,48,768]{3,2,1,0:T(8,128)S(1)} collective-permute-done((f32[2,4,48,768]{3,2,1,0:T(8,128)S(1)}, f32[2,4,48,768]{3,2,1,0:T(8,128)S(1)}, u32[]{:S(2)}, u32[]{:S(2)}) %collective-permute-start.27) | collective-permute-done | bytes 1179680 | tf_op jit(solution)/shard_map/ppermute | solution.py:238
  165.0 1.9 add_own.3
  166.9 0.5 collective-permute-start.29
  167.4 2.0 %collective-permute-start.30 = (f32[4,48,768]{2,1,0:T(8,128)}, f32[4,48,768]{2,1,0:T(8,128)}, u32[]{:S(2)}, u32[]{:S(2)}) collective-permute-start(f32[4,48,768]{2,1,0:T(8,128)} %get-tuple-element.59), channel_id=1, source_target_pairs={{0,2},{1,3},{2,0},{3,1},{4,6},{5,7},{6,4},{7,5},{8,10},{9,11},{10,... | collective-permute-start | bytes 1769480 | tf_op jit(solution)/shard_map/ppermute | solution.py:241
  169.4 1.7 collective-permute-start.31
  171.1 13.4 %collective-permute-done.29.refs_5_ = f32[4,48,768]{2,1,0:T(8,128)S(1)} collective-permute-done((f32[4,48,768]{2,1,0:T(8,128)}, f32[4,48,768]{2,1,0:T(8,128)S(1)}, u32[]{:S(2)}, u32[]{:S(2)}) %collective-permute-start.29) | collective-permute-done | bytes 589856 | tf_op jit(solution)/shard_map/ppermute | solution.py:241
  184.5 1.0 collective-permute-done.31.refs_7_
  185.5 3.4 %finish.1 = f32[48,8,768]{2,1,0:T(8,128)} custom-call(s32[8]{0:T(128)S(1)} %copy-done.2, s32[2]{0:T(128)S(1)} %pad_add_fusion.origin, f32[4,48,768]{2,1,0:T(8,128)S(1)} %get-tuple-element.50.refs_0_, f32[4,48,768]{2,1,0:T(8,128)S(1)} %collective-permute-done.24.refs_1_, f32[4,48,768]{2,1,0:T(8,128)S(1)} %collective-permute-done.25.refs_2_, ...), custom_call_target="tpu_custom_call" | custom-call | tf_op jit(solution)/shard_map/finish/pallas_call | solution.py:193
  (53 shorter events, 2.3 us)
Async XLA Ops:
  21.7 22.0 %collective-permute-start.5 = (f32[4,96,384]{2,1,0:T(8,128)S(1)}, f32[4,96,384]{2,1,0:T(8,128)S(1)}, u32[]{:S(2)}, u32[]{:S(2)}) collective-permute-start(f32[4,96,384]{2,1,0:T(8,128)S(1)} %bitcast.21), channel_id=1, source_target_pairs={{0,64},{16,80},{32,96},{48,112},{64,0},{80,16},{96,32},{112,48},{1... | collective-permute-start | bytes 1769480 | tf_op jit(solution)/shard_map/ppermute | solution.py:231
  25.7 25.2 %collective-permute-start.3 = (f32[4,96,384]{2,1,0:T(8,128)S(1)}, f32[4,96,384]{2,1,0:T(8,128)S(1)}, u32[]{:S(2)}, u32[]{:S(2)}) collective-permute-start(f32[4,96,384]{2,1,0:T(8,128)S(1)} %bitcast.22), channel_id=1, source_target_pairs={{0,96},{16,48},{32,0},{48,80},{64,32},{80,112},{96,64},{112,16},{1... | collective-permute-start | bytes 1769480 | tf_op jit(solution)/shard_map/ppermute | solution.py:231
  26.4 24.5 %collective-permute-start.1 = (f32[4,96,384]{2,1,0:T(8,128)S(1)}, f32[4,96,384]{2,1,0:T(8,128)}, u32[]{:S(2)}, u32[]{:S(2)}) collective-permute-start(f32[4,96,384]{2,1,0:T(8,128)S(1)} %bitcast.23), channel_id=1, source_target_pairs={{0,32},{16,112},{32,64},{48,16},{64,96},{80,48},{96,0},{112,80},{1... | collective-permute-start | bytes 1769480 | tf_op jit(solution)/shard_map/ppermute | solution.py:231
  43.1 9.1 %collective-permute-start.7 = (f32[4,96,384]{2,1,0:T(8,128)S(1)}, f32[4,96,384]{2,1,0:T(8,128)S(1)}, u32[]{:S(2)}, u32[]{:S(2)}) collective-permute-start(f32[4,96,384]{2,1,0:T(8,128)S(1)} %bitcast.19), channel_id=1, source_target_pairs={{0,16},{16,0},{32,48},{48,32},{64,80},{80,64},{96,112},{112,96},{1... | collective-permute-start | bytes 1769480 | tf_op jit(solution)/shard_map/ppermute | solution.py:228
  43.2 10.7 %collective-permute-start = (f32[4,96,384]{2,1,0:T(8,128)S(1)}, f32[4,96,384]{2,1,0:T(8,128)}, u32[]{:S(2)}, u32[]{:S(2)}) collective-permute-start(f32[4,96,384]{2,1,0:T(8,128)S(1)} %bitcast.24), channel_id=1, source_target_pairs={{0,16},{16,0},{32,48},{48,32},{64,80},{80,64},{96,112},{112,96},{1... | collective-permute-start | bytes 1769480 | tf_op jit(solution)/shard_map/ppermute | solution.py:228
  43.7 11.9 %collective-permute-start.6 = (f32[4,96,384]{2,1,0:T(8,128)S(1)}, f32[4,96,384]{2,1,0:T(8,128)}, u32[]{:S(2)}, u32[]{:S(2)}) collective-permute-start(f32[4,96,384]{2,1,0:T(8,128)S(1)} %collective-permute-done.5.refs_6_.refs_3_), channel_id=1, source_target_pairs={{0,16},{16,0},{32,48},{48,32},{64,80},{80,64},{96,112},{112,96},{1... | collective-permute-start | bytes 1769480 | tf_op jit(solution)/shard_map/ppermute | solution.py:228
  50.9 4.7 %collective-permute-start.4 = (f32[4,96,384]{2,1,0:T(8,128)S(1)}, f32[4,96,384]{2,1,0:T(8,128)}, u32[]{:S(2)}, u32[]{:S(2)}) collective-permute-start(f32[4,96,384]{2,1,0:T(8,128)S(1)} %collective-permute-done.3.refs_4_.refs_2_), channel_id=1, source_target_pairs={{0,16},{16,0},{32,48},{48,32},{64,80},{80,64},{96,112},{112,96},{1... | collective-permute-start | bytes 1769480 | tf_op jit(solution)/shard_map/ppermute | solution.py:228
  50.9 4.7 %collective-permute-start.2 = (f32[4,96,384]{2,1,0:T(8,128)}, f32[4,96,384]{2,1,0:T(8,128)}, u32[]{:S(2)}, u32[]{:S(2)}) collective-permute-start(f32[4,96,384]{2,1,0:T(8,128)} %collective-permute-done.1.refs_2_.refs_1_), channel_id=1, source_target_pairs={{0,16},{16,0},{32,48},{48,32},{64,80},{80,64},{96,112},{112,96},{1... | collective-permute-start | bytes 1769480 | tf_op jit(solution)/shard_map/ppermute | solution.py:228
  52.2 3.4 %copy-start.1 = (s32[8]{0:T(128)S(1)}, s32[8]{0:T(128)}, u32[]{:S(2)}) copy-start(s32[8]{0:T(128)} %sizes.4) | copy-start | bytes 100
  52.2 35.5 %slice-start = ((s8[9437184]{0:T(1024)(128)(4,1)}), s8[4194304]{0:T(1024)(128)(4,1)S(1)}, s32[]{:S(2)}) async-start(s8[9437184]{0:T(1024)(128)(4,1)} %bitcast.17), calls=%async_computation.2 | async-start | bytes 8388608
  52.2 35.5 %slice-start.1 = ((s8[9437184]{0:T(1024)(128)(4,1)}), s8[4194304]{0:T(1024)(128)(4,1)S(1)}, s32[]{:S(2)}) async-start(s8[9437184]{0:T(1024)(128)(4,1)} %bitcast.17), calls=%async_computation.3 | async-start | bytes 8388608
  52.2 35.5 %slice-start.2 = ((s8[9437184]{0:T(1024)(128)(4,1)}), s8[1048576]{0:T(1024)(128)(4,1)S(1)}, s32[]{:S(2)}) async-start(s8[9437184]{0:T(1024)(128)(4,1)} %bitcast.17), calls=%async_computation.4 | async-start | bytes 2097152
  52.2 17.8 %collective-permute-start.14 = (f32[4,96,384]{2,1,0:T(8,128)S(1)}, f32[4,96,384]{2,1,0:T(8,128)S(1)}, u32[]{:S(2)}, u32[]{:S(2)}) collective-permute-start(f32[4,96,384]{2,1,0:T(8,128)S(1)} %tie.3.refs_0_), channel_id=1, source_target_pairs={{0,64},{16,80},{32,96},{48,112},{64,0},{80,16},{96,32},{112,48},{1... | collective-permute-start | bytes 1769480 | tf_op jit(solution)/shard_map/ppermute | solution.py:231
  53.9 26.0 %collective-permute-start.13 = (f32[4,96,384]{2,1,0:T(8,128)S(1)}, f32[4,96,384]{2,1,0:T(8,128)S(1)}, u32[]{:S(2)}, u32[]{:S(2)}) collective-permute-start(f32[4,96,384]{2,1,0:T(8,128)S(1)} %tie.3.refs_0_), channel_id=1, source_target_pairs={{0,96},{16,48},{32,0},{48,80},{64,32},{80,112},{96,64},{112,16},{1... | collective-permute-start | bytes 1769480 | tf_op jit(solution)/shard_map/ppermute | solution.py:231
  67.0 16.2 %collective-permute-start.11 = (f32[2,4,48,768]{3,2,1,0:T(8,128)S(1)}, f32[2,4,48,768]{3,2,1,0:T(8,128)S(1)}, u32[]{:S(2)}, u32[]{:S(2)}) collective-permute-start(f32[2,4,48,768]{3,2,1,0:T(8,128)S(1)} %get-tuple-element.39), channel_id=1, source_target_pairs={{0,12},{1,13},{2,14},{3,15},{4,0},{5,1},{6,2},{7,3},{8,4},{9,5},{1... | collective-permute-start | bytes 3538952 | tf_op jit(solution)/shard_map/ppermute | solution.py:238
  68.3 17.4 %collective-permute-start.10 = (f32[2,4,48,768]{3,2,1,0:T(8,128)S(1)}, f32[2,4,48,768]{3,2,1,0:T(8,128)S(1)}, u32[]{:S(2)}, u32[]{:S(2)}) collective-permute-start(f32[2,4,48,768]{3,2,1,0:T(8,128)S(1)} %get-tuple-element.38.refs_2_), channel_id=1, source_target_pairs={{0,4},{1,5},{2,6},{3,7},{4,8},{5,9},{6,10},{7,11},{8,12},{9,13},{1... | collective-permute-start | bytes 3538952 | tf_op jit(solution)/shard_map/ppermute | solution.py:238
  69.1 12.6 %collective-permute-start.12 = (f32[4,96,384]{2,1,0:T(8,128)S(1)}, f32[4,96,384]{2,1,0:T(8,128)S(1)}, u32[]{:S(2)}, u32[]{:S(2)}) collective-permute-start(f32[4,96,384]{2,1,0:T(8,128)S(1)} %tie.3.refs_0_), channel_id=1, source_target_pairs={{0,32},{16,112},{32,64},{48,16},{64,96},{80,48},{96,0},{112,80},{1... | collective-permute-start | bytes 1769480 | tf_op jit(solution)/shard_map/ppermute | solution.py:231
  79.9 2.4 %collective-permute-start.15 = (f32[4,96,384]{2,1,0:T(8,128)S(1)}, f32[4,96,384]{2,1,0:T(8,128)S(1)}, u32[]{:S(2)}, u32[]{:S(2)}) collective-permute-start(f32[4,96,384]{2,1,0:T(8,128)S(1)} %get-tuple-element.40.refs_4_), channel_id=1, source_target_pairs={{0,16},{16,0},{32,48},{48,32},{64,80},{80,64},{96,112},{112,96},{1... | collective-permute-start | bytes 1769480 | tf_op jit(solution)/shard_map/ppermute | solution.py:228
  79.9 5.8 %collective-permute-start.17 = (f32[4,96,384]{2,1,0:T(8,128)S(1)}, f32[4,96,384]{2,1,0:T(8,128)S(1)}, u32[]{:S(2)}, u32[]{:S(2)}) collective-permute-start(f32[4,96,384]{2,1,0:T(8,128)S(1)} %get-tuple-element.41.refs_6_), channel_id=1, source_target_pairs={{0,16},{16,0},{32,48},{48,32},{64,80},{80,64},{96,112},{112,96},{1... | collective-permute-start | bytes 1769480 | tf_op jit(solution)/shard_map/ppermute | solution.py:228
  81.7 17.4 %collective-permute-start.8 = (f32[2,4,48,768]{3,2,1,0:T(8,128)S(1)}, f32[2,4,48,768]{3,2,1,0:T(8,128)S(1)}, u32[]{:S(2)}, u32[]{:S(2)}) collective-permute-start(f32[2,4,48,768]{3,2,1,0:T(8,128)S(1)} %get-tuple-element.34), channel_id=1, source_target_pairs={{0,4},{1,5},{2,6},{3,7},{4,8},{5,9},{6,10},{7,11},{8,12},{9,13},{1... | collective-permute-start | bytes 3538952 | tf_op jit(solution)/shard_map/ppermute | solution.py:238
  85.7 2.0 %collective-permute-start.16 = (f32[4,96,384]{2,1,0:T(8,128)S(1)}, f32[4,96,384]{2,1,0:T(8,128)S(1)}, u32[]{:S(2)}, u32[]{:S(2)}) collective-permute-start(f32[4,96,384]{2,1,0:T(8,128)S(1)} %tie.5.refs_2_), channel_id=1, source_target_pairs={{0,16},{16,0},{32,48},{48,32},{64,80},{80,64},{96,112},{112,96},{1... | collective-permute-start | bytes 1769480 | tf_op jit(solution)/shard_map/ppermute | solution.py:228
  85.7 16.2 %collective-permute-start.9 = (f32[2,4,48,768]{3,2,1,0:T(8,128)S(1)}, f32[2,4,48,768]{3,2,1,0:T(8,128)S(1)}, u32[]{:S(2)}, u32[]{:S(2)}) collective-permute-start(f32[2,4,48,768]{3,2,1,0:T(8,128)S(1)} %get-tuple-element.35), channel_id=1, source_target_pairs={{0,12},{1,13},{2,14},{3,15},{4,0},{5,1},{6,2},{7,3},{8,4},{9,5},{1... | collective-permute-start | bytes 3538952 | tf_op jit(solution)/shard_map/ppermute | solution.py:238
  96.7 17.8 %collective-permute-start.21 = (f32[2,4,48,768]{3,2,1,0:T(8,128)S(1)}, f32[2,4,48,768]{3,2,1,0:T(8,128)S(1)}, u32[]{:S(2)}, u32[]{:S(2)}) collective-permute-start(f32[2,4,48,768]{3,2,1,0:T(8,128)S(1)} %get-tuple-element.47), channel_id=1, source_target_pairs={{0,12},{1,13},{2,14},{3,15},{4,0},{5,1},{6,2},{7,3},{8,4},{9,5},{1... | collective-permute-start | bytes 3538952 | tf_op jit(solution)/shard_map/ppermute | solution.py:238
  96.8 17.7 %collective-permute-start.20 = (f32[2,4,48,768]{3,2,1,0:T(8,128)S(1)}, f32[2,4,48,768]{3,2,1,0:T(8,128)S(1)}, u32[]{:S(2)}, u32[]{:S(2)}) collective-permute-start(f32[2,4,48,768]{3,2,1,0:T(8,128)S(1)} %get-tuple-element.42.refs_0_), channel_id=1, source_target_pairs={{0,4},{1,5},{2,6},{3,7},{4,8},{5,9},{6,10},{7,11},{8,12},{9,13},{1... | collective-permute-start | bytes 3538952 | tf_op jit(solution)/shard_map/ppermute | solution.py:238
  102.7 24.4 %collective-permute-start.18 = (f32[2,4,48,768]{3,2,1,0:T(8,128)S(1)}, f32[2,4,48,768]{3,2,1,0:T(8,128)S(1)}, u32[]{:S(2)}, u32[]{:S(2)}) collective-permute-start(f32[2,4,48,768]{3,2,1,0:T(8,128)S(1)} %get-tuple-element.43), channel_id=1, source_target_pairs={{0,4},{1,5},{2,6},{3,7},{4,8},{5,9},{6,10},{7,11},{8,12},{9,13},{1... | collective-permute-start | bytes 3538952 | tf_op jit(solution)/shard_map/ppermute | solution.py:238
  102.8 24.4 %collective-permute-start.19 = (f32[2,4,48,768]{3,2,1,0:T(8,128)S(1)}, f32[2,4,48,768]{3,2,1,0:T(8,128)S(1)}, u32[]{:S(2)}, u32[]{:S(2)}) collective-permute-start(f32[2,4,48,768]{3,2,1,0:T(8,128)S(1)} %get-tuple-element.44), channel_id=1, source_target_pairs={{0,12},{1,13},{2,14},{3,15},{4,0},{5,1},{6,2},{7,3},{8,4},{9,5},{1... | collective-permute-start | bytes 3538952 | tf_op jit(solution)/shard_map/ppermute | solution.py:238
  114.5 25.3 %copy-start = (f32[4,4,48,768]{3,2,1,0:T(8,128)S(1)}, f32[4,4,48,768]{3,2,1,0:T(8,128)}, u32[]{:S(2)}) copy-start(f32[4,4,48,768]{3,2,1,0:T(8,128)} %get-tuple-element.33.own) | copy-start | bytes 7077892
  115.3 24.4 %collective-permute-start.22 = (f32[2,4,48,768]{3,2,1,0:T(8,128)S(1)}, f32[2,4,48,768]{3,2,1,0:T(8,128)S(1)}, u32[]{:S(2)}, u32[]{:S(2)}) collective-permute-start(f32[2,4,48,768]{3,2,1,0:T(8,128)S(1)} %get-tuple-element.48), channel_id=1, source_target_pairs={{0,4},{1,5},{2,6},{3,7},{4,8},{5,9},{6,10},{7,11},{8,12},{9,13},{1... | collective-permute-start | bytes 3538952 | tf_op jit(solution)/shard_map/ppermute | solution.py:238
  115.8 24.0 %collective-permute-start.23 = (f32[2,4,48,768]{3,2,1,0:T(8,128)S(1)}, f32[2,4,48,768]{3,2,1,0:T(8,128)S(1)}, u32[]{:S(2)}, u32[]{:S(2)}) collective-permute-start(f32[2,4,48,768]{3,2,1,0:T(8,128)S(1)} %get-tuple-element.49), channel_id=1, source_target_pairs={{0,12},{1,13},{2,14},{3,15},{4,0},{5,1},{6,2},{7,3},{8,4},{9,5},{1... | collective-permute-start | bytes 3538952 | tf_op jit(solution)/shard_map/ppermute | solution.py:238
  118.6 46.4 %collective-permute-start.27 = (f32[2,4,48,768]{3,2,1,0:T(8,128)S(1)}, f32[2,4,48,768]{3,2,1,0:T(8,128)S(1)}, u32[]{:S(2)}, u32[]{:S(2)}) collective-permute-start(f32[2,4,48,768]{3,2,1,0:T(8,128)S(1)} %get-tuple-element.55), channel_id=1, source_target_pairs={{0,4},{1,5},{2,6},{3,7},{4,8},{5,9},{6,10},{7,11},{8,12},{9,13},{1... | collective-permute-start | bytes 3538952 | tf_op jit(solution)/shard_map/ppermute | solution.py:238
  127.1 37.9 %collective-permute-start.28 = (f32[2,4,48,768]{3,2,1,0:T(8,128)S(1)}, f32[2,4,48,768]{3,2,1,0:T(8,128)S(1)}, u32[]{:S(2)}, u32[]{:S(2)}) collective-permute-start(f32[2,4,48,768]{3,2,1,0:T(8,128)S(1)} %get-tuple-element.56), channel_id=1, source_target_pairs={{0,12},{1,13},{2,14},{3,15},{4,0},{5,1},{6,2},{7,3},{8,4},{9,5},{1... | collective-permute-start | bytes 3538952 | tf_op jit(solution)/shard_map/ppermute | solution.py:238
  141.5 27.9 %collective-permute-start.24 = (f32[4,48,768]{2,1,0:T(8,128)S(1)}, f32[4,48,768]{2,1,0:T(8,128)S(1)}, u32[]{:S(2)}, u32[]{:S(2)}) collective-permute-start(f32[4,48,768]{2,1,0:T(8,128)S(1)} %get-tuple-element.51), channel_id=1, source_target_pairs={{0,1},{1,2},{2,3},{3,0},{4,5},{5,6},{6,7},{7,4},{8,9},{9,10},{10,1... | collective-permute-start | bytes 1769480 | tf_op jit(solution)/shard_map/ppermute | solution.py:241
  142.0 29.1 %collective-permute-start.25 = (f32[4,48,768]{2,1,0:T(8,128)}, f32[4,48,768]{2,1,0:T(8,128)S(1)}, u32[]{:S(2)}, u32[]{:S(2)}) collective-permute-start(f32[4,48,768]{2,1,0:T(8,128)} %get-tuple-element.52), channel_id=1, source_target_pairs={{0,2},{1,3},{2,0},{3,1},{4,6},{5,7},{6,4},{7,5},{8,10},{9,11},{10,... | collective-permute-start | bytes 1769480 | tf_op jit(solution)/shard_map/ppermute | solution.py:241
  144.1 27.0 %collective-permute-start.26 = (f32[4,48,768]{2,1,0:T(8,128)}, f32[4,48,768]{2,1,0:T(8,128)S(1)}, u32[]{:S(2)}, u32[]{:S(2)}) collective-permute-start(f32[4,48,768]{2,1,0:T(8,128)} %get-tuple-element.53), channel_id=1, source_target_pairs={{0,3},{1,0},{2,1},{3,2},{4,7},{5,4},{6,5},{7,6},{8,11},{9,8},{10,9... | collective-permute-start | bytes 1769480 | tf_op jit(solution)/shard_map/ppermute | solution.py:241
  165.0 20.5 %copy-start.2 = (s32[8]{0:T(128)S(1)}, s32[8]{0:T(128)}, u32[]{:S(2)}) copy-start(s32[8]{0:T(128)} %sizes.5) | copy-start | bytes 100
  166.9 17.6 %collective-permute-start.29 = (f32[4,48,768]{2,1,0:T(8,128)}, f32[4,48,768]{2,1,0:T(8,128)S(1)}, u32[]{:S(2)}, u32[]{:S(2)}) collective-permute-start(f32[4,48,768]{2,1,0:T(8,128)} %get-tuple-element.58), channel_id=1, source_target_pairs={{0,1},{1,2},{2,3},{3,0},{4,5},{5,6},{6,7},{7,4},{8,9},{9,10},{10,1... | collective-permute-start | bytes 1769480 | tf_op jit(solution)/shard_map/ppermute | solution.py:241
  167.4 17.1 %collective-permute-start.30 = (f32[4,48,768]{2,1,0:T(8,128)}, f32[4,48,768]{2,1,0:T(8,128)}, u32[]{:S(2)}, u32[]{:S(2)}) collective-permute-start(f32[4,48,768]{2,1,0:T(8,128)} %get-tuple-element.59), channel_id=1, source_target_pairs={{0,2},{1,3},{2,0},{3,1},{4,6},{5,7},{6,4},{7,5},{8,10},{9,11},{10,... | collective-permute-start | bytes 1769480 | tf_op jit(solution)/shard_map/ppermute | solution.py:241
  169.4 16.1 %collective-permute-start.31 = (f32[4,48,768]{2,1,0:T(8,128)}, f32[4,48,768]{2,1,0:T(8,128)}, u32[]{:S(2)}, u32[]{:S(2)}) collective-permute-start(f32[4,48,768]{2,1,0:T(8,128)} %get-tuple-element.60), channel_id=1, source_target_pairs={{0,3},{1,0},{2,1},{3,2},{4,7},{5,4},{6,5},{7,6},{8,11},{9,8},{10,9... | collective-permute-start | bytes 1769480 | tf_op jit(solution)/shard_map/ppermute | solution.py:241

commit v15 on v14

--- a/solution.py
+++ b/solution.py
@@ -175,20 +175,38 @@
     )(own, n1, n2, p2, m2, *after)
 
 
+def sum_kernel(a, b, c, d, out):
+    out[...] = (a[...] + b[...]) + (c[...] + d[...])
+
+
+def add_parts(parts):
+    count, rows, cols = parts[0].shape
+    spec = pl.BlockSpec((1, rows, cols), lambda g: (g, 0, 0))
+    return pl.pallas_call(
+        sum_kernel,
+        grid=(count,),
+        in_specs=[spec] * 4,
+        out_specs=spec,
+        out_shape=jax.ShapeDtypeStruct(parts[0].shape, jnp.float32),
+        compiler_params=pltpu.CompilerParams(vmem_limit_bytes=VMEM),
+        cost_estimate=LIGHT,
+        name="add_parts",
+    )(*parts)
+
+
 def finish_kernel(sizes, origin, *refs):
     out = refs[-1]
     rows, irreps, cols = out.shape
     row = origin[0] + lax.broadcasted_iota(jnp.int32, (rows, cols), 0)
-    g = 0
-    for i in range(0, len(refs) - 1, 4):
-        a, b, c, d = refs[i : i + 4]
-        for k in range(a.shape[0]):
-            out[:, g, :] = jnp.where(row < sizes[g], (a[k] + b[k]) + (c[k] + d[k]), 0.0)
-            g += 1
-
-
-def finish(groups, row_sizes, origin, irreps):
-    parts = [part for group in groups for part in group]
+    summed, a, b, c, d = refs[:-1]
+    split = summed.shape[0]
+    for g in range(irreps):
+        k = g - split
+        total = summed[g] if k < 0 else (a[k] + b[k]) + (c[k] + d[k])
+        out[:, g, :] = jnp.where(row < sizes[g], total, 0.0)
+
+
+def finish(parts, row_sizes, origin, irreps):
     _, rows, cols = parts[0].shape
     return pl.pallas_call(
         finish_kernel,
@@ -261,7 +279,7 @@
     sums = across(add_own(own, *near, *handed, late_handed))
     late_sums = across(add_own(late_own, *late_near, *late_handed, []))
     origin = jnp.stack([ob * out_rows, vb * cols]).astype(jnp.int32)
-    return finish([sums, late_sums], row_sizes, origin, irreps)
+    return finish([add_parts(sums), *late_sums], row_sizes, origin, irreps)
 
 
 def solution(mesh):

time: 189 us -> 188 us (level)
  waiting for transfers between devices: 90.7 us -> 88.3 us
    ppermute x6, waiting for transfers between devices: 14.4 us -> 12 us  [across(): lax.ppermute(four[k], BOTH, FAR[d])]
    pallas_call x0 -> x1, Pallas kernels: none -> 2.23 us  [add_parts(): pl.pallas_call(sum_kernel, grid=(count,), in_specs=[spec] * 4, out_specs=...]
  transfers between devices with their start and end apart: 32 -> 32, of which waited for: 17 -> 17; matrix products, arithmetic and copies ran while one was open for 1% -> 1% of each run, Pallas kernels for 13% -> 15%
where the time goes in v15:
time: 188 us; the launch traced here: 187 us
  waiting for transfers between devices  88.3 us (47%)
  blocking collectives  33.8 us (18%)
  starting transfers between devices  31.2 us (17%)
  Pallas kernels  29.8 us (16%)
  local copies, waits for them, and re-layouts  3.98 us (2%)
    ppermute x12, waiting for transfers between devices, to_neighbours(): return (lax.ppermute(p, BOTH, NEAR[1]), lax.ppermute(m, BOTH, NEAR[-1]))  55.5 us
    all_to_all x2, blocking collectives, exchange(): part = lax.all_to_all(part, 'ob', split_axis=0, concat_axis=0, tiled=True)  33.8 us
    pallas_call x2, Pallas kernels, product(): pl.pallas_call(functools.partial(product_kernel, first), grid_spec=pltpu....  20.4 us
    ppermute x6, waiting for transfers between devices, along_z(): return [lax.ppermute(held, 'vb', steps) for steps in Z_STEPS]  18.8 us
    ppermute x6, waiting for transfers between devices, across(): lax.ppermute(four[k], BOTH, FAR[d])  12 us
    ppermute x12, starting transfers between devices, to_neighbours(): return (lax.ppermute(p, BOTH, NEAR[1]), lax.ppermute(m, BOTH, NEAR[-1]))  11.5 us
    ppermute x6, starting transfers between devices, along_z(): return [lax.ppermute(held, 'vb', steps) for steps in Z_STEPS]  9.71 us
    ppermute x6, starting transfers between devices, across(): lax.ppermute(four[k], BOTH, FAR[d])  8.34 us
  transfers between devices with their start and end apart: 32, of which 17 were waited for; matrix products, arithmetic and copies ran while one was open for 1% of the time, Pallas kernels for 15%

profile of v15, /device:TPU:0, one launch (start us, length us, event | category | flops | bytes accessed | tf_op | source)
XLA Modules:
  0.0 187.4 jit_solution(10231245428211176733)
XLA Ops:
  0.0 1.9 fusion
  2.4 19.1 %all_to_all.10 = f32[16,24,384]{2,1,0:T(8,128)S(1)} all-to-all(f32[16,24,384]{2,1,0:T(8,128)S(1)} %copy.10), channel_id=1, replica_groups=mesh['vb'=8,'ob'=16] {'ob'}, dimensions={0} | all-to-all | bytes 1179648 | tf_op jit(solution)/shard_map/all_to_all | solution.py:240
  21.7 4.0 %collective-permute-start.5 = (f32[4,96,384]{2,1,0:T(8,128)S(1)}, f32[4,96,384]{2,1,0:T(8,128)S(1)}, u32[]{:S(2)}, u32[]{:S(2)}) collective-permute-start(f32[4,96,384]{2,1,0:T(8,128)S(1)} %bitcast.21), channel_id=1, source_target_pairs={{0,64},{16,80},{32,96},{48,112},{64,0},{80,16},{96,32},{112,48},{1... | collective-permute-start | bytes 1769480 | tf_op jit(solution)/shard_map/ppermute | solution.py:249
  25.7 0.7 collective-permute-start.3
  26.4 1.3 collective-permute-start.1
  28.2 14.7 %all_to_all.11 = f32[16,24,384]{2,1,0:T(8,128)S(1)} all-to-all(f32[16,24,384]{2,1,0:T(8,128)S(1)} %copy.12), channel_id=1, replica_groups=mesh['vb'=8,'ob'=16] {'ob'}, dimensions={0} | all-to-all | bytes 1179648 | tf_op jit(solution)/shard_map/all_to_all | solution.py:240
  43.2 0.5 collective-permute-start
  43.8 7.1 %collective-permute-done.3.refs_4_.refs_2_ = f32[4,96,384]{2,1,0:T(8,128)S(1)} collective-permute-done((f32[4,96,384]{2,1,0:T(8,128)S(1)}, f32[4,96,384]{2,1,0:T(8,128)S(1)}, u32[]{:S(2)}, u32[]{:S(2)}) %collective-permute-start.3) | collective-permute-done | bytes 589856 | tf_op jit(solution)/shard_map/ppermute | solution.py:249
  50.9 0.5 collective-permute-start.2
  51.5 0.7 dynamic-slice_bitcast_fusion.place
  52.2 1.7 collective-permute-start.14
  53.9 1.7 collective-permute-start.13
  55.6 11.4 %product.2 = (f32[2,4,48,768]{3,2,1,0:T(8,128)S(1)}, f32[2,4,48,768]{3,2,1,0:T(8,128)S(1)}, f32[2,4,48,768]{3,2,1,0:T(8,128)S(1)}, f32[2,4,48,768]{3,2,1,0:T(8,1...) custom-call(s32[16]{0:T(128)S(1)} %dynamic-slice_bitcast_fusion.place, ...), custom_call_target="tpu_custom_call" | custom-call | tf_op jit(solution)/shard_map/product/pallas_call | solution.py:91
  67.0 1.2 collective-permute-start.11
  68.3 0.8 collective-permute-start.10
  69.1 0.4 collective-permute-start.12
  69.5 0.6 collective-permute-done.14.refs_1_
  70.1 9.9 %collective-permute-done.13.refs_0_ = f32[4,96,384]{2,1,0:T(8,128)S(1)} collective-permute-done((f32[4,96,384]{2,1,0:T(8,128)S(1)}, f32[4,96,384]{2,1,0:T(8,128)S(1)}, u32[]{:S(2)}, u32[]{:S(2)}) %collective-permute-start.13) | collective-permute-done | bytes 589856 | tf_op jit(solution)/shard_map/ppermute | solution.py:249
  79.9 0.5 collective-permute-start.17
  80.4 1.3 collective-permute-done.12.refs_0_
  81.7 0.7 collective-permute-start.8
  82.4 0.9 collective-permute-done.11.refs_2_.recv_m
  83.3 2.4 %collective-permute-done.10.refs_1_.recv_p = f32[2,4,48,768]{3,2,1,0:T(8,128)S(1)} collective-permute-done((f32[2,4,48,768]{3,2,1,0:T(8,128)S(1)}, f32[2,4,48,768]{3,2,1,0:T(8,128)S(1)}, u32[]{:S(2)}, u32[]{:S(2)}) %collective-permute-start.10) | collective-permute-done | bytes 1179680 | tf_op jit(solution)/shard_map/ppermute | solution.py:256
  85.8 1.9 %collective-permute-done.16.refs_3_ = f32[4,96,384]{2,1,0:T(8,128)S(1)} collective-permute-done((f32[4,96,384]{2,1,0:T(8,128)S(1)}, f32[4,96,384]{2,1,0:T(8,128)S(1)}, u32[]{:S(2)}, u32[]{:S(2)}) %collective-permute-start.16) | collective-permute-done | bytes 589856 | tf_op jit(solution)/shard_map/ppermute | solution.py:246
  87.7 9.0 %product.3 = (f32[2,4,48,768]{3,2,1,0:T(8,128)S(1)}, f32[2,4,48,768]{3,2,1,0:T(8,128)S(1)}, f32[2,4,48,768]{3,2,1,0:T(8,128)S(1)}, f32[2,4,48,768]{3,2,1,0:T(8,1...) custom-call(s32[16]{0:T(128)S(1)} %dynamic-slice_bitcast_fusion.place, ...), custom_call_target="tpu_custom_call" | custom-call | tf_op jit(solution)/shard_map/product/pallas_call | solution.py:91
  96.8 2.0 %collective-permute-start.20 = (f32[2,4,48,768]{3,2,1,0:T(8,128)S(1)}, f32[2,4,48,768]{3,2,1,0:T(8,128)S(1)}, u32[]{:S(2)}, u32[]{:S(2)}) collective-permute-start(f32[2,4,48,768]{3,2,1,0:T(8,128)S(1)} %get-tuple-element.42.refs_0_), channel_id=1, source_target_pairs={{0,4},{1,5},{2,6},{3,7},{4,8},{5,9},{6,10},{7,11},{8,12},{9,13},{1... | collective-permute-start | bytes 3538952 | tf_op jit(solution)/shard_map/ppermute | solution.py:256
  99.1 2.8 %collective-permute-done.9.refs_2_.n2 = f32[2,4,48,768]{3,2,1,0:T(8,128)S(1)} collective-permute-done((f32[2,4,48,768]{3,2,1,0:T(8,128)S(1)}, f32[2,4,48,768]{3,2,1,0:T(8,128)S(1)}, u32[]{:S(2)}, u32[]{:S(2)}) %collective-permute-start.9) | collective-permute-done | bytes 1179680 | tf_op jit(solution)/shard_map/ppermute | solution.py:256
  101.9 0.8 add_far.2
  102.8 3.2 %collective-permute-start.19 = (f32[2,4,48,768]{3,2,1,0:T(8,128)S(1)}, f32[2,4,48,768]{3,2,1,0:T(8,128)S(1)}, u32[]{:S(2)}, u32[]{:S(2)}) collective-permute-start(f32[2,4,48,768]{3,2,1,0:T(8,128)S(1)} %get-tuple-element.44), channel_id=1, source_target_pairs={{0,12},{1,13},{2,14},{3,15},{4,0},{5,1},{6,2},{7,3},{8,4},{9,5},{1... | collective-permute-start | bytes 3538952 | tf_op jit(solution)/shard_map/ppermute | solution.py:256
  106.0 8.6 %collective-permute-done.21.recv_m = f32[2,4,48,768]{3,2,1,0:T(8,128)S(1)} collective-permute-done((f32[2,4,48,768]{3,2,1,0:T(8,128)S(1)}, f32[2,4,48,768]{3,2,1,0:T(8,128)S(1)}, u32[]{:S(2)}, u32[]{:S(2)}) %collective-permute-start.21) | collective-permute-done | bytes 1179680 | tf_op jit(solution)/shard_map/ppermute | solution.py:256
  114.5 0.8 add_far.3
  115.3 0.5 collective-permute-start.22
  115.8 2.8 %collective-permute-start.23 = (f32[2,4,48,768]{3,2,1,0:T(8,128)S(1)}, f32[2,4,48,768]{3,2,1,0:T(8,128)S(1)}, u32[]{:S(2)}, u32[]{:S(2)}) collective-permute-start(f32[2,4,48,768]{3,2,1,0:T(8,128)S(1)} %get-tuple-element.49), channel_id=1, source_target_pairs={{0,12},{1,13},{2,14},{3,15},{4,0},{5,1},{6,2},{7,3},{8,4},{9,5},{1... | collective-permute-start | bytes 3538952 | tf_op jit(solution)/shard_map/ppermute | solution.py:256
  118.6 8.4 %collective-permute-done.18.p2 = f32[2,4,48,768]{3,2,1,0:T(8,128)S(1)} collective-permute-done((f32[2,4,48,768]{3,2,1,0:T(8,128)S(1)}, f32[2,4,48,768]{3,2,1,0:T(8,128)S(1)}, u32[]{:S(2)}, u32[]{:S(2)}) %collective-permute-start.18) | collective-permute-done | bytes 1179680 | tf_op jit(solution)/shard_map/ppermute | solution.py:256
  127.2 12.5 %collective-permute-done.22.refs_0_.p2 = f32[2,4,48,768]{3,2,1,0:T(8,128)S(1)} collective-permute-done((f32[2,4,48,768]{3,2,1,0:T(8,128)S(1)}, f32[2,4,48,768]{3,2,1,0:T(8,128)S(1)}, u32[]{:S(2)}, u32[]{:S(2)}) %collective-permute-start.22) | collective-permute-done | bytes 1179680 | tf_op jit(solution)/shard_map/ppermute | solution.py:256
  139.8 1.7 add_own.2
  141.5 0.5 collective-permute-start.24
  142.0 2.1 %collective-permute-start.25 = (f32[4,48,768]{2,1,0:T(8,128)}, f32[4,48,768]{2,1,0:T(8,128)}, u32[]{:S(2)}, u32[]{:S(2)}) collective-permute-start(f32[4,48,768]{2,1,0:T(8,128)} %get-tuple-element.52), channel_id=1, source_target_pairs={{0,2},{1,3},{2,0},{3,1},{4,6},{5,7},{6,4},{7,5},{8,10},{9,11},{10,... | collective-permute-start | bytes 1769480 | tf_op jit(solution)/shard_map/ppermute | solution.py:259
  144.1 1.5 collective-permute-start.26
  145.6 19.3 %collective-permute-done.27.n1 = f32[2,4,48,768]{3,2,1,0:T(8,128)S(1)} collective-permute-done((f32[2,4,48,768]{3,2,1,0:T(8,128)S(1)}, f32[2,4,48,768]{3,2,1,0:T(8,128)S(1)}, u32[]{:S(2)}, u32[]{:S(2)}) %collective-permute-start.27) | collective-permute-done | bytes 1179680 | tf_op jit(solution)/shard_map/ppermute | solution.py:256
  165.0 1.9 add_own.3
  166.9 0.5 collective-permute-start.29
  167.4 2.0 %collective-permute-start.30 = (f32[4,48,768]{2,1,0:T(8,128)}, f32[4,48,768]{2,1,0:T(8,128)S(1)}, u32[]{:S(2)}, u32[]{:S(2)}) collective-permute-start(f32[4,48,768]{2,1,0:T(8,128)} %get-tuple-element.59), channel_id=1, source_target_pairs={{0,2},{1,3},{2,0},{3,1},{4,6},{5,7},{6,4},{7,5},{8,10},{9,11},{10,... | collective-permute-start | bytes 1769480 | tf_op jit(solution)/shard_map/ppermute | solution.py:259
  169.3 1.7 collective-permute-start.31
  171.1 2.2 %add_parts.1.refs_0_ = f32[4,48,768]{2,1,0:T(8,128)S(1)} custom-call(f32[4,48,768]{2,1,0:T(8,128)S(1)} %get-tuple-element.50.a, f32[4,48,768]{2,1,0:T(8,128)S(1)} %collective-permute-done.24.b, f32[4,48,768]{2,1,0:T(8,128)} %collective-permute-done.25.c, f32[4,48,768]{2,1,0:T(8,128)} %collective-permute-done.26.d), custom_call_target="tpu_custom_call" | custom-call | tf_op jit(solution)/shard_map/add_parts/pallas_call | solution.py:185
  173.4 11.1 %collective-permute-done.29.refs_2_ = f32[4,48,768]{2,1,0:T(8,128)S(1)} collective-permute-done((f32[4,48,768]{2,1,0:T(8,128)}, f32[4,48,768]{2,1,0:T(8,128)S(1)}, u32[]{:S(2)}, u32[]{:S(2)}) %collective-permute-start.29) | collective-permute-done | bytes 589856 | tf_op jit(solution)/shard_map/ppermute | solution.py:259
  184.5 0.9 collective-permute-done.31.refs_4_
  185.4 2.0 %finish.1 = f32[48,8,768]{2,1,0:T(8,128)} custom-call(s32[8]{0:T(128)S(1)} %copy-done.2, s32[2]{0:T(128)S(1)} %pad_add_fusion.origin, f32[4,48,768]{2,1,0:T(8,128)S(1)} %add_parts.1.refs_0_, f32[4,48,768]{2,1,0:T(8,128)S(1)} %get-tuple-element.57.refs_1_, f32[4,48,768]{2,1,0:T(8,128)S(1)} %collective-permute-done.29.refs_2_, ...), custom_call_target="tpu_custom_call" | custom-call | tf_op jit(solution)/shard_map/finish/pallas_call | solution.py:211
  (54 shorter events, 2.6 us)
Async XLA Ops:
  21.7 22.0 %collective-permute-start.5 = (f32[4,96,384]{2,1,0:T(8,128)S(1)}, f32[4,96,384]{2,1,0:T(8,128)S(1)}, u32[]{:S(2)}, u32[]{:S(2)}) collective-permute-start(f32[4,96,384]{2,1,0:T(8,128)S(1)} %bitcast.21), channel_id=1, source_target_pairs={{0,64},{16,80},{32,96},{48,112},{64,0},{80,16},{96,32},{112,48},{1... | collective-permute-start | bytes 1769480 | tf_op jit(solution)/shard_map/ppermute | solution.py:249
  25.7 25.2 %collective-permute-start.3 = (f32[4,96,384]{2,1,0:T(8,128)S(1)}, f32[4,96,384]{2,1,0:T(8,128)S(1)}, u32[]{:S(2)}, u32[]{:S(2)}) collective-permute-start(f32[4,96,384]{2,1,0:T(8,128)S(1)} %bitcast.22), channel_id=1, source_target_pairs={{0,96},{16,48},{32,0},{48,80},{64,32},{80,112},{96,64},{112,16},{1... | collective-permute-start | bytes 1769480 | tf_op jit(solution)/shard_map/ppermute | solution.py:249
  26.4 24.5 %collective-permute-start.1 = (f32[4,96,384]{2,1,0:T(8,128)S(1)}, f32[4,96,384]{2,1,0:T(8,128)}, u32[]{:S(2)}, u32[]{:S(2)}) collective-permute-start(f32[4,96,384]{2,1,0:T(8,128)S(1)} %bitcast.23), channel_id=1, source_target_pairs={{0,32},{16,112},{32,64},{48,16},{64,96},{80,48},{96,0},{112,80},{1... | collective-permute-start | bytes 1769480 | tf_op jit(solution)/shard_map/ppermute | solution.py:249
  43.1 9.1 %collective-permute-start.7 = (f32[4,96,384]{2,1,0:T(8,128)S(1)}, f32[4,96,384]{2,1,0:T(8,128)S(1)}, u32[]{:S(2)}, u32[]{:S(2)}) collective-permute-start(f32[4,96,384]{2,1,0:T(8,128)S(1)} %bitcast.19), channel_id=1, source_target_pairs={{0,16},{16,0},{32,48},{48,32},{64,80},{80,64},{96,112},{112,96},{1... | collective-permute-start | bytes 1769480 | tf_op jit(solution)/shard_map/ppermute | solution.py:246
  43.2 10.7 %collective-permute-start = (f32[4,96,384]{2,1,0:T(8,128)S(1)}, f32[4,96,384]{2,1,0:T(8,128)}, u32[]{:S(2)}, u32[]{:S(2)}) collective-permute-start(f32[4,96,384]{2,1,0:T(8,128)S(1)} %bitcast.24), channel_id=1, source_target_pairs={{0,16},{16,0},{32,48},{48,32},{64,80},{80,64},{96,112},{112,96},{1... | collective-permute-start | bytes 1769480 | tf_op jit(solution)/shard_map/ppermute | solution.py:246
  43.7 11.9 %collective-permute-start.6 = (f32[4,96,384]{2,1,0:T(8,128)S(1)}, f32[4,96,384]{2,1,0:T(8,128)}, u32[]{:S(2)}, u32[]{:S(2)}) collective-permute-start(f32[4,96,384]{2,1,0:T(8,128)S(1)} %collective-permute-done.5.refs_6_.refs_3_), channel_id=1, source_target_pairs={{0,16},{16,0},{32,48},{48,32},{64,80},{80,64},{96,112},{112,96},{1... | collective-permute-start | bytes 1769480 | tf_op jit(solution)/shard_map/ppermute | solution.py:246
  50.9 4.7 %collective-permute-start.4 = (f32[4,96,384]{2,1,0:T(8,128)S(1)}, f32[4,96,384]{2,1,0:T(8,128)}, u32[]{:S(2)}, u32[]{:S(2)}) collective-permute-start(f32[4,96,384]{2,1,0:T(8,128)S(1)} %collective-permute-done.3.refs_4_.refs_2_), channel_id=1, source_target_pairs={{0,16},{16,0},{32,48},{48,32},{64,80},{80,64},{96,112},{112,96},{1... | collective-permute-start | bytes 1769480 | tf_op jit(solution)/shard_map/ppermute | solution.py:246
  50.9 4.7 %collective-permute-start.2 = (f32[4,96,384]{2,1,0:T(8,128)}, f32[4,96,384]{2,1,0:T(8,128)}, u32[]{:S(2)}, u32[]{:S(2)}) collective-permute-start(f32[4,96,384]{2,1,0:T(8,128)} %collective-permute-done.1.refs_2_.refs_1_), channel_id=1, source_target_pairs={{0,16},{16,0},{32,48},{48,32},{64,80},{80,64},{96,112},{112,96},{1... | collective-permute-start | bytes 1769480 | tf_op jit(solution)/shard_map/ppermute | solution.py:246
  52.2 3.4 %copy-start.1 = (s32[8]{0:T(128)S(1)}, s32[8]{0:T(128)}, u32[]{:S(2)}) copy-start(s32[8]{0:T(128)} %sizes.4) | copy-start | bytes 100
  52.2 35.5 %slice-start = ((s8[9437184]{0:T(1024)(128)(4,1)}), s8[4194304]{0:T(1024)(128)(4,1)S(1)}, s32[]{:S(2)}) async-start(s8[9437184]{0:T(1024)(128)(4,1)} %bitcast.17), calls=%async_computation.2 | async-start | bytes 8388608
  52.2 35.5 %slice-start.1 = ((s8[9437184]{0:T(1024)(128)(4,1)}), s8[4194304]{0:T(1024)(128)(4,1)S(1)}, s32[]{:S(2)}) async-start(s8[9437184]{0:T(1024)(128)(4,1)} %bitcast.17), calls=%async_computation.3 | async-start | bytes 8388608
  52.2 35.5 %slice-start.2 = ((s8[9437184]{0:T(1024)(128)(4,1)}), s8[1048576]{0:T(1024)(128)(4,1)S(1)}, s32[]{:S(2)}) async-start(s8[9437184]{0:T(1024)(128)(4,1)} %bitcast.17), calls=%async_computation.4 | async-start | bytes 2097152
  52.2 17.8 %collective-permute-start.14 = (f32[4,96,384]{2,1,0:T(8,128)S(1)}, f32[4,96,384]{2,1,0:T(8,128)S(1)}, u32[]{:S(2)}, u32[]{:S(2)}) collective-permute-start(f32[4,96,384]{2,1,0:T(8,128)S(1)} %tie.3.refs_0_), channel_id=1, source_target_pairs={{0,64},{16,80},{32,96},{48,112},{64,0},{80,16},{96,32},{112,48},{1... | collective-permute-start | bytes 1769480 | tf_op jit(solution)/shard_map/ppermute | solution.py:249
  53.9 26.0 %collective-permute-start.13 = (f32[4,96,384]{2,1,0:T(8,128)S(1)}, f32[4,96,384]{2,1,0:T(8,128)S(1)}, u32[]{:S(2)}, u32[]{:S(2)}) collective-permute-start(f32[4,96,384]{2,1,0:T(8,128)S(1)} %tie.3.refs_0_), channel_id=1, source_target_pairs={{0,96},{16,48},{32,0},{48,80},{64,32},{80,112},{96,64},{112,16},{1... | collective-permute-start | bytes 1769480 | tf_op jit(solution)/shard_map/ppermute | solution.py:249
  67.0 16.2 %collective-permute-start.11 = (f32[2,4,48,768]{3,2,1,0:T(8,128)S(1)}, f32[2,4,48,768]{3,2,1,0:T(8,128)S(1)}, u32[]{:S(2)}, u32[]{:S(2)}) collective-permute-start(f32[2,4,48,768]{3,2,1,0:T(8,128)S(1)} %get-tuple-element.39), channel_id=1, source_target_pairs={{0,12},{1,13},{2,14},{3,15},{4,0},{5,1},{6,2},{7,3},{8,4},{9,5},{1... | collective-permute-start | bytes 3538952 | tf_op jit(solution)/shard_map/ppermute | solution.py:256
  68.3 17.4 %collective-permute-start.10 = (f32[2,4,48,768]{3,2,1,0:T(8,128)S(1)}, f32[2,4,48,768]{3,2,1,0:T(8,128)S(1)}, u32[]{:S(2)}, u32[]{:S(2)}) collective-permute-start(f32[2,4,48,768]{3,2,1,0:T(8,128)S(1)} %get-tuple-element.38.refs_2_), channel_id=1, source_target_pairs={{0,4},{1,5},{2,6},{3,7},{4,8},{5,9},{6,10},{7,11},{8,12},{9,13},{1... | collective-permute-start | bytes 3538952 | tf_op jit(solution)/shard_map/ppermute | solution.py:256
  69.1 12.6 %collective-permute-start.12 = (f32[4,96,384]{2,1,0:T(8,128)S(1)}, f32[4,96,384]{2,1,0:T(8,128)S(1)}, u32[]{:S(2)}, u32[]{:S(2)}) collective-permute-start(f32[4,96,384]{2,1,0:T(8,128)S(1)} %tie.3.refs_0_), channel_id=1, source_target_pairs={{0,32},{16,112},{32,64},{48,16},{64,96},{80,48},{96,0},{112,80},{1... | collective-permute-start | bytes 1769480 | tf_op jit(solution)/shard_map/ppermute | solution.py:249
  79.9 2.4 %collective-permute-start.15 = (f32[4,96,384]{2,1,0:T(8,128)S(1)}, f32[4,96,384]{2,1,0:T(8,128)S(1)}, u32[]{:S(2)}, u32[]{:S(2)}) collective-permute-start(f32[4,96,384]{2,1,0:T(8,128)S(1)} %get-tuple-element.40.refs_4_), channel_id=1, source_target_pairs={{0,16},{16,0},{32,48},{48,32},{64,80},{80,64},{96,112},{112,96},{1... | collective-permute-start | bytes 1769480 | tf_op jit(solution)/shard_map/ppermute | solution.py:246
  79.9 5.8 %collective-permute-start.17 = (f32[4,96,384]{2,1,0:T(8,128)S(1)}, f32[4,96,384]{2,1,0:T(8,128)S(1)}, u32[]{:S(2)}, u32[]{:S(2)}) collective-permute-start(f32[4,96,384]{2,1,0:T(8,128)S(1)} %get-tuple-element.41.refs_6_), channel_id=1, source_target_pairs={{0,16},{16,0},{32,48},{48,32},{64,80},{80,64},{96,112},{112,96},{1... | collective-permute-start | bytes 1769480 | tf_op jit(solution)/shard_map/ppermute | solution.py:246
  81.7 17.4 %collective-permute-start.8 = (f32[2,4,48,768]{3,2,1,0:T(8,128)S(1)}, f32[2,4,48,768]{3,2,1,0:T(8,128)S(1)}, u32[]{:S(2)}, u32[]{:S(2)}) collective-permute-start(f32[2,4,48,768]{3,2,1,0:T(8,128)S(1)} %get-tuple-element.34), channel_id=1, source_target_pairs={{0,4},{1,5},{2,6},{3,7},{4,8},{5,9},{6,10},{7,11},{8,12},{9,13},{1... | collective-permute-start | bytes 3538952 | tf_op jit(solution)/shard_map/ppermute | solution.py:256
  85.7 2.0 %collective-permute-start.16 = (f32[4,96,384]{2,1,0:T(8,128)S(1)}, f32[4,96,384]{2,1,0:T(8,128)S(1)}, u32[]{:S(2)}, u32[]{:S(2)}) collective-permute-start(f32[4,96,384]{2,1,0:T(8,128)S(1)} %tie.5.refs_2_), channel_id=1, source_target_pairs={{0,16},{16,0},{32,48},{48,32},{64,80},{80,64},{96,112},{112,96},{1... | collective-permute-start | bytes 1769480 | tf_op jit(solution)/shard_map/ppermute | solution.py:246
  85.7 16.2 %collective-permute-start.9 = (f32[2,4,48,768]{3,2,1,0:T(8,128)S(1)}, f32[2,4,48,768]{3,2,1,0:T(8,128)S(1)}, u32[]{:S(2)}, u32[]{:S(2)}) collective-permute-start(f32[2,4,48,768]{3,2,1,0:T(8,128)S(1)} %get-tuple-element.35), channel_id=1, source_target_pairs={{0,12},{1,13},{2,14},{3,15},{4,0},{5,1},{6,2},{7,3},{8,4},{9,5},{1... | collective-permute-start | bytes 3538952 | tf_op jit(solution)/shard_map/ppermute | solution.py:256
  96.7 17.8 %collective-permute-start.21 = (f32[2,4,48,768]{3,2,1,0:T(8,128)S(1)}, f32[2,4,48,768]{3,2,1,0:T(8,128)S(1)}, u32[]{:S(2)}, u32[]{:S(2)}) collective-permute-start(f32[2,4,48,768]{3,2,1,0:T(8,128)S(1)} %get-tuple-element.47), channel_id=1, source_target_pairs={{0,12},{1,13},{2,14},{3,15},{4,0},{5,1},{6,2},{7,3},{8,4},{9,5},{1... | collective-permute-start | bytes 3538952 | tf_op jit(solution)/shard_map/ppermute | solution.py:256
  96.8 17.7 %collective-permute-start.20 = (f32[2,4,48,768]{3,2,1,0:T(8,128)S(1)}, f32[2,4,48,768]{3,2,1,0:T(8,128)S(1)}, u32[]{:S(2)}, u32[]{:S(2)}) collective-permute-start(f32[2,4,48,768]{3,2,1,0:T(8,128)S(1)} %get-tuple-element.42.refs_0_), channel_id=1, source_target_pairs={{0,4},{1,5},{2,6},{3,7},{4,8},{5,9},{6,10},{7,11},{8,12},{9,13},{1... | collective-permute-start | bytes 3538952 | tf_op jit(solution)/shard_map/ppermute | solution.py:256
  102.7 24.4 %collective-permute-start.18 = (f32[2,4,48,768]{3,2,1,0:T(8,128)S(1)}, f32[2,4,48,768]{3,2,1,0:T(8,128)S(1)}, u32[]{:S(2)}, u32[]{:S(2)}) collective-permute-start(f32[2,4,48,768]{3,2,1,0:T(8,128)S(1)} %get-tuple-element.43), channel_id=1, source_target_pairs={{0,4},{1,5},{2,6},{3,7},{4,8},{5,9},{6,10},{7,11},{8,12},{9,13},{1... | collective-permute-start | bytes 3538952 | tf_op jit(solution)/shard_map/ppermute | solution.py:256
  102.8 24.4 %collective-permute-start.19 = (f32[2,4,48,768]{3,2,1,0:T(8,128)S(1)}, f32[2,4,48,768]{3,2,1,0:T(8,128)S(1)}, u32[]{:S(2)}, u32[]{:S(2)}) collective-permute-start(f32[2,4,48,768]{3,2,1,0:T(8,128)S(1)} %get-tuple-element.44), channel_id=1, source_target_pairs={{0,12},{1,13},{2,14},{3,15},{4,0},{5,1},{6,2},{7,3},{8,4},{9,5},{1... | collective-permute-start | bytes 3538952 | tf_op jit(solution)/shard_map/ppermute | solution.py:256
  114.5 25.3 %copy-start = (f32[4,4,48,768]{3,2,1,0:T(8,128)S(1)}, f32[4,4,48,768]{3,2,1,0:T(8,128)}, u32[]{:S(2)}) copy-start(f32[4,4,48,768]{3,2,1,0:T(8,128)} %get-tuple-element.33.own) | copy-start | bytes 7077892
  115.3 24.4 %collective-permute-start.22 = (f32[2,4,48,768]{3,2,1,0:T(8,128)S(1)}, f32[2,4,48,768]{3,2,1,0:T(8,128)S(1)}, u32[]{:S(2)}, u32[]{:S(2)}) collective-permute-start(f32[2,4,48,768]{3,2,1,0:T(8,128)S(1)} %get-tuple-element.48), channel_id=1, source_target_pairs={{0,4},{1,5},{2,6},{3,7},{4,8},{5,9},{6,10},{7,11},{8,12},{9,13},{1... | collective-permute-start | bytes 3538952 | tf_op jit(solution)/shard_map/ppermute | solution.py:256
  115.8 24.0 %collective-permute-start.23 = (f32[2,4,48,768]{3,2,1,0:T(8,128)S(1)}, f32[2,4,48,768]{3,2,1,0:T(8,128)S(1)}, u32[]{:S(2)}, u32[]{:S(2)}) collective-permute-start(f32[2,4,48,768]{3,2,1,0:T(8,128)S(1)} %get-tuple-element.49), channel_id=1, source_target_pairs={{0,12},{1,13},{2,14},{3,15},{4,0},{5,1},{6,2},{7,3},{8,4},{9,5},{1... | collective-permute-start | bytes 3538952 | tf_op jit(solution)/shard_map/ppermute | solution.py:256
  118.6 46.4 %collective-permute-start.27 = (f32[2,4,48,768]{3,2,1,0:T(8,128)S(1)}, f32[2,4,48,768]{3,2,1,0:T(8,128)S(1)}, u32[]{:S(2)}, u32[]{:S(2)}) collective-permute-start(f32[2,4,48,768]{3,2,1,0:T(8,128)S(1)} %get-tuple-element.55), channel_id=1, source_target_pairs={{0,4},{1,5},{2,6},{3,7},{4,8},{5,9},{6,10},{7,11},{8,12},{9,13},{1... | collective-permute-start | bytes 3538952 | tf_op jit(solution)/shard_map/ppermute | solution.py:256
  127.1 37.9 %collective-permute-start.28 = (f32[2,4,48,768]{3,2,1,0:T(8,128)S(1)}, f32[2,4,48,768]{3,2,1,0:T(8,128)S(1)}, u32[]{:S(2)}, u32[]{:S(2)}) collective-permute-start(f32[2,4,48,768]{3,2,1,0:T(8,128)S(1)} %get-tuple-element.56), channel_id=1, source_target_pairs={{0,12},{1,13},{2,14},{3,15},{4,0},{5,1},{6,2},{7,3},{8,4},{9,5},{1... | collective-permute-start | bytes 3538952 | tf_op jit(solution)/shard_map/ppermute | solution.py:256
  141.5 27.9 %collective-permute-start.24 = (f32[4,48,768]{2,1,0:T(8,128)S(1)}, f32[4,48,768]{2,1,0:T(8,128)S(1)}, u32[]{:S(2)}, u32[]{:S(2)}) collective-permute-start(f32[4,48,768]{2,1,0:T(8,128)S(1)} %get-tuple-element.51), channel_id=1, source_target_pairs={{0,1},{1,2},{2,3},{3,0},{4,5},{5,6},{6,7},{7,4},{8,9},{9,10},{10,1... | collective-permute-start | bytes 1769480 | tf_op jit(solution)/shard_map/ppermute | solution.py:259
  142.0 29.1 %collective-permute-start.25 = (f32[4,48,768]{2,1,0:T(8,128)}, f32[4,48,768]{2,1,0:T(8,128)}, u32[]{:S(2)}, u32[]{:S(2)}) collective-permute-start(f32[4,48,768]{2,1,0:T(8,128)} %get-tuple-element.52), channel_id=1, source_target_pairs={{0,2},{1,3},{2,0},{3,1},{4,6},{5,7},{6,4},{7,5},{8,10},{9,11},{10,... | collective-permute-start | bytes 1769480 | tf_op jit(solution)/shard_map/ppermute | solution.py:259
  144.1 27.0 %collective-permute-start.26 = (f32[4,48,768]{2,1,0:T(8,128)}, f32[4,48,768]{2,1,0:T(8,128)}, u32[]{:S(2)}, u32[]{:S(2)}) collective-permute-start(f32[4,48,768]{2,1,0:T(8,128)} %get-tuple-element.53), channel_id=1, source_target_pairs={{0,3},{1,0},{2,1},{3,2},{4,7},{5,4},{6,5},{7,6},{8,11},{9,8},{10,9... | collective-permute-start | bytes 1769480 | tf_op jit(solution)/shard_map/ppermute | solution.py:259
  166.9 17.6 %collective-permute-start.29 = (f32[4,48,768]{2,1,0:T(8,128)}, f32[4,48,768]{2,1,0:T(8,128)S(1)}, u32[]{:S(2)}, u32[]{:S(2)}) collective-permute-start(f32[4,48,768]{2,1,0:T(8,128)} %get-tuple-element.58), channel_id=1, source_target_pairs={{0,1},{1,2},{2,3},{3,0},{4,5},{5,6},{6,7},{7,4},{8,9},{9,10},{10,1... | collective-permute-start | bytes 1769480 | tf_op jit(solution)/shard_map/ppermute | solution.py:259
  167.4 17.1 %collective-permute-start.30 = (f32[4,48,768]{2,1,0:T(8,128)}, f32[4,48,768]{2,1,0:T(8,128)S(1)}, u32[]{:S(2)}, u32[]{:S(2)}) collective-permute-start(f32[4,48,768]{2,1,0:T(8,128)} %get-tuple-element.59), channel_id=1, source_target_pairs={{0,2},{1,3},{2,0},{3,1},{4,6},{5,7},{6,4},{7,5},{8,10},{9,11},{10,... | collective-permute-start | bytes 1769480 | tf_op jit(solution)/shard_map/ppermute | solution.py:259
  169.3 16.0 %collective-permute-start.31 = (f32[4,48,768]{2,1,0:T(8,128)}, f32[4,48,768]{2,1,0:T(8,128)S(1)}, u32[]{:S(2)}, u32[]{:S(2)}) collective-permute-start(f32[4,48,768]{2,1,0:T(8,128)} %get-tuple-element.60), channel_id=1, source_target_pairs={{0,3},{1,0},{2,1},{3,2},{4,7},{5,4},{6,5},{7,6},{8,11},{9,8},{10,9... | collective-permute-start | bytes 1769480 | tf_op jit(solution)/shard_map/ppermute | solution.py:259
  171.1 14.3 %copy-start.2 = (s32[8]{0:T(128)S(1)}, s32[8]{0:T(128)}, u32[]{:S(2)}) copy-start(s32[8]{0:T(128)} %sizes.5) | copy-start | bytes 100

commit v16 on v15

--- a/solution.py
+++ b/solution.py
@@ -175,6 +175,55 @@
     )(own, n1, n2, p2, m2, *after)
 
 
+def early_kernel(own, p2, m2, out):
+    out[0:2] = own[0:2] + p2[...]
+    out[2:4] = own[2:4] + m2[...]
+
+
+def add_early(own, p2, m2):
+    _, count, rows, cols = own.shape
+
+    def spec(lead):
+        return pl.BlockSpec((lead, 1, rows, cols), lambda g: (0, g, 0, 0))
+
+    return pl.pallas_call(
+        early_kernel,
+        grid=(count,),
+        in_specs=[spec(4), spec(2), spec(2)],
+        out_specs=spec(4),
+        out_shape=jax.ShapeDtypeStruct(own.shape, jnp.float32),
+        compiler_params=pltpu.CompilerParams(vmem_limit_bytes=VMEM),
+        cost_estimate=LIGHT,
+        name="add_early",
+    )(own, p2, m2)
+
+
+def last_kernel(own, n1, n2, *outs):
+    outs[0][...] = own[0] + n2[0]
+    outs[1][...] = own[1] + n2[1]
+    outs[2][...] = own[2] + n1[0]
+    outs[3][...] = own[3] + n1[1]
+
+
+def add_last(own, n1, n2):
+    _, count, rows, cols = own.shape
+    step = 1 if count % 2 else 2
+
+    def spec(lead):
+        return pl.BlockSpec((lead, step, rows, cols), lambda g: (0, g, 0, 0))
+
+    return pl.pallas_call(
+        last_kernel,
+        grid=(count // step,),
+        in_specs=[spec(4), spec(2), spec(2)],
+        out_specs=[pl.BlockSpec((step, rows, cols), lambda g: (g, 0, 0))] * 4,
+        out_shape=[jax.ShapeDtypeStruct((count, rows, cols), jnp.float32)] * 4,
+        compiler_params=pltpu.CompilerParams(vmem_limit_bytes=VMEM),
+        cost_estimate=LIGHT,
+        name="add_last",
+    )(own, n1, n2)
+
+
 def sum_kernel(a, b, c, d, out):
     out[...] = (a[...] + b[...]) + (c[...] + d[...])
 
@@ -277,7 +326,7 @@
     late_far, late_near = to_neighbours(late_far_p, late_far_m), to_neighbours(late_near_p, late_near_m)
     late_handed = to_neighbours(*add_far(late_up, late_down, *late_far, []))
     sums = across(add_own(own, *near, *handed, late_handed))
-    late_sums = across(add_own(late_own, *late_near, *late_handed, []))
+    late_sums = across(add_last(add_early(late_own, *late_handed), *late_near))
     origin = jnp.stack([ob * out_rows, vb * cols]).astype(jnp.int32)
     return finish([add_parts(sums), *late_sums], row_sizes, origin, irreps)
 

time: 188 us -> 189 us (level)
  starting transfers between devices: 31.2 us -> 33.9 us
  waiting for transfers between devices: 88.3 us -> 86.1 us
    ppermute x12, starting transfers between devices: 11.5 us -> 14.1 us  [to_neighbours(): return (lax.ppermute(p, BOTH, NEAR[1]), lax.ppermute(m, BOTH, NEAR[-1]))]
    pallas_call x0 -> x2, Pallas kernels: none -> 2.46 us  [the longest x1 1.65 us: add_last(): pl.pallas_call(last_kernel, grid=(count // step,), in_specs=[spec(4), spe...]
  transfers between devices with their start and end apart: 32 -> 32, of which waited for: 17 -> 15; matrix products, arithmetic and copies ran while one was open for 1% -> 1% of each run, Pallas kernels for 15% -> 15%
where the time goes in v16:
time: 189 us
  waiting for transfers between devices  86.1 us (46%)
  starting transfers between devices  33.9 us (18%)
  blocking collectives  33.8 us (18%)
  Pallas kernels  30.4 us (16%)
  local copies, waits for them, and re-layouts  3.98 us (2%)
    ppermute x12, waiting for transfers between devices, to_neighbours(): return (lax.ppermute(p, BOTH, NEAR[1]), lax.ppermute(m, BOTH, NEAR[-1]))  55 us
    all_to_all x2, blocking collectives, exchange(): part = lax.all_to_all(part, 'ob', split_axis=0, concat_axis=0, tiled=True)  33.8 us
    pallas_call x2, Pallas kernels, product(): pl.pallas_call(functools.partial(product_kernel, first), grid_spec=pltpu....  20.5 us
    ppermute x6, waiting for transfers between devices, along_z(): return [lax.ppermute(held, 'vb', steps) for steps in Z_STEPS]  18.8 us
    ppermute x12, starting transfers between devices, to_neighbours(): return (lax.ppermute(p, BOTH, NEAR[1]), lax.ppermute(m, BOTH, NEAR[-1]))  14.1 us
    ppermute x6, waiting for transfers between devices, across(): lax.ppermute(four[k], BOTH, FAR[d])  12 us
    ppermute x6, starting transfers between devices, along_z(): return [lax.ppermute(held, 'vb', steps) for steps in Z_STEPS]  9.71 us
    ppermute x6, starting transfers between devices, across(): lax.ppermute(four[k], BOTH, FAR[d])  8.34 us
  transfers between devices with their start and end apart: 32, of which 15 were waited for; matrix products, arithmetic and copies ran while one was open for 1% of the time, Pallas kernels for 15%

profile of v16, /device:TPU:0, one launch (start us, length us, event | category | flops | bytes accessed | tf_op | source)
XLA Modules:
  0.0 188.6 jit_solution(15709865509603604204)
XLA Ops:
  0.0 1.9 fusion
  2.4 19.1 %all_to_all.10 = f32[16,24,384]{2,1,0:T(8,128)S(1)} all-to-all(f32[16,24,384]{2,1,0:T(8,128)S(1)} %copy.10), channel_id=1, replica_groups=mesh['vb'=8,'ob'=16] {'ob'}, dimensions={0} | all-to-all | bytes 1179648 | tf_op jit(solution)/shard_map/all_to_all | solution.py:289
  21.7 4.0 %collective-permute-start.5 = (f32[4,96,384]{2,1,0:T(8,128)S(1)}, f32[4,96,384]{2,1,0:T(8,128)S(1)}, u32[]{:S(2)}, u32[]{:S(2)}) collective-permute-start(f32[4,96,384]{2,1,0:T(8,128)S(1)} %bitcast.21), channel_id=1, source_target_pairs={{0,64},{16,80},{32,96},{48,112},{64,0},{80,16},{96,32},{112,48},{1... | collective-permute-start | bytes 1769480 | tf_op jit(solution)/shard_map/ppermute | solution.py:298
  25.7 0.7 collective-permute-start.3
  26.4 1.3 collective-permute-start.1
  28.2 14.7 %all_to_all.11 = f32[16,24,384]{2,1,0:T(8,128)S(1)} all-to-all(f32[16,24,384]{2,1,0:T(8,128)S(1)} %copy.12), channel_id=1, replica_groups=mesh['vb'=8,'ob'=16] {'ob'}, dimensions={0} | all-to-all | bytes 1179648 | tf_op jit(solution)/shard_map/all_to_all | solution.py:289
  43.2 0.5 collective-permute-start
  43.8 7.1 %collective-permute-done.3.refs_4_.refs_2_ = f32[4,96,384]{2,1,0:T(8,128)S(1)} collective-permute-done((f32[4,96,384]{2,1,0:T(8,128)S(1)}, f32[4,96,384]{2,1,0:T(8,128)S(1)}, u32[]{:S(2)}, u32[]{:S(2)}) %collective-permute-start.3) | collective-permute-done | bytes 589856 | tf_op jit(solution)/shard_map/ppermute | solution.py:298
  50.9 0.5 collective-permute-start.2
  51.5 0.7 dynamic-slice_bitcast_fusion.place
  52.2 1.7 collective-permute-start.14
  53.9 1.7 collective-permute-start.13
  55.6 11.4 %product.2 = (f32[2,4,48,768]{3,2,1,0:T(8,128)S(1)}, f32[2,4,48,768]{3,2,1,0:T(8,128)S(1)}, f32[2,4,48,768]{3,2,1,0:T(8,128)S(1)}, f32[2,4,48,768]{3,2,1,0:T(8,1...) custom-call(s32[16]{0:T(128)S(1)} %dynamic-slice_bitcast_fusion.place, ...), custom_call_target="tpu_custom_call" | custom-call | tf_op jit(solution)/shard_map/product/pallas_call | solution.py:91
  67.0 1.2 collective-permute-start.11
  68.3 0.8 collective-permute-start.10
  69.5 0.6 collective-permute-done.14.refs_1_
  70.1 9.9 %collective-permute-done.13.refs_0_ = f32[4,96,384]{2,1,0:T(8,128)S(1)} collective-permute-done((f32[4,96,384]{2,1,0:T(8,128)S(1)}, f32[4,96,384]{2,1,0:T(8,128)S(1)}, u32[]{:S(2)}, u32[]{:S(2)}) %collective-permute-start.13) | collective-permute-done | bytes 589856 | tf_op jit(solution)/shard_map/ppermute | solution.py:298
  79.9 0.5 collective-permute-start.17
  80.4 1.3 collective-permute-done.12.refs_0_
  81.9 1.3 collective-permute-done.11.refs_2_.recv_m
  83.3 2.4 %collective-permute-done.10.refs_1_.recv_p = f32[2,4,48,768]{3,2,1,0:T(8,128)S(1)} collective-permute-done((f32[2,4,48,768]{3,2,1,0:T(8,128)S(1)}, f32[2,4,48,768]{3,2,1,0:T(8,128)S(1)}, u32[]{:S(2)}, u32[]{:S(2)}) %collective-permute-start.10) | collective-permute-done | bytes 1179680 | tf_op jit(solution)/shard_map/ppermute | solution.py:305
  85.7 3.2 %collective-permute-start.9 = (f32[2,4,48,768]{3,2,1,0:T(8,128)S(1)}, f32[2,4,48,768]{3,2,1,0:T(8,128)S(1)}, u32[]{:S(2)}, u32[]{:S(2)}) collective-permute-start(f32[2,4,48,768]{3,2,1,0:T(8,128)S(1)} %get-tuple-element.35), channel_id=1, source_target_pairs={{0,12},{1,13},{2,14},{3,15},{4,0},{5,1},{6,2},{7,3},{8,4},{9,5},{1... | collective-permute-start | bytes 3538952 | tf_op jit(solution)/shard_map/ppermute | solution.py:305
  89.0 9.0 %product.3 = (f32[2,4,48,768]{3,2,1,0:T(8,128)S(1)}, f32[2,4,48,768]{3,2,1,0:T(8,128)S(1)}, f32[2,4,48,768]{3,2,1,0:T(8,128)S(1)}, f32[2,4,48,768]{3,2,1,0:T(8,1...) custom-call(s32[16]{0:T(128)S(1)} %dynamic-slice_bitcast_fusion.place, ...), custom_call_target="tpu_custom_call" | custom-call | tf_op jit(solution)/shard_map/product/pallas_call | solution.py:91
  98.1 2.0 %collective-permute-start.20 = (f32[2,4,48,768]{3,2,1,0:T(8,128)S(1)}, f32[2,4,48,768]{3,2,1,0:T(8,128)S(1)}, u32[]{:S(2)}, u32[]{:S(2)}) collective-permute-start(f32[2,4,48,768]{3,2,1,0:T(8,128)S(1)} %get-tuple-element.42.refs_0_), channel_id=1, source_target_pairs={{0,4},{1,5},{2,6},{3,7},{4,8},{5,9},{6,10},{7,11},{8,12},{9,13},{1... | collective-permute-start | bytes 3538952 | tf_op jit(solution)/shard_map/ppermute | solution.py:305
  100.1 3.0 %collective-permute-done.8.refs_1_.n1 = f32[2,4,48,768]{3,2,1,0:T(8,128)S(1)} collective-permute-done((f32[2,4,48,768]{3,2,1,0:T(8,128)S(1)}, f32[2,4,48,768]{3,2,1,0:T(8,128)S(1)}, u32[]{:S(2)}, u32[]{:S(2)}) %collective-permute-start.8) | collective-permute-done | bytes 1179680 | tf_op jit(solution)/shard_map/ppermute | solution.py:305
  103.1 0.8 add_far.2
  104.0 3.3 %collective-permute-start.19 = (f32[2,4,48,768]{3,2,1,0:T(8,128)S(1)}, f32[2,4,48,768]{3,2,1,0:T(8,128)S(1)}, u32[]{:S(2)}, u32[]{:S(2)}) collective-permute-start(f32[2,4,48,768]{3,2,1,0:T(8,128)S(1)} %get-tuple-element.44), channel_id=1, source_target_pairs={{0,12},{1,13},{2,14},{3,15},{4,0},{5,1},{6,2},{7,3},{8,4},{9,5},{1... | collective-permute-start | bytes 3538952 | tf_op jit(solution)/shard_map/ppermute | solution.py:305
  107.3 8.0 %collective-permute-done.21.recv_m = f32[2,4,48,768]{3,2,1,0:T(8,128)S(1)} collective-permute-done((f32[2,4,48,768]{3,2,1,0:T(8,128)S(1)}, f32[2,4,48,768]{3,2,1,0:T(8,128)S(1)}, u32[]{:S(2)}, u32[]{:S(2)}) %collective-permute-start.21) | collective-permute-done | bytes 1179680 | tf_op jit(solution)/shard_map/ppermute | solution.py:305
  115.3 0.5 collective-permute-done.20.recv_p
  115.8 0.8 add_far.3
  116.5 0.6 collective-permute-start.22
  117.2 2.8 %collective-permute-start.23 = (f32[2,4,48,768]{3,2,1,0:T(8,128)S(1)}, f32[2,4,48,768]{3,2,1,0:T(8,128)S(1)}, u32[]{:S(2)}, u32[]{:S(2)}) collective-permute-start(f32[2,4,48,768]{3,2,1,0:T(8,128)S(1)} %get-tuple-element.49), channel_id=1, source_target_pairs={{0,12},{1,13},{2,14},{3,15},{4,0},{5,1},{6,2},{7,3},{8,4},{9,5},{1... | collective-permute-start | bytes 3538952 | tf_op jit(solution)/shard_map/ppermute | solution.py:305
  119.9 8.5 %collective-permute-done.18.p2 = f32[2,4,48,768]{3,2,1,0:T(8,128)S(1)} collective-permute-done((f32[2,4,48,768]{3,2,1,0:T(8,128)S(1)}, f32[2,4,48,768]{3,2,1,0:T(8,128)S(1)}, u32[]{:S(2)}, u32[]{:S(2)}) %collective-permute-start.18) | collective-permute-done | bytes 1179680 | tf_op jit(solution)/shard_map/ppermute | solution.py:305
  128.4 12.6 %collective-permute-done.22.refs_0_.p2 = f32[2,4,48,768]{3,2,1,0:T(8,128)S(1)} collective-permute-done((f32[2,4,48,768]{3,2,1,0:T(8,128)S(1)}, f32[2,4,48,768]{3,2,1,0:T(8,128)S(1)}, u32[]{:S(2)}, u32[]{:S(2)}) %collective-permute-start.22) | collective-permute-done | bytes 1179680 | tf_op jit(solution)/shard_map/ppermute | solution.py:305
  141.0 1.7 add_own.1
  142.7 0.5 collective-permute-start.24
  143.2 2.1 %collective-permute-start.25 = (f32[4,48,768]{2,1,0:T(8,128)}, f32[4,48,768]{2,1,0:T(8,128)}, u32[]{:S(2)}, u32[]{:S(2)}) collective-permute-start(f32[4,48,768]{2,1,0:T(8,128)} %get-tuple-element.52), channel_id=1, source_target_pairs={{0,2},{1,3},{2,0},{3,1},{4,6},{5,7},{6,4},{7,5},{8,10},{9,11},{10,... | collective-permute-start | bytes 1769480 | tf_op jit(solution)/shard_map/ppermute | solution.py:308
  145.4 1.5 collective-permute-start.26
  146.9 0.8 add_early.1.own
  147.7 18.6 %collective-permute-done.27.n1 = f32[2,4,48,768]{3,2,1,0:T(8,128)S(1)} collective-permute-done((f32[2,4,48,768]{3,2,1,0:T(8,128)S(1)}, f32[2,4,48,768]{3,2,1,0:T(8,128)S(1)}, u32[]{:S(2)}, u32[]{:S(2)}) %collective-permute-start.27) | collective-permute-done | bytes 1179680 | tf_op jit(solution)/shard_map/ppermute | solution.py:305
  166.3 1.6 add_last.1
  168.0 0.5 collective-permute-start.29
  168.5 1.5 collective-permute-start.30
  170.0 2.1 %collective-permute-start.31 = (f32[4,48,768]{2,1,0:T(8,128)}, f32[4,48,768]{2,1,0:T(8,128)S(1)}, u32[]{:S(2)}, u32[]{:S(2)}) collective-permute-start(f32[4,48,768]{2,1,0:T(8,128)} %get-tuple-element.60), channel_id=1, source_target_pairs={{0,3},{1,0},{2,1},{3,2},{4,7},{5,4},{6,5},{7,6},{8,11},{9,8},{10,9... | collective-permute-start | bytes 1769480 | tf_op jit(solution)/shard_map/ppermute | solution.py:308
  172.2 2.2 %add_parts.1.refs_0_ = f32[4,48,768]{2,1,0:T(8,128)S(1)} custom-call(f32[4,48,768]{2,1,0:T(8,128)S(1)} %get-tuple-element.50.a, f32[4,48,768]{2,1,0:T(8,128)S(1)} %collective-permute-done.24.b, f32[4,48,768]{2,1,0:T(8,128)} %collective-permute-done.25.c, f32[4,48,768]{2,1,0:T(8,128)} %collective-permute-done.26.d), custom_call_target="tpu_custom_call" | custom-call | tf_op jit(solution)/shard_map/add_parts/pallas_call | solution.py:234
  174.5 11.1 %collective-permute-done.29.refs_2_ = f32[4,48,768]{2,1,0:T(8,128)S(1)} collective-permute-done((f32[4,48,768]{2,1,0:T(8,128)}, f32[4,48,768]{2,1,0:T(8,128)S(1)}, u32[]{:S(2)}, u32[]{:S(2)}) %collective-permute-start.29) | collective-permute-done | bytes 589856 | tf_op jit(solution)/shard_map/ppermute | solution.py:308
  185.6 0.9 collective-permute-done.31.refs_4_
  186.5 2.0 %finish.1 = f32[48,8,768]{2,1,0:T(8,128)} custom-call(s32[8]{0:T(128)S(1)} %copy-done.2, s32[2]{0:T(128)S(1)} %pad_add_fusion.origin, f32[4,48,768]{2,1,0:T(8,128)S(1)} %add_parts.1.refs_0_, f32[4,48,768]{2,1,0:T(8,128)S(1)} %get-tuple-element.57.refs_1_, f32[4,48,768]{2,1,0:T(8,128)S(1)} %collective-permute-done.29.refs_2_, ...), custom_call_target="tpu_custom_call" | custom-call | tf_op jit(solution)/shard_map/finish/pallas_call | solution.py:260
  (55 shorter events, 2.6 us)
Async XLA Ops:
  21.7 22.0 %collective-permute-start.5 = (f32[4,96,384]{2,1,0:T(8,128)S(1)}, f32[4,96,384]{2,1,0:T(8,128)S(1)}, u32[]{:S(2)}, u32[]{:S(2)}) collective-permute-start(f32[4,96,384]{2,1,0:T(8,128)S(1)} %bitcast.21), channel_id=1, source_target_pairs={{0,64},{16,80},{32,96},{48,112},{64,0},{80,16},{96,32},{112,48},{1... | collective-permute-start | bytes 1769480 | tf_op jit(solution)/shard_map/ppermute | solution.py:298
  25.7 25.2 %collective-permute-start.3 = (f32[4,96,384]{2,1,0:T(8,128)S(1)}, f32[4,96,384]{2,1,0:T(8,128)S(1)}, u32[]{:S(2)}, u32[]{:S(2)}) collective-permute-start(f32[4,96,384]{2,1,0:T(8,128)S(1)} %bitcast.22), channel_id=1, source_target_pairs={{0,96},{16,48},{32,0},{48,80},{64,32},{80,112},{96,64},{112,16},{1... | collective-permute-start | bytes 1769480 | tf_op jit(solution)/shard_map/ppermute | solution.py:298
  26.4 24.5 %collective-permute-start.1 = (f32[4,96,384]{2,1,0:T(8,128)S(1)}, f32[4,96,384]{2,1,0:T(8,128)}, u32[]{:S(2)}, u32[]{:S(2)}) collective-permute-start(f32[4,96,384]{2,1,0:T(8,128)S(1)} %bitcast.23), channel_id=1, source_target_pairs={{0,32},{16,112},{32,64},{48,16},{64,96},{80,48},{96,0},{112,80},{1... | collective-permute-start | bytes 1769480 | tf_op jit(solution)/shard_map/ppermute | solution.py:298
  43.1 9.1 %collective-permute-start.7 = (f32[4,96,384]{2,1,0:T(8,128)S(1)}, f32[4,96,384]{2,1,0:T(8,128)S(1)}, u32[]{:S(2)}, u32[]{:S(2)}) collective-permute-start(f32[4,96,384]{2,1,0:T(8,128)S(1)} %bitcast.19), channel_id=1, source_target_pairs={{0,16},{16,0},{32,48},{48,32},{64,80},{80,64},{96,112},{112,96},{1... | collective-permute-start | bytes 1769480 | tf_op jit(solution)/shard_map/ppermute | solution.py:295
  43.2 10.7 %collective-permute-start = (f32[4,96,384]{2,1,0:T(8,128)S(1)}, f32[4,96,384]{2,1,0:T(8,128)}, u32[]{:S(2)}, u32[]{:S(2)}) collective-permute-start(f32[4,96,384]{2,1,0:T(8,128)S(1)} %bitcast.24), channel_id=1, source_target_pairs={{0,16},{16,0},{32,48},{48,32},{64,80},{80,64},{96,112},{112,96},{1... | collective-permute-start | bytes 1769480 | tf_op jit(solution)/shard_map/ppermute | solution.py:295
  43.7 11.9 %collective-permute-start.6 = (f32[4,96,384]{2,1,0:T(8,128)S(1)}, f32[4,96,384]{2,1,0:T(8,128)}, u32[]{:S(2)}, u32[]{:S(2)}) collective-permute-start(f32[4,96,384]{2,1,0:T(8,128)S(1)} %collective-permute-done.5.refs_6_.refs_3_), channel_id=1, source_target_pairs={{0,16},{16,0},{32,48},{48,32},{64,80},{80,64},{96,112},{112,96},{1... | collective-permute-start | bytes 1769480 | tf_op jit(solution)/shard_map/ppermute | solution.py:295
  50.9 4.7 %collective-permute-start.4 = (f32[4,96,384]{2,1,0:T(8,128)S(1)}, f32[4,96,384]{2,1,0:T(8,128)}, u32[]{:S(2)}, u32[]{:S(2)}) collective-permute-start(f32[4,96,384]{2,1,0:T(8,128)S(1)} %collective-permute-done.3.refs_4_.refs_2_), channel_id=1, source_target_pairs={{0,16},{16,0},{32,48},{48,32},{64,80},{80,64},{96,112},{112,96},{1... | collective-permute-start | bytes 1769480 | tf_op jit(solution)/shard_map/ppermute | solution.py:295
  50.9 4.7 %collective-permute-start.2 = (f32[4,96,384]{2,1,0:T(8,128)}, f32[4,96,384]{2,1,0:T(8,128)}, u32[]{:S(2)}, u32[]{:S(2)}) collective-permute-start(f32[4,96,384]{2,1,0:T(8,128)} %collective-permute-done.1.refs_2_.refs_1_), channel_id=1, source_target_pairs={{0,16},{16,0},{32,48},{48,32},{64,80},{80,64},{96,112},{112,96},{1... | collective-permute-start | bytes 1769480 | tf_op jit(solution)/shard_map/ppermute | solution.py:295
  52.2 3.4 %copy-start.1 = (s32[8]{0:T(128)S(1)}, s32[8]{0:T(128)}, u32[]{:S(2)}) copy-start(s32[8]{0:T(128)} %sizes.4) | copy-start | bytes 100
  52.2 36.7 %slice-start = ((s8[9437184]{0:T(1024)(128)(4,1)}), s8[4194304]{0:T(1024)(128)(4,1)S(1)}, s32[]{:S(2)}) async-start(s8[9437184]{0:T(1024)(128)(4,1)} %bitcast.17), calls=%async_computation.2 | async-start | bytes 8388608
  52.2 36.7 %slice-start.1 = ((s8[9437184]{0:T(1024)(128)(4,1)}), s8[4194304]{0:T(1024)(128)(4,1)S(1)}, s32[]{:S(2)}) async-start(s8[9437184]{0:T(1024)(128)(4,1)} %bitcast.17), calls=%async_computation.3 | async-start | bytes 8388608
  52.2 36.7 %slice-start.2 = ((s8[9437184]{0:T(1024)(128)(4,1)}), s8[1048576]{0:T(1024)(128)(4,1)S(1)}, s32[]{:S(2)}) async-start(s8[9437184]{0:T(1024)(128)(4,1)} %bitcast.17), calls=%async_computation.4 | async-start | bytes 2097152
  52.2 17.8 %collective-permute-start.14 = (f32[4,96,384]{2,1,0:T(8,128)S(1)}, f32[4,96,384]{2,1,0:T(8,128)S(1)}, u32[]{:S(2)}, u32[]{:S(2)}) collective-permute-start(f32[4,96,384]{2,1,0:T(8,128)S(1)} %tie.3.refs_0_), channel_id=1, source_target_pairs={{0,64},{16,80},{32,96},{48,112},{64,0},{80,16},{96,32},{112,48},{1... | collective-permute-start | bytes 1769480 | tf_op jit(solution)/shard_map/ppermute | solution.py:298
  53.9 26.0 %collective-permute-start.13 = (f32[4,96,384]{2,1,0:T(8,128)S(1)}, f32[4,96,384]{2,1,0:T(8,128)S(1)}, u32[]{:S(2)}, u32[]{:S(2)}) collective-permute-start(f32[4,96,384]{2,1,0:T(8,128)S(1)} %tie.3.refs_0_), channel_id=1, source_target_pairs={{0,96},{16,48},{32,0},{48,80},{64,32},{80,112},{96,64},{112,16},{1... | collective-permute-start | bytes 1769480 | tf_op jit(solution)/shard_map/ppermute | solution.py:298
  67.0 16.2 %collective-permute-start.11 = (f32[2,4,48,768]{3,2,1,0:T(8,128)S(1)}, f32[2,4,48,768]{3,2,1,0:T(8,128)S(1)}, u32[]{:S(2)}, u32[]{:S(2)}) collective-permute-start(f32[2,4,48,768]{3,2,1,0:T(8,128)S(1)} %get-tuple-element.39), channel_id=1, source_target_pairs={{0,12},{1,13},{2,14},{3,15},{4,0},{5,1},{6,2},{7,3},{8,4},{9,5},{1... | collective-permute-start | bytes 3538952 | tf_op jit(solution)/shard_map/ppermute | solution.py:305
  68.3 17.4 %collective-permute-start.10 = (f32[2,4,48,768]{3,2,1,0:T(8,128)S(1)}, f32[2,4,48,768]{3,2,1,0:T(8,128)S(1)}, u32[]{:S(2)}, u32[]{:S(2)}) collective-permute-start(f32[2,4,48,768]{3,2,1,0:T(8,128)S(1)} %get-tuple-element.38.refs_2_), channel_id=1, source_target_pairs={{0,4},{1,5},{2,6},{3,7},{4,8},{5,9},{6,10},{7,11},{8,12},{9,13},{1... | collective-permute-start | bytes 3538952 | tf_op jit(solution)/shard_map/ppermute | solution.py:305
  69.1 12.6 %collective-permute-start.12 = (f32[4,96,384]{2,1,0:T(8,128)S(1)}, f32[4,96,384]{2,1,0:T(8,128)S(1)}, u32[]{:S(2)}, u32[]{:S(2)}) collective-permute-start(f32[4,96,384]{2,1,0:T(8,128)S(1)} %tie.3.refs_0_), channel_id=1, source_target_pairs={{0,32},{16,112},{32,64},{48,16},{64,96},{80,48},{96,0},{112,80},{1... | collective-permute-start | bytes 1769480 | tf_op jit(solution)/shard_map/ppermute | solution.py:298
  79.9 2.0 %collective-permute-start.15 = (f32[4,96,384]{2,1,0:T(8,128)S(1)}, f32[4,96,384]{2,1,0:T(8,128)S(1)}, u32[]{:S(2)}, u32[]{:S(2)}) collective-permute-start(f32[4,96,384]{2,1,0:T(8,128)S(1)} %get-tuple-element.40.refs_4_), channel_id=1, source_target_pairs={{0,16},{16,0},{32,48},{48,32},{64,80},{80,64},{96,112},{112,96},{1... | collective-permute-start | bytes 1769480 | tf_op jit(solution)/shard_map/ppermute | solution.py:295
  79.9 9.0 %collective-permute-start.17 = (f32[4,96,384]{2,1,0:T(8,128)S(1)}, f32[4,96,384]{2,1,0:T(8,128)S(1)}, u32[]{:S(2)}, u32[]{:S(2)}) collective-permute-start(f32[4,96,384]{2,1,0:T(8,128)S(1)} %get-tuple-element.41.refs_6_), channel_id=1, source_target_pairs={{0,16},{16,0},{32,48},{48,32},{64,80},{80,64},{96,112},{112,96},{1... | collective-permute-start | bytes 1769480 | tf_op jit(solution)/shard_map/ppermute | solution.py:295
  85.7 3.2 %collective-permute-start.16 = (f32[4,96,384]{2,1,0:T(8,128)S(1)}, f32[4,96,384]{2,1,0:T(8,128)S(1)}, u32[]{:S(2)}, u32[]{:S(2)}) collective-permute-start(f32[4,96,384]{2,1,0:T(8,128)S(1)} %tie.5.refs_2_), channel_id=1, source_target_pairs={{0,16},{16,0},{32,48},{48,32},{64,80},{80,64},{96,112},{112,96},{1... | collective-permute-start | bytes 1769480 | tf_op jit(solution)/shard_map/ppermute | solution.py:295
  85.7 17.4 %collective-permute-start.8 = (f32[2,4,48,768]{3,2,1,0:T(8,128)S(1)}, f32[2,4,48,768]{3,2,1,0:T(8,128)S(1)}, u32[]{:S(2)}, u32[]{:S(2)}) collective-permute-start(f32[2,4,48,768]{3,2,1,0:T(8,128)S(1)} %get-tuple-element.34), channel_id=1, source_target_pairs={{0,4},{1,5},{2,6},{3,7},{4,8},{5,9},{6,10},{7,11},{8,12},{9,13},{1... | collective-permute-start | bytes 3538952 | tf_op jit(solution)/shard_map/ppermute | solution.py:305
  85.7 17.4 %collective-permute-start.9 = (f32[2,4,48,768]{3,2,1,0:T(8,128)S(1)}, f32[2,4,48,768]{3,2,1,0:T(8,128)S(1)}, u32[]{:S(2)}, u32[]{:S(2)}) collective-permute-start(f32[2,4,48,768]{3,2,1,0:T(8,128)S(1)} %get-tuple-element.35), channel_id=1, source_target_pairs={{0,12},{1,13},{2,14},{3,15},{4,0},{5,1},{6,2},{7,3},{8,4},{9,5},{1... | collective-permute-start | bytes 3538952 | tf_op jit(solution)/shard_map/ppermute | solution.py:305
  98.0 17.3 %collective-permute-start.21 = (f32[2,4,48,768]{3,2,1,0:T(8,128)S(1)}, f32[2,4,48,768]{3,2,1,0:T(8,128)S(1)}, u32[]{:S(2)}, u32[]{:S(2)}) collective-permute-start(f32[2,4,48,768]{3,2,1,0:T(8,128)S(1)} %get-tuple-element.47), channel_id=1, source_target_pairs={{0,12},{1,13},{2,14},{3,15},{4,0},{5,1},{6,2},{7,3},{8,4},{9,5},{1... | collective-permute-start | bytes 3538952 | tf_op jit(solution)/shard_map/ppermute | solution.py:305
  98.1 17.7 %collective-permute-start.20 = (f32[2,4,48,768]{3,2,1,0:T(8,128)S(1)}, f32[2,4,48,768]{3,2,1,0:T(8,128)S(1)}, u32[]{:S(2)}, u32[]{:S(2)}) collective-permute-start(f32[2,4,48,768]{3,2,1,0:T(8,128)S(1)} %get-tuple-element.42.refs_0_), channel_id=1, source_target_pairs={{0,4},{1,5},{2,6},{3,7},{4,8},{5,9},{6,10},{7,11},{8,12},{9,13},{1... | collective-permute-start | bytes 3538952 | tf_op jit(solution)/shard_map/ppermute | solution.py:305
  103.9 24.5 %collective-permute-start.18 = (f32[2,4,48,768]{3,2,1,0:T(8,128)S(1)}, f32[2,4,48,768]{3,2,1,0:T(8,128)S(1)}, u32[]{:S(2)}, u32[]{:S(2)}) collective-permute-start(f32[2,4,48,768]{3,2,1,0:T(8,128)S(1)} %get-tuple-element.43), channel_id=1, source_target_pairs={{0,4},{1,5},{2,6},{3,7},{4,8},{5,9},{6,10},{7,11},{8,12},{9,13},{1... | collective-permute-start | bytes 3538952 | tf_op jit(solution)/shard_map/ppermute | solution.py:305
  104.0 24.4 %collective-permute-start.19 = (f32[2,4,48,768]{3,2,1,0:T(8,128)S(1)}, f32[2,4,48,768]{3,2,1,0:T(8,128)S(1)}, u32[]{:S(2)}, u32[]{:S(2)}) collective-permute-start(f32[2,4,48,768]{3,2,1,0:T(8,128)S(1)} %get-tuple-element.44), channel_id=1, source_target_pairs={{0,12},{1,13},{2,14},{3,15},{4,0},{5,1},{6,2},{7,3},{8,4},{9,5},{1... | collective-permute-start | bytes 3538952 | tf_op jit(solution)/shard_map/ppermute | solution.py:305
  115.8 25.3 %copy-start = (f32[4,4,48,768]{3,2,1,0:T(8,128)S(1)}, f32[4,4,48,768]{3,2,1,0:T(8,128)}, u32[]{:S(2)}) copy-start(f32[4,4,48,768]{3,2,1,0:T(8,128)} %get-tuple-element.33.own) | copy-start | bytes 7077892
  116.5 24.5 %collective-permute-start.22 = (f32[2,4,48,768]{3,2,1,0:T(8,128)S(1)}, f32[2,4,48,768]{3,2,1,0:T(8,128)S(1)}, u32[]{:S(2)}, u32[]{:S(2)}) collective-permute-start(f32[2,4,48,768]{3,2,1,0:T(8,128)S(1)} %get-tuple-element.48), channel_id=1, source_target_pairs={{0,4},{1,5},{2,6},{3,7},{4,8},{5,9},{6,10},{7,11},{8,12},{9,13},{1... | collective-permute-start | bytes 3538952 | tf_op jit(solution)/shard_map/ppermute | solution.py:305
  117.2 23.9 %collective-permute-start.23 = (f32[2,4,48,768]{3,2,1,0:T(8,128)S(1)}, f32[2,4,48,768]{3,2,1,0:T(8,128)S(1)}, u32[]{:S(2)}, u32[]{:S(2)}) collective-permute-start(f32[2,4,48,768]{3,2,1,0:T(8,128)S(1)} %get-tuple-element.49), channel_id=1, source_target_pairs={{0,12},{1,13},{2,14},{3,15},{4,0},{5,1},{6,2},{7,3},{8,4},{9,5},{1... | collective-permute-start | bytes 3538952 | tf_op jit(solution)/shard_map/ppermute | solution.py:305
  119.9 46.4 %collective-permute-start.27 = (f32[2,4,48,768]{3,2,1,0:T(8,128)S(1)}, f32[2,4,48,768]{3,2,1,0:T(8,128)S(1)}, u32[]{:S(2)}, u32[]{:S(2)}) collective-permute-start(f32[2,4,48,768]{3,2,1,0:T(8,128)S(1)} %get-tuple-element.55), channel_id=1, source_target_pairs={{0,4},{1,5},{2,6},{3,7},{4,8},{5,9},{6,10},{7,11},{8,12},{9,13},{1... | collective-permute-start | bytes 3538952 | tf_op jit(solution)/shard_map/ppermute | solution.py:305
  128.4 37.9 %collective-permute-start.28 = (f32[2,4,48,768]{3,2,1,0:T(8,128)S(1)}, f32[2,4,48,768]{3,2,1,0:T(8,128)S(1)}, u32[]{:S(2)}, u32[]{:S(2)}) collective-permute-start(f32[2,4,48,768]{3,2,1,0:T(8,128)S(1)} %get-tuple-element.56), channel_id=1, source_target_pairs={{0,12},{1,13},{2,14},{3,15},{4,0},{5,1},{6,2},{7,3},{8,4},{9,5},{1... | collective-permute-start | bytes 3538952 | tf_op jit(solution)/shard_map/ppermute | solution.py:305
  142.7 27.3 %collective-permute-start.24 = (f32[4,48,768]{2,1,0:T(8,128)S(1)}, f32[4,48,768]{2,1,0:T(8,128)S(1)}, u32[]{:S(2)}, u32[]{:S(2)}) collective-permute-start(f32[4,48,768]{2,1,0:T(8,128)S(1)} %get-tuple-element.51), channel_id=1, source_target_pairs={{0,1},{1,2},{2,3},{3,0},{4,5},{5,6},{6,7},{7,4},{8,9},{9,10},{10,1... | collective-permute-start | bytes 1769480 | tf_op jit(solution)/shard_map/ppermute | solution.py:308
  143.2 29.0 %collective-permute-start.25 = (f32[4,48,768]{2,1,0:T(8,128)}, f32[4,48,768]{2,1,0:T(8,128)}, u32[]{:S(2)}, u32[]{:S(2)}) collective-permute-start(f32[4,48,768]{2,1,0:T(8,128)} %get-tuple-element.52), channel_id=1, source_target_pairs={{0,2},{1,3},{2,0},{3,1},{4,6},{5,7},{6,4},{7,5},{8,10},{9,11},{10,... | collective-permute-start | bytes 1769480 | tf_op jit(solution)/shard_map/ppermute | solution.py:308
  145.4 26.8 %collective-permute-start.26 = (f32[4,48,768]{2,1,0:T(8,128)}, f32[4,48,768]{2,1,0:T(8,128)}, u32[]{:S(2)}, u32[]{:S(2)}) collective-permute-start(f32[4,48,768]{2,1,0:T(8,128)} %get-tuple-element.53), channel_id=1, source_target_pairs={{0,3},{1,0},{2,1},{3,2},{4,7},{5,4},{6,5},{7,6},{8,11},{9,8},{10,9... | collective-permute-start | bytes 1769480 | tf_op jit(solution)/shard_map/ppermute | solution.py:308
  168.0 17.6 %collective-permute-start.29 = (f32[4,48,768]{2,1,0:T(8,128)}, f32[4,48,768]{2,1,0:T(8,128)S(1)}, u32[]{:S(2)}, u32[]{:S(2)}) collective-permute-start(f32[4,48,768]{2,1,0:T(8,128)} %get-tuple-element.58), channel_id=1, source_target_pairs={{0,1},{1,2},{2,3},{3,0},{4,5},{5,6},{6,7},{7,4},{8,9},{9,10},{10,1... | collective-permute-start | bytes 1769480 | tf_op jit(solution)/shard_map/ppermute | solution.py:308
  168.5 17.1 %collective-permute-start.30 = (f32[4,48,768]{2,1,0:T(8,128)}, f32[4,48,768]{2,1,0:T(8,128)S(1)}, u32[]{:S(2)}, u32[]{:S(2)}) collective-permute-start(f32[4,48,768]{2,1,0:T(8,128)} %get-tuple-element.59), channel_id=1, source_target_pairs={{0,2},{1,3},{2,0},{3,1},{4,6},{5,7},{6,4},{7,5},{8,10},{9,11},{10,... | collective-permute-start | bytes 1769480 | tf_op jit(solution)/shard_map/ppermute | solution.py:308
  170.0 16.5 %collective-permute-start.31 = (f32[4,48,768]{2,1,0:T(8,128)}, f32[4,48,768]{2,1,0:T(8,128)S(1)}, u32[]{:S(2)}, u32[]{:S(2)}) collective-permute-start(f32[4,48,768]{2,1,0:T(8,128)} %get-tuple-element.60), channel_id=1, source_target_pairs={{0,3},{1,0},{2,1},{3,2},{4,7},{5,4},{6,5},{7,6},{8,11},{9,8},{10,9... | collective-permute-start | bytes 1769480 | tf_op jit(solution)/shard_map/ppermute | solution.py:308
  172.2 14.3 %copy-start.2 = (s32[8]{0:T(128)S(1)}, s32[8]{0:T(128)}, u32[]{:S(2)}) copy-start(s32[8]{0:T(128)} %sizes.5) | copy-start | bytes 100
